TPU v7x, 32 devices: a whole 2x2x4 slice. The times are simulated.
32 devices in a mesh: cuts: 2 (over core), fsdp: 4 (over y, x), tp: 4 (over z).
Axes of the slice: x: 2, y: 2, z: 4, core: 2. Of those that a mesh axis runs over, the one named last changes fastest.
Arguments:
- tokens: bfloat16 [8192, 2048], P(('cuts', 'fsdp')), may hold values from -6 to 6
- cotangent: bfloat16 [8192, 2048], P(('cuts', 'fsdp')), may hold values from -6 to 6
- gate_frozen_matrix: bfloat16 [2048, 4096], P(('cuts', 'fsdp'), 'tp'), may hold values from -0.125 to 0.125
- up_frozen_matrix: bfloat16 [2048, 4096], P(('cuts', 'fsdp'), 'tp'), may hold values from -0.125 to 0.125
- down_frozen_matrix: bfloat16 [4096, 2048], P('tp', ('cuts', 'fsdp')), may hold values from -0.09375 to 0.09375
- gate_adapter_input_factor: bfloat16 [2048, 64], replicated, may hold values from -0.125 to 0.125
- up_adapter_input_factor: bfloat16 [2048, 64], replicated, may hold values from -0.125 to 0.125
- gate_adapter_output_factor: bfloat16 [64, 4096], P(None, 'tp'), may hold values from -0.75 to 0.75
- up_adapter_output_factor: bfloat16 [64, 4096], P(None, 'tp'), may hold values from -0.75 to 0.75
- down_adapter_input_factor: bfloat16 [4096, 64], P('tp'), may hold values from -0.09375 to 0.09375
- down_leave: bfloat16 [2048, 64], replicated, may hold values from -0.75 to 0.75
Outputs:
- token_input_gradient: bfloat16 [8192, 2048], P(('cuts', 'fsdp'), 'tp')
- wide_grads: float32 [2048, 192], P(('cuts', 'fsdp', 'tp'))
- narrow_grads: float32 [4096, 192], P('tp')
All inputs are finite; a program needn't handle non-finite values.
Results may differ from a plain program's by a relative error of at most 0.0055.
Values may be sent and summed in bfloat16 or wider, within the bound.
No kernel may reach another device: no remote copies, remote signals or barrier semaphores. Data moves between devices by JAX's collectives and lax.ppermute only.
A program may use at most 128 MiB of HBM per device.

v0:
```python
import functools
import math

import jax
import jax.numpy as jnp
from jax import lax
from jax.experimental import pallas as pl
from jax.experimental.pallas import tpu as pltpu
from jax.sharding import PartitionSpec as P

adapter_scaling = 0.5
MEBIBYTE = 1024 * 1024
COST = 20
HALVES = 2
LIMITS = {"first": 14, "next": 10, "last": 18, "token": 8, "adapter": 12, "small": 4}
TILE = 512
STRIP = 256
QUARTER_ORDER = ((3, 2, 1, 0), (0, 3, 2, 1), (3, 0, 1, 2), (0, 1, 2, 3))


def matrix_product(left, right):
    return jnp.dot(left, right, preferred_element_type=jnp.float32)


def contract_trailing_axis(left, right):
    return lax.dot_general(
        left, right, (((1,), (1,)), ((), ())), preferred_element_type=jnp.float32
    )


def contract_first(left, right):
    return lax.dot_general(
        left, right, (((0,), (0,)), ((), ())), preferred_element_type=jnp.float32
    )


def any_plane(
    tokens,
    cotangent,
    gate_frozen_matrix,
    up_frozen_matrix,
    down_frozen_matrix,
    gate_adapter_input_factor,
    up_adapter_input_factor,
    gate_adapter_output_factor,
    up_adapter_output_factor,
    down_adapter_input_factor,
    down_leave,
):
    token_groups = lax.axis_size(("cuts", "fsdp"))
    quarters = lax.axis_size("tp")
    tp_index = lax.axis_index("tp")
    token_rows = tokens.shape[0]
    width = tokens.shape[1]
    gradient_scaling = adapter_scaling / math.sqrt(token_rows * token_groups)
    gate_adapter_hidden = matrix_product(tokens, gate_adapter_input_factor).astype(jnp.bfloat16)
    up_adapter_hidden = matrix_product(tokens, up_adapter_input_factor).astype(jnp.bfloat16)
    pieces = (
        lax.all_gather(gate_frozen_matrix, ("cuts", "fsdp"), axis=0, tiled=True),
        lax.all_gather(up_frozen_matrix, ("cuts", "fsdp"), axis=0, tiled=True),
    )
    columns = tokens
    gate_frozen_output = matrix_product(columns, pieces[0])
    up_frozen_output = matrix_product(columns, pieces[1])
    gate_preactivation = gate_frozen_output + adapter_scaling * matrix_product(
        gate_adapter_hidden, gate_adapter_output_factor
    )
    up_preactivation = up_frozen_output + adapter_scaling * matrix_product(
        up_adapter_hidden, up_adapter_output_factor
    )
    sig = jax.nn.sigmoid(gate_preactivation)
    hidden = (gate_preactivation * sig * up_preactivation).astype(jnp.bfloat16)
    down_part = matrix_product(hidden, down_adapter_input_factor)
    down_low = lax.psum(down_part.astype(jnp.bfloat16), "tp")
    backward_adapter_input = matrix_product(cotangent, down_leave).astype(jnp.bfloat16)
    columns = cotangent
    hidden_state_gradient = contract_trailing_axis(
        columns, lax.all_gather(down_frozen_matrix, ("cuts", "fsdp"), axis=1, tiled=True)
    )
    hidden_state_gradient = hidden_state_gradient + adapter_scaling * contract_trailing_axis(
        backward_adapter_input, down_adapter_input_factor
    )
    gate_output_gradient = (
        hidden_state_gradient * up_preactivation * sig * (1.0 + gate_preactivation * (1.0 - sig))
    ).astype(jnp.bfloat16)
    up_output_gradient = (hidden_state_gradient * gate_preactivation * sig).astype(jnp.bfloat16)
    gate_part = contract_trailing_axis(gate_output_gradient, gate_adapter_output_factor)
    up_part = contract_trailing_axis(up_output_gradient, up_adapter_output_factor)
    gate_sum, up_sum = lax.psum((gate_part, up_part), "tp")
    gate_backward_adapter = gate_sum.astype(jnp.bfloat16)
    up_backward_adapter = up_sum.astype(jnp.bfloat16)
    pieces = lax.all_gather(
        (gate_frozen_matrix, up_frozen_matrix), ("cuts", "fsdp"), axis=0, tiled=True
    )
    partial_value = contract_trailing_axis(
        gate_output_gradient, pieces[0]
    ) + contract_trailing_axis(up_output_gradient, pieces[1])
    frozen_path_gradient = lax.psum_scatter(partial_value, "tp", scatter_dimension=1, tiled=True)
    slice_width = width // quarters
    gate_slice = lax.dynamic_slice_in_dim(
        gate_adapter_input_factor, tp_index * slice_width, slice_width, 0
    )
    up_slice = lax.dynamic_slice_in_dim(
        up_adapter_input_factor, tp_index * slice_width, slice_width, 0
    )
    adapter_hidden_gradient = contract_trailing_axis(
        gate_backward_adapter, gate_slice
    ) + contract_trailing_axis(up_backward_adapter, up_slice)
    token_input_gradient = (
        frozen_path_gradient + adapter_scaling * adapter_hidden_gradient
    ).astype(jnp.bfloat16)
    narrow_part = gradient_scaling * jnp.concatenate(
        [
            contract_first(hidden, backward_adapter_input),
            contract_first(gate_output_gradient, gate_adapter_hidden),
            contract_first(up_output_gradient, up_adapter_hidden),
        ],
        axis=1,
    )
    narrow_grads = lax.psum(narrow_part, ("cuts", "fsdp"))
    token_side = jnp.concatenate([gate_backward_adapter, up_backward_adapter], axis=1)
    group_rows = lax.psum_scatter(
        gradient_scaling
        * jnp.concatenate(
            [contract_first(tokens, token_side), contract_first(cotangent, down_low)], axis=1
        ),
        ("cuts", "fsdp"),
        scatter_dimension=0,
        tiled=True,
    )
    fine_rows = width // (token_groups * quarters)
    wide_grads = lax.dynamic_slice_in_dim(group_rows, tp_index * fine_rows, fine_rows, 0)
    return (token_input_gradient, wide_grads, narrow_grads)


def flip(array, axis, bit):
    size = lax.axis_size(axis)
    return lax.ppermute(array, axis, [(i, i ^ bit) for i in range(size)])


def vmem_call(kernel, scalars, arrays, ahead, results, aliases, scratch, limit, flops, name):
    vmem = pl.BlockSpec(memory_space=pltpu.VMEM)
    first = len(scalars)
    return pl.pallas_call(
        kernel,
        in_specs=[pl.BlockSpec(memory_space=pltpu.SMEM)] * first
        + [vmem] * len(arrays)
        + [pl.BlockSpec(memory_space=pl.ANY)] * len(ahead),
        out_specs=[vmem] * len(results),
        out_shape=[pltpu.VMEM(shape, kind) for shape, kind in results],
        scratch_shapes=scratch,
        input_output_aliases={first + source: target for source, target in aliases.items()},
        compiler_params=pltpu.CompilerParams(vmem_limit_bytes=limit * MEBIBYTE),
        cost_estimate=pl.CostEstimate(flops=COST * flops, bytes_accessed=0, transcendentals=0),
        name=name,
    )(
        *scalars,
        *[pltpu.with_memory_space_constraint(array, pltpu.VMEM) for array in arrays],
        *ahead,
    )


def width_part(ref, part, here, masks, rows):
    return jnp.concatenate(
        [
            ref[part, pl.ds(pl.multiple_of(lax.bitwise_xor(here[0], mask) * rows, rows), rows)]
            for mask in masks
        ],
        axis=1,
    )


def stacked(units, which, span):
    return jnp.concatenate([unit[which, :, span] for unit in units], axis=0)


def put_in_place(units, here, masks, gate_full, up_full):
    half = units[0].shape[1]
    for number, unit in enumerate(units):
        block = lax.bitwise_xor(here[0], masks[number // 2])
        row = pl.ds(pl.multiple_of((2 * block + number % 2) * half, half), half)
        gate_full[row, :] = unit[0]
        up_full[row, :] = unit[1]


def first_kernel(masks, n_units, here, *refs):
    tokens, cotangent, gate_in, up_in, leave, gate_out, up_out, down_in = refs[:8]
    units = refs[8 : 8 + n_units]
    sums, (turned, gate_full, up_full) = refs[-9:-3], refs[-3:]
    rows = 2 * units[0].shape[1]
    hidden = units[0].shape[2]
    rank = leave.shape[0]
    put_in_place(units, here, masks, gate_full, up_full)
    tile = tokens.shape[0] // HALVES
    for half in range(HALVES):
        part = slice(half * tile, (half + 1) * tile)
        lows = []
        for number, (ref, factor) in enumerate(
            ((tokens, gate_in), (tokens, up_in), (cotangent, leave))
        ):
            low = contract_trailing_axis(ref[part, :], factor[...]).astype(jnp.bfloat16)
            turned[number * rank : (number + 1) * rank, part] = low.astype(jnp.float32).T.astype(
                jnp.bfloat16
            )
            lows.append(low)
        left = width_part(tokens, part, here, masks, rows)
        back = width_part(cotangent, part, here, masks, rows)
        for column in range(0, hidden, TILE):
            span = slice(column, column + TILE)
            for which, factor in enumerate((gate_out, up_out, down_in)):
                sums[3 * half + which][:, span] = matrix_product(
                    back if which == 2 else left, stacked(units, which, span)
                ) + adapter_scaling * matrix_product(lows[which], factor[:, span])


def next_kernel(masks, n_units, here, *refs):
    tokens, cotangent = refs[:2]
    units = refs[2 : 2 + n_units]
    before = refs[2 + n_units : 8 + n_units]
    sums, (gate_full, up_full) = refs[-8:-2], refs[-2:]
    rows = 2 * units[0].shape[1]
    hidden = units[0].shape[2]
    put_in_place(units, here, masks, gate_full, up_full)
    tile = tokens.shape[0] // HALVES
    for half in range(HALVES):
        part = slice(half * tile, (half + 1) * tile)
        left = width_part(tokens, part, here, masks, rows)
        back = width_part(cotangent, part, here, masks, rows)
        for column in range(0, hidden, TILE):
            span = slice(column, column + TILE)
            for which in range(3):
                number = 3 * half + which
                sums[number][:, span] = before[number][:, span] + matrix_product(
                    back if which == 2 else left, stacked(units, which, span)
                )


def last_kernel(masks, n_units, half, n_full, here, *refs):
    tokens, cotangent, gate_out, up_out = refs[:4]
    units = refs[4 : 4 + n_units]
    sums = refs[4 + n_units : 7 + n_units]
    hidden_out, gate_grad_out, up_grad_out, low_out = refs[len(refs) - 4 - n_full :][:4]
    if n_full:
        put_in_place(units, here, masks, *refs[-2:])
    rows = 2 * units[0].shape[1]
    count, hidden = hidden_out.shape
    part = slice(half * count, (half + 1) * count)
    left = width_part(tokens, part, here, masks, rows)
    back = width_part(cotangent, part, here, masks, rows)
    gate_low = up_low = 0.0
    for column in range(0, hidden, STRIP):
        span = slice(column, column + STRIP)
        gate = sums[0][:, span] + matrix_product(left, stacked(units, 0, span))
        up = sums[1][:, span] + matrix_product(left, stacked(units, 1, span))
        hidden_grad = sums[2][:, span] + matrix_product(back, stacked(units, 2, span))
        sig = 1.0 / (1.0 + jnp.exp(-gate))
        gated = gate * sig
        hidden_out[:, span] = (gated * up).astype(jnp.bfloat16)
        gate_grad = (hidden_grad * up * sig * (1.0 + gate * (1.0 - sig))).astype(jnp.bfloat16)
        up_grad = (hidden_grad * gated).astype(jnp.bfloat16)
        gate_grad_out[:, span] = gate_grad
        up_grad_out[:, span] = up_grad
        gate_low += contract_trailing_axis(gate_grad, gate_out[:, span])
        up_low += contract_trailing_axis(up_grad, up_out[:, span])
    low_out[...] = jnp.concatenate([gate_low, up_low], axis=1)


def sums_and_full(rows, width, hidden):
    return [((rows // HALVES, hidden), jnp.float32)] * (3 * HALVES), [
        ((width, hidden), jnp.bfloat16)
    ] * 2


def first_sums(here, tokens, cotangent, factors, masks, units):
    rows, width = tokens.shape
    hidden = units[0].shape[2]
    sums, full = sums_and_full(rows, width, hidden)
    rank = factors[0].shape[0]
    outs = vmem_call(
        functools.partial(first_kernel, masks, len(units)),
        [here],
        [tokens, cotangent, *factors, *units],
        [],
        [*sums, ((3 * rank, rows), jnp.bfloat16), *full],
        {},
        [],
        LIMITS["first"],
        12 * rows * hidden * units[0].shape[1] * len(units),
        "first_sums",
    )
    return outs[: len(sums)], outs[len(sums)], outs[len(sums) + 1 :]


def next_sums(here, tokens, cotangent, masks, units, before, full):
    rows, width = tokens.shape
    hidden = units[0].shape[2]
    sums, shapes = sums_and_full(rows, width, hidden)
    first = 2 + len(units)
    outs = vmem_call(
        functools.partial(next_kernel, masks, len(units)),
        [here],
        [tokens, cotangent, *units, *before, *full],
        [],
        [*sums, *shapes],
        {first + number: number for number in range(len(sums) + 2)},
        [],
        LIMITS["next"],
        12 * rows * hidden * units[0].shape[1] * len(units),
        "next_sums",
    )
    return outs[: len(sums)], outs[len(sums) :]


def hidden_and_grads(half, here, tokens, cotangent, factors, masks, units, sums, full, ahead):
    rows = tokens.shape[0] // HALVES
    rank, hidden = factors[0].shape
    arrays = [tokens, cotangent, *factors, *units, *sums[3 * half : 3 * half + 3]]
    outs = vmem_call(
        functools.partial(last_kernel, masks, len(units), half, len(full)),
        [here],
        [*arrays, *full],
        ahead,
        [((rows, hidden), jnp.bfloat16)] * 3
        + [((rows, 2 * rank), jnp.float32)]
        + [(array.shape, array.dtype) for array in full],
        {len(arrays) + number: 4 + number for number in range(len(full))},
        [],
        LIMITS["last"],
        24 * rows * hidden * units[0].shape[1] * len(units),
        "hidden_and_grads",
    )
    return outs[:4], outs[4:]


def token_grad_kernel(mode, step, here, gate_grad, up_grad, low, factor, gate, up, *refs):
    came = refs[: {"first": 0, "sum": 1, "both": 3, "last": 2}[mode]]
    outs = refs[-2:] if mode == "both" else refs[-1:]
    columns = outs[0].shape[1]
    quarter = sum(
        jnp.where(here[1] == place, order[step], 0) for place, order in enumerate(QUARTER_ORDER)
    )
    span = pl.ds(pl.multiple_of(quarter * columns, columns), columns)
    total = contract_trailing_axis(gate_grad[...], gate[span, :])
    total += contract_trailing_axis(up_grad[...], up[span, :])
    total += matrix_product((adapter_scaling * low[...]).astype(jnp.bfloat16), factor[:, span])
    came = [ref[...].astype(jnp.float32) for ref in came]
    if mode == "both":
        first, left, right = came
        outs[0][...] = (jnp.where(here[1] == 2, first, total) + left).astype(jnp.bfloat16)
        outs[1][...] = (jnp.where(here[1] == 1, first, total) + right).astype(jnp.bfloat16)
    else:
        outs[0][...] = sum(came, total).astype(jnp.bfloat16)


def token_grad(mode, step, here, arrays, columns, came, ahead):
    rows, hidden = arrays[0].shape
    outs = vmem_call(
        functools.partial(token_grad_kernel, mode, step),
        [here],
        [*arrays, *came],
        ahead,
        [((rows, columns), jnp.bfloat16)] * (2 if mode == "both" else 1),
        {},
        [],
        LIMITS["token"],
        8 * rows * columns * hidden,
        "token_grad",
    )
    return outs if mode == "both" else outs[0]


def adapter_kernel(scaling, here, *refs):
    hidden, gate_grad, up_grad, low = (
        refs[number * HALVES : (number + 1) * HALVES] for number in range(4)
    )
    tokens, cotangent, turned, down_in = refs[4 * HALVES : 4 * HALVES + 4]
    keep, send, wide, narrow = refs[-4:]
    rank = down_in.shape[0]
    rows = hidden[0].shape[0]
    parts = [slice(half * rows, (half + 1) * rows) for half in range(HALVES)]
    wide[: 2 * rank, :] = scaling * sum(
        matrix_product(low[half][...].T.astype(jnp.bfloat16), tokens[part, :])
        for half, part in enumerate(parts)
    )
    wide[2 * rank :, :] = scaling * sum(
        matrix_product(
            contract_trailing_axis(down_in[...], hidden[half][...]).astype(jnp.bfloat16),
            cotangent[part, :],
        )
        for half, part in enumerate(parts)
    )
    for number, arrays in enumerate((hidden, gate_grad, up_grad)):
        source = (2, 0, 1)[number]
        narrow[number * rank : (number + 1) * rank, :] = scaling * sum(
            matrix_product(turned[source * rank : (source + 1) * rank, part], arrays[half][...])
            for half, part in enumerate(parts)
        )
    groups = 2 * keep.shape[0]
    wide_columns, narrow_columns = wide.shape[1] // groups, narrow.shape[1] // groups
    for mask in range(groups):
        out = (keep if mask < groups // 2 else send).at[mask % (groups // 2)]
        block = lax.bitwise_xor(here[0], mask)
        out[:, :wide_columns] = wide[
            :, pl.ds(pl.multiple_of(block * wide_columns, wide_columns), wide_columns)
        ]
        out[:, wide_columns:] = narrow[
            :, pl.ds(pl.multiple_of(block * narrow_columns, narrow_columns), narrow_columns)
        ]


def adapter_grads(scaling, here, groups, arrays, ahead):
    rows, width = arrays[-4].shape
    rank, hidden = arrays[-1].shape
    return vmem_call(
        functools.partial(adapter_kernel, scaling),
        [here],
        arrays,
        ahead,
        [((groups // 2, 3 * rank, (width + hidden) // groups), jnp.float32)] * 2,
        {},
        [pltpu.VMEM((3 * rank, width), jnp.float32), pltpu.VMEM((3 * rank, hidden), jnp.float32)],
        LIMITS["adapter"],
        24 * rank * rows * (width + hidden),
        "adapter_grads",
    )


def halve_kernel(here, keep, came, *outs):
    count = keep.shape[0] // len(outs)
    for number, out in enumerate(outs):
        span = slice(number * count, (number + 1) * count)
        out[...] = keep[span] + came[span]


def halve(here, keep, came, parts=2):
    return vmem_call(
        halve_kernel,
        [here],
        [keep, came],
        [],
        [((keep.shape[0] // parts, *keep.shape[1:]), keep.dtype)] * parts,
        {},
        [],
        LIMITS["small"],
        500 * MEBIBYTE,
        "halve",
    )


def turn_kernel(wide_columns, here, kept, came, narrow, keep, send, wide):
    total = kept[0] + came[0]
    narrow[...] = total[:, wide_columns:].T
    wide[...] = total[:, :wide_columns].T
    rows = keep.shape[1]
    for mask in range(4):
        block = pl.ds(pl.multiple_of(lax.bitwise_xor(here[1], mask) * rows, rows), rows)
        (keep if mask < 2 else send)[mask % 2] = wide[block, :]


def turn(here, keep, came, wide_columns):
    _, rows, columns = keep.shape
    return vmem_call(
        functools.partial(turn_kernel, wide_columns),
        [here],
        [keep, came],
        [],
        [((columns - wide_columns, rows), keep.dtype)]
        + [((2, wide_columns // 4, rows), keep.dtype)] * 2,
        {},
        [pltpu.VMEM((wide_columns, rows), keep.dtype)],
        LIMITS["small"],
        500 * MEBIBYTE,
        "turn",
    )


def whole_kernel(here, near, far, out):
    rows = near.shape[1]
    for number in range(2 * near.shape[0]):
        ref = near if number < near.shape[0] else far
        block = lax.bitwise_xor(here[0], number) * rows
        out[pl.ds(pl.multiple_of(block, rows), rows), :] = ref[number % near.shape[0]]


def whole(here, near, far):
    count, rows, columns = near.shape
    return vmem_call(
        whole_kernel,
        [here],
        [near, far],
        [],
        [((2 * count * rows, columns), near.dtype)],
        {},
        [],
        LIMITS["small"],
        500 * MEBIBYTE,
        "whole",
    )[0]


def square_plane(
    tokens,
    cotangent,
    gate_frozen_matrix,
    up_frozen_matrix,
    down_frozen_matrix,
    gate_adapter_input_factor,
    up_adapter_input_factor,
    gate_adapter_output_factor,
    up_adapter_output_factor,
    down_adapter_input_factor,
    down_leave,
):
    groups = lax.axis_size(("cuts", "fsdp"))
    quarters = lax.axis_size("tp")
    rows, width = tokens.shape
    gradient_scaling = adapter_scaling / math.sqrt(rows * groups)
    here = jnp.stack([lax.axis_index(("cuts", "fsdp")), lax.axis_index("tp")]).astype(jnp.int32)
    gate_in, up_in, leave, down_in = (
        array.T
        for array in (
            gate_adapter_input_factor,
            up_adapter_input_factor,
            down_leave,
            down_adapter_input_factor,
        )
    )
    gate_out, up_out = gate_adapter_output_factor, up_adapter_output_factor
    half_rows = gate_frozen_matrix.shape[0] // 2

    units = {}
    for half in range(2):
        span = slice(half * half_rows, (half + 1) * half_rows)
        units[0, half] = jnp.stack(
            [gate_frozen_matrix[span], up_frozen_matrix[span], down_frozen_matrix[:, span].T]
        )
    units[1, 0] = flip(units[0, 0], "fsdp", 1)
    units[2, 1] = flip(units[0, 1], "fsdp", 2)
    units[1, 1] = flip(units[0, 1], "fsdp", 1)
    units[2, 0] = flip(units[0, 0], "fsdp", 2)
    units[3, 0] = flip(units[1, 0], "fsdp", 2)
    units[3, 1] = flip(units[2, 1], "fsdp", 1)
    for mask in range(4):
        for half in range(2):
            units[mask | 4, half] = flip(units[mask, half], "cuts", 1)
    pick = lambda masks: [units[mask, half] for mask in masks for half in range(2)]

    sums, turned, full = first_sums(
        here,
        tokens,
        cotangent,
        [gate_in, up_in, leave, gate_out, up_out, down_in],
        (0, 4),
        pick((0, 4)),
    )
    masks = (1, 2, 5, 6)
    sums, full = next_sums(here, tokens, cotangent, masks, pick(masks), sums, full)

    factor = jnp.concatenate([gate_in, up_in])
    shift = lambda array, pairs: lax.ppermute(array, "tp", pairs)
    states, first = [], []
    share = lambda step, half, mode, came=(), ahead=(): token_grad(
        mode,
        step,
        here,
        [*states[half][1:], factor, *full],
        width // quarters,
        came,
        ahead,
    )
    both = range(HALVES)
    for half in both:
        state, placed = hidden_and_grads(
            half,
            here,
            tokens,
            cotangent,
            [gate_out, up_out],
            (3, 7),
            pick((3, 7)),
            sums,
            [] if half else full,
            first[:],
        )
        full = placed or full
        states.append(state)
        first.append(share(0, half, "first"))
    came = [shift(part, [(0, 1), (3, 2)]) for part in first]
    partial = [share(1, half, "sum", [came[half]], first[1:]) for half in both]
    from_left = [shift(part, [(0, 1), (1, 2)]) for part in partial]
    from_right = [shift(part, [(3, 2), (2, 1)]) for part in partial]
    partial = [
        share(2, half, "both", [first[half], from_left[half], from_right[half]], partial[1:])
        for half in both
    ]
    from_left = [shift(part[0], [(0, 1), (1, 2), (2, 3)]) for part in partial]
    from_right = [shift(part[1], [(3, 2), (2, 1), (1, 0)]) for part in partial]

    keep, send = adapter_grads(
        gradient_scaling,
        here,
        groups,
        [
            *[state[number] for number in range(4) for state in states],
            tokens,
            cotangent,
            turned,
            down_in,
        ],
        [came[1], *first],
    )
    keep, send = halve(here, keep, flip(send, "cuts", 1))
    keep, send = halve(here, keep, flip(send, "fsdp", 2))
    narrow, keep, send = turn(here, keep, flip(send, "fsdp", 1), width // groups)
    keep, send = halve(here, keep, flip(send, "tp", 2))
    wide_grads = halve(here, keep, flip(send, "tp", 1), 1)[0][0]
    near = jnp.stack([narrow, flip(narrow, "fsdp", 1)])
    near = jnp.concatenate([near, flip(near, "fsdp", 2)])
    narrow_grads = whole(here, near, flip(near, "cuts", 1))

    token_input_gradient = jnp.concatenate(
        [
            share(
                3,
                half,
                "last",
                [from_left[half], from_right[half]],
                [*partial[1], wide_grads, narrow_grads] if half else partial[1],
            )
            for half in both
        ]
    )
    return (token_input_gradient, wide_grads, narrow_grads)


def per_device(*arrays):
    sizes = [lax.axis_size(axis) for axis in ("cuts", "fsdp", "tp")]
    return (square_plane if sizes == [2, 4, 4] else any_plane)(*arrays)


def solution(mesh):
    in_specs = (
        P(("cuts", "fsdp"), None),
        P(("cuts", "fsdp"), None),
        P(("cuts", "fsdp"), "tp"),
        P(("cuts", "fsdp"), "tp"),
        P("tp", ("cuts", "fsdp")),
        P(),
        P(),
        P(None, "tp"),
        P(None, "tp"),
        P("tp", None),
        P(),
    )
    out_specs = (P(("cuts", "fsdp"), "tp"), P(("cuts", "fsdp", "tp"), None), P("tp", None))
    return jax.shard_map(
        per_device, mesh=mesh, in_specs=in_specs, out_specs=out_specs, check_vma=False
    )
```

profile of v0, /device:TPU:0, one launch (start us, length us, event | category | flops | bytes accessed | tf_op | source)
XLA Modules:
  0.0 230.5 jit_solution(2891540721162908504)
XLA Ops:
  1.9 2.0 slice_bitcast_fusion
  4.5 2.6 %collective-permute-start.2 = (bf16[3,128,1024]{2,1,0:T(8,128)(2,1)S(1)}, bf16[3,128,1024]{2,1,0:T(8,128)(2,1)S(1)}, u32[]{:S(2)}, u32[]{:S(2)}) collective-permute-start(bf16[3,128,1024]{2,1,0:T(8,128)(2,1)S(1)} %pad_maximum_fusion.2.refs_9_), channel_id=1, source_target_pairs={{0,8},{4,12},{8,0},{12,4},{1,9},{5,13},{9,1},{13,5},{2,10},{6,14},... | collective-permute-start | bytes 2359304 | tf_op jit(solution)/shard_map/ppermute | solution.py:138
  8.5 1.5 collective-permute-start
  10.8 14.7 %collective-permute-done.2.refs_5_ = bf16[3,128,1024]{2,1,0:T(8,128)(2,1)S(1)} collective-permute-done((bf16[3,128,1024]{2,1,0:T(8,128)(2,1)S(1)}, bf16[3,128,1024]{2,1,0:T(8,128)(2,1)S(1)}, u32[]{:S(2)}, u32[]{:S(2)}) %collective-permute-start.2) | collective-permute-done | bytes 786464 | tf_op jit(solution)/shard_map/ppermute | solution.py:138
  25.6 2.0 collective-permute-start.3
  27.6 1.4 collective-permute-done.refs_2_
  28.9 16.8 %collective-permute-done.6.refs_3_ = bf16[3,128,1024]{2,1,0:T(8,128)(2,1)} collective-permute-done((bf16[3,128,1024]{2,1,0:T(8,128)(2,1)S(1)}, bf16[3,128,1024]{2,1,0:T(8,128)(2,1)}, u32[]{:S(2)}, u32[]{:S(2)}) %collective-permute-start.6) | collective-permute-done | bytes 786464 | tf_op jit(solution)/shard_map/ppermute | solution.py:138
  46.6 2.2 copy-done.2
  48.8 2.2 copy-done.4
  53.7 10.0 %first_sums.1 = (f32[512,1024]{1,0:T(8,128)S(1)}, f32[512,1024]{1,0:T(8,128)S(1)}, f32[512,1024]{1,0:T(8,128)S(1)}, f32[512,1024]{1,0:T(8,128)S(1)}, f32[512,102...) custom-call(s32[2]{0:T(128)S(1)} %pad_add_fusion.here, ...), custom_call_target="tpu_custom_call" | custom-call | flops 128849018880 | tf_op jit(solution)/shard_map/first_sums/pallas_call | solution.py:144
  63.8 2.0 copy-done.12
  65.8 2.0 copy-done.19
  67.8 1.3 copy-done.31
  69.1 1.4 copy-done.35
  70.5 1.3 copy-done.39
  71.9 1.3 copy-done.43
  73.2 1.3 copy-done.47
  75.8 2.2 copy-done.13
  78.0 2.2 copy-done.20
  80.2 1.6 copy-done.32
  81.8 1.6 copy-done.36
  83.4 1.6 copy-done.40
  84.9 1.6 copy-done.44
  86.5 1.6 copy-done.48
  88.1 10.1 %next_sums.1 = (f32[512,1024]{1,0:T(8,128)S(1)}, f32[512,1024]{1,0:T(8,128)S(1)}, f32[512,1024]{1,0:T(8,128)S(1)}, f32[512,1024]{1,0:T(8,128)S(1)}, f32[512,1024...) custom-call(s32[2]{0:T(128)S(1)} %pad_add_fusion.here, ...), custom_call_target="tpu_custom_call", output_to_operand_aliasing={{0}: (11, {}), {1}: (12, {}), {2}: (13, {}), {3}: (14, {}),... | custom-call | flops 257698037760 | tf_op jit(solution)/shard_map/next_sums/pallas_call | solution.py:144
  98.2 2.0 copy-done.14
  100.2 2.0 copy-done.21
  102.3 1.3 copy-done.33
  104.9 1.3 copy-done.41
  106.2 1.4 copy-done.45
  107.6 1.3 copy-done.49
  109.0 2.2 copy-done.15
  111.1 2.2 copy-done.22
  113.3 1.6 copy-done.34
  114.9 1.6 copy-done.38
  116.5 5.1 %hidden_and_grads.2 = (bf16[512,1024]{1,0:T(8,128)(2,1)S(1)}, bf16[512,1024]{1,0:T(8,128)(2,1)S(1)}, bf16[512,1024]{1,0:T(8,128)(2,1)S(1)}, f32[512,128]{1,0:T(8...) custom-call(s32[2]{0:T(128)S(1)} %pad_add_fusion.here, ...), custom_call_target="tpu_custom_call", output_to_operand_aliasing={{4}: (12, {}), {5}: (13, {})} | custom-call | flops 128849018880 | tf_op jit(solution)/shard_map/hidden_and_grads/pallas_call | solution.py:144
  121.7 2.8 %token_grad.8.refs_11_.refs_0_.refs_13_ = bf16[512,512]{1,0:T(8,128)(2,1)} custom-call(s32[2]{0:T(128)S(1)} %pad_add_fusion.here, bf16[512,1024]{1,0:T(8,128)(2,1)S(1)} %get-tuple-element.58.gate_grad.refs_2_, bf16[512,1024]{1,0:T(8,128)(2,1)S(1)} %get-tuple-element.59.up_grad.refs_4_, f32[512,128]{1,0:T(8,128)S(1)} %get-tuple-element.60.low.refs_6_, ...), custom_call_target="tpu_custom_call" | custom-call | flops 42949672960 | tf_op jit(solution)/shard_map/token_grad/pallas_call | solution.py:144
  124.5 1.6 copy-done.23
  126.0 4.7 %collective-permute-start.14 = (bf16[512,512]{1,0:T(8,128)(2,1)}, bf16[512,512]{1,0:T(8,128)(2,1)}, u32[]{:S(2)}, u32[]{:S(2)}) collective-permute-start(bf16[512,512]{1,0:T(8,128)(2,1)} %token_grad.8.refs_11_.refs_0_.refs_13_), channel_id=1, source_target_pairs={{0,1},{3,2},{4,5},{7,6},{8,9},{11,10},{12,13},{15,14},{16,17},{19,... | collective-permute-start | bytes 1572872 | tf_op jit(solution)/shard_map/ppermute | solution.py:560
  130.7 5.2 %hidden_and_grads.3 = (bf16[512,1024]{1,0:T(8,128)(2,1)S(1)}, bf16[512,1024]{1,0:T(8,128)(2,1)S(1)}, bf16[512,1024]{1,0:T(8,128)(2,1)S(1)}, f32[512,128]{1,0:T(8,128)S(1)}) custom-call(s32[2]{0:T(128)S(1)} %pad_add_fusion.here, bf16[1024,2048]{1,0:T(8,128)(2,1)S(1)} %copy-done.3, bf16[1024,2048]{1,0:T(8,128)(2,1)S(1)} %copy-done.5, ...), custom_call_target="tpu_custom_call" | custom-call | flops 128849018880 | tf_op jit(solution)/shard_map/hidden_and_grads/pallas_call | solution.py:144
  135.9 2.0 token_grad.9.refs_1_.refs_0_.refs_14_
  137.9 1.5 collective-permute-start.17
  139.4 3.1 %collective-permute-done.14.refs_0_ = bf16[512,512]{1,0:T(8,128)(2,1)} collective-permute-done((bf16[512,512]{1,0:T(8,128)(2,1)}, bf16[512,512]{1,0:T(8,128)(2,1)}, u32[]{:S(2)}, u32[]{:S(2)}) %collective-permute-start.14) | collective-permute-done | bytes 524320 | tf_op jit(solution)/shard_map/ppermute | solution.py:560
  142.5 3.3 %token_grad.10 = bf16[512,512]{1,0:T(8,128)(2,1)} custom-call(s32[2]{0:T(128)S(1)} %pad_add_fusion.here, bf16[512,1024]{1,0:T(8,128)(2,1)S(1)} %get-tuple-element.58.gate_grad.refs_2_, bf16[512,1024]{1,0:T(8,128)(2,1)S(1)} %get-tuple-element.59.up_grad.refs_4_, f32[512,128]{1,0:T(8,128)S(1)} %get-tuple-element.60.low.refs_6_, ...), custom_call_target="tpu_custom_call" | custom-call | flops 42949672960 | tf_op jit(solution)/shard_map/token_grad/pallas_call | solution.py:144
  145.7 5.2 %collective-permute-start.15 = (bf16[512,512]{1,0:T(8,128)(2,1)}, bf16[512,512]{1,0:T(8,128)(2,1)}, u32[]{:S(2)}, u32[]{:S(2)}) collective-permute-start(bf16[512,512]{1,0:T(8,128)(2,1)} %token_grad.10), channel_id=1, source_target_pairs={{0,1},{1,2},{4,5},{5,6},{8,9},{9,10},{12,13},{13,14},{16,17},{17,1... | collective-permute-start | bytes 1572872 | tf_op jit(solution)/shard_map/ppermute | solution.py:560
  150.9 1.5 collective-permute-start.16
  153.6 4.0 %adapter_grads.1 = (f32[4,192,384]{2,1,0:T(8,128)S(1)}, f32[4,192,384]{2,1,0:T(8,128)S(1)}) custom-call(s32[2]{0:T(128)S(1)} %pad_add_fusion.here, bf16[512,1024]{1,0:T(8,128)(2,1)S(1)} %get-tuple-element.73.refs_0_, bf16[512,1024]{1,0:T(8,128)(2,1)S(1)} %get-tuple-element.74.refs_1_, bf16[512,1024]{1,0:T(8,128)(2,1)S(1)} %get-tuple-element.58.gate_grad.refs_2_, ...), custom_call_target="tpu_custom_call" | custom-call | flops 96636764160 | tf_op jit(solution)/shard_map/adapter_grads/pallas_call | solution.py:144
  157.7 2.0 token_grad.11.refs_3_
  159.7 4.4 %collective-permute-start.20 = (bf16[512,512]{1,0:T(8,128)(2,1)S(1)}, bf16[512,512]{1,0:T(8,128)(2,1)S(1)}, u32[]{:S(2)}, u32[]{:S(2)}) collective-permute-start(bf16[512,512]{1,0:T(8,128)(2,1)S(1)} %token_grad.11.refs_3_), channel_id=1, source_target_pairs={{0,1},{1,2},{4,5},{5,6},{8,9},{9,10},{12,13},{13,14},{16,17},{17,1... | collective-permute-start | bytes 1572872 | tf_op jit(solution)/shard_map/ppermute | solution.py:560
  165.5 1.6 collective-permute-start.25
  167.1 2.9 %token_grad.12 = (bf16[512,512]{1,0:T(8,128)(2,1)S(1)}, bf16[512,512]{1,0:T(8,128)(2,1)S(1)}) custom-call(s32[2]{0:T(128)S(1)} %pad_add_fusion.here, bf16[512,1024]{1,0:T(8,128)(2,1)S(1)} %get-tuple-element.58.gate_grad.refs_2_, bf16[512,1024]{1,0:T(8,128)(2,1)S(1)} %get-tuple-element.59.up_grad.refs_4_, f32[512,128]{1,0:T(8,128)S(1)} %get-tuple-element.60.low.refs_6_, ...), custom_call_target="tpu_custom_call" | custom-call | flops 42949672960 | tf_op jit(solution)/shard_map/token_grad/pallas_call | solution.py:144
  170.1 4.1 %collective-permute-start.18 = (bf16[512,512]{1,0:T(8,128)(2,1)S(1)}, bf16[512,512]{1,0:T(8,128)(2,1)S(1)}, u32[]{:S(2)}, u32[]{:S(2)}) collective-permute-start(bf16[512,512]{1,0:T(8,128)(2,1)S(1)} %get-tuple-element.69), channel_id=1, source_target_pairs={{0,1},{1,2},{2,3},{4,5},{5,6},{6,7},{8,9},{9,10},{10,11},{12,13},{... | collective-permute-start | bytes 1572872 | tf_op jit(solution)/shard_map/ppermute | solution.py:560
  175.5 5.6 %collective-permute-done.25.came = f32[2,192,384]{2,1,0:T(8,128)S(1)} collective-permute-done((f32[2,192,384]{2,1,0:T(8,128)S(1)}, f32[2,192,384]{2,1,0:T(8,128)S(1)}, u32[]{:S(2)}, u32[]{:S(2)}) %collective-permute-start.25) | collective-permute-done | bytes 589856 | tf_op jit(solution)/shard_map/ppermute | solution.py:138
  181.7 1.5 collective-permute-start.26
  183.2 2.9 %token_grad.13 = (bf16[512,512]{1,0:T(8,128)(2,1)S(1)}, bf16[512,512]{1,0:T(8,128)(2,1)}) custom-call(s32[2]{0:T(128)S(1)} %pad_add_fusion.here, bf16[512,1024]{1,0:T(8,128)(2,1)S(1)} %get-tuple-element.66.gate_grad.refs_3_, bf16[512,1024]{1,0:T(8,128)(2,1)S(1)} %get-tuple-element.67.up_grad.refs_5_, f32[512,128]{1,0:T(8,128)S(1)} %get-tuple-element.68.low.refs_7_, ...), custom_call_target="tpu_custom_call" | custom-call | flops 42949672960 | tf_op jit(solution)/shard_map/token_grad/pallas_call | solution.py:144
  186.2 4.8 %collective-permute-start.22 = (bf16[512,512]{1,0:T(8,128)(2,1)S(1)}, bf16[512,512]{1,0:T(8,128)(2,1)}, u32[]{:S(2)}, u32[]{:S(2)}) collective-permute-start(bf16[512,512]{1,0:T(8,128)(2,1)S(1)} %get-tuple-element.71.refs_2_), channel_id=1, source_target_pairs={{0,1},{1,2},{2,3},{4,5},{5,6},{6,7},{8,9},{9,10},{10,11},{12,13},{... | collective-permute-start | bytes 1572872 | tf_op jit(solution)/shard_map/ppermute | solution.py:560
  193.6 2.0 token_grad.14
  195.6 3.7 %collective-permute-start.27 = (f32[2,64,192]{2,1,0:T(8,128)S(1)}, f32[2,64,192]{2,1,0:T(8,128)S(1)}, u32[]{:S(2)}, u32[]{:S(2)}) collective-permute-start(f32[2,64,192]{2,1,0:T(8,128)S(1)} %get-tuple-element.83), channel_id=1, source_target_pairs={{0,2},{1,3},{2,0},{3,1},{4,6},{5,7},{6,4},{7,5},{8,10},{9,11},{10,... | collective-permute-start | bytes 294920 | tf_op jit(solution)/shard_map/ppermute | solution.py:138
  199.4 1.6 collective-permute-start.30
  201.0 11.1 %collective-permute-done.27.came = f32[2,64,192]{2,1,0:T(8,128)S(1)} collective-permute-done((f32[2,64,192]{2,1,0:T(8,128)S(1)}, f32[2,64,192]{2,1,0:T(8,128)S(1)}, u32[]{:S(2)}, u32[]{:S(2)}) %collective-permute-start.27) | collective-permute-done | bytes 98336 | tf_op jit(solution)/shard_map/ppermute | solution.py:138
  212.8 4.1 %collective-permute-done.28.came = f32[1,64,192]{2,1,0:T(8,128)S(1)} collective-permute-done((f32[1,64,192]{2,1,0:T(8,128)S(1)}, f32[1,64,192]{2,1,0:T(8,128)S(1)}, u32[]{:S(2)}, u32[]{:S(2)}) %collective-permute-start.28) | collective-permute-done | bytes 49184 | tf_op jit(solution)/shard_map/ppermute | solution.py:138
  220.0 2.2 copy-done.18
  222.2 2.2 copy-done.26
  226.8 2.7 %token_grad.15 = bf16[512,512]{1,0:T(8,128)(2,1)S(1)} custom-call(s32[2]{0:T(128)S(1)} %pad_add_fusion.here, bf16[512,1024]{1,0:T(8,128)(2,1)S(1)} %copy-done.28, bf16[512,1024]{1,0:T(8,128)(2,1)S(1)} %copy-done.30, f32[512,128]{1,0:T(8,128)S(1)} %get-tuple-element.68.low.refs_7_, bf16[128,2048]{1,0:T(8,128)(2,1)S(1)} %pad_maximum_fusion.3.factor, ...), custom_call_target="tpu_custom_call" | custom-call | flops 42949672960 | tf_op jit(solution)/shard_map/token_grad/pallas_call | solution.py:144
  (138 shorter events, 24.9 us)
Async XLA Ops:
  3.8 21.7 %copy-start = (bf16[2048,64]{0,1:T(8,128)(2,1)S(1)}, bf16[2048,64]{0,1:T(8,128)(2,1)}, u32[]{:S(2)}) copy-start(bf16[2048,64]{0,1:T(8,128)(2,1)} %param.16) | copy-start | bytes 786436
  3.8 21.7 %copy-start.1 = (bf16[2048,64]{0,1:T(8,128)(2,1)S(1)}, bf16[2048,64]{0,1:T(8,128)(2,1)}, u32[]{:S(2)}) copy-start(bf16[2048,64]{0,1:T(8,128)(2,1)} %param.17) | copy-start | bytes 786436
  3.8 42.7 %copy-start.7 = (bf16[64,1024]{1,0:T(8,128)(2,1)S(1)}, bf16[64,1024]{1,0:T(8,128)(2,1)}, u32[]{:S(2)}) copy-start(bf16[64,1024]{1,0:T(8,128)(2,1)} %refs_2_.3) | copy-start | bytes 393220
  3.9 6.6 %collective-permute-start.13 = (bf16[3,128,1024]{2,1,0:T(8,128)(2,1)S(1)}, bf16[3,128,1024]{2,1,0:T(8,128)(2,1)}, u32[]{:S(2)}, u32[]{:S(2)}) collective-permute-start(bf16[3,128,1024]{2,1,0:T(8,128)(2,1)S(1)} %pad_maximum_fusion.2.refs_9_), channel_id=1, source_target_pairs={{0,16},{16,0},{1,17},{17,1},{2,18},{18,2},{3,19},{19,3},{4,20},{20... | collective-permute-start | bytes 2359304 | tf_op jit(solution)/shard_map/ppermute | solution.py:138
  4.5 21.0 %collective-permute-start.2 = (bf16[3,128,1024]{2,1,0:T(8,128)(2,1)S(1)}, bf16[3,128,1024]{2,1,0:T(8,128)(2,1)S(1)}, u32[]{:S(2)}, u32[]{:S(2)}) collective-permute-start(bf16[3,128,1024]{2,1,0:T(8,128)(2,1)S(1)} %pad_maximum_fusion.2.refs_9_), channel_id=1, source_target_pairs={{0,8},{4,12},{8,0},{12,4},{1,9},{5,13},{9,1},{13,5},{2,10},{6,14},... | collective-permute-start | bytes 2359304 | tf_op jit(solution)/shard_map/ppermute | solution.py:138
  8.2 17.3 %collective-permute-start.12 = (bf16[3,128,1024]{2,1,0:T(8,128)(2,1)S(1)}, bf16[3,128,1024]{2,1,0:T(8,128)(2,1)}, u32[]{:S(2)}, u32[]{:S(2)}) collective-permute-start(bf16[3,128,1024]{2,1,0:T(8,128)(2,1)S(1)} %pad_maximum_fusion.1.refs_8_), channel_id=1, source_target_pairs={{0,16},{16,0},{1,17},{17,1},{2,18},{18,2},{3,19},{19,3},{4,20},{20... | collective-permute-start | bytes 2359304 | tf_op jit(solution)/shard_map/ppermute | solution.py:138
  8.5 20.5 %collective-permute-start = (bf16[3,128,1024]{2,1,0:T(8,128)(2,1)S(1)}, bf16[3,128,1024]{2,1,0:T(8,128)(2,1)}, u32[]{:S(2)}, u32[]{:S(2)}) collective-permute-start(bf16[3,128,1024]{2,1,0:T(8,128)(2,1)S(1)} %pad_maximum_fusion.1.refs_8_), channel_id=1, source_target_pairs={{0,4},{4,0},{8,12},{12,8},{1,5},{5,1},{9,13},{13,9},{2,6},{6,2},{1... | collective-permute-start | bytes 2359304 | tf_op jit(solution)/shard_map/ppermute | solution.py:138
  10.0 35.8 %collective-permute-start.6 = (bf16[3,128,1024]{2,1,0:T(8,128)(2,1)S(1)}, bf16[3,128,1024]{2,1,0:T(8,128)(2,1)}, u32[]{:S(2)}, u32[]{:S(2)}) collective-permute-start(bf16[3,128,1024]{2,1,0:T(8,128)(2,1)S(1)} %pad_maximum_fusion.2.refs_9_), channel_id=1, source_target_pairs={{0,4},{4,0},{8,12},{12,8},{1,5},{5,1},{9,13},{13,9},{2,6},{6,2},{1... | collective-permute-start | bytes 2359304 | tf_op jit(solution)/shard_map/ppermute | solution.py:138
  10.5 35.6 %collective-permute-start.7 = (bf16[3,128,1024]{2,1,0:T(8,128)(2,1)S(1)}, bf16[3,128,1024]{2,1,0:T(8,128)(2,1)}, u32[]{:S(2)}, u32[]{:S(2)}) collective-permute-start(bf16[3,128,1024]{2,1,0:T(8,128)(2,1)S(1)} %pad_maximum_fusion.1.refs_8_), channel_id=1, source_target_pairs={{0,8},{4,12},{8,0},{12,4},{1,9},{5,13},{9,1},{13,5},{2,10},{6,14},... | collective-permute-start | bytes 2359304 | tf_op jit(solution)/shard_map/ppermute | solution.py:138
  25.4 20.6 %collective-permute-start.11 = (bf16[3,128,1024]{2,1,0:T(8,128)(2,1)S(1)}, bf16[3,128,1024]{2,1,0:T(8,128)(2,1)}, u32[]{:S(2)}, u32[]{:S(2)}) collective-permute-start(bf16[3,128,1024]{2,1,0:T(8,128)(2,1)S(1)} %collective-permute-done.2.refs_5_), channel_id=1, source_target_pairs={{0,16},{16,0},{1,17},{17,1},{2,18},{18,2},{3,19},{19,3},{4,20},{20... | collective-permute-start | bytes 2359304 | tf_op jit(solution)/shard_map/ppermute | solution.py:138
  25.6 49.7 %collective-permute-start.3 = (bf16[3,128,1024]{2,1,0:T(8,128)(2,1)S(1)}, bf16[3,128,1024]{2,1,0:T(8,128)(2,1)}, u32[]{:S(2)}, u32[]{:S(2)}) collective-permute-start(bf16[3,128,1024]{2,1,0:T(8,128)(2,1)S(1)} %collective-permute-done.2.refs_5_), channel_id=1, source_target_pairs={{0,4},{4,0},{8,12},{12,8},{1,5},{5,1},{9,13},{13,9},{2,6},{6,2},{1... | collective-permute-start | bytes 2359304 | tf_op jit(solution)/shard_map/ppermute | solution.py:138
  28.9 46.8 %collective-permute-start.8 = (bf16[3,128,1024]{2,1,0:T(8,128)(2,1)}, bf16[3,128,1024]{2,1,0:T(8,128)(2,1)S(1)}, u32[]{:S(2)}, u32[]{:S(2)}) collective-permute-start(bf16[3,128,1024]{2,1,0:T(8,128)(2,1)} %collective-permute-done.refs_2_), channel_id=1, source_target_pairs={{0,16},{16,0},{1,17},{17,1},{2,18},{18,2},{3,19},{19,3},{4,20},{20... | collective-permute-start | bytes 2359304 | tf_op jit(solution)/shard_map/ppermute | solution.py:138
  45.8 29.5 %collective-permute-start.1 = (bf16[3,128,1024]{2,1,0:T(8,128)(2,1)}, bf16[3,128,1024]{2,1,0:T(8,128)(2,1)}, u32[]{:S(2)}, u32[]{:S(2)}) collective-permute-start(bf16[3,128,1024]{2,1,0:T(8,128)(2,1)} %collective-permute-done.refs_2_), channel_id=1, source_target_pairs={{0,8},{4,12},{8,0},{12,4},{1,9},{5,13},{9,1},{13,5},{2,10},{6,14},... | collective-permute-start | bytes 2359304 | tf_op jit(solution)/shard_map/ppermute | solution.py:138
  46.1 29.7 %collective-permute-start.9 = (bf16[3,128,1024]{2,1,0:T(8,128)(2,1)}, bf16[3,128,1024]{2,1,0:T(8,128)(2,1)S(1)}, u32[]{:S(2)}, u32[]{:S(2)}) collective-permute-start(bf16[3,128,1024]{2,1,0:T(8,128)(2,1)} %collective-permute-done.6.refs_3_), channel_id=1, source_target_pairs={{0,16},{16,0},{1,17},{17,1},{2,18},{18,2},{3,19},{19,3},{4,20},{20... | collective-permute-start | bytes 2359304 | tf_op jit(solution)/shard_map/ppermute | solution.py:138
  46.1 29.7 %collective-permute-start.10 = (bf16[3,128,1024]{2,1,0:T(8,128)(2,1)}, bf16[3,128,1024]{2,1,0:T(8,128)(2,1)S(1)}, u32[]{:S(2)}, u32[]{:S(2)}) collective-permute-start(bf16[3,128,1024]{2,1,0:T(8,128)(2,1)} %collective-permute-done.7.refs_4_), channel_id=1, source_target_pairs={{0,16},{16,0},{1,17},{17,1},{2,18},{18,2},{3,19},{19,3},{4,20},{20... | collective-permute-start | bytes 2359304 | tf_op jit(solution)/shard_map/ppermute | solution.py:138
  46.6 2.2 copy-start.2
  48.8 2.2 copy-start.4
  53.7 22.0 %copy-start.3 = (bf16[1024,2048]{1,0:T(8,128)(2,1)S(1)}, bf16[1024,2048]{1,0:T(8,128)(2,1)}, u32[]{:S(2)}) copy-start(bf16[1024,2048]{1,0:T(8,128)(2,1)} %refs_8_.1) | copy-start | bytes 12582916
  53.7 22.1 %copy-start.5 = (bf16[1024,2048]{1,0:T(8,128)(2,1)S(1)}, bf16[1024,2048]{1,0:T(8,128)(2,1)}, u32[]{:S(2)}) copy-start(bf16[1024,2048]{1,0:T(8,128)(2,1)} %refs_9_.1) | copy-start | bytes 12582916
  63.8 2.0 copy-start.12
  65.8 2.0 copy-start.19
  75.2 33.7 %collective-permute-start.5 = (bf16[3,128,1024]{2,1,0:T(8,128)(2,1)}, bf16[3,128,1024]{2,1,0:T(8,128)(2,1)}, u32[]{:S(2)}, u32[]{:S(2)}) collective-permute-start(bf16[3,128,1024]{2,1,0:T(8,128)(2,1)} %collective-permute-done.3.refs_5_), channel_id=1, source_target_pairs={{0,16},{16,0},{1,17},{17,1},{2,18},{18,2},{3,19},{19,3},{4,20},{20... | collective-permute-start | bytes 2359304 | tf_op jit(solution)/shard_map/ppermute | solution.py:138
  75.3 33.6 %collective-permute-start.4 = (bf16[3,128,1024]{2,1,0:T(8,128)(2,1)}, bf16[3,128,1024]{2,1,0:T(8,128)(2,1)}, u32[]{:S(2)}, u32[]{:S(2)}) collective-permute-start(bf16[3,128,1024]{2,1,0:T(8,128)(2,1)} %collective-permute-done.1.refs_4_), channel_id=1, source_target_pairs={{0,16},{16,0},{1,17},{17,1},{2,18},{18,2},{3,19},{19,3},{4,20},{20... | collective-permute-start | bytes 2359304 | tf_op jit(solution)/shard_map/ppermute | solution.py:138
  75.8 2.2 copy-start.13
  78.0 2.2 copy-start.20
  83.4 1.6 copy-start.40
  84.9 1.6 copy-start.44
  88.1 20.8 %copy-start.9 = (bf16[64,1024]{1,0:T(8,128)(2,1)S(1)}, bf16[64,1024]{1,0:T(8,128)(2,1)}, u32[]{:S(2)}) copy-start(bf16[64,1024]{1,0:T(8,128)(2,1)} %refs_3_.3) | copy-start | bytes 393220
  98.2 2.0 copy-start.14
  100.2 2.0 copy-start.21
  108.9 2.2 copy-start.15
  111.1 2.2 copy-start.22
  121.7 2.8 %copy-start.16 = (bf16[2048,1024]{1,0:T(8,128)(2,1)}, bf16[2048,1024]{1,0:T(8,128)(2,1)S(1)}, u32[]{:S(2)}) copy-start(bf16[2048,1024]{1,0:T(8,128)(2,1)S(1)} %get-tuple-element.61.gate) | copy-start | bytes 12582916
  121.7 4.4 %copy-start.23 = (bf16[2048,1024]{1,0:T(8,128)(2,1)}, bf16[2048,1024]{1,0:T(8,128)(2,1)S(1)}, u32[]{:S(2)}) copy-start(bf16[2048,1024]{1,0:T(8,128)(2,1)S(1)} %get-tuple-element.62.up) | copy-start | bytes 12582916
  121.7 9.0 %copy-start.42 = (f32[512,1024]{1,0:T(8,128)S(1)}, f32[512,1024]{1,0:T(8,128)}, u32[]{:S(2)}) copy-start(f32[512,1024]{1,0:T(8,128)} %copy-done.41) | copy-start | bytes 6291460
  121.7 9.0 %copy-start.46 = (f32[512,1024]{1,0:T(8,128)S(1)}, f32[512,1024]{1,0:T(8,128)}, u32[]{:S(2)}) copy-start(f32[512,1024]{1,0:T(8,128)} %copy-done.45) | copy-start | bytes 6291460
  121.7 9.0 %copy-start.50 = (f32[512,1024]{1,0:T(8,128)S(1)}, f32[512,1024]{1,0:T(8,128)}, u32[]{:S(2)}) copy-start(f32[512,1024]{1,0:T(8,128)} %copy-done.49) | copy-start | bytes 6291460
  126.0 16.4 %collective-permute-start.14 = (bf16[512,512]{1,0:T(8,128)(2,1)}, bf16[512,512]{1,0:T(8,128)(2,1)}, u32[]{:S(2)}, u32[]{:S(2)}) collective-permute-start(bf16[512,512]{1,0:T(8,128)(2,1)} %token_grad.8.refs_11_.refs_0_.refs_13_), channel_id=1, source_target_pairs={{0,1},{3,2},{4,5},{7,6},{8,9},{11,10},{12,13},{15,14},{16,17},{19,... | collective-permute-start | bytes 1572872 | tf_op jit(solution)/shard_map/ppermute | solution.py:560
  130.7 5.2 %copy-start.17 = (bf16[2048,1024]{1,0:T(8,128)(2,1)S(1)}, bf16[2048,1024]{1,0:T(8,128)(2,1)}, u32[]{:S(2)}) copy-start(bf16[2048,1024]{1,0:T(8,128)(2,1)} %copy-done.16) | copy-start | bytes 12582916
  130.7 5.2 %copy-start.24 = (bf16[2048,1024]{1,0:T(8,128)(2,1)S(1)}, bf16[2048,1024]{1,0:T(8,128)(2,1)}, u32[]{:S(2)}) copy-start(bf16[2048,1024]{1,0:T(8,128)(2,1)} %copy-done.23) | copy-start | bytes 12582916
  135.9 47.3 %copy-start.27 = (bf16[512,1024]{1,0:T(8,128)(2,1)}, bf16[512,1024]{1,0:T(8,128)(2,1)S(1)}, u32[]{:S(2)}) copy-start(bf16[512,1024]{1,0:T(8,128)(2,1)S(1)} %get-tuple-element.66.gate_grad.refs_3_) | copy-start | bytes 3145732
  135.9 47.3 %copy-start.29 = (bf16[512,1024]{1,0:T(8,128)(2,1)}, bf16[512,1024]{1,0:T(8,128)(2,1)S(1)}, u32[]{:S(2)}) copy-start(bf16[512,1024]{1,0:T(8,128)(2,1)S(1)} %get-tuple-element.67.up_grad.refs_5_) | copy-start | bytes 3145732
  137.9 15.7 %copy-start.11 = (bf16[1024,64]{0,1:T(8,128)(2,1)S(1)}, bf16[1024,64]{0,1:T(8,128)(2,1)}, u32[]{:S(2)}) copy-start(bf16[1024,64]{0,1:T(8,128)(2,1)} %param.20) | copy-start | bytes 393220
  137.9 15.7 %copy-start.52 = (bf16[192,1024]{1,0:T(8,128)(2,1)S(1)}, bf16[192,1024]{1,0:T(8,128)(2,1)}, u32[]{:S(2)}) copy-start(bf16[192,1024]{1,0:T(8,128)(2,1)} %copy-done.51) | copy-start | bytes 1179652
  137.9 15.7 %collective-permute-start.17 = (bf16[512,512]{1,0:T(8,128)(2,1)S(1)}, bf16[512,512]{1,0:T(8,128)(2,1)S(1)}, u32[]{:S(2)}, u32[]{:S(2)}) collective-permute-start(bf16[512,512]{1,0:T(8,128)(2,1)S(1)} %token_grad.9.refs_1_.refs_0_.refs_14_), channel_id=1, source_target_pairs={{0,1},{3,2},{4,5},{7,6},{8,9},{11,10},{12,13},{15,14},{16,17},{19,... | collective-permute-start | bytes 1572872 | tf_op jit(solution)/shard_map/ppermute | solution.py:560
  145.7 21.4 %collective-permute-start.15 = (bf16[512,512]{1,0:T(8,128)(2,1)}, bf16[512,512]{1,0:T(8,128)(2,1)}, u32[]{:S(2)}, u32[]{:S(2)}) collective-permute-start(bf16[512,512]{1,0:T(8,128)(2,1)} %token_grad.10), channel_id=1, source_target_pairs={{0,1},{1,2},{4,5},{5,6},{8,9},{9,10},{12,13},{13,14},{16,17},{17,1... | collective-permute-start | bytes 1572872 | tf_op jit(solution)/shard_map/ppermute | solution.py:560
  150.9 16.2 %collective-permute-start.16 = (bf16[512,512]{1,0:T(8,128)(2,1)}, bf16[512,512]{1,0:T(8,128)(2,1)}, u32[]{:S(2)}, u32[]{:S(2)}) collective-permute-start(bf16[512,512]{1,0:T(8,128)(2,1)} %token_grad.10), channel_id=1, source_target_pairs={{3,2},{2,1},{7,6},{6,5},{11,10},{10,9},{15,14},{14,13},{19,18},{18... | collective-permute-start | bytes 1572872 | tf_op jit(solution)/shard_map/ppermute | solution.py:560
  153.6 4.1 %copy-start.25 = (bf16[2048,1024]{1,0:T(8,128)(2,1)S(1)}, bf16[2048,1024]{1,0:T(8,128)(2,1)}, u32[]{:S(2)}) copy-start(bf16[2048,1024]{1,0:T(8,128)(2,1)} %copy-done.23) | copy-start | bytes 12582916
  157.7 7.2 %collective-permute-start.24 = (f32[4,192,384]{2,1,0:T(8,128)S(1)}, f32[4,192,384]{2,1,0:T(8,128)S(1)}, u32[]{:S(2)}, u32[]{:S(2)}) collective-permute-start(f32[4,192,384]{2,1,0:T(8,128)S(1)} %get-tuple-element.77), channel_id=1, source_target_pairs={{0,16},{16,0},{1,17},{17,1},{2,18},{18,2},{3,19},{19,3},{4,20},{20... | collective-permute-start | bytes 3538952 | tf_op jit(solution)/shard_map/ppermute | solution.py:138
  159.7 23.5 %collective-permute-start.20 = (bf16[512,512]{1,0:T(8,128)(2,1)S(1)}, bf16[512,512]{1,0:T(8,128)(2,1)S(1)}, u32[]{:S(2)}, u32[]{:S(2)}) collective-permute-start(bf16[512,512]{1,0:T(8,128)(2,1)S(1)} %token_grad.11.refs_3_), channel_id=1, source_target_pairs={{0,1},{1,2},{4,5},{5,6},{8,9},{9,10},{12,13},{13,14},{16,17},{17,1... | collective-permute-start | bytes 1572872 | tf_op jit(solution)/shard_map/ppermute | solution.py:560
  164.1 19.1 %collective-permute-start.21 = (bf16[512,512]{1,0:T(8,128)(2,1)S(1)}, bf16[512,512]{1,0:T(8,128)(2,1)S(1)}, u32[]{:S(2)}, u32[]{:S(2)}) collective-permute-start(bf16[512,512]{1,0:T(8,128)(2,1)S(1)} %token_grad.11.refs_3_), channel_id=1, source_target_pairs={{3,2},{2,1},{7,6},{6,5},{11,10},{10,9},{15,14},{14,13},{19,18},{18... | collective-permute-start | bytes 1572872 | tf_op jit(solution)/shard_map/ppermute | solution.py:560
  165.5 15.5 %collective-permute-start.25 = (f32[2,192,384]{2,1,0:T(8,128)S(1)}, f32[2,192,384]{2,1,0:T(8,128)S(1)}, u32[]{:S(2)}, u32[]{:S(2)}) collective-permute-start(f32[2,192,384]{2,1,0:T(8,128)S(1)} %get-tuple-element.79), channel_id=1, source_target_pairs={{0,8},{4,12},{8,0},{12,4},{1,9},{5,13},{9,1},{13,5},{2,10},{6,14},... | collective-permute-start | bytes 1769480 | tf_op jit(solution)/shard_map/ppermute | solution.py:138
  170.1 23.6 %collective-permute-start.18 = (bf16[512,512]{1,0:T(8,128)(2,1)S(1)}, bf16[512,512]{1,0:T(8,128)(2,1)S(1)}, u32[]{:S(2)}, u32[]{:S(2)}) collective-permute-start(bf16[512,512]{1,0:T(8,128)(2,1)S(1)} %get-tuple-element.69), channel_id=1, source_target_pairs={{0,1},{1,2},{2,3},{4,5},{5,6},{6,7},{8,9},{9,10},{10,11},{12,13},{... | collective-permute-start | bytes 1572872 | tf_op jit(solution)/shard_map/ppermute | solution.py:560
  174.2 19.5 %collective-permute-start.19 = (bf16[512,512]{1,0:T(8,128)(2,1)S(1)}, bf16[512,512]{1,0:T(8,128)(2,1)S(1)}, u32[]{:S(2)}, u32[]{:S(2)}) collective-permute-start(bf16[512,512]{1,0:T(8,128)(2,1)S(1)} %get-tuple-element.70), channel_id=1, source_target_pairs={{3,2},{2,1},{1,0},{7,6},{6,5},{5,4},{11,10},{10,9},{9,8},{15,14},{... | collective-permute-start | bytes 1572872 | tf_op jit(solution)/shard_map/ppermute | solution.py:560
  181.7 10.6 %collective-permute-start.26 = (f32[1,192,384]{2,1,0:T(8,128)S(1)}, f32[1,192,384]{2,1,0:T(8,128)S(1)}, u32[]{:S(2)}, u32[]{:S(2)}) collective-permute-start(f32[1,192,384]{2,1,0:T(8,128)S(1)} %get-tuple-element.81), channel_id=1, source_target_pairs={{0,4},{4,0},{8,12},{12,8},{1,5},{5,1},{9,13},{13,9},{2,6},{6,2},{1... | collective-permute-start | bytes 884744 | tf_op jit(solution)/shard_map/ppermute | solution.py:138
  186.2 33.8 %collective-permute-start.22 = (bf16[512,512]{1,0:T(8,128)(2,1)S(1)}, bf16[512,512]{1,0:T(8,128)(2,1)}, u32[]{:S(2)}, u32[]{:S(2)}) collective-permute-start(bf16[512,512]{1,0:T(8,128)(2,1)S(1)} %get-tuple-element.71.refs_2_), channel_id=1, source_target_pairs={{0,1},{1,2},{2,3},{4,5},{5,6},{6,7},{8,9},{9,10},{10,11},{12,13},{... | collective-permute-start | bytes 1572872 | tf_op jit(solution)/shard_map/ppermute | solution.py:560
  191.0 29.0 %collective-permute-start.23 = (bf16[512,512]{1,0:T(8,128)(2,1)}, bf16[512,512]{1,0:T(8,128)(2,1)}, u32[]{:S(2)}, u32[]{:S(2)}) collective-permute-start(bf16[512,512]{1,0:T(8,128)(2,1)} %get-tuple-element.72.refs_3_), channel_id=1, source_target_pairs={{3,2},{2,1},{1,0},{7,6},{6,5},{5,4},{11,10},{10,9},{9,8},{15,14},{... | collective-permute-start | bytes 1572872 | tf_op jit(solution)/shard_map/ppermute | solution.py:560
  193.0 6.4 %collective-permute-start.29 = (f32[128,192]{1,0:T(8,128)S(1)}, f32[128,192]{1,0:T(8,128)S(1)}, u32[]{:S(2)}, u32[]{:S(2)}) collective-permute-start(f32[128,192]{1,0:T(8,128)S(1)} %get-tuple-element.86), channel_id=1, source_target_pairs={{0,4},{4,0},{8,12},{12,8},{1,5},{5,1},{9,13},{13,9},{2,6},{6,2},{1... | collective-permute-start | bytes 294920 | tf_op jit(solution)/shard_map/ppermute | solution.py:138
  195.6 16.4 %collective-permute-start.27 = (f32[2,64,192]{2,1,0:T(8,128)S(1)}, f32[2,64,192]{2,1,0:T(8,128)S(1)}, u32[]{:S(2)}, u32[]{:S(2)}) collective-permute-start(f32[2,64,192]{2,1,0:T(8,128)S(1)} %get-tuple-element.83), channel_id=1, source_target_pairs={{0,2},{1,3},{2,0},{3,1},{4,6},{5,7},{6,4},{7,5},{8,10},{9,11},{10,... | collective-permute-start | bytes 294920 | tf_op jit(solution)/shard_map/ppermute | solution.py:138
  199.4 13.3 %collective-permute-start.30 = (f32[2,128,192]{2,1,0:T(8,128)S(1)}, f32[2,128,192]{2,1,0:T(8,128)S(1)}, u32[]{:S(2)}, u32[]{:S(2)}) collective-permute-start(f32[2,128,192]{2,1,0:T(8,128)S(1)} %pad_maximum_fusion.5), channel_id=1, source_target_pairs={{0,8},{4,12},{8,0},{12,4},{1,9},{5,13},{9,1},{13,5},{2,10},{6,14},... | collective-permute-start | bytes 589832 | tf_op jit(solution)/shard_map/ppermute | solution.py:138
  212.6 4.3 %collective-permute-start.28 = (f32[1,64,192]{2,1,0:T(8,128)S(1)}, f32[1,64,192]{2,1,0:T(8,128)S(1)}, u32[]{:S(2)}, u32[]{:S(2)}) collective-permute-start(f32[1,64,192]{2,1,0:T(8,128)S(1)} %get-tuple-element.85), channel_id=1, source_target_pairs={{0,1},{1,0},{2,3},{3,2},{4,5},{5,4},{6,7},{7,6},{8,9},{9,8},{10,11... | collective-permute-start | bytes 147464 | tf_op jit(solution)/shard_map/ppermute | solution.py:138
  212.8 5.4 %collective-permute-start.31 = (f32[4,128,192]{2,1,0:T(8,128)S(1)}, f32[4,128,192]{2,1,0:T(8,128)S(1)}, u32[]{:S(2)}, u32[]{:S(2)}) collective-permute-start(f32[4,128,192]{2,1,0:T(8,128)S(1)} %pad_maximum_fusion.4.near), channel_id=1, source_target_pairs={{0,16},{16,0},{1,17},{17,1},{2,18},{18,2},{3,19},{19,3},{4,20},{20... | collective-permute-start | bytes 1179656 | tf_op jit(solution)/shard_map/ppermute | solution.py:138
  220.0 2.2 copy-start.18
  222.2 2.2 copy-start.26
  (21 other events, 27.3 us)
where the time goes:
time: 232 us; the launch traced here: 231 us
  local copies, waits for them, and re-layouts  62.8 us (27%)
  Pallas kernels  58.7 us (25%)
  waiting for transfers between devices  58 us (25%)
  starting transfers between devices  47.5 us (20%)
  other arithmetic  2.34 us (1%)
    unnamed x110, local copies, waits for them, and re-layouts  59.7 us
    pallas_call x19, Pallas kernels, vmem_call(): pl.pallas_call(kernel, in_specs=[pl.BlockSpec(memory_space=pltpu.SMEM)] *...  58.7 us
    ppermute x22, waiting for transfers between devices, flip(): return lax.ppermute(array, axis, [(i, i ^ bit) for i in range(size)])  53.7 us
    ppermute x10, starting transfers between devices, square_plane(): shift = lambda array, pairs: lax.ppermute(array, 'tp', pairs)  29.3 us
    ppermute x22, starting transfers between devices, flip(): return lax.ppermute(array, axis, [(i, i ^ bit) for i in range(size)])  18.2 us
  transfers between devices with their start and end apart: 32, of which 8 were waited for; matrix products, arithmetic and copies ran while one was open for 1% of the time, Pallas kernels for 21%

commit v1 on v0

--- a/solution.py
+++ b/solution.py
@@ -12,7 +12,8 @@
 MEBIBYTE = 1024 * 1024
 COST = 20
 HALVES = 2
-LIMITS = {"first": 14, "next": 10, "last": 18, "token": 8, "adapter": 12, "small": 4}
+COSTS = {"sums": 1, "pair": 1}
+LIMITS = {"low": 6, "sums": 12, "last": 14, "token": 8, "adapter": 12, "small": 4}
 TILE = 512
 STRIP = 256
 QUARTER_ORDER = ((3, 2, 1, 0), (0, 3, 2, 1), (3, 0, 1, 2), (0, 1, 2, 3))
@@ -138,7 +139,9 @@
     return lax.ppermute(array, axis, [(i, i ^ bit) for i in range(size)])
 
 
-def vmem_call(kernel, scalars, arrays, ahead, results, aliases, scratch, limit, flops, name):
+def vmem_call(
+    kernel, scalars, arrays, ahead, results, aliases, scratch, limit, flops, name, final=False
+):
     vmem = pl.BlockSpec(memory_space=pltpu.VMEM)
     first = len(scalars)
     return pl.pallas_call(
@@ -147,7 +150,10 @@
         + [vmem] * len(arrays)
         + [pl.BlockSpec(memory_space=pl.ANY)] * len(ahead),
         out_specs=[vmem] * len(results),
-        out_shape=[pltpu.VMEM(shape, kind) for shape, kind in results],
+        out_shape=[
+            jax.ShapeDtypeStruct(shape, kind) if final else pltpu.VMEM(shape, kind)
+            for shape, kind in results
+        ],
         scratch_shapes=scratch,
         input_output_aliases={first + source: target for source, target in aliases.items()},
         compiler_params=pltpu.CompilerParams(vmem_limit_bytes=limit * MEBIBYTE),
@@ -174,85 +180,134 @@
     return jnp.concatenate([unit[which, :, span] for unit in units], axis=0)
 
 
-def put_in_place(units, here, masks, gate_full, up_full):
+def put_in_place(units, here, gate_full, up_full):
     half = units[0].shape[1]
     for number, unit in enumerate(units):
-        block = lax.bitwise_xor(here[0], masks[number // 2])
+        block = lax.bitwise_xor(here[0], number // 2)
         row = pl.ds(pl.multiple_of((2 * block + number % 2) * half, half), half)
         gate_full[row, :] = unit[0]
         up_full[row, :] = unit[1]
 
 
-def first_kernel(masks, n_units, here, *refs):
-    tokens, cotangent, gate_in, up_in, leave, gate_out, up_out, down_in = refs[:8]
-    units = refs[8 : 8 + n_units]
-    sums, (turned, gate_full, up_full) = refs[-9:-3], refs[-3:]
+def lows_kernel(tokens, cotangent, gate_in, up_in, leave, *refs):
+    gate_low, up_low, back_low, turned = refs[-4:]
+    rank = leave.shape[0]
+    for number, (ref, factor, out) in enumerate(
+        ((tokens, gate_in, gate_low), (tokens, up_in, up_low), (cotangent, leave, back_low))
+    ):
+        low = contract_trailing_axis(ref[...], factor[...]).astype(jnp.bfloat16)
+        out[...] = low
+        turned[number * rank : (number + 1) * rank, :] = low.astype(jnp.float32).T.astype(
+            jnp.bfloat16
+        )
+
+
+def low_rank_values(tokens, cotangent, factors, ahead):
+    rows, width = tokens.shape
+    rank = factors[0].shape[0]
+    return vmem_call(
+        lows_kernel,
+        [],
+        [tokens, cotangent, *factors],
+        ahead,
+        [((rows, rank), jnp.bfloat16)] * 3 + [((3 * rank, rows), jnp.bfloat16)],
+        {},
+        [],
+        LIMITS["low"],
+        24 * rows * width * rank,
+        "low_rank_values",
+    )
+
+
+def pair_kernel(first, second, *refs):
+    refs[-1][0] = first[...]
+    refs[-1][1] = second[...]
+
+
+def pair(first, second, ahead):
+    return vmem_call(
+        pair_kernel,
+        [],
+        [first, second],
+        ahead,
+        [((2, *first.shape), first.dtype)],
+        {},
+        [],
+        LIMITS["small"],
+        COSTS["pair"],
+        "pair",
+    )[0]
+
+
+def single_units(refs):
+    return [
+        part
+        for ref in refs
+        for part in ([ref] if len(ref.shape) == 3 else [ref.at[0], ref.at[1]])
+    ]
+
+
+def sums_kernel(masks, order, n_arrays, last, here, *refs):
+    tokens, cotangent, gate_low, up_low, back_low, gate_out, up_out, down_in = refs[:8]
+    units = single_units(refs[8 : 8 + n_arrays])
+    units = [units[number] for number in order]
+    sums, rest = refs[-8:-2], refs[-2:]
     rows = 2 * units[0].shape[1]
     hidden = units[0].shape[2]
-    rank = leave.shape[0]
-    put_in_place(units, here, masks, gate_full, up_full)
-    tile = tokens.shape[0] // HALVES
-    for half in range(HALVES):
-        part = slice(half * tile, (half + 1) * tile)
-        lows = []
-        for number, (ref, factor) in enumerate(
-            ((tokens, gate_in), (tokens, up_in), (cotangent, leave))
-        ):
-            low = contract_trailing_axis(ref[part, :], factor[...]).astype(jnp.bfloat16)
-            turned[number * rank : (number + 1) * rank, part] = low.astype(jnp.float32).T.astype(
-                jnp.bfloat16
-            )
-            lows.append(low)
-        left = width_part(tokens, part, here, masks, rows)
-        back = width_part(cotangent, part, here, masks, rows)
-        for column in range(0, hidden, TILE):
-            span = slice(column, column + TILE)
-            for which, factor in enumerate((gate_out, up_out, down_in)):
-                sums[3 * half + which][:, span] = matrix_product(
-                    back if which == 2 else left, stacked(units, which, span)
-                ) + adapter_scaling * matrix_product(lows[which], factor[:, span])
-
-
-def next_kernel(masks, n_units, here, *refs):
-    tokens, cotangent = refs[:2]
-    units = refs[2 : 2 + n_units]
-    before = refs[2 + n_units : 8 + n_units]
-    sums, (gate_full, up_full) = refs[-8:-2], refs[-2:]
-    rows = 2 * units[0].shape[1]
-    hidden = units[0].shape[2]
-    put_in_place(units, here, masks, gate_full, up_full)
     tile = tokens.shape[0] // HALVES
     for half in range(HALVES):
         part = slice(half * tile, (half + 1) * tile)
         left = width_part(tokens, part, here, masks, rows)
         back = width_part(cotangent, part, here, masks, rows)
+        for ref, out in zip((tokens, cotangent), rest):
+            out[part, :] = width_part(ref, part, here, last, rows)
         for column in range(0, hidden, TILE):
             span = slice(column, column + TILE)
-            for which in range(3):
-                number = 3 * half + which
-                sums[number][:, span] = before[number][:, span] + matrix_product(
+            for which, (low, factor) in enumerate(
+                ((gate_low, gate_out), (up_low, up_out), (back_low, down_in))
+            ):
+                sums[3 * half + which][:, span] = matrix_product(
                     back if which == 2 else left, stacked(units, which, span)
-                )
-
-
-def last_kernel(masks, n_units, half, n_full, here, *refs):
-    tokens, cotangent, gate_out, up_out = refs[:4]
-    units = refs[4 : 4 + n_units]
-    sums = refs[4 + n_units : 7 + n_units]
-    hidden_out, gate_grad_out, up_grad_out, low_out = refs[len(refs) - 4 - n_full :][:4]
-    if n_full:
-        put_in_place(units, here, masks, *refs[-2:])
-    rows = 2 * units[0].shape[1]
-    count, hidden = hidden_out.shape
-    part = slice(half * count, (half + 1) * count)
-    left = width_part(tokens, part, here, masks, rows)
-    back = width_part(cotangent, part, here, masks, rows)
+                ) + adapter_scaling * matrix_product(low[part, :], factor[:, span])
+
+
+def width_sums(here, tokens, cotangent, lows, factors, masks, order, arrays, last):
+    rows, width = tokens.shape
+    _, half, hidden = arrays[0].shape[-3:]
+    outs = vmem_call(
+        functools.partial(sums_kernel, masks, order, len(arrays), last),
+        [here],
+        [tokens, cotangent, *lows, *factors, *arrays],
+        [],
+        [((rows // HALVES, hidden), jnp.float32)] * (3 * HALVES)
+        + [((rows, 2 * half * len(last)), jnp.bfloat16)] * 2,
+        {},
+        [],
+        LIMITS["sums"],
+        COSTS["sums"],
+        "width_sums",
+    )
+    return outs[:-2], outs[-2:]
+
+
+def last_kernel(half, n_arrays, order, count, here, *refs):
+    left, back, gate_out, up_out = refs[:4]
+    units = single_units(refs[4 : 4 + n_arrays])
+    units = [units[number] for number in order]
+    sums = refs[4 + n_arrays : 7 + n_arrays]
+    outs = refs[-6:] if len(units) > count else refs[-4:]
+    hidden_out, gate_grad_out, up_grad_out, low_out = outs[:4]
+    if len(units) > count:
+        put_in_place(units, here, *outs[4:])
+        units = units[6:8] + units[14:16]
+    rows, hidden = hidden_out.shape
+    part = slice(half * rows, (half + 1) * rows)
     gate_low = up_low = 0.0
     for column in range(0, hidden, STRIP):
         span = slice(column, column + STRIP)
-        gate = sums[0][:, span] + matrix_product(left, stacked(units, 0, span))
-        up = sums[1][:, span] + matrix_product(left, stacked(units, 1, span))
-        hidden_grad = sums[2][:, span] + matrix_product(back, stacked(units, 2, span))
+        gate = sums[0][:, span] + matrix_product(left[part, :], stacked(units, 0, span))
+        up = sums[1][:, span] + matrix_product(left[part, :], stacked(units, 1, span))
+        hidden_grad = sums[2][:, span] + matrix_product(back[part, :], stacked(units, 2, span))
         sig = 1.0 / (1.0 + jnp.exp(-gate))
         gated = gate * sig
         hidden_out[:, span] = (gated * up).astype(jnp.bfloat16)
@@ -265,68 +320,21 @@
     low_out[...] = jnp.concatenate([gate_low, up_low], axis=1)
 
 
-def sums_and_full(rows, width, hidden):
-    return [((rows // HALVES, hidden), jnp.float32)] * (3 * HALVES), [
-        ((width, hidden), jnp.bfloat16)
-    ] * 2
-
-
-def first_sums(here, tokens, cotangent, factors, masks, units):
-    rows, width = tokens.shape
-    hidden = units[0].shape[2]
-    sums, full = sums_and_full(rows, width, hidden)
-    rank = factors[0].shape[0]
+def hidden_and_grads(half, here, parts, factors, order, count, arrays, sums, width, ahead):
+    rows = parts[0].shape[0] // HALVES
+    rank, hidden = factors[0].shape
+    arrays = [*parts, *factors, *arrays, *sums[3 * half : 3 * half + 3]]
+    full = [((width, hidden), jnp.bfloat16)] * 2 if len(order) > count else []
     outs = vmem_call(
-        functools.partial(first_kernel, masks, len(units)),
-        [here],
-        [tokens, cotangent, *factors, *units],
-        [],
-        [*sums, ((3 * rank, rows), jnp.bfloat16), *full],
-        {},
-        [],
-        LIMITS["first"],
-        12 * rows * hidden * units[0].shape[1] * len(units),
-        "first_sums",
-    )
-    return outs[: len(sums)], outs[len(sums)], outs[len(sums) + 1 :]
-
-
-def next_sums(here, tokens, cotangent, masks, units, before, full):
-    rows, width = tokens.shape
-    hidden = units[0].shape[2]
-    sums, shapes = sums_and_full(rows, width, hidden)
-    first = 2 + len(units)
-    outs = vmem_call(
-        functools.partial(next_kernel, masks, len(units)),
-        [here],
-        [tokens, cotangent, *units, *before, *full],
-        [],
-        [*sums, *shapes],
-        {first + number: number for number in range(len(sums) + 2)},
-        [],
-        LIMITS["next"],
-        12 * rows * hidden * units[0].shape[1] * len(units),
-        "next_sums",
-    )
-    return outs[: len(sums)], outs[len(sums) :]
-
-
-def hidden_and_grads(half, here, tokens, cotangent, factors, masks, units, sums, full, ahead):
-    rows = tokens.shape[0] // HALVES
-    rank, hidden = factors[0].shape
-    arrays = [tokens, cotangent, *factors, *units, *sums[3 * half : 3 * half + 3]]
-    outs = vmem_call(
-        functools.partial(last_kernel, masks, len(units), half, len(full)),
-        [here],
-        [*arrays, *full],
+        functools.partial(last_kernel, half, len(arrays) - 7, order, count),
+        [here],
+        arrays,
         ahead,
-        [((rows, hidden), jnp.bfloat16)] * 3
-        + [((rows, 2 * rank), jnp.float32)]
-        + [(array.shape, array.dtype) for array in full],
-        {len(arrays) + number: 4 + number for number in range(len(full))},
+        [((rows, hidden), jnp.bfloat16)] * 3 + [((rows, 2 * rank), jnp.float32)] + full,
+        {},
         [],
         LIMITS["last"],
-        24 * rows * hidden * units[0].shape[1] * len(units),
+        24 * rows * hidden * parts[0].shape[1],
         "hidden_and_grads",
     )
     return outs[:4], outs[4:]
@@ -365,6 +373,7 @@
         LIMITS["token"],
         8 * rows * columns * hidden,
         "token_grad",
+        mode == "last",
     )
     return outs if mode == "both" else outs[0]
 
@@ -425,20 +434,20 @@
     )
 
 
-def halve_kernel(here, keep, came, *outs):
-    count = keep.shape[0] // len(outs)
-    for number, out in enumerate(outs):
-        span = slice(number * count, (number + 1) * count)
-        out[...] = keep[span] + came[span]
-
-
-def halve(here, keep, came, parts=2):
+def halve_kernel(here, keep, came, kept, send):
+    count = kept.shape[0]
+    kept[...] = keep[:count] + came[:count].astype(jnp.float32)
+    send[...] = (keep[count:] + came[count:].astype(jnp.float32)).astype(send.dtype)
+
+
+def halve(here, keep, came):
+    shape = (keep.shape[0] // 2, *keep.shape[1:])
     return vmem_call(
         halve_kernel,
         [here],
         [keep, came],
         [],
-        [((keep.shape[0] // parts, *keep.shape[1:]), keep.dtype)] * parts,
+        [(shape, jnp.float32), (shape, jnp.bfloat16)],
         {},
         [],
         LIMITS["small"],
@@ -447,14 +456,34 @@
     )
 
 
+def sum_kernel(here, keep, came, out):
+    out[...] = keep[0] + came[0].astype(jnp.float32)
+
+
+def last_sum(here, keep, came):
+    return vmem_call(
+        sum_kernel,
+        [here],
+        [keep, came],
+        [],
+        [(keep.shape[1:], jnp.float32)],
+        {},
+        [],
+        LIMITS["small"],
+        500 * MEBIBYTE,
+        "last_sum",
+        True,
+    )[0]
+
+
 def turn_kernel(wide_columns, here, kept, came, narrow, keep, send, wide):
-    total = kept[0] + came[0]
+    total = kept[0] + came[0].astype(jnp.float32)
     narrow[...] = total[:, wide_columns:].T
     wide[...] = total[:, :wide_columns].T
     rows = keep.shape[1]
     for mask in range(4):
         block = pl.ds(pl.multiple_of(lax.bitwise_xor(here[1], mask) * rows, rows), rows)
-        (keep if mask < 2 else send)[mask % 2] = wide[block, :]
+        (keep if mask < 2 else send)[mask % 2] = wide[block, :].astype((keep if mask < 2 else send).dtype)
 
 
 def turn(here, keep, came, wide_columns):
@@ -465,7 +494,7 @@
         [keep, came],
         [],
         [((columns - wide_columns, rows), keep.dtype)]
-        + [((2, wide_columns // 4, rows), keep.dtype)] * 2,
+        + [((2, wide_columns // 4, rows), kind) for kind in (jnp.float32, jnp.bfloat16)],
         {},
         [pltpu.VMEM((wide_columns, rows), keep.dtype)],
         LIMITS["small"],
@@ -495,6 +524,7 @@
         LIMITS["small"],
         500 * MEBIBYTE,
         "whole",
+        True,
     )[0]
 
 
@@ -540,25 +570,32 @@
     units[2, 0] = flip(units[0, 0], "fsdp", 2)
     units[3, 0] = flip(units[1, 0], "fsdp", 2)
     units[3, 1] = flip(units[2, 1], "fsdp", 1)
-    for mask in range(4):
-        for half in range(2):
-            units[mask | 4, half] = flip(units[mask, half], "cuts", 1)
-    pick = lambda masks: [units[mask, half] for mask in masks for half in range(2)]
-
-    sums, turned, full = first_sums(
-        here,
-        tokens,
-        cotangent,
-        [gate_in, up_in, leave, gate_out, up_out, down_in],
-        (0, 4),
-        pick((0, 4)),
-    )
-    masks = (1, 2, 5, 6)
-    sums, full = next_sums(here, tokens, cotangent, masks, pick(masks), sums, full)
+    for half in range(2):
+        units[4, half] = flip(units[0, half], "cuts", 1)
+    *lows, turned = low_rank_values(
+        tokens, cotangent, [gate_in, up_in, leave], [units[1, 0], units[2, 1]]
+    )
+    pairs = {}
+    for number, (one, two, ahead) in enumerate(
+        (((1, 0), (2, 1), [turned]), ((1, 1), (2, 0), [turned]))
+    ):
+        pairs[number] = flip(pair(units[one], units[two], ahead), "cuts", 1)
+    keys = [(0, 0), (0, 1), (1, 0), (1, 1), (2, 0), (2, 1), (4, 0), (4, 1)]
+    placed = keys + [(5, 0), (6, 1), (5, 1), (6, 0)]
+    arrays = [units[key] for key in keys] + [pairs[0], pairs[1]]
+    masks = (0, 1, 2, 4, 5, 6)
+    order = [placed.index((mask, half)) for mask in masks for half in range(2)]
+    sums, parts = width_sums(
+        here, tokens, cotangent, lows, [gate_out, up_out, down_in], masks, order, arrays, (3, 7)
+    )
+    tail = [units[3, 0], units[3, 1]]
+    tail.append(flip(pair(*tail, [sums[0]]), "cuts", 1))
+    placed = [(3, 0), (3, 1), (7, 0), (7, 1), *placed]
+    order = [placed.index((mask, half)) for mask in range(8) for half in range(2)]
 
     factor = jnp.concatenate([gate_in, up_in])
     shift = lambda array, pairs: lax.ppermute(array, "tp", pairs)
-    states, first = [], []
+    states, first, full = [], [], []
     share = lambda step, half, mode, came=(), ahead=(): token_grad(
         mode,
         step,
@@ -573,13 +610,13 @@
         state, placed = hidden_and_grads(
             half,
             here,
-            tokens,
-            cotangent,
+            parts,
             [gate_out, up_out],
-            (3, 7),
-            pick((3, 7)),
+            range(4) if half else order,
+            4,
+            tail if half else tail + arrays,
             sums,
-            [] if half else full,
+            width,
             first[:],
         )
         full = placed or full
@@ -607,13 +644,13 @@
             turned,
             down_in,
         ],
-        [came[1], *first],
+        first,
     )
     keep, send = halve(here, keep, flip(send, "cuts", 1))
     keep, send = halve(here, keep, flip(send, "fsdp", 2))
     narrow, keep, send = turn(here, keep, flip(send, "fsdp", 1), width // groups)
     keep, send = halve(here, keep, flip(send, "tp", 2))
-    wide_grads = halve(here, keep, flip(send, "tp", 1), 1)[0][0]
+    wide_grads = last_sum(here, keep, flip(send, "tp", 1))
     near = jnp.stack([narrow, flip(narrow, "fsdp", 1)])
     near = jnp.concatenate([near, flip(near, "fsdp", 2)])
     narrow_grads = whole(here, near, flip(near, "cuts", 1))

time: 232 us -> 200 us (0.86)
  local copies, waits for them, and re-layouts: 62.8 us -> 29.2 us
  waiting for transfers between devices: 58 us -> 50.1 us
  starting transfers between devices: 47.5 us -> 53.1 us
  Pallas kernels: 58.7 us -> 62.1 us
    unnamed x110 -> x97, local copies, waits for them, and re-layouts: 59.7 us -> 26.9 us
    ppermute x22 -> x19, waiting for transfers between devices: 53.7 us -> 31.7 us  [flip(): return lax.ppermute(array, axis, [(i, i ^ bit) for i in range(size)])]
    ppermute x10, waiting for transfers between devices: 4.32 us -> 18.5 us  [square_plane(): shift = lambda array, pairs: lax.ppermute(array, 'tp', pairs)]
    pallas_call x19 -> x22, Pallas kernels: 58.7 us -> 62.1 us  [vmem_call(): pl.pallas_call(kernel, in_specs=[pl.BlockSpec(memory_space=pltpu.SMEM)] *...]
    ppermute x10, starting transfers between devices: 29.3 us -> 32.4 us  [square_plane(): shift = lambda array, pairs: lax.ppermute(array, 'tp', pairs)]
    ppermute x22 -> x19, starting transfers between devices: 18.2 us -> 20.7 us  [flip(): return lax.ppermute(array, axis, [(i, i ^ bit) for i in range(size)])]
  transfers between devices with their start and end apart: 32 -> 29, of which waited for: 8 -> 12; matrix products, arithmetic and copies ran while one was open for 1% -> 1% of each run, Pallas kernels for 21% -> 24%
where the time goes in v1:
time: 200 us; the launch traced here: 199 us
  Pallas kernels  62.1 us (31%)
  starting transfers between devices  53.1 us (27%)
  waiting for transfers between devices  50.1 us (25%)
  local copies, waits for them, and re-layouts  29.2 us (15%)
  other arithmetic  3.14 us (2%)
    pallas_call x22, Pallas kernels, vmem_call(): pl.pallas_call(kernel, in_specs=[pl.BlockSpec(memory_space=pltpu.SMEM)] *...  62.1 us
    ppermute x10, starting transfers between devices, square_plane(): shift = lambda array, pairs: lax.ppermute(array, 'tp', pairs)  32.4 us
    ppermute x19, waiting for transfers between devices, flip(): return lax.ppermute(array, axis, [(i, i ^ bit) for i in range(size)])  31.7 us
    unnamed x97, local copies, waits for them, and re-layouts  26.9 us
    ppermute x19, starting transfers between devices, flip(): return lax.ppermute(array, axis, [(i, i ^ bit) for i in range(size)])  20.7 us
    ppermute x10, waiting for transfers between devices, square_plane(): shift = lambda array, pairs: lax.ppermute(array, 'tp', pairs)  18.5 us
  transfers between devices with their start and end apart: 29, of which 12 were waited for; matrix products, arithmetic and copies ran while one was open for 1% of the time, Pallas kernels for 24%

profile of v1, /device:TPU:0, one launch (start us, length us, event | category | flops | bytes accessed | tf_op | source)
XLA Modules:
  0.0 199.0 jit_solution(13799505418289263262)
XLA Ops:
  0.6 1.1 fusion
  1.9 1.3 slice_bitcast_fusion
  3.1 1.0 pad_maximum_fusion.1.refs_8_.refs_7_
  4.1 2.9 %collective-permute-start = (bf16[3,128,1024]{2,1,0:T(8,128)(2,1)}, bf16[3,128,1024]{2,1,0:T(8,128)(2,1)S(1)}, u32[]{:S(2)}, u32[]{:S(2)}) collective-permute-start(bf16[3,128,1024]{2,1,0:T(8,128)(2,1)} %pad_maximum_fusion.1.refs_8_.refs_7_), channel_id=1, source_target_pairs={{0,4},{4,0},{8,12},{12,8},{1,5},{5,1},{9,13},{13,9},{2,6},{6,2},{1... | collective-permute-start | bytes 2359304 | tf_op jit(solution)/shard_map/ppermute | solution.py:139
  7.2 1.0 pad_maximum_fusion.2.refs_9_.refs_8_
  8.1 1.5 collective-permute-start.1
  10.2 15.4 %collective-permute-done.refs_0_.first.refs_10_.refs_9_ = bf16[3,128,1024]{2,1,0:T(8,128)(2,1)S(1)} collective-permute-done((bf16[3,128,1024]{2,1,0:T(8,128)(2,1)}, bf16[3,128,1024]{2,1,0:T(8,128)(2,1)S(1)}, u32[]{:S(2)}, u32[]{:S(2)}) %collective-permute-start) | collective-permute-done | bytes 786464 | tf_op jit(solution)/shard_map/ppermute | solution.py:139
  25.6 3.2 %collective-permute-done.1.refs_1_.second.refs_13_.refs_12_ = bf16[3,128,1024]{2,1,0:T(8,128)(2,1)S(1)} collective-permute-done((bf16[3,128,1024]{2,1,0:T(8,128)(2,1)}, bf16[3,128,1024]{2,1,0:T(8,128)(2,1)S(1)}, u32[]{:S(2)}, u32[]{:S(2)}) %collective-permute-start.1) | collective-permute-done | bytes 786464 | tf_op jit(solution)/shard_map/ppermute | solution.py:139
  28.8 2.2 %copy-done = bf16[1024,2048]{1,0:T(8,128)(2,1)S(1)} copy-done((bf16[1024,2048]{1,0:T(8,128)(2,1)S(1)}, bf16[1024,2048]{1,0:T(8,128)(2,1)}, u32[]{:S(2)}) %copy-start) | copy-done | bytes 4194328
  31.0 2.2 %copy-done.3 = bf16[1024,2048]{1,0:T(8,128)(2,1)S(1)} copy-done((bf16[1024,2048]{1,0:T(8,128)(2,1)S(1)}, bf16[1024,2048]{1,0:T(8,128)(2,1)}, u32[]{:S(2)}) %copy-start.3) | copy-done | bytes 4194328
  33.2 0.9 copy-done.17
  34.1 0.9 copy-done.19
  35.1 0.9 copy-done.28
  36.0 3.5 %low_rank_values.1 = (bf16[1024,64]{1,0:T(8,128)(2,1)S(1)}, bf16[1024,64]{1,0:T(8,128)(2,1)S(1)}, bf16[1024,64]{1,0:T(8,128)(2,1)S(1)}, bf16[192,1024]{1,0:T(8,128)(2,1)S(1)}) custom-call(bf16[1024,2048]{1,0:T(8,128)(2,1)S(1)} %copy-done, bf16[1024,2048]{1,0:T(8,128)(2,1)S(1)} %copy-done.3, bf16[64,2048]{1,0:T(8,128)(2,1)S(1)} %bitcast.24, ...), custom_call_target="tpu_custom_call" | custom-call | flops 64424509440 | tf_op jit(solution)/shard_map/low_rank_values/pallas_call | solution.py:147
  39.6 1.4 pair.3
  41.6 2.6 %collective-permute-done.3.second.refs_12_.refs_11_ = bf16[3,128,1024]{2,1,0:T(8,128)(2,1)S(1)} collective-permute-done((bf16[3,128,1024]{2,1,0:T(8,128)(2,1)}, bf16[3,128,1024]{2,1,0:T(8,128)(2,1)S(1)}, u32[]{:S(2)}, u32[]{:S(2)}) %collective-permute-start.3) | collective-permute-done | bytes 786464 | tf_op jit(solution)/shard_map/ppermute | solution.py:139
  44.2 1.3 pair.4
  46.1 1.5 collective-permute-start.8
  47.6 3.4 %collective-permute-done.4.refs_14_.refs_13_ = bf16[3,128,1024]{2,1,0:T(8,128)(2,1)S(1)} collective-permute-done((bf16[3,128,1024]{2,1,0:T(8,128)(2,1)}, bf16[3,128,1024]{2,1,0:T(8,128)(2,1)S(1)}, u32[]{:S(2)}, u32[]{:S(2)}) %collective-permute-start.4) | collective-permute-done | bytes 786464 | tf_op jit(solution)/shard_map/ppermute | solution.py:139
  52.4 2.2 %copy-done.1 = bf16[1024,2048]{1,0:T(8,128)(2,1)S(1)} copy-done((bf16[1024,2048]{1,0:T(8,128)(2,1)S(1)}, bf16[1024,2048]{1,0:T(8,128)(2,1)}, u32[]{:S(2)}) %copy-start.1) | copy-done | bytes 4194328
  54.6 2.2 %copy-done.4 = bf16[1024,2048]{1,0:T(8,128)(2,1)S(1)} copy-done((bf16[1024,2048]{1,0:T(8,128)(2,1)S(1)}, bf16[1024,2048]{1,0:T(8,128)(2,1)}, u32[]{:S(2)}) %copy-start.4) | copy-done | bytes 4194328
  56.8 1.1 copy-done.9
  57.9 0.9 copy-done.14
  61.6 14.3 %width_sums.1 = (f32[512,1024]{1,0:T(8,128)S(1)}, f32[512,1024]{1,0:T(8,128)S(1)}, f32[512,1024]{1,0:T(8,128)S(1)}, f32[512,1024]{1,0:T(8,128)S(1)}, f32[512,102...) custom-call(s32[2]{0:T(128)S(1)} %pad_add_fusion.here, ...), custom_call_target="tpu_custom_call" | custom-call | flops 20 | tf_op jit(solution)/shard_map/width_sums/pallas_call | solution.py:147
  76.0 1.7 pair.5
  78.0 3.3 %collective-permute-done.10.refs_6_ = bf16[2,3,128,1024]{3,2,1,0:T(8,128)(2,1)S(1)} collective-permute-done((bf16[2,3,128,1024]{3,2,1,0:T(8,128)(2,1)S(1)}, bf16[2,3,128,1024]{3,2,1,0:T(8,128)(2,1)S(1)}, u32[]{:S(2)}, u32[]{:S(2)}) %collective-permute-start.10) | collective-permute-done | bytes 1572896 | tf_op jit(solution)/shard_map/ppermute | solution.py:139
  81.3 7.4 %hidden_and_grads.2 = (bf16[512,1024]{1,0:T(8,128)(2,1)S(1)}, bf16[512,1024]{1,0:T(8,128)(2,1)S(1)}, bf16[512,1024]{1,0:T(8,128)(2,1)S(1)}, f32[512,128]{1,0:T(8...) custom-call(s32[2]{0:T(128)S(1)} %pad_add_fusion.here, ...), custom_call_target="tpu_custom_call" | custom-call | flops 128849018880 | tf_op jit(solution)/shard_map/hidden_and_grads/pallas_call | solution.py:147
  88.8 3.5 %token_grad.8.refs_10_.refs_0_.refs_12_ = bf16[512,512]{1,0:T(8,128)(2,1)} custom-call(s32[2]{0:T(128)S(1)} %pad_add_fusion.here, bf16[512,1024]{1,0:T(8,128)(2,1)S(1)} %get-tuple-element.49.gate_grad.refs_2_, bf16[512,1024]{1,0:T(8,128)(2,1)S(1)} %get-tuple-element.50.up_grad.refs_4_, f32[512,128]{1,0:T(8,128)S(1)} %get-tuple-element.51.low.refs_6_, ...), custom_call_target="tpu_custom_call" | custom-call | flops 42949672960 | tf_op jit(solution)/shard_map/token_grad/pallas_call | solution.py:147
  92.3 4.5 %collective-permute-start.11 = (bf16[512,512]{1,0:T(8,128)(2,1)}, bf16[512,512]{1,0:T(8,128)(2,1)}, u32[]{:S(2)}, u32[]{:S(2)}) collective-permute-start(bf16[512,512]{1,0:T(8,128)(2,1)} %token_grad.8.refs_10_.refs_0_.refs_12_), channel_id=1, source_target_pairs={{0,1},{3,2},{4,5},{7,6},{8,9},{11,10},{12,13},{15,14},{16,17},{19,... | collective-permute-start | bytes 1572872 | tf_op jit(solution)/shard_map/ppermute | solution.py:597
  96.8 4.8 %hidden_and_grads.3 = (bf16[512,1024]{1,0:T(8,128)(2,1)S(1)}, bf16[512,1024]{1,0:T(8,128)(2,1)S(1)}, bf16[512,1024]{1,0:T(8,128)(2,1)S(1)}, f32[512,128]{1,0:T(8,128)S(1)}) custom-call(s32[2]{0:T(128)S(1)} %pad_add_fusion.here, bf16[1024,512]{1,0:T(8,128)(2,1)S(1)} %get-tuple-element.44.refs_0_, bf16[1024,512]{1,0:T(8,128)(2,1)S(1)} %get-tuple-element.45.refs_1_, ...), custom_call_target="tpu_custom_call" | custom-call | flops 128849018880 | tf_op jit(solution)/shard_map/hidden_and_grads/pallas_call | solution.py:147
  101.7 2.0 token_grad.9.refs_1_.refs_0_.refs_13_
  103.7 1.8 collective-permute-start.14
  106.6 4.0 %adapter_grads.1 = (f32[4,192,384]{2,1,0:T(8,128)S(1)}, f32[4,192,384]{2,1,0:T(8,128)S(1)}) custom-call(s32[2]{0:T(128)S(1)} %pad_add_fusion.here, bf16[512,1024]{1,0:T(8,128)(2,1)S(1)} %get-tuple-element.64.refs_0_, bf16[512,1024]{1,0:T(8,128)(2,1)S(1)} %get-tuple-element.65.refs_1_, bf16[512,1024]{1,0:T(8,128)(2,1)S(1)} %copy-done.40, ...), custom_call_target="tpu_custom_call" | custom-call | flops 96636764160 | tf_op jit(solution)/shard_map/adapter_grads/pallas_call | solution.py:147
  110.7 8.2 %collective-permute-done.14.refs_0_ = bf16[512,512]{1,0:T(8,128)(2,1)S(1)} collective-permute-done((bf16[512,512]{1,0:T(8,128)(2,1)S(1)}, bf16[512,512]{1,0:T(8,128)(2,1)S(1)}, u32[]{:S(2)}, u32[]{:S(2)}) %collective-permute-start.14) | collective-permute-done | bytes 524320 | tf_op jit(solution)/shard_map/ppermute | solution.py:597
  118.9 2.0 token_grad.11.refs_3_
  120.9 4.4 %collective-permute-start.17 = (bf16[512,512]{1,0:T(8,128)(2,1)S(1)}, bf16[512,512]{1,0:T(8,128)(2,1)S(1)}, u32[]{:S(2)}, u32[]{:S(2)}) collective-permute-start(bf16[512,512]{1,0:T(8,128)(2,1)S(1)} %token_grad.11.refs_3_), channel_id=1, source_target_pairs={{0,1},{1,2},{4,5},{5,6},{8,9},{9,10},{12,13},{13,14},{16,17},{17,1... | collective-permute-start | bytes 1572872 | tf_op jit(solution)/shard_map/ppermute | solution.py:597
  126.0 2.5 %token_grad.10 = bf16[512,512]{1,0:T(8,128)(2,1)S(1)} custom-call(s32[2]{0:T(128)S(1)} %pad_add_fusion.here, bf16[512,1024]{1,0:T(8,128)(2,1)S(1)} %copy-done.40, bf16[512,1024]{1,0:T(8,128)(2,1)S(1)} %copy-done.42, f32[512,128]{1,0:T(8,128)S(1)} %copy-done.46, bf16[128,2048]{1,0:T(8,128)(2,1)S(1)} %pad_maximum_fusion.3.factor, ...), custom_call_target="tpu_custom_call" | custom-call | flops 42949672960 | tf_op jit(solution)/shard_map/token_grad/pallas_call | solution.py:147
  128.5 4.1 %collective-permute-start.12 = (bf16[512,512]{1,0:T(8,128)(2,1)S(1)}, bf16[512,512]{1,0:T(8,128)(2,1)S(1)}, u32[]{:S(2)}, u32[]{:S(2)}) collective-permute-start(bf16[512,512]{1,0:T(8,128)(2,1)S(1)} %token_grad.10), channel_id=1, source_target_pairs={{0,1},{1,2},{4,5},{5,6},{8,9},{9,10},{12,13},{13,14},{16,17},{17,1... | collective-permute-start | bytes 1572872 | tf_op jit(solution)/shard_map/ppermute | solution.py:597
  134.0 1.6 collective-permute-start.22
  135.5 2.1 %collective-permute-done.17.refs_1_ = bf16[512,512]{1,0:T(8,128)(2,1)S(1)} collective-permute-done((bf16[512,512]{1,0:T(8,128)(2,1)S(1)}, bf16[512,512]{1,0:T(8,128)(2,1)S(1)}, u32[]{:S(2)}, u32[]{:S(2)}) %collective-permute-start.17) | collective-permute-done | bytes 524320 | tf_op jit(solution)/shard_map/ppermute | solution.py:597
  137.6 2.1 %token_grad.13 = (bf16[512,512]{1,0:T(8,128)(2,1)S(1)}, bf16[512,512]{1,0:T(8,128)(2,1)S(1)}) custom-call(s32[2]{0:T(128)S(1)} %pad_add_fusion.here, bf16[512,1024]{1,0:T(8,128)(2,1)S(1)} %get-tuple-element.57.gate_grad.refs_3_, bf16[512,1024]{1,0:T(8,128)(2,1)S(1)} %get-tuple-element.58.up_grad.refs_5_, f32[512,128]{1,0:T(8,128)S(1)} %get-tuple-element.59.low.refs_7_, ...), custom_call_target="tpu_custom_call" | custom-call | flops 42949672960 | tf_op jit(solution)/shard_map/token_grad/pallas_call | solution.py:147
  139.8 8.7 %collective-permute-start.19 = (bf16[512,512]{1,0:T(8,128)(2,1)S(1)}, bf16[512,512]{1,0:T(8,128)(2,1)}, u32[]{:S(2)}, u32[]{:S(2)}) collective-permute-start(bf16[512,512]{1,0:T(8,128)(2,1)S(1)} %get-tuple-element.62.refs_2_), channel_id=1, source_target_pairs={{0,1},{1,2},{2,3},{4,5},{5,6},{6,7},{8,9},{9,10},{10,11},{12,13},{... | collective-permute-start | bytes 1572872 | tf_op jit(solution)/shard_map/ppermute | solution.py:597
  148.5 1.3 collective-permute-start.20
  150.4 1.5 collective-permute-start.23
  151.9 2.6 %token_grad.12 = (bf16[512,512]{1,0:T(8,128)(2,1)S(1)}, bf16[512,512]{1,0:T(8,128)(2,1)S(1)}) custom-call(s32[2]{0:T(128)S(1)} %pad_add_fusion.here, bf16[512,1024]{1,0:T(8,128)(2,1)S(1)} %copy-done.40, bf16[512,1024]{1,0:T(8,128)(2,1)S(1)} %copy-done.42, f32[512,128]{1,0:T(8,128)S(1)} %copy-done.46, bf16[128,2048]{1,0:T(8,128)(2,1)S(1)} %pad_maximum_fusion.3.factor, ...), custom_call_target="tpu_custom_call" | custom-call | flops 42949672960 | tf_op jit(solution)/shard_map/token_grad/pallas_call | solution.py:147
  154.6 4.9 %collective-permute-start.15 = (bf16[512,512]{1,0:T(8,128)(2,1)S(1)}, bf16[512,512]{1,0:T(8,128)(2,1)S(1)}, u32[]{:S(2)}, u32[]{:S(2)}) collective-permute-start(bf16[512,512]{1,0:T(8,128)(2,1)S(1)} %get-tuple-element.60), channel_id=1, source_target_pairs={{0,1},{1,2},{2,3},{4,5},{5,6},{6,7},{8,9},{9,10},{10,11},{12,13},{... | collective-permute-start | bytes 1572872 | tf_op jit(solution)/shard_map/ppermute | solution.py:597
  159.4 1.3 collective-permute-start.16
  161.5 1.5 collective-permute-start.26
  163.0 6.6 %collective-permute-done.15.refs_0_ = bf16[512,512]{1,0:T(8,128)(2,1)S(1)} collective-permute-done((bf16[512,512]{1,0:T(8,128)(2,1)S(1)}, bf16[512,512]{1,0:T(8,128)(2,1)S(1)}, u32[]{:S(2)}, u32[]{:S(2)}) %collective-permute-start.15) | collective-permute-done | bytes 524320 | tf_op jit(solution)/shard_map/ppermute | solution.py:597
  169.6 1.6 collective-permute-done.16.refs_1_
  171.2 2.0 %token_grad.14 = bf16[512,512]{1,0:T(8,128)(2,1)S(1)} custom-call(s32[2]{0:T(128)S(1)} %pad_add_fusion.here, bf16[512,1024]{1,0:T(8,128)(2,1)S(1)} %copy-done.40, bf16[512,1024]{1,0:T(8,128)(2,1)S(1)} %copy-done.42, f32[512,128]{1,0:T(8,128)S(1)} %copy-done.46, bf16[128,2048]{1,0:T(8,128)(2,1)S(1)} %pad_maximum_fusion.3.factor, ...), custom_call_target="tpu_custom_call" | custom-call | flops 42949672960 | tf_op jit(solution)/shard_map/token_grad/pallas_call | solution.py:147
  173.2 3.2 %collective-permute-start.24 = (bf16[2,64,192]{2,1,0:T(8,128)(2,1)S(1)}, bf16[2,64,192]{2,1,0:T(8,128)(2,1)S(1)}, u32[]{:S(2)}, u32[]{:S(2)}) collective-permute-start(bf16[2,64,192]{2,1,0:T(8,128)(2,1)S(1)} %get-tuple-element.73), channel_id=1, source_target_pairs={{0,2},{1,3},{2,0},{3,1},{4,6},{5,7},{6,4},{7,5},{8,10},{9,11},{10,... | collective-permute-start | bytes 147464 | tf_op jit(solution)/shard_map/ppermute | solution.py:139
  176.5 1.6 collective-permute-start.27
  178.1 1.4 collective-permute-done.24.came
  180.0 3.5 %collective-permute-start.25 = (bf16[1,64,192]{2,1,0:T(8,128)(2,1)S(1)}, bf16[1,64,192]{2,1,0:T(8,128)(2,1)S(1)}, u32[]{:S(2)}, u32[]{:S(2)}) collective-permute-start(bf16[1,64,192]{2,1,0:T(8,128)(2,1)S(1)} %get-tuple-element.75), channel_id=1, source_target_pairs={{0,1},{1,0},{2,3},{3,2},{4,5},{5,4},{6,7},{7,6},{8,9},{9,8},{10,11... | collective-permute-start | bytes 73736 | tf_op jit(solution)/shard_map/ppermute | solution.py:139
  183.6 1.8 collective-permute-done.25.came
  185.4 1.2 last_sum.1.refs_4_
  187.2 1.2 copy.16
  188.5 2.2 %copy-done.32 = bf16[2048,1024]{1,0:T(8,128)(2,1)S(1)} copy-done((bf16[2048,1024]{1,0:T(8,128)(2,1)S(1)}, bf16[2048,1024]{1,0:T(8,128)(2,1)}, u32[]{:S(2)}) %copy-start.32) | copy-done | bytes 4194328
  190.6 2.2 %copy-done.34 = bf16[2048,1024]{1,0:T(8,128)(2,1)S(1)} copy-done((bf16[2048,1024]{1,0:T(8,128)(2,1)S(1)}, bf16[2048,1024]{1,0:T(8,128)(2,1)}, u32[]{:S(2)}) %copy-start.34) | copy-done | bytes 4194328
  192.8 1.2 copy-done.36
  194.1 1.2 copy-done.38
  195.3 2.7 %token_grad.15 = bf16[512,512]{1,0:T(8,128)(2,1)S(1)} custom-call(s32[2]{0:T(128)S(1)} %pad_add_fusion.here, bf16[512,1024]{1,0:T(8,128)(2,1)S(1)} %copy-done.36, bf16[512,1024]{1,0:T(8,128)(2,1)S(1)} %copy-done.38, f32[512,128]{1,0:T(8,128)S(1)} %copy-done.44, bf16[128,2048]{1,0:T(8,128)(2,1)S(1)} %copy-done.12, bf16[2048,1024]{1,0:T(8,128)(2,1)S(1)} %copy-done.32, ...), custom_call_target="tpu_custom_call" | custom-call | flops 42949672960 | tf_op jit(solution)/shard_map/token_grad/pallas_call | solution.py:147
  198.0 1.0 pad_maximum_fusion
  (122 shorter events, 12.5 us)
Async XLA Ops:
  4.1 21.5 %collective-permute-start = (bf16[3,128,1024]{2,1,0:T(8,128)(2,1)}, bf16[3,128,1024]{2,1,0:T(8,128)(2,1)S(1)}, u32[]{:S(2)}, u32[]{:S(2)}) collective-permute-start(bf16[3,128,1024]{2,1,0:T(8,128)(2,1)} %pad_maximum_fusion.1.refs_8_.refs_7_), channel_id=1, source_target_pairs={{0,4},{4,0},{8,12},{12,8},{1,5},{5,1},{9,13},{13,9},{2,6},{6,2},{1... | collective-permute-start | bytes 2359304 | tf_op jit(solution)/shard_map/ppermute | solution.py:139
  8.1 20.7 %collective-permute-start.1 = (bf16[3,128,1024]{2,1,0:T(8,128)(2,1)}, bf16[3,128,1024]{2,1,0:T(8,128)(2,1)S(1)}, u32[]{:S(2)}, u32[]{:S(2)}) collective-permute-start(bf16[3,128,1024]{2,1,0:T(8,128)(2,1)} %pad_maximum_fusion.2.refs_9_.refs_8_), channel_id=1, source_target_pairs={{0,8},{4,12},{8,0},{12,4},{1,9},{5,13},{9,1},{13,5},{2,10},{6,14},... | collective-permute-start | bytes 2359304 | tf_op jit(solution)/shard_map/ppermute | solution.py:139
  9.7 32.0 %collective-permute-start.2 = (bf16[3,128,1024]{2,1,0:T(8,128)(2,1)}, bf16[3,128,1024]{2,1,0:T(8,128)(2,1)S(1)}, u32[]{:S(2)}, u32[]{:S(2)}) collective-permute-start(bf16[3,128,1024]{2,1,0:T(8,128)(2,1)} %pad_maximum_fusion.2.refs_9_.refs_8_), channel_id=1, source_target_pairs={{0,4},{4,0},{8,12},{12,8},{1,5},{5,1},{9,13},{13,9},{2,6},{6,2},{1... | collective-permute-start | bytes 2359304 | tf_op jit(solution)/shard_map/ppermute | solution.py:139
  10.2 34.0 %collective-permute-start.3 = (bf16[3,128,1024]{2,1,0:T(8,128)(2,1)}, bf16[3,128,1024]{2,1,0:T(8,128)(2,1)S(1)}, u32[]{:S(2)}, u32[]{:S(2)}) collective-permute-start(bf16[3,128,1024]{2,1,0:T(8,128)(2,1)} %pad_maximum_fusion.1.refs_8_.refs_7_), channel_id=1, source_target_pairs={{0,8},{4,12},{8,0},{12,4},{1,9},{5,13},{9,1},{13,5},{2,10},{6,14},... | collective-permute-start | bytes 2359304 | tf_op jit(solution)/shard_map/ppermute | solution.py:139
  28.8 2.2 %copy-start = (bf16[1024,2048]{1,0:T(8,128)(2,1)S(1)}, bf16[1024,2048]{1,0:T(8,128)(2,1)}, u32[]{:S(2)}) copy-start(bf16[1024,2048]{1,0:T(8,128)(2,1)} %refs_8_.1) | copy-start | bytes 12582916
  31.0 2.2 %copy-start.3 = (bf16[1024,2048]{1,0:T(8,128)(2,1)S(1)}, bf16[1024,2048]{1,0:T(8,128)(2,1)}, u32[]{:S(2)}) copy-start(bf16[1024,2048]{1,0:T(8,128)(2,1)} %refs_9_.1) | copy-start | bytes 12582916
  39.5 5.9 %copy-start.6 = (bf16[192,1024]{1,0:T(8,128)(2,1)}, bf16[192,1024]{1,0:T(8,128)(2,1)S(1)}, u32[]{:S(2)}) copy-start(bf16[192,1024]{1,0:T(8,128)(2,1)S(1)} %get-tuple-element.43.refs_0_.refs_10_) | copy-start | bytes 1179652
  39.5 5.9 %copy-start.13 = (bf16[1024,64]{1,0:T(8,128)(2,1)}, bf16[1024,64]{1,0:T(8,128)(2,1)S(1)}, u32[]{:S(2)}) copy-start(bf16[1024,64]{1,0:T(8,128)(2,1)S(1)} %get-tuple-element.41.refs_3_) | copy-start | bytes 393220
  39.5 5.9 %copy-start.15 = (bf16[1024,64]{1,0:T(8,128)(2,1)}, bf16[1024,64]{1,0:T(8,128)(2,1)S(1)}, u32[]{:S(2)}) copy-start(bf16[1024,64]{1,0:T(8,128)(2,1)S(1)} %get-tuple-element.42.refs_4_) | copy-start | bytes 393220
  41.0 11.4 %copy-start.21 = (bf16[64,1024]{1,0:T(8,128)(2,1)S(1)}, bf16[64,1024]{1,0:T(8,128)(2,1)}, u32[]{:S(2)}) copy-start(bf16[64,1024]{1,0:T(8,128)(2,1)} %refs_2_.3) | copy-start | bytes 393220
  41.0 11.4 %collective-permute-start.6 = (bf16[2,3,128,1024]{3,2,1,0:T(8,128)(2,1)}, bf16[2,3,128,1024]{3,2,1,0:T(8,128)(2,1)}, u32[]{:S(2)}, u32[]{:S(2)}) collective-permute-start(bf16[2,3,128,1024]{3,2,1,0:T(8,128)(2,1)} %pair.3), channel_id=1, source_target_pairs={{0,16},{16,0},{1,17},{17,1},{2,18},{18,2},{3,19},{19,3},{4,20},{20... | collective-permute-start | bytes 4718600 | tf_op jit(solution)/shard_map/ppermute | solution.py:139
  45.5 6.9 %collective-permute-start.7 = (bf16[2,3,128,1024]{3,2,1,0:T(8,128)(2,1)}, bf16[2,3,128,1024]{3,2,1,0:T(8,128)(2,1)}, u32[]{:S(2)}, u32[]{:S(2)}) collective-permute-start(bf16[2,3,128,1024]{3,2,1,0:T(8,128)(2,1)} %pair.4), channel_id=1, source_target_pairs={{0,16},{16,0},{1,17},{17,1},{2,18},{18,2},{3,19},{19,3},{4,20},{20... | collective-permute-start | bytes 4718600 | tf_op jit(solution)/shard_map/ppermute | solution.py:139
  45.6 5.5 %collective-permute-start.4 = (bf16[3,128,1024]{2,1,0:T(8,128)(2,1)}, bf16[3,128,1024]{2,1,0:T(8,128)(2,1)S(1)}, u32[]{:S(2)}, u32[]{:S(2)}) collective-permute-start(bf16[3,128,1024]{2,1,0:T(8,128)(2,1)} %pad_maximum_fusion.1.refs_8_.refs_7_), channel_id=1, source_target_pairs={{0,16},{16,0},{1,17},{17,1},{2,18},{18,2},{3,19},{19,3},{4,20},{20... | collective-permute-start | bytes 2359304 | tf_op jit(solution)/shard_map/ppermute | solution.py:139
  46.0 6.3 %collective-permute-start.5 = (bf16[3,128,1024]{2,1,0:T(8,128)(2,1)}, bf16[3,128,1024]{2,1,0:T(8,128)(2,1)}, u32[]{:S(2)}, u32[]{:S(2)}) collective-permute-start(bf16[3,128,1024]{2,1,0:T(8,128)(2,1)} %pad_maximum_fusion.2.refs_9_.refs_8_), channel_id=1, source_target_pairs={{0,16},{16,0},{1,17},{17,1},{2,18},{18,2},{3,19},{19,3},{4,20},{20... | collective-permute-start | bytes 2359304 | tf_op jit(solution)/shard_map/ppermute | solution.py:139
  46.1 29.9 %collective-permute-start.8 = (bf16[3,128,1024]{2,1,0:T(8,128)(2,1)S(1)}, bf16[3,128,1024]{2,1,0:T(8,128)(2,1)}, u32[]{:S(2)}, u32[]{:S(2)}) collective-permute-start(bf16[3,128,1024]{2,1,0:T(8,128)(2,1)S(1)} %collective-permute-done.refs_0_.first.refs_10_.refs_9_), channel_id=1, source_target_pairs={{0,8},{4,12},{8,0},{12,4},{1,9},{5,13},{9,1},{13,5},{2,10},{6,14},... | collective-permute-start | bytes 2359304 | tf_op jit(solution)/shard_map/ppermute | solution.py:139
  52.0 24.0 %collective-permute-start.9 = (bf16[3,128,1024]{2,1,0:T(8,128)(2,1)S(1)}, bf16[3,128,1024]{2,1,0:T(8,128)(2,1)}, u32[]{:S(2)}, u32[]{:S(2)}) collective-permute-start(bf16[3,128,1024]{2,1,0:T(8,128)(2,1)S(1)} %collective-permute-done.1.refs_1_.second.refs_13_.refs_12_), channel_id=1, source_target_pairs={{0,4},{4,0},{8,12},{12,8},{1,5},{5,1},{9,13},{13,9},{2,6},{6,2},{1... | collective-permute-start | bytes 2359304 | tf_op jit(solution)/shard_map/ppermute | solution.py:139
  52.4 2.2 %copy-start.1 = (bf16[1024,2048]{1,0:T(8,128)(2,1)S(1)}, bf16[1024,2048]{1,0:T(8,128)(2,1)}, u32[]{:S(2)}) copy-start(bf16[1024,2048]{1,0:T(8,128)(2,1)} %refs_8_.1) | copy-start | bytes 12582916
  54.6 2.2 %copy-start.4 = (bf16[1024,2048]{1,0:T(8,128)(2,1)S(1)}, bf16[1024,2048]{1,0:T(8,128)(2,1)}, u32[]{:S(2)}) copy-start(bf16[1024,2048]{1,0:T(8,128)(2,1)} %refs_9_.1) | copy-start | bytes 12582916
  76.0 1.9 copy-start.18
  76.0 1.9 copy-start.20
  76.0 5.2 %copy-start.10 = (bf16[3,128,1024]{2,1,0:T(8,128)(2,1)S(1)}, bf16[3,128,1024]{2,1,0:T(8,128)(2,1)}, u32[]{:S(2)}) copy-start(bf16[3,128,1024]{2,1,0:T(8,128)(2,1)} %copy-done.8) | copy-start | bytes 2359300
  77.8 3.5 %collective-permute-start.10 = (bf16[2,3,128,1024]{3,2,1,0:T(8,128)(2,1)S(1)}, bf16[2,3,128,1024]{3,2,1,0:T(8,128)(2,1)S(1)}, u32[]{:S(2)}, u32[]{:S(2)}) collective-permute-start(bf16[2,3,128,1024]{3,2,1,0:T(8,128)(2,1)S(1)} %pair.5), channel_id=1, source_target_pairs={{0,16},{16,0},{1,17},{17,1},{2,18},{18,2},{3,19},{19,3},{4,20},{20... | collective-permute-start | bytes 4718600 | tf_op jit(solution)/shard_map/ppermute | solution.py:139
  78.0 93.2 %copy-start.11 = (bf16[128,2048]{1,0:T(8,128)(2,1)}, bf16[128,2048]{1,0:T(8,128)(2,1)S(1)}, u32[]{:S(2)}) copy-start(bf16[128,2048]{1,0:T(8,128)(2,1)S(1)} %pad_maximum_fusion.3.factor) | copy-start | bytes 1572868
  81.3 7.4 %copy-start.26 = (bf16[2,3,128,1024]{3,2,1,0:T(8,128)(2,1)}, bf16[2,3,128,1024]{3,2,1,0:T(8,128)(2,1)S(1)}, u32[]{:S(2)}) copy-start(bf16[2,3,128,1024]{3,2,1,0:T(8,128)(2,1)S(1)} %collective-permute-done.10.refs_6_) | copy-start | bytes 4718596
  88.7 3.5 %copy-start.30 = (bf16[2048,1024]{1,0:T(8,128)(2,1)}, bf16[2048,1024]{1,0:T(8,128)(2,1)S(1)}, u32[]{:S(2)}) copy-start(bf16[2048,1024]{1,0:T(8,128)(2,1)S(1)} %get-tuple-element.52.gate) | copy-start | bytes 12582916
  88.7 3.5 %copy-start.39 = (bf16[512,1024]{1,0:T(8,128)(2,1)}, bf16[512,1024]{1,0:T(8,128)(2,1)S(1)}, u32[]{:S(2)}) copy-start(bf16[512,1024]{1,0:T(8,128)(2,1)S(1)} %get-tuple-element.49.gate_grad.refs_2_) | copy-start | bytes 3145732
  88.7 3.5 %copy-start.41 = (bf16[512,1024]{1,0:T(8,128)(2,1)}, bf16[512,1024]{1,0:T(8,128)(2,1)S(1)}, u32[]{:S(2)}) copy-start(bf16[512,1024]{1,0:T(8,128)(2,1)S(1)} %get-tuple-element.50.up_grad.refs_4_) | copy-start | bytes 3145732
  88.7 3.5 %copy-start.45 = (f32[512,128]{1,0:T(8,128)}, f32[512,128]{1,0:T(8,128)S(1)}, u32[]{:S(2)}) copy-start(f32[512,128]{1,0:T(8,128)S(1)} %get-tuple-element.51.low.refs_6_) | copy-start | bytes 786436
  88.8 82.5 %copy-start.33 = (bf16[2048,1024]{1,0:T(8,128)(2,1)}, bf16[2048,1024]{1,0:T(8,128)(2,1)S(1)}, u32[]{:S(2)}) copy-start(bf16[2048,1024]{1,0:T(8,128)(2,1)S(1)} %get-tuple-element.53.up) | copy-start | bytes 12582916
  88.8 8.1 %copy-start.23 = (bf16[64,1024]{1,0:T(8,128)(2,1)S(1)}, bf16[64,1024]{1,0:T(8,128)(2,1)}, u32[]{:S(2)}) copy-start(bf16[64,1024]{1,0:T(8,128)(2,1)} %refs_3_.3) | copy-start | bytes 393220
  88.8 8.0 %copy-start.27 = (bf16[2,3,128,1024]{3,2,1,0:T(8,128)(2,1)S(1)}, bf16[2,3,128,1024]{3,2,1,0:T(8,128)(2,1)}, u32[]{:S(2)}) copy-start(bf16[2,3,128,1024]{3,2,1,0:T(8,128)(2,1)} %copy-done.26) | copy-start | bytes 4718596
  92.3 33.7 %collective-permute-start.11 = (bf16[512,512]{1,0:T(8,128)(2,1)}, bf16[512,512]{1,0:T(8,128)(2,1)}, u32[]{:S(2)}, u32[]{:S(2)}) collective-permute-start(bf16[512,512]{1,0:T(8,128)(2,1)} %token_grad.8.refs_10_.refs_0_.refs_12_), channel_id=1, source_target_pairs={{0,1},{3,2},{4,5},{7,6},{8,9},{11,10},{12,13},{15,14},{16,17},{19,... | collective-permute-start | bytes 1572872 | tf_op jit(solution)/shard_map/ppermute | solution.py:597
  96.8 4.8 %copy-start.31 = (bf16[2048,1024]{1,0:T(8,128)(2,1)S(1)}, bf16[2048,1024]{1,0:T(8,128)(2,1)}, u32[]{:S(2)}) copy-start(bf16[2048,1024]{1,0:T(8,128)(2,1)} %copy-done.30) | copy-start | bytes 12582916
  101.6 36.0 %copy-start.35 = (bf16[512,1024]{1,0:T(8,128)(2,1)}, bf16[512,1024]{1,0:T(8,128)(2,1)S(1)}, u32[]{:S(2)}) copy-start(bf16[512,1024]{1,0:T(8,128)(2,1)S(1)} %get-tuple-element.57.gate_grad.refs_3_) | copy-start | bytes 3145732
  101.6 36.0 %copy-start.37 = (bf16[512,1024]{1,0:T(8,128)(2,1)}, bf16[512,1024]{1,0:T(8,128)(2,1)S(1)}, u32[]{:S(2)}) copy-start(bf16[512,1024]{1,0:T(8,128)(2,1)S(1)} %get-tuple-element.58.up_grad.refs_5_) | copy-start | bytes 3145732
  101.6 36.0 %copy-start.43 = (f32[512,128]{1,0:T(8,128)}, f32[512,128]{1,0:T(8,128)S(1)}, u32[]{:S(2)}) copy-start(f32[512,128]{1,0:T(8,128)S(1)} %get-tuple-element.59.low.refs_7_) | copy-start | bytes 786436
  101.6 3.9 %copy-start.2 = (bf16[1024,2048]{1,0:T(8,128)(2,1)S(1)}, bf16[1024,2048]{1,0:T(8,128)(2,1)}, u32[]{:S(2)}) copy-start(bf16[1024,2048]{1,0:T(8,128)(2,1)} %refs_8_.1) | copy-start | bytes 12582916
  101.7 4.3 %copy-start.5 = (bf16[1024,2048]{1,0:T(8,128)(2,1)S(1)}, bf16[1024,2048]{1,0:T(8,128)(2,1)}, u32[]{:S(2)}) copy-start(bf16[1024,2048]{1,0:T(8,128)(2,1)} %refs_9_.1) | copy-start | bytes 12582916
  101.7 4.3 %copy-start.7 = (bf16[192,1024]{1,0:T(8,128)(2,1)S(1)}, bf16[192,1024]{1,0:T(8,128)(2,1)}, u32[]{:S(2)}) copy-start(bf16[192,1024]{1,0:T(8,128)(2,1)} %copy-done.6) | copy-start | bytes 1179652
  101.7 4.3 %copy-start.25 = (bf16[1024,64]{0,1:T(8,128)(2,1)S(1)}, bf16[1024,64]{0,1:T(8,128)(2,1)}, u32[]{:S(2)}) copy-start(bf16[1024,64]{0,1:T(8,128)(2,1)} %param.20) | copy-start | bytes 393220
  101.7 4.6 %copy-start.40 = (bf16[512,1024]{1,0:T(8,128)(2,1)S(1)}, bf16[512,1024]{1,0:T(8,128)(2,1)}, u32[]{:S(2)}) copy-start(bf16[512,1024]{1,0:T(8,128)(2,1)} %copy-done.39) | copy-start | bytes 3145732
  101.7 4.9 %copy-start.42 = (bf16[512,1024]{1,0:T(8,128)(2,1)S(1)}, bf16[512,1024]{1,0:T(8,128)(2,1)}, u32[]{:S(2)}) copy-start(bf16[512,1024]{1,0:T(8,128)(2,1)} %copy-done.41) | copy-start | bytes 3145732
  101.7 4.9 %copy-start.46 = (f32[512,128]{1,0:T(8,128)S(1)}, f32[512,128]{1,0:T(8,128)}, u32[]{:S(2)}) copy-start(f32[512,128]{1,0:T(8,128)} %copy-done.45) | copy-start | bytes 786436
  103.7 15.2 %collective-permute-start.14 = (bf16[512,512]{1,0:T(8,128)(2,1)S(1)}, bf16[512,512]{1,0:T(8,128)(2,1)S(1)}, u32[]{:S(2)}, u32[]{:S(2)}) collective-permute-start(bf16[512,512]{1,0:T(8,128)(2,1)S(1)} %token_grad.9.refs_1_.refs_0_.refs_13_), channel_id=1, source_target_pairs={{0,1},{3,2},{4,5},{7,6},{8,9},{11,10},{12,13},{15,14},{16,17},{19,... | collective-permute-start | bytes 1572872 | tf_op jit(solution)/shard_map/ppermute | solution.py:597
  110.7 22.6 %collective-permute-start.21 = (f32[4,192,384]{2,1,0:T(8,128)S(1)}, f32[4,192,384]{2,1,0:T(8,128)S(1)}, u32[]{:S(2)}, u32[]{:S(2)}) collective-permute-start(f32[4,192,384]{2,1,0:T(8,128)S(1)} %get-tuple-element.67), channel_id=1, source_target_pairs={{0,16},{16,0},{1,17},{17,1},{2,18},{18,2},{3,19},{19,3},{4,20},{20... | collective-permute-start | bytes 3538952 | tf_op jit(solution)/shard_map/ppermute | solution.py:139
  120.9 16.8 %collective-permute-start.17 = (bf16[512,512]{1,0:T(8,128)(2,1)S(1)}, bf16[512,512]{1,0:T(8,128)(2,1)S(1)}, u32[]{:S(2)}, u32[]{:S(2)}) collective-permute-start(bf16[512,512]{1,0:T(8,128)(2,1)S(1)} %token_grad.11.refs_3_), channel_id=1, source_target_pairs={{0,1},{1,2},{4,5},{5,6},{8,9},{9,10},{12,13},{13,14},{16,17},{17,1... | collective-permute-start | bytes 1572872 | tf_op jit(solution)/shard_map/ppermute | solution.py:597
  125.3 12.3 %collective-permute-start.18 = (bf16[512,512]{1,0:T(8,128)(2,1)S(1)}, bf16[512,512]{1,0:T(8,128)(2,1)S(1)}, u32[]{:S(2)}, u32[]{:S(2)}) collective-permute-start(bf16[512,512]{1,0:T(8,128)(2,1)S(1)} %token_grad.11.refs_3_), channel_id=1, source_target_pairs={{3,2},{2,1},{7,6},{6,5},{11,10},{10,9},{15,14},{14,13},{19,18},{18... | collective-permute-start | bytes 1572872 | tf_op jit(solution)/shard_map/ppermute | solution.py:597
  128.5 23.4 %collective-permute-start.12 = (bf16[512,512]{1,0:T(8,128)(2,1)S(1)}, bf16[512,512]{1,0:T(8,128)(2,1)S(1)}, u32[]{:S(2)}, u32[]{:S(2)}) collective-permute-start(bf16[512,512]{1,0:T(8,128)(2,1)S(1)} %token_grad.10), channel_id=1, source_target_pairs={{0,1},{1,2},{4,5},{5,6},{8,9},{9,10},{12,13},{13,14},{16,17},{17,1... | collective-permute-start | bytes 1572872 | tf_op jit(solution)/shard_map/ppermute | solution.py:597
  132.6 19.3 %collective-permute-start.13 = (bf16[512,512]{1,0:T(8,128)(2,1)S(1)}, bf16[512,512]{1,0:T(8,128)(2,1)S(1)}, u32[]{:S(2)}, u32[]{:S(2)}) collective-permute-start(bf16[512,512]{1,0:T(8,128)(2,1)S(1)} %token_grad.10), channel_id=1, source_target_pairs={{3,2},{2,1},{7,6},{6,5},{11,10},{10,9},{15,14},{14,13},{19,18},{18... | collective-permute-start | bytes 1572872 | tf_op jit(solution)/shard_map/ppermute | solution.py:597
  134.0 15.8 %collective-permute-start.22 = (bf16[2,192,384]{2,1,0:T(8,128)(2,1)S(1)}, bf16[2,192,384]{2,1,0:T(8,128)(2,1)S(1)}, u32[]{:S(2)}, u32[]{:S(2)}) collective-permute-start(bf16[2,192,384]{2,1,0:T(8,128)(2,1)S(1)} %get-tuple-element.69), channel_id=1, source_target_pairs={{0,8},{4,12},{8,0},{12,4},{1,9},{5,13},{9,1},{13,5},{2,10},{6,14},... | collective-permute-start | bytes 884744 | tf_op jit(solution)/shard_map/ppermute | solution.py:139
  139.8 48.6 %collective-permute-start.19 = (bf16[512,512]{1,0:T(8,128)(2,1)S(1)}, bf16[512,512]{1,0:T(8,128)(2,1)}, u32[]{:S(2)}, u32[]{:S(2)}) collective-permute-start(bf16[512,512]{1,0:T(8,128)(2,1)S(1)} %get-tuple-element.62.refs_2_), channel_id=1, source_target_pairs={{0,1},{1,2},{2,3},{4,5},{5,6},{6,7},{8,9},{9,10},{10,11},{12,13},{... | collective-permute-start | bytes 1572872 | tf_op jit(solution)/shard_map/ppermute | solution.py:597
  148.5 40.0 %collective-permute-start.20 = (bf16[512,512]{1,0:T(8,128)(2,1)S(1)}, bf16[512,512]{1,0:T(8,128)(2,1)}, u32[]{:S(2)}, u32[]{:S(2)}) collective-permute-start(bf16[512,512]{1,0:T(8,128)(2,1)S(1)} %get-tuple-element.63.refs_3_), channel_id=1, source_target_pairs={{3,2},{2,1},{1,0},{7,6},{6,5},{5,4},{11,10},{10,9},{9,8},{15,14},{... | collective-permute-start | bytes 1572872 | tf_op jit(solution)/shard_map/ppermute | solution.py:597
  150.4 10.4 %collective-permute-start.23 = (bf16[1,192,384]{2,1,0:T(8,128)(2,1)S(1)}, bf16[1,192,384]{2,1,0:T(8,128)(2,1)S(1)}, u32[]{:S(2)}, u32[]{:S(2)}) collective-permute-start(bf16[1,192,384]{2,1,0:T(8,128)(2,1)S(1)} %get-tuple-element.71), channel_id=1, source_target_pairs={{0,4},{4,0},{8,12},{12,8},{1,5},{5,1},{9,13},{13,9},{2,6},{6,2},{1... | collective-permute-start | bytes 442376 | tf_op jit(solution)/shard_map/ppermute | solution.py:139
  154.6 15.0 %collective-permute-start.15 = (bf16[512,512]{1,0:T(8,128)(2,1)S(1)}, bf16[512,512]{1,0:T(8,128)(2,1)S(1)}, u32[]{:S(2)}, u32[]{:S(2)}) collective-permute-start(bf16[512,512]{1,0:T(8,128)(2,1)S(1)} %get-tuple-element.60), channel_id=1, source_target_pairs={{0,1},{1,2},{2,3},{4,5},{5,6},{6,7},{8,9},{9,10},{10,11},{12,13},{... | collective-permute-start | bytes 1572872 | tf_op jit(solution)/shard_map/ppermute | solution.py:597
  159.4 11.8 %collective-permute-start.16 = (bf16[512,512]{1,0:T(8,128)(2,1)S(1)}, bf16[512,512]{1,0:T(8,128)(2,1)S(1)}, u32[]{:S(2)}, u32[]{:S(2)}) collective-permute-start(bf16[512,512]{1,0:T(8,128)(2,1)S(1)} %get-tuple-element.61), channel_id=1, source_target_pairs={{3,2},{2,1},{1,0},{7,6},{6,5},{5,4},{11,10},{10,9},{9,8},{15,14},{... | collective-permute-start | bytes 1572872 | tf_op jit(solution)/shard_map/ppermute | solution.py:597
  161.5 15.0 %collective-permute-start.26 = (f32[128,192]{1,0:T(8,128)S(1)}, f32[128,192]{1,0:T(8,128)S(1)}, u32[]{:S(2)}, u32[]{:S(2)}) collective-permute-start(f32[128,192]{1,0:T(8,128)S(1)} %get-tuple-element.76), channel_id=1, source_target_pairs={{0,4},{4,0},{8,12},{12,8},{1,5},{5,1},{9,13},{13,9},{2,6},{6,2},{1... | collective-permute-start | bytes 294920 | tf_op jit(solution)/shard_map/ppermute | solution.py:139
  173.2 6.2 %collective-permute-start.24 = (bf16[2,64,192]{2,1,0:T(8,128)(2,1)S(1)}, bf16[2,64,192]{2,1,0:T(8,128)(2,1)S(1)}, u32[]{:S(2)}, u32[]{:S(2)}) collective-permute-start(bf16[2,64,192]{2,1,0:T(8,128)(2,1)S(1)} %get-tuple-element.73), channel_id=1, source_target_pairs={{0,2},{1,3},{2,0},{3,1},{4,6},{5,7},{6,4},{7,5},{8,10},{9,11},{10,... | collective-permute-start | bytes 147464 | tf_op jit(solution)/shard_map/ppermute | solution.py:139
  176.5 7.0 %collective-permute-start.27 = (f32[2,128,192]{2,1,0:T(8,128)S(1)}, f32[2,128,192]{2,1,0:T(8,128)S(1)}, u32[]{:S(2)}, u32[]{:S(2)}) collective-permute-start(f32[2,128,192]{2,1,0:T(8,128)S(1)} %pad_maximum_fusion.5), channel_id=1, source_target_pairs={{0,8},{4,12},{8,0},{12,4},{1,9},{5,13},{9,1},{13,5},{2,10},{6,14},... | collective-permute-start | bytes 589832 | tf_op jit(solution)/shard_map/ppermute | solution.py:139
  180.0 5.4 %collective-permute-start.25 = (bf16[1,64,192]{2,1,0:T(8,128)(2,1)S(1)}, bf16[1,64,192]{2,1,0:T(8,128)(2,1)S(1)}, u32[]{:S(2)}, u32[]{:S(2)}) collective-permute-start(bf16[1,64,192]{2,1,0:T(8,128)(2,1)S(1)} %get-tuple-element.75), channel_id=1, source_target_pairs={{0,1},{1,0},{2,3},{3,2},{4,5},{5,4},{6,7},{7,6},{8,9},{9,8},{10,11... | collective-permute-start | bytes 73736 | tf_op jit(solution)/shard_map/ppermute | solution.py:139
  183.6 3.0 %collective-permute-start.28 = (f32[4,128,192]{2,1,0:T(8,128)S(1)}, f32[4,128,192]{2,1,0:T(8,128)S(1)}, u32[]{:S(2)}, u32[]{:S(2)}) collective-permute-start(f32[4,128,192]{2,1,0:T(8,128)S(1)} %pad_maximum_fusion.4.near), channel_id=1, source_target_pairs={{0,16},{16,0},{1,17},{17,1},{2,18},{18,2},{3,19},{19,3},{4,20},{20... | collective-permute-start | bytes 1179656 | tf_op jit(solution)/shard_map/ppermute | solution.py:139
  186.6 1.8 copy-start.29
  186.6 1.9 copy-start.44
  188.5 2.2 %copy-start.32 = (bf16[2048,1024]{1,0:T(8,128)(2,1)S(1)}, bf16[2048,1024]{1,0:T(8,128)(2,1)}, u32[]{:S(2)}) copy-start(bf16[2048,1024]{1,0:T(8,128)(2,1)} %copy-done.30) | copy-start | bytes 12582916
  190.6 2.2 %copy-start.34 = (bf16[2048,1024]{1,0:T(8,128)(2,1)S(1)}, bf16[2048,1024]{1,0:T(8,128)(2,1)}, u32[]{:S(2)}) copy-start(bf16[2048,1024]{1,0:T(8,128)(2,1)} %copy-done.33) | copy-start | bytes 12582916
  (12 other events, 12.9 us)

commit v2 on v1

--- a/solution.py
+++ b/solution.py
@@ -205,18 +205,46 @@
 def low_rank_values(tokens, cotangent, factors, ahead):
     rows, width = tokens.shape
     rank = factors[0].shape[0]
-    return vmem_call(
+    tile = rows // 4
+    by_rows = lambda columns: pl.BlockSpec((tile, columns), lambda i: (i, 0))
+    return pl.pallas_call(
         lows_kernel,
-        [],
-        [tokens, cotangent, *factors],
-        ahead,
-        [((rows, rank), jnp.bfloat16)] * 3 + [((3 * rank, rows), jnp.bfloat16)],
-        {},
-        [],
-        LIMITS["low"],
-        24 * rows * width * rank,
-        "low_rank_values",
-    )
+        grid=(rows // tile,),
+        in_specs=[by_rows(width)] * 2
+        + [pl.BlockSpec((rank, width), lambda i: (0, 0))] * 3
+        + [pl.BlockSpec(memory_space=pl.ANY)] * len(ahead),
+        out_specs=[by_rows(rank)] * 3 + [pl.BlockSpec((3 * rank, tile), lambda i: (0, i))],
+        out_shape=[jax.ShapeDtypeStruct((rows, rank), jnp.bfloat16)] * 3
+        + [jax.ShapeDtypeStruct((3 * rank, rows), jnp.bfloat16)],
+        compiler_params=pltpu.CompilerParams(vmem_limit_bytes=LIMITS["low"] * MEBIBYTE),
+        cost_estimate=pl.CostEstimate(
+            flops=24 * COST * rows * width * rank, bytes_accessed=0, transcendentals=0
+        ),
+        name="low_rank_values",
+    )(tokens, cotangent, *factors, *ahead)
+
+
+def own_kernel(gate, up, down, *units):
+    for half, unit in enumerate(units):
+        rows = unit.shape[1]
+        part = slice(half * rows, (half + 1) * rows)
+        unit[0] = gate[part, :]
+        unit[1] = up[part, :]
+        unit[2] = down[:, part].astype(jnp.float32).T.astype(jnp.bfloat16)
+
+
+def own_units(gate, up, down):
+    rows, hidden = gate.shape
+    vmem = pl.BlockSpec(memory_space=pltpu.VMEM)
+    return pl.pallas_call(
+        own_kernel,
+        in_specs=[vmem] * 3,
+        out_specs=[vmem] * 2,
+        out_shape=[pltpu.VMEM((3, rows // 2, hidden), jnp.bfloat16)] * 2,
+        compiler_params=pltpu.CompilerParams(vmem_limit_bytes=LIMITS["low"] * MEBIBYTE),
+        cost_estimate=pl.CostEstimate(flops=MEBIBYTE, bytes_accessed=0, transcendentals=0),
+        name="own_units",
+    )(gate, up, down)
 
 
 def pair_kernel(first, second, *refs):
@@ -373,9 +401,33 @@
         LIMITS["token"],
         8 * rows * columns * hidden,
         "token_grad",
-        mode == "last",
     )
     return outs if mode == "both" else outs[0]
+
+
+def last_token_grad(step, half, here, arrays, columns, came, ahead, before):
+    rows, hidden = arrays[0].shape
+    arrays = [*arrays, *came]
+    return pl.pallas_call(
+        functools.partial(token_grad_kernel, "last", step),
+        grid=(1,),
+        in_specs=[pl.BlockSpec(memory_space=pltpu.SMEM)]
+        + [pl.BlockSpec(memory_space=pltpu.VMEM)] * len(arrays)
+        + [pl.BlockSpec(memory_space=pl.ANY)] * (len(before) + len(ahead)),
+        out_specs=pl.BlockSpec((rows, columns), lambda i: (half, 0)),
+        out_shape=jax.ShapeDtypeStruct((HALVES * rows, columns), jnp.bfloat16),
+        input_output_aliases={1 + len(arrays): 0} if before else {},
+        compiler_params=pltpu.CompilerParams(vmem_limit_bytes=LIMITS["token"] * MEBIBYTE),
+        cost_estimate=pl.CostEstimate(
+            flops=8 * COST * rows * columns * hidden, bytes_accessed=0, transcendentals=0
+        ),
+        name="last_token_grad",
+    )(
+        here,
+        *[pltpu.with_memory_space_constraint(array, pltpu.VMEM) for array in arrays],
+        *before,
+        *ahead,
+    )
 
 
 def adapter_kernel(scaling, here, *refs):
@@ -451,7 +503,7 @@
         {},
         [],
         LIMITS["small"],
-        500 * MEBIBYTE,
+        20 * MEBIBYTE,
         "halve",
     )
 
@@ -470,7 +522,7 @@
         {},
         [],
         LIMITS["small"],
-        500 * MEBIBYTE,
+        20 * MEBIBYTE,
         "last_sum",
         True,
     )[0]
@@ -478,7 +530,7 @@
 
 def turn_kernel(wide_columns, here, kept, came, narrow, keep, send, wide):
     total = kept[0] + came[0].astype(jnp.float32)
-    narrow[...] = total[:, wide_columns:].T
+    narrow[...] = total[:, wide_columns:]
     wide[...] = total[:, :wide_columns].T
     rows = keep.shape[1]
     for mask in range(4):
@@ -493,22 +545,22 @@
         [here],
         [keep, came],
         [],
-        [((columns - wide_columns, rows), keep.dtype)]
+        [((rows, columns - wide_columns), keep.dtype)]
         + [((2, wide_columns // 4, rows), kind) for kind in (jnp.float32, jnp.bfloat16)],
         {},
         [pltpu.VMEM((wide_columns, rows), keep.dtype)],
         LIMITS["small"],
-        500 * MEBIBYTE,
+        20 * MEBIBYTE,
         "turn",
     )
 
 
 def whole_kernel(here, near, far, out):
-    rows = near.shape[1]
+    columns = near.shape[2]
     for number in range(2 * near.shape[0]):
         ref = near if number < near.shape[0] else far
-        block = lax.bitwise_xor(here[0], number) * rows
-        out[pl.ds(pl.multiple_of(block, rows), rows), :] = ref[number % near.shape[0]]
+        block = lax.bitwise_xor(here[0], number) * columns
+        out[:, pl.ds(pl.multiple_of(block, columns), columns)] = ref[number % near.shape[0]]
 
 
 def whole(here, near, far):
@@ -518,11 +570,11 @@
         [here],
         [near, far],
         [],
-        [((2 * count * rows, columns), near.dtype)],
+        [((rows, 2 * count * columns), near.dtype)],
         {},
         [],
         LIMITS["small"],
-        500 * MEBIBYTE,
+        20 * MEBIBYTE,
         "whole",
         True,
     )[0]
@@ -556,14 +608,11 @@
         )
     )
     gate_out, up_out = gate_adapter_output_factor, up_adapter_output_factor
-    half_rows = gate_frozen_matrix.shape[0] // 2
 
     units = {}
-    for half in range(2):
-        span = slice(half * half_rows, (half + 1) * half_rows)
-        units[0, half] = jnp.stack(
-            [gate_frozen_matrix[span], up_frozen_matrix[span], down_frozen_matrix[:, span].T]
-        )
+    units[0, 0], units[0, 1] = own_units(
+        gate_frozen_matrix, up_frozen_matrix, down_frozen_matrix
+    )
     units[1, 0] = flip(units[0, 0], "fsdp", 1)
     units[2, 1] = flip(units[0, 1], "fsdp", 2)
     units[1, 1] = flip(units[0, 1], "fsdp", 1)
@@ -623,13 +672,23 @@
         states.append(state)
         first.append(share(0, half, "first"))
     came = [shift(part, [(0, 1), (3, 2)]) for part in first]
-    partial = [share(1, half, "sum", [came[half]], first[1:]) for half in both]
+    partial = []
+    for half in both:
+        partial.append(share(1, half, "sum", [came[half]], partial or first[1:]))
+    second = partial
     from_left = [shift(part, [(0, 1), (1, 2)]) for part in partial]
     from_right = [shift(part, [(3, 2), (2, 1)]) for part in partial]
-    partial = [
-        share(2, half, "both", [first[half], from_left[half], from_right[half]], partial[1:])
-        for half in both
-    ]
+    partial = []
+    for half in both:
+        partial.append(
+            share(
+                2,
+                half,
+                "both",
+                [first[half], from_left[half], from_right[half]],
+                partial[0] if partial else second[1:],
+            )
+        )
     from_left = [shift(part[0], [(0, 1), (1, 2), (2, 3)]) for part in partial]
     from_right = [shift(part[1], [(3, 2), (2, 1), (1, 0)]) for part in partial]
 
@@ -644,7 +703,7 @@
             turned,
             down_in,
         ],
-        first,
+        [came[0], *first],
     )
     keep, send = halve(here, keep, flip(send, "cuts", 1))
     keep, send = halve(here, keep, flip(send, "fsdp", 2))
@@ -653,20 +712,24 @@
     wide_grads = last_sum(here, keep, flip(send, "tp", 1))
     near = jnp.stack([narrow, flip(narrow, "fsdp", 1)])
     near = jnp.concatenate([near, flip(near, "fsdp", 2)])
-    narrow_grads = whole(here, near, flip(near, "cuts", 1))
-
-    token_input_gradient = jnp.concatenate(
-        [
-            share(
+    narrow_turned = whole(here, near, flip(near, "cuts", 1))
+    narrow_grads = narrow_turned.T
+
+    results = []
+    for half in both:
+        results.append(
+            last_token_grad(
                 3,
                 half,
-                "last",
+                here,
+                [*states[half][1:], factor, *full],
+                width // quarters,
                 [from_left[half], from_right[half]],
-                [*partial[1], wide_grads, narrow_grads] if half else partial[1],
+                [wide_grads, narrow_turned] if half else partial[1],
+                results[:],
             )
-            for half in both
-        ]
-    )
+        )
+    token_input_gradient = results[-1]
     return (token_input_gradient, wide_grads, narrow_grads)
 
 

time: 200 us -> 189 us (0.945)
  local copies, waits for them, and re-layouts: 29.2 us -> 23.7 us
  starting transfers between devices: 53.1 us -> 48.9 us
  other arithmetic: 3.14 us -> 0.17 us
    ppermute x10, waiting for transfers between devices: 18.5 us -> 6.17 us  [square_plane(): shift = lambda array, pairs: lax.ppermute(array, 'tp', pairs)]
    ppermute x19, waiting for transfers between devices: 31.7 us -> 43.4 us  [flip(): return lax.ppermute(array, axis, [(i, i ^ bit) for i in range(size)])]
    pallas_call x0 -> x4, Pallas kernels: none -> 10.8 us  [the longest x2 5.58 us: last_token_grad(): pl.pallas_call(functools.partial(token_grad_kernel, 'last', step), grid=(...]
    pallas_call x22 -> x19, Pallas kernels: 62.1 us -> 53.3 us  [vmem_call(): pl.pallas_call(kernel, in_specs=[pl.BlockSpec(memory_space=pltpu.SMEM)] *...]
    ppermute x10, starting transfers between devices: 32.4 us -> 28 us  [square_plane(): shift = lambda array, pairs: lax.ppermute(array, 'tp', pairs)]
    unnamed x97 -> x82, local copies, waits for them, and re-layouts: 26.9 us -> 23.7 us
  transfers between devices with their start and end apart: 29 -> 29, of which waited for: 12 -> 12; matrix products, arithmetic and copies ran while one was open for 1% -> 0% of each run, Pallas kernels for 24% -> 24%
where the time goes in v2:
time: 189 us; the launch traced here: 187 us
  Pallas kernels  64.1 us (34%)
  waiting for transfers between devices  49.5 us (26%)
  starting transfers between devices  48.9 us (26%)
  local copies, waits for them, and re-layouts  23.7 us (13%)
    pallas_call x19, Pallas kernels, vmem_call(): pl.pallas_call(kernel, in_specs=[pl.BlockSpec(memory_space=pltpu.SMEM)] *...  53.3 us
    ppermute x19, waiting for transfers between devices, flip(): return lax.ppermute(array, axis, [(i, i ^ bit) for i in range(size)])  43.4 us
    ppermute x10, starting transfers between devices, square_plane(): shift = lambda array, pairs: lax.ppermute(array, 'tp', pairs)  28 us
    unnamed x82, local copies, waits for them, and re-layouts  23.7 us
    ppermute x19, starting transfers between devices, flip(): return lax.ppermute(array, axis, [(i, i ^ bit) for i in range(size)])  20.9 us
    ppermute x10, waiting for transfers between devices, square_plane(): shift = lambda array, pairs: lax.ppermute(array, 'tp', pairs)  6.17 us
    pallas_call x2, Pallas kernels, last_token_grad(): pl.pallas_call(functools.partial(token_grad_kernel, 'last', step), grid=(...  5.58 us
    pallas_call x1, Pallas kernels, low_rank_values(): pl.pallas_call(lows_kernel, grid=(rows // tile,), in_specs=[by_rows(width...  4.12 us
  transfers between devices with their start and end apart: 29, of which 12 were waited for; matrix products, arithmetic and copies ran while one was open for 0% of the time, Pallas kernels for 24%

profile of v2, /device:TPU:0, one launch (start us, length us, event | category | flops | bytes accessed | tf_op | source)
XLA Modules:
  0.0 187.5 jit_solution(8055214689358505813)
XLA Ops:
  0.6 1.0 copy-done.15
  1.7 1.0 copy-done.16
  2.7 1.0 copy-done.17
  3.8 1.1 own_units.1
  4.9 2.9 %collective-permute-start = (bf16[3,128,1024]{2,1,0:T(8,128)(2,1)S(1)}, bf16[3,128,1024]{2,1,0:T(8,128)(2,1)S(1)}, u32[]{:S(2)}, u32[]{:S(2)}) collective-permute-start(bf16[3,128,1024]{2,1,0:T(8,128)(2,1)S(1)} %get-tuple-element.42.refs_8_.refs_7_), channel_id=1, source_target_pairs={{0,4},{4,0},{8,12},{12,8},{1,5},{5,1},{9,13},{13,9},{2,6},{6,2},{1... | collective-permute-start | bytes 2359304 | tf_op jit(solution)/shard_map/ppermute | solution.py:139
  7.8 1.5 collective-permute-start.1
  9.9 16.3 %collective-permute-done.refs_0_.first.refs_10_.refs_9_ = bf16[3,128,1024]{2,1,0:T(8,128)(2,1)S(1)} collective-permute-done((bf16[3,128,1024]{2,1,0:T(8,128)(2,1)S(1)}, bf16[3,128,1024]{2,1,0:T(8,128)(2,1)S(1)}, u32[]{:S(2)}, u32[]{:S(2)}) %collective-permute-start) | collective-permute-done | bytes 786464 | tf_op jit(solution)/shard_map/ppermute | solution.py:139
  26.2 2.3 %collective-permute-done.1.refs_1_.second.refs_13_.refs_12_ = bf16[3,128,1024]{2,1,0:T(8,128)(2,1)S(1)} collective-permute-done((bf16[3,128,1024]{2,1,0:T(8,128)(2,1)}, bf16[3,128,1024]{2,1,0:T(8,128)(2,1)S(1)}, u32[]{:S(2)}, u32[]{:S(2)}) %collective-permute-start.1) | collective-permute-done | bytes 786464 | tf_op jit(solution)/shard_map/ppermute | solution.py:139
  28.5 2.2 %copy-done = bf16[1024,2048]{1,0:T(8,128)(2,1)S(1)} copy-done((bf16[1024,2048]{1,0:T(8,128)(2,1)S(1)}, bf16[1024,2048]{1,0:T(8,128)(2,1)}, u32[]{:S(2)}) %copy-start) | copy-done | bytes 4194328
  30.7 2.2 %copy-done.3 = bf16[1024,2048]{1,0:T(8,128)(2,1)S(1)} copy-done((bf16[1024,2048]{1,0:T(8,128)(2,1)S(1)}, bf16[1024,2048]{1,0:T(8,128)(2,1)}, u32[]{:S(2)}) %copy-start.3) | copy-done | bytes 4194328
  32.9 0.9 copy-done.22
  33.8 0.9 copy-done.24
  34.8 0.9 copy-done.31
  35.7 4.1 %low_rank_values.1 = (bf16[1024,64]{1,0:T(8,128)(2,1)S(1)}, bf16[1024,64]{1,0:T(8,128)(2,1)S(1)}, bf16[1024,64]{1,0:T(8,128)(2,1)S(1)}, bf16[192,1024]{1,0:T(8,128)(2,1)S(1)}) custom-call(bf16[1024,2048]{1,0:T(8,128)(2,1)S(1)} %copy-done, bf16[1024,2048]{1,0:T(8,128)(2,1)S(1)} %copy-done.3, bf16[64,2048]{1,0:T(8,128)(2,1)S(1)} %bitcast.12, ...), custom_call_target="tpu_custom_call" | custom-call | flops 64424509440 | tf_op jit(solution)/shard_map/low_rank_values/pallas_call | solution.py:210
  39.9 1.4 pair.3
  41.3 0.9 collective-permute-done.2.first.refs_11_.refs_10_
  42.2 1.7 collective-permute-done.3.second.refs_12_.refs_11_
  43.9 1.3 pair.4
  45.8 1.5 collective-permute-start.8
  47.3 3.2 %collective-permute-done.4.refs_14_.refs_13_ = bf16[3,128,1024]{2,1,0:T(8,128)(2,1)S(1)} collective-permute-done((bf16[3,128,1024]{2,1,0:T(8,128)(2,1)S(1)}, bf16[3,128,1024]{2,1,0:T(8,128)(2,1)S(1)}, u32[]{:S(2)}, u32[]{:S(2)}) %collective-permute-start.4) | collective-permute-done | bytes 786464 | tf_op jit(solution)/shard_map/ppermute | solution.py:139
  51.8 2.2 %copy-done.1 = bf16[1024,2048]{1,0:T(8,128)(2,1)S(1)} copy-done((bf16[1024,2048]{1,0:T(8,128)(2,1)S(1)}, bf16[1024,2048]{1,0:T(8,128)(2,1)}, u32[]{:S(2)}) %copy-start.1) | copy-done | bytes 4194328
  54.0 2.2 %copy-done.4 = bf16[1024,2048]{1,0:T(8,128)(2,1)S(1)} copy-done((bf16[1024,2048]{1,0:T(8,128)(2,1)S(1)}, bf16[1024,2048]{1,0:T(8,128)(2,1)}, u32[]{:S(2)}) %copy-start.4) | copy-done | bytes 4194328
  56.2 1.1 copy-done.9
  57.3 1.1 copy-done.12
  58.5 0.9 copy-done.19
  59.4 0.9 copy-done.21
  60.4 0.9 copy-done.27
  61.3 0.9 copy-done.29
  62.2 14.1 %width_sums.1 = (f32[512,1024]{1,0:T(8,128)S(1)}, f32[512,1024]{1,0:T(8,128)S(1)}, f32[512,1024]{1,0:T(8,128)S(1)}, f32[512,1024]{1,0:T(8,128)S(1)}, f32[512,102...) custom-call(s32[2]{0:T(128)S(1)} %pad_add_fusion.here, ...), custom_call_target="tpu_custom_call" | custom-call | flops 20 | tf_op jit(solution)/shard_map/width_sums/pallas_call | solution.py:147
  76.3 1.6 pair.5
  78.2 3.3 %collective-permute-done.10.refs_6_ = bf16[2,3,128,1024]{3,2,1,0:T(8,128)(2,1)S(1)} collective-permute-done((bf16[2,3,128,1024]{3,2,1,0:T(8,128)(2,1)S(1)}, bf16[2,3,128,1024]{3,2,1,0:T(8,128)(2,1)S(1)}, u32[]{:S(2)}, u32[]{:S(2)}) %collective-permute-start.10) | collective-permute-done | bytes 1572896 | tf_op jit(solution)/shard_map/ppermute | solution.py:139
  81.4 6.7 %hidden_and_grads.2 = (bf16[512,1024]{1,0:T(8,128)(2,1)S(1)}, bf16[512,1024]{1,0:T(8,128)(2,1)S(1)}, bf16[512,1024]{1,0:T(8,128)(2,1)S(1)}, f32[512,128]{1,0:T(8...) custom-call(s32[2]{0:T(128)S(1)} %pad_add_fusion.here, ...), custom_call_target="tpu_custom_call" | custom-call | flops 128849018880 | tf_op jit(solution)/shard_map/hidden_and_grads/pallas_call | solution.py:147
  88.2 2.9 %token_grad.6.refs_10_.refs_0_.refs_13_ = bf16[512,512]{1,0:T(8,128)(2,1)} custom-call(s32[2]{0:T(128)S(1)} %pad_add_fusion.here, bf16[512,1024]{1,0:T(8,128)(2,1)S(1)} %get-tuple-element.56.gate_grad.refs_2_, bf16[512,1024]{1,0:T(8,128)(2,1)S(1)} %get-tuple-element.57.up_grad.refs_4_, f32[512,128]{1,0:T(8,128)S(1)} %get-tuple-element.58.low.refs_6_, ...), custom_call_target="tpu_custom_call" | custom-call | flops 42949672960 | tf_op jit(solution)/shard_map/token_grad/pallas_call | solution.py:147
  91.2 4.5 %collective-permute-start.12 = (bf16[512,512]{1,0:T(8,128)(2,1)}, bf16[512,512]{1,0:T(8,128)(2,1)}, u32[]{:S(2)}, u32[]{:S(2)}) collective-permute-start(bf16[512,512]{1,0:T(8,128)(2,1)} %token_grad.6.refs_10_.refs_0_.refs_13_), channel_id=1, source_target_pairs={{0,1},{3,2},{4,5},{7,6},{8,9},{11,10},{12,13},{15,14},{16,17},{19,... | collective-permute-start | bytes 1572872 | tf_op jit(solution)/shard_map/ppermute | solution.py:646
  95.7 4.8 %hidden_and_grads.3 = (bf16[512,1024]{1,0:T(8,128)(2,1)S(1)}, bf16[512,1024]{1,0:T(8,128)(2,1)S(1)}, bf16[512,1024]{1,0:T(8,128)(2,1)S(1)}, f32[512,128]{1,0:T(8,128)S(1)}) custom-call(s32[2]{0:T(128)S(1)} %pad_add_fusion.here, bf16[1024,512]{1,0:T(8,128)(2,1)S(1)} %get-tuple-element.48.refs_0_, bf16[1024,512]{1,0:T(8,128)(2,1)S(1)} %get-tuple-element.49.refs_1_, ...), custom_call_target="tpu_custom_call" | custom-call | flops 128849018880 | tf_op jit(solution)/shard_map/hidden_and_grads/pallas_call | solution.py:147
  100.6 2.0 %token_grad.7.refs_1_.refs_0_.refs_14_ = bf16[512,512]{1,0:T(8,128)(2,1)S(1)} custom-call(s32[2]{0:T(128)S(1)} %pad_add_fusion.here, bf16[512,1024]{1,0:T(8,128)(2,1)S(1)} %get-tuple-element.61.gate_grad.refs_3_, bf16[512,1024]{1,0:T(8,128)(2,1)S(1)} %get-tuple-element.62.up_grad.refs_5_, f32[512,128]{1,0:T(8,128)S(1)} %get-tuple-element.63.low.refs_7_, ...), custom_call_target="tpu_custom_call" | custom-call | flops 42949672960 | tf_op jit(solution)/shard_map/token_grad/pallas_call | solution.py:147
  102.6 4.1 %collective-permute-done.12.refs_0_.refs_12_ = bf16[512,512]{1,0:T(8,128)(2,1)} collective-permute-done((bf16[512,512]{1,0:T(8,128)(2,1)}, bf16[512,512]{1,0:T(8,128)(2,1)}, u32[]{:S(2)}, u32[]{:S(2)}) %collective-permute-start.12) | collective-permute-done | bytes 524320 | tf_op jit(solution)/shard_map/ppermute | solution.py:646
  106.7 4.0 %adapter_grads.1 = (f32[4,192,384]{2,1,0:T(8,128)S(1)}, f32[4,192,384]{2,1,0:T(8,128)S(1)}) custom-call(s32[2]{0:T(128)S(1)} %pad_add_fusion.here, bf16[512,1024]{1,0:T(8,128)(2,1)S(1)} %get-tuple-element.68.refs_0_, bf16[512,1024]{1,0:T(8,128)(2,1)S(1)} %get-tuple-element.69.refs_1_, bf16[512,1024]{1,0:T(8,128)(2,1)S(1)} %copy-done.36, ...), custom_call_target="tpu_custom_call" | custom-call | flops 96636764160 | tf_op jit(solution)/shard_map/adapter_grads/pallas_call | solution.py:147
  110.8 4.4 %collective-permute-start.11 = (bf16[512,512]{1,0:T(8,128)(2,1)S(1)}, bf16[512,512]{1,0:T(8,128)(2,1)S(1)}, u32[]{:S(2)}, u32[]{:S(2)}) collective-permute-start(bf16[512,512]{1,0:T(8,128)(2,1)S(1)} %token_grad.7.refs_1_.refs_0_.refs_14_), channel_id=1, source_target_pairs={{0,1},{3,2},{4,5},{7,6},{8,9},{11,10},{12,13},{15,14},{16,17},{19,... | collective-permute-start | bytes 1572872 | tf_op jit(solution)/shard_map/ppermute | solution.py:646
  115.9 1.6 collective-permute-start.22
  117.5 2.5 %token_grad.8.refs_1_ = bf16[512,512]{1,0:T(8,128)(2,1)S(1)} custom-call(s32[2]{0:T(128)S(1)} %pad_add_fusion.here, bf16[512,1024]{1,0:T(8,128)(2,1)S(1)} %copy-done.36, bf16[512,1024]{1,0:T(8,128)(2,1)S(1)} %copy-done.38, f32[512,128]{1,0:T(8,128)S(1)} %copy-done.40, bf16[128,2048]{1,0:T(8,128)(2,1)S(1)} %pad_maximum_fusion.factor, ...), custom_call_target="tpu_custom_call" | custom-call | flops 42949672960 | tf_op jit(solution)/shard_map/token_grad/pallas_call | solution.py:147
  120.0 2.8 %collective-permute-start.15 = (bf16[512,512]{1,0:T(8,128)(2,1)S(1)}, bf16[512,512]{1,0:T(8,128)(2,1)S(1)}, u32[]{:S(2)}, u32[]{:S(2)}) collective-permute-start(bf16[512,512]{1,0:T(8,128)(2,1)S(1)} %token_grad.8.refs_1_), channel_id=1, source_target_pairs={{0,1},{1,2},{4,5},{5,6},{8,9},{9,10},{12,13},{13,14},{16,17},{17,1... | collective-permute-start | bytes 1572872 | tf_op jit(solution)/shard_map/ppermute | solution.py:646
  123.5 1.6 collective-permute-done.22.came
  125.7 1.5 collective-permute-start.23
  127.4 2.0 %token_grad.9.refs_3_ = bf16[512,512]{1,0:T(8,128)(2,1)S(1)} custom-call(s32[2]{0:T(128)S(1)} %pad_add_fusion.here, bf16[512,1024]{1,0:T(8,128)(2,1)S(1)} %get-tuple-element.61.gate_grad.refs_3_, bf16[512,1024]{1,0:T(8,128)(2,1)S(1)} %get-tuple-element.62.up_grad.refs_5_, f32[512,128]{1,0:T(8,128)S(1)} %get-tuple-element.63.low.refs_7_, ...), custom_call_target="tpu_custom_call" | custom-call | flops 42949672960 | tf_op jit(solution)/shard_map/token_grad/pallas_call | solution.py:147
  129.4 4.4 %collective-permute-start.13 = (bf16[512,512]{1,0:T(8,128)(2,1)S(1)}, bf16[512,512]{1,0:T(8,128)(2,1)S(1)}, u32[]{:S(2)}, u32[]{:S(2)}) collective-permute-start(bf16[512,512]{1,0:T(8,128)(2,1)S(1)} %token_grad.9.refs_3_), channel_id=1, source_target_pairs={{0,1},{1,2},{4,5},{5,6},{8,9},{9,10},{12,13},{13,14},{16,17},{17,1... | collective-permute-start | bytes 1572872 | tf_op jit(solution)/shard_map/ppermute | solution.py:646
  135.2 1.5 collective-permute-start.26
  136.8 1.9 %collective-permute-done.15.refs_1_ = bf16[512,512]{1,0:T(8,128)(2,1)S(1)} collective-permute-done((bf16[512,512]{1,0:T(8,128)(2,1)S(1)}, bf16[512,512]{1,0:T(8,128)(2,1)S(1)}, u32[]{:S(2)}, u32[]{:S(2)}) %collective-permute-start.15) | collective-permute-done | bytes 524320 | tf_op jit(solution)/shard_map/ppermute | solution.py:646
  138.7 2.7 %token_grad.10 = (bf16[512,512]{1,0:T(8,128)(2,1)S(1)}, bf16[512,512]{1,0:T(8,128)(2,1)S(1)}) custom-call(s32[2]{0:T(128)S(1)} %pad_add_fusion.here, bf16[512,1024]{1,0:T(8,128)(2,1)S(1)} %copy-done.36, bf16[512,1024]{1,0:T(8,128)(2,1)S(1)} %copy-done.38, f32[512,128]{1,0:T(8,128)S(1)} %copy-done.40, bf16[128,2048]{1,0:T(8,128)(2,1)S(1)} %pad_maximum_fusion.factor, ...), custom_call_target="tpu_custom_call" | custom-call | flops 42949672960 | tf_op jit(solution)/shard_map/token_grad/pallas_call | solution.py:147
  141.3 4.6 %collective-permute-start.19 = (bf16[512,512]{1,0:T(8,128)(2,1)S(1)}, bf16[512,512]{1,0:T(8,128)(2,1)S(1)}, u32[]{:S(2)}, u32[]{:S(2)}) collective-permute-start(bf16[512,512]{1,0:T(8,128)(2,1)S(1)} %get-tuple-element.64.refs_3_), channel_id=1, source_target_pairs={{0,1},{1,2},{2,3},{4,5},{5,6},{6,7},{8,9},{9,10},{10,11},{12,13},{... | collective-permute-start | bytes 1572872 | tf_op jit(solution)/shard_map/ppermute | solution.py:646
  146.0 1.3 collective-permute-start.20
  147.3 3.7 %collective-permute-start.24 = (bf16[2,64,192]{2,1,0:T(8,128)(2,1)S(1)}, bf16[2,64,192]{2,1,0:T(8,128)(2,1)S(1)}, u32[]{:S(2)}, u32[]{:S(2)}) collective-permute-start(bf16[2,64,192]{2,1,0:T(8,128)(2,1)S(1)} %get-tuple-element.77), channel_id=1, source_target_pairs={{0,2},{1,3},{2,0},{3,1},{4,6},{5,7},{6,4},{7,5},{8,10},{9,11},{10,... | collective-permute-start | bytes 147464 | tf_op jit(solution)/shard_map/ppermute | solution.py:139
  151.0 1.6 collective-permute-start.27
  152.6 2.1 %token_grad.11 = (bf16[512,512]{1,0:T(8,128)(2,1)S(1)}, bf16[512,512]{1,0:T(8,128)(2,1)S(1)}) custom-call(s32[2]{0:T(128)S(1)} %pad_add_fusion.here, bf16[512,1024]{1,0:T(8,128)(2,1)S(1)} %get-tuple-element.61.gate_grad.refs_3_, bf16[512,1024]{1,0:T(8,128)(2,1)S(1)} %get-tuple-element.62.up_grad.refs_5_, f32[512,128]{1,0:T(8,128)S(1)} %get-tuple-element.63.low.refs_7_, ...), custom_call_target="tpu_custom_call" | custom-call | flops 42949672960 | tf_op jit(solution)/shard_map/token_grad/pallas_call | solution.py:147
  154.7 3.2 %collective-permute-start.17 = (bf16[512,512]{1,0:T(8,128)(2,1)S(1)}, bf16[512,512]{1,0:T(8,128)(2,1)S(1)}, u32[]{:S(2)}, u32[]{:S(2)}) collective-permute-start(bf16[512,512]{1,0:T(8,128)(2,1)S(1)} %get-tuple-element.66.refs_2_), channel_id=1, source_target_pairs={{0,1},{1,2},{2,3},{4,5},{5,6},{6,7},{8,9},{9,10},{10,11},{12,13},{... | collective-permute-start | bytes 1572872 | tf_op jit(solution)/shard_map/ppermute | solution.py:646
  157.9 5.2 %collective-permute-done.24.came = bf16[2,64,192]{2,1,0:T(8,128)(2,1)S(1)} collective-permute-done((bf16[2,64,192]{2,1,0:T(8,128)(2,1)S(1)}, bf16[2,64,192]{2,1,0:T(8,128)(2,1)S(1)}, u32[]{:S(2)}, u32[]{:S(2)}) %collective-permute-start.24) | collective-permute-done | bytes 49184 | tf_op jit(solution)/shard_map/ppermute | solution.py:139
  163.1 1.3 collective-permute-start.18
  165.0 3.2 %collective-permute-start.25 = (bf16[1,64,192]{2,1,0:T(8,128)(2,1)S(1)}, bf16[1,64,192]{2,1,0:T(8,128)(2,1)S(1)}, u32[]{:S(2)}, u32[]{:S(2)}) collective-permute-start(bf16[1,64,192]{2,1,0:T(8,128)(2,1)S(1)} %get-tuple-element.79), channel_id=1, source_target_pairs={{0,1},{1,0},{2,3},{3,2},{4,5},{5,4},{6,7},{7,6},{8,9},{9,8},{10,11... | collective-permute-start | bytes 73736 | tf_op jit(solution)/shard_map/ppermute | solution.py:139
  168.3 2.8 %last_token_grad.2.refs_2_ = bf16[1024,512]{1,0:T(8,128)(2,1)} custom-call(s32[2]{0:T(128)S(1)} %pad_add_fusion.here, bf16[512,1024]{1,0:T(8,128)(2,1)S(1)} %copy-done.36, bf16[512,1024]{1,0:T(8,128)(2,1)S(1)} %copy-done.38, f32[512,128]{1,0:T(8,128)S(1)} %copy-done.40, bf16[128,2048]{1,0:T(8,128)(2,1)S(1)} %pad_maximum_fusion.factor, ...), custom_call_target="tpu_custom_call" | custom-call | flops 42949672960 | tf_op jit(solution)/shard_map/last_token_grad/pallas_call | solution.py:411
  171.1 8.9 %collective-permute-done.25.came = bf16[1,64,192]{2,1,0:T(8,128)(2,1)S(1)} collective-permute-done((bf16[1,64,192]{2,1,0:T(8,128)(2,1)S(1)}, bf16[1,64,192]{2,1,0:T(8,128)(2,1)S(1)}, u32[]{:S(2)}, u32[]{:S(2)}) %collective-permute-start.25) | collective-permute-done | bytes 24608 | tf_op jit(solution)/shard_map/ppermute | solution.py:139
  180.0 1.2 last_sum.1.refs_3_
  181.2 1.5 whole.1.refs_4_
  182.7 1.1 copy-done.14
  184.7 2.8 %last_token_grad.3 = bf16[1024,512]{1,0:T(8,128)(2,1)} custom-call(s32[2]{0:T(128)S(1)} %pad_add_fusion.here, bf16[512,1024]{1,0:T(8,128)(2,1)S(1)} %get-tuple-element.61.gate_grad.refs_3_, bf16[512,1024]{1,0:T(8,128)(2,1)S(1)} %get-tuple-element.62.up_grad.refs_5_, f32[512,128]{1,0:T(8,128)S(1)} %get-tuple-element.63.low.refs_7_, ...), custom_call_target="tpu_custom_call", output_to_operand_aliasing={{}: (9, {})} | custom-call | flops 42949672960 | tf_op jit(solution)/shard_map/last_token_grad/pallas_call | solution.py:411
  (103 shorter events, 8.0 us)
Async XLA Ops:
  0.6 1.0 copy-start.15
  1.7 1.0 copy-start.16
  2.7 1.0 copy-start.17
  4.9 40.4 %copy-start.8 = (bf16[3,128,1024]{2,1,0:T(8,128)(2,1)}, bf16[3,128,1024]{2,1,0:T(8,128)(2,1)S(1)}, u32[]{:S(2)}) copy-start(bf16[3,128,1024]{2,1,0:T(8,128)(2,1)S(1)} %get-tuple-element.42.refs_8_.refs_7_) | copy-start | bytes 2359300
  4.9 21.3 %collective-permute-start = (bf16[3,128,1024]{2,1,0:T(8,128)(2,1)S(1)}, bf16[3,128,1024]{2,1,0:T(8,128)(2,1)S(1)}, u32[]{:S(2)}, u32[]{:S(2)}) collective-permute-start(bf16[3,128,1024]{2,1,0:T(8,128)(2,1)S(1)} %get-tuple-element.42.refs_8_.refs_7_), channel_id=1, source_target_pairs={{0,4},{4,0},{8,12},{12,8},{1,5},{5,1},{9,13},{13,9},{2,6},{6,2},{1... | collective-permute-start | bytes 2359304 | tf_op jit(solution)/shard_map/ppermute | solution.py:139
  7.8 20.7 %collective-permute-start.1 = (bf16[3,128,1024]{2,1,0:T(8,128)(2,1)}, bf16[3,128,1024]{2,1,0:T(8,128)(2,1)S(1)}, u32[]{:S(2)}, u32[]{:S(2)}) collective-permute-start(bf16[3,128,1024]{2,1,0:T(8,128)(2,1)} %get-tuple-element.43.refs_9_.refs_8_), channel_id=1, source_target_pairs={{0,8},{4,12},{8,0},{12,4},{1,9},{5,13},{9,1},{13,5},{2,10},{6,14},... | collective-permute-start | bytes 2359304 | tf_op jit(solution)/shard_map/ppermute | solution.py:139
  9.3 32.9 %collective-permute-start.2 = (bf16[3,128,1024]{2,1,0:T(8,128)(2,1)}, bf16[3,128,1024]{2,1,0:T(8,128)(2,1)S(1)}, u32[]{:S(2)}, u32[]{:S(2)}) collective-permute-start(bf16[3,128,1024]{2,1,0:T(8,128)(2,1)} %get-tuple-element.43.refs_9_.refs_8_), channel_id=1, source_target_pairs={{0,4},{4,0},{8,12},{12,8},{1,5},{5,1},{9,13},{13,9},{2,6},{6,2},{1... | collective-permute-start | bytes 2359304 | tf_op jit(solution)/shard_map/ppermute | solution.py:139
  9.9 34.0 %collective-permute-start.3 = (bf16[3,128,1024]{2,1,0:T(8,128)(2,1)S(1)}, bf16[3,128,1024]{2,1,0:T(8,128)(2,1)S(1)}, u32[]{:S(2)}, u32[]{:S(2)}) collective-permute-start(bf16[3,128,1024]{2,1,0:T(8,128)(2,1)S(1)} %get-tuple-element.42.refs_8_.refs_7_), channel_id=1, source_target_pairs={{0,8},{4,12},{8,0},{12,4},{1,9},{5,13},{9,1},{13,5},{2,10},{6,14},... | collective-permute-start | bytes 2359304 | tf_op jit(solution)/shard_map/ppermute | solution.py:139
  28.5 2.2 %copy-start = (bf16[1024,2048]{1,0:T(8,128)(2,1)S(1)}, bf16[1024,2048]{1,0:T(8,128)(2,1)}, u32[]{:S(2)}) copy-start(bf16[1024,2048]{1,0:T(8,128)(2,1)} %refs_8_.1) | copy-start | bytes 12582916
  30.7 2.2 %copy-start.3 = (bf16[1024,2048]{1,0:T(8,128)(2,1)S(1)}, bf16[1024,2048]{1,0:T(8,128)(2,1)}, u32[]{:S(2)}) copy-start(bf16[1024,2048]{1,0:T(8,128)(2,1)} %refs_9_.1) | copy-start | bytes 12582916
  32.8 0.9 copy-start.22
  33.8 0.9 copy-start.24
  34.8 0.9 copy-start.31
  39.8 5.3 %copy-start.6 = (bf16[192,1024]{1,0:T(8,128)(2,1)}, bf16[192,1024]{1,0:T(8,128)(2,1)S(1)}, u32[]{:S(2)}) copy-start(bf16[192,1024]{1,0:T(8,128)(2,1)S(1)} %get-tuple-element.47.refs_0_.refs_10_) | copy-start | bytes 1179652
  39.8 5.3 %copy-start.18 = (bf16[1024,64]{1,0:T(8,128)(2,1)}, bf16[1024,64]{1,0:T(8,128)(2,1)S(1)}, u32[]{:S(2)}) copy-start(bf16[1024,64]{1,0:T(8,128)(2,1)S(1)} %get-tuple-element.45.refs_3_) | copy-start | bytes 393220
  39.8 5.3 %copy-start.20 = (bf16[1024,64]{1,0:T(8,128)(2,1)}, bf16[1024,64]{1,0:T(8,128)(2,1)S(1)}, u32[]{:S(2)}) copy-start(bf16[1024,64]{1,0:T(8,128)(2,1)S(1)} %get-tuple-element.46.refs_4_) | copy-start | bytes 393220
  41.2 10.6 %copy-start.26 = (bf16[64,1024]{1,0:T(8,128)(2,1)S(1)}, bf16[64,1024]{1,0:T(8,128)(2,1)}, u32[]{:S(2)}) copy-start(bf16[64,1024]{1,0:T(8,128)(2,1)} %refs_2_.3) | copy-start | bytes 393220
  41.3 10.6 %collective-permute-start.6 = (bf16[2,3,128,1024]{3,2,1,0:T(8,128)(2,1)}, bf16[2,3,128,1024]{3,2,1,0:T(8,128)(2,1)}, u32[]{:S(2)}, u32[]{:S(2)}) collective-permute-start(bf16[2,3,128,1024]{3,2,1,0:T(8,128)(2,1)} %pair.3), channel_id=1, source_target_pairs={{0,16},{16,0},{1,17},{17,1},{2,18},{18,2},{3,19},{19,3},{4,20},{20... | collective-permute-start | bytes 4718600 | tf_op jit(solution)/shard_map/ppermute | solution.py:139
  45.1 6.7 %collective-permute-start.7 = (bf16[2,3,128,1024]{3,2,1,0:T(8,128)(2,1)}, bf16[2,3,128,1024]{3,2,1,0:T(8,128)(2,1)}, u32[]{:S(2)}, u32[]{:S(2)}) collective-permute-start(bf16[2,3,128,1024]{3,2,1,0:T(8,128)(2,1)} %pair.4), channel_id=1, source_target_pairs={{0,16},{16,0},{1,17},{17,1},{2,18},{18,2},{3,19},{19,3},{4,20},{20... | collective-permute-start | bytes 4718600 | tf_op jit(solution)/shard_map/ppermute | solution.py:139
  45.2 5.3 %collective-permute-start.4 = (bf16[3,128,1024]{2,1,0:T(8,128)(2,1)S(1)}, bf16[3,128,1024]{2,1,0:T(8,128)(2,1)S(1)}, u32[]{:S(2)}, u32[]{:S(2)}) collective-permute-start(bf16[3,128,1024]{2,1,0:T(8,128)(2,1)S(1)} %get-tuple-element.42.refs_8_.refs_7_), channel_id=1, source_target_pairs={{0,16},{16,0},{1,17},{17,1},{2,18},{18,2},{3,19},{19,3},{4,20},{20... | collective-permute-start | bytes 2359304 | tf_op jit(solution)/shard_map/ppermute | solution.py:139
  45.7 6.1 %collective-permute-start.5 = (bf16[3,128,1024]{2,1,0:T(8,128)(2,1)}, bf16[3,128,1024]{2,1,0:T(8,128)(2,1)}, u32[]{:S(2)}, u32[]{:S(2)}) collective-permute-start(bf16[3,128,1024]{2,1,0:T(8,128)(2,1)} %get-tuple-element.43.refs_9_.refs_8_), channel_id=1, source_target_pairs={{0,16},{16,0},{1,17},{17,1},{2,18},{18,2},{3,19},{19,3},{4,20},{20... | collective-permute-start | bytes 2359304 | tf_op jit(solution)/shard_map/ppermute | solution.py:139
  45.8 30.4 %collective-permute-start.8 = (bf16[3,128,1024]{2,1,0:T(8,128)(2,1)S(1)}, bf16[3,128,1024]{2,1,0:T(8,128)(2,1)}, u32[]{:S(2)}, u32[]{:S(2)}) collective-permute-start(bf16[3,128,1024]{2,1,0:T(8,128)(2,1)S(1)} %collective-permute-done.refs_0_.first.refs_10_.refs_9_), channel_id=1, source_target_pairs={{0,8},{4,12},{8,0},{12,4},{1,9},{5,13},{9,1},{13,5},{2,10},{6,14},... | collective-permute-start | bytes 2359304 | tf_op jit(solution)/shard_map/ppermute | solution.py:139
  51.4 24.9 %collective-permute-start.9 = (bf16[3,128,1024]{2,1,0:T(8,128)(2,1)S(1)}, bf16[3,128,1024]{2,1,0:T(8,128)(2,1)}, u32[]{:S(2)}, u32[]{:S(2)}) collective-permute-start(bf16[3,128,1024]{2,1,0:T(8,128)(2,1)S(1)} %collective-permute-done.1.refs_1_.second.refs_13_.refs_12_), channel_id=1, source_target_pairs={{0,4},{4,0},{8,12},{12,8},{1,5},{5,1},{9,13},{13,9},{2,6},{6,2},{1... | collective-permute-start | bytes 2359304 | tf_op jit(solution)/shard_map/ppermute | solution.py:139
  51.8 2.2 %copy-start.1 = (bf16[1024,2048]{1,0:T(8,128)(2,1)S(1)}, bf16[1024,2048]{1,0:T(8,128)(2,1)}, u32[]{:S(2)}) copy-start(bf16[1024,2048]{1,0:T(8,128)(2,1)} %refs_8_.1) | copy-start | bytes 12582916
  54.0 2.2 %copy-start.4 = (bf16[1024,2048]{1,0:T(8,128)(2,1)S(1)}, bf16[1024,2048]{1,0:T(8,128)(2,1)}, u32[]{:S(2)}) copy-start(bf16[1024,2048]{1,0:T(8,128)(2,1)} %refs_9_.1) | copy-start | bytes 12582916
  56.2 1.1 copy-start.9
  57.3 1.1 copy-start.12
  76.3 1.9 copy-start.23
  76.3 1.8 copy-start.25
  76.3 5.1 %copy-start.10 = (bf16[3,128,1024]{2,1,0:T(8,128)(2,1)S(1)}, bf16[3,128,1024]{2,1,0:T(8,128)(2,1)}, u32[]{:S(2)}) copy-start(bf16[3,128,1024]{2,1,0:T(8,128)(2,1)} %copy-done.8) | copy-start | bytes 2359300
  76.3 5.1 %copy-start.13 = (bf16[3,128,1024]{2,1,0:T(8,128)(2,1)S(1)}, bf16[3,128,1024]{2,1,0:T(8,128)(2,1)}, u32[]{:S(2)}) copy-start(bf16[3,128,1024]{2,1,0:T(8,128)(2,1)} %copy-done.11) | copy-start | bytes 2359300
  76.3 5.1 %copy-start.28 = (bf16[64,1024]{1,0:T(8,128)(2,1)S(1)}, bf16[64,1024]{1,0:T(8,128)(2,1)}, u32[]{:S(2)}) copy-start(bf16[64,1024]{1,0:T(8,128)(2,1)} %refs_3_.3) | copy-start | bytes 393220
  78.0 3.5 %collective-permute-start.10 = (bf16[2,3,128,1024]{3,2,1,0:T(8,128)(2,1)S(1)}, bf16[2,3,128,1024]{3,2,1,0:T(8,128)(2,1)S(1)}, u32[]{:S(2)}, u32[]{:S(2)}) collective-permute-start(bf16[2,3,128,1024]{3,2,1,0:T(8,128)(2,1)S(1)} %pair.5), channel_id=1, source_target_pairs={{0,16},{16,0},{1,17},{17,1},{2,18},{18,2},{3,19},{19,3},{4,20},{20... | collective-permute-start | bytes 4718600 | tf_op jit(solution)/shard_map/ppermute | solution.py:139
  88.1 3.0 %copy-start.33 = (bf16[2048,1024]{1,0:T(8,128)(2,1)}, bf16[2048,1024]{1,0:T(8,128)(2,1)S(1)}, u32[]{:S(2)}) copy-start(bf16[2048,1024]{1,0:T(8,128)(2,1)S(1)} %get-tuple-element.59.gate) | copy-start | bytes 12582916
  88.2 3.0 %copy-start.35 = (bf16[512,1024]{1,0:T(8,128)(2,1)}, bf16[512,1024]{1,0:T(8,128)(2,1)S(1)}, u32[]{:S(2)}) copy-start(bf16[512,1024]{1,0:T(8,128)(2,1)S(1)} %get-tuple-element.56.gate_grad.refs_2_) | copy-start | bytes 3145732
  88.2 3.0 %copy-start.37 = (bf16[512,1024]{1,0:T(8,128)(2,1)}, bf16[512,1024]{1,0:T(8,128)(2,1)S(1)}, u32[]{:S(2)}) copy-start(bf16[512,1024]{1,0:T(8,128)(2,1)S(1)} %get-tuple-element.57.up_grad.refs_4_) | copy-start | bytes 3145732
  88.2 3.0 %copy-start.39 = (f32[512,128]{1,0:T(8,128)}, f32[512,128]{1,0:T(8,128)S(1)}, u32[]{:S(2)}) copy-start(f32[512,128]{1,0:T(8,128)S(1)} %get-tuple-element.58.low.refs_6_) | copy-start | bytes 786436
  91.2 15.5 %collective-permute-start.12 = (bf16[512,512]{1,0:T(8,128)(2,1)}, bf16[512,512]{1,0:T(8,128)(2,1)}, u32[]{:S(2)}, u32[]{:S(2)}) collective-permute-start(bf16[512,512]{1,0:T(8,128)(2,1)} %token_grad.6.refs_10_.refs_0_.refs_13_), channel_id=1, source_target_pairs={{0,1},{3,2},{4,5},{7,6},{8,9},{11,10},{12,13},{15,14},{16,17},{19,... | collective-permute-start | bytes 1572872 | tf_op jit(solution)/shard_map/ppermute | solution.py:646
  95.7 4.8 %copy-start.34 = (bf16[2048,1024]{1,0:T(8,128)(2,1)S(1)}, bf16[2048,1024]{1,0:T(8,128)(2,1)}, u32[]{:S(2)}) copy-start(bf16[2048,1024]{1,0:T(8,128)(2,1)} %copy-done.33) | copy-start | bytes 12582916
  100.5 6.1 %copy-start.2 = (bf16[1024,2048]{1,0:T(8,128)(2,1)S(1)}, bf16[1024,2048]{1,0:T(8,128)(2,1)}, u32[]{:S(2)}) copy-start(bf16[1024,2048]{1,0:T(8,128)(2,1)} %refs_8_.1) | copy-start | bytes 12582916
  100.5 6.1 %copy-start.5 = (bf16[1024,2048]{1,0:T(8,128)(2,1)S(1)}, bf16[1024,2048]{1,0:T(8,128)(2,1)}, u32[]{:S(2)}) copy-start(bf16[1024,2048]{1,0:T(8,128)(2,1)} %refs_9_.1) | copy-start | bytes 12582916
  100.6 6.1 %copy-start.7 = (bf16[192,1024]{1,0:T(8,128)(2,1)S(1)}, bf16[192,1024]{1,0:T(8,128)(2,1)}, u32[]{:S(2)}) copy-start(bf16[192,1024]{1,0:T(8,128)(2,1)} %copy-done.6) | copy-start | bytes 1179652
  100.6 6.1 %copy-start.30 = (bf16[1024,64]{0,1:T(8,128)(2,1)S(1)}, bf16[1024,64]{0,1:T(8,128)(2,1)}, u32[]{:S(2)}) copy-start(bf16[1024,64]{0,1:T(8,128)(2,1)} %param.20) | copy-start | bytes 393220
  100.6 6.1 %copy-start.36 = (bf16[512,1024]{1,0:T(8,128)(2,1)S(1)}, bf16[512,1024]{1,0:T(8,128)(2,1)}, u32[]{:S(2)}) copy-start(bf16[512,1024]{1,0:T(8,128)(2,1)} %copy-done.35) | copy-start | bytes 3145732
  100.6 6.1 %copy-start.38 = (bf16[512,1024]{1,0:T(8,128)(2,1)S(1)}, bf16[512,1024]{1,0:T(8,128)(2,1)}, u32[]{:S(2)}) copy-start(bf16[512,1024]{1,0:T(8,128)(2,1)} %copy-done.37) | copy-start | bytes 3145732
  100.6 6.1 %copy-start.40 = (f32[512,128]{1,0:T(8,128)S(1)}, f32[512,128]{1,0:T(8,128)}, u32[]{:S(2)}) copy-start(f32[512,128]{1,0:T(8,128)} %copy-done.39) | copy-start | bytes 786436
  110.7 4.5 %collective-permute-start.21 = (f32[4,192,384]{2,1,0:T(8,128)S(1)}, f32[4,192,384]{2,1,0:T(8,128)S(1)}, u32[]{:S(2)}, u32[]{:S(2)}) collective-permute-start(f32[4,192,384]{2,1,0:T(8,128)S(1)} %get-tuple-element.71), channel_id=1, source_target_pairs={{0,16},{16,0},{1,17},{17,1},{2,18},{18,2},{3,19},{19,3},{4,20},{20... | collective-permute-start | bytes 3538952 | tf_op jit(solution)/shard_map/ppermute | solution.py:139
  110.8 16.6 %collective-permute-start.11 = (bf16[512,512]{1,0:T(8,128)(2,1)S(1)}, bf16[512,512]{1,0:T(8,128)(2,1)S(1)}, u32[]{:S(2)}, u32[]{:S(2)}) collective-permute-start(bf16[512,512]{1,0:T(8,128)(2,1)S(1)} %token_grad.7.refs_1_.refs_0_.refs_14_), channel_id=1, source_target_pairs={{0,1},{3,2},{4,5},{7,6},{8,9},{11,10},{12,13},{15,14},{16,17},{19,... | collective-permute-start | bytes 1572872 | tf_op jit(solution)/shard_map/ppermute | solution.py:646
  115.9 9.2 %collective-permute-start.22 = (bf16[2,192,384]{2,1,0:T(8,128)(2,1)S(1)}, bf16[2,192,384]{2,1,0:T(8,128)(2,1)S(1)}, u32[]{:S(2)}, u32[]{:S(2)}) collective-permute-start(bf16[2,192,384]{2,1,0:T(8,128)(2,1)S(1)} %get-tuple-element.73), channel_id=1, source_target_pairs={{0,8},{4,12},{8,0},{12,4},{1,9},{5,13},{9,1},{13,5},{2,10},{6,14},... | collective-permute-start | bytes 884744 | tf_op jit(solution)/shard_map/ppermute | solution.py:139
  120.0 18.7 %collective-permute-start.15 = (bf16[512,512]{1,0:T(8,128)(2,1)S(1)}, bf16[512,512]{1,0:T(8,128)(2,1)S(1)}, u32[]{:S(2)}, u32[]{:S(2)}) collective-permute-start(bf16[512,512]{1,0:T(8,128)(2,1)S(1)} %token_grad.8.refs_1_), channel_id=1, source_target_pairs={{0,1},{1,2},{4,5},{5,6},{8,9},{9,10},{12,13},{13,14},{16,17},{17,1... | collective-permute-start | bytes 1572872 | tf_op jit(solution)/shard_map/ppermute | solution.py:646
  122.8 15.9 %collective-permute-start.16 = (bf16[512,512]{1,0:T(8,128)(2,1)S(1)}, bf16[512,512]{1,0:T(8,128)(2,1)S(1)}, u32[]{:S(2)}, u32[]{:S(2)}) collective-permute-start(bf16[512,512]{1,0:T(8,128)(2,1)S(1)} %token_grad.8.refs_1_), channel_id=1, source_target_pairs={{3,2},{2,1},{7,6},{6,5},{11,10},{10,9},{15,14},{14,13},{19,18},{18... | collective-permute-start | bytes 1572872 | tf_op jit(solution)/shard_map/ppermute | solution.py:646
  125.7 8.8 %collective-permute-start.23 = (bf16[1,192,384]{2,1,0:T(8,128)(2,1)S(1)}, bf16[1,192,384]{2,1,0:T(8,128)(2,1)S(1)}, u32[]{:S(2)}, u32[]{:S(2)}) collective-permute-start(bf16[1,192,384]{2,1,0:T(8,128)(2,1)S(1)} %get-tuple-element.75), channel_id=1, source_target_pairs={{0,4},{4,0},{8,12},{12,8},{1,5},{5,1},{9,13},{13,9},{2,6},{6,2},{1... | collective-permute-start | bytes 442376 | tf_op jit(solution)/shard_map/ppermute | solution.py:139
  129.4 21.6 %collective-permute-start.13 = (bf16[512,512]{1,0:T(8,128)(2,1)S(1)}, bf16[512,512]{1,0:T(8,128)(2,1)S(1)}, u32[]{:S(2)}, u32[]{:S(2)}) collective-permute-start(bf16[512,512]{1,0:T(8,128)(2,1)S(1)} %token_grad.9.refs_3_), channel_id=1, source_target_pairs={{0,1},{1,2},{4,5},{5,6},{8,9},{9,10},{12,13},{13,14},{16,17},{17,1... | collective-permute-start | bytes 1572872 | tf_op jit(solution)/shard_map/ppermute | solution.py:646
  133.8 18.7 %collective-permute-start.14 = (bf16[512,512]{1,0:T(8,128)(2,1)S(1)}, bf16[512,512]{1,0:T(8,128)(2,1)S(1)}, u32[]{:S(2)}, u32[]{:S(2)}) collective-permute-start(bf16[512,512]{1,0:T(8,128)(2,1)S(1)} %token_grad.9.refs_3_), channel_id=1, source_target_pairs={{3,2},{2,1},{7,6},{6,5},{11,10},{10,9},{15,14},{14,13},{19,18},{18... | collective-permute-start | bytes 1572872 | tf_op jit(solution)/shard_map/ppermute | solution.py:646
  135.2 12.0 %collective-permute-start.26 = (f32[192,128]{1,0:T(8,128)S(1)}, f32[192,128]{1,0:T(8,128)S(1)}, u32[]{:S(2)}, u32[]{:S(2)}) collective-permute-start(f32[192,128]{1,0:T(8,128)S(1)} %get-tuple-element.80), channel_id=1, source_target_pairs={{0,4},{4,0},{8,12},{12,8},{1,5},{5,1},{9,13},{13,9},{2,6},{6,2},{1... | collective-permute-start | bytes 294920 | tf_op jit(solution)/shard_map/ppermute | solution.py:139
  141.3 26.9 %collective-permute-start.19 = (bf16[512,512]{1,0:T(8,128)(2,1)S(1)}, bf16[512,512]{1,0:T(8,128)(2,1)S(1)}, u32[]{:S(2)}, u32[]{:S(2)}) collective-permute-start(bf16[512,512]{1,0:T(8,128)(2,1)S(1)} %get-tuple-element.64.refs_3_), channel_id=1, source_target_pairs={{0,1},{1,2},{2,3},{4,5},{5,6},{6,7},{8,9},{9,10},{10,11},{12,13},{... | collective-permute-start | bytes 1572872 | tf_op jit(solution)/shard_map/ppermute | solution.py:646
  146.0 22.4 %collective-permute-start.20 = (bf16[512,512]{1,0:T(8,128)(2,1)S(1)}, bf16[512,512]{1,0:T(8,128)(2,1)S(1)}, u32[]{:S(2)}, u32[]{:S(2)}) collective-permute-start(bf16[512,512]{1,0:T(8,128)(2,1)S(1)} %get-tuple-element.65.refs_4_), channel_id=1, source_target_pairs={{3,2},{2,1},{1,0},{7,6},{6,5},{5,4},{11,10},{10,9},{9,8},{15,14},{... | collective-permute-start | bytes 1572872 | tf_op jit(solution)/shard_map/ppermute | solution.py:646
  147.3 15.8 %collective-permute-start.24 = (bf16[2,64,192]{2,1,0:T(8,128)(2,1)S(1)}, bf16[2,64,192]{2,1,0:T(8,128)(2,1)S(1)}, u32[]{:S(2)}, u32[]{:S(2)}) collective-permute-start(bf16[2,64,192]{2,1,0:T(8,128)(2,1)S(1)} %get-tuple-element.77), channel_id=1, source_target_pairs={{0,2},{1,3},{2,0},{3,1},{4,6},{5,7},{6,4},{7,5},{8,10},{9,11},{10,... | collective-permute-start | bytes 147464 | tf_op jit(solution)/shard_map/ppermute | solution.py:139
  151.0 14.0 %collective-permute-start.27 = (f32[2,192,128]{2,1,0:T(8,128)S(1)}, f32[2,192,128]{2,1,0:T(8,128)S(1)}, u32[]{:S(2)}, u32[]{:S(2)}) collective-permute-start(f32[2,192,128]{2,1,0:T(8,128)S(1)} %pad_maximum_fusion.2), channel_id=1, source_target_pairs={{0,8},{4,12},{8,0},{12,4},{1,9},{5,13},{9,1},{13,5},{2,10},{6,14},... | collective-permute-start | bytes 589832 | tf_op jit(solution)/shard_map/ppermute | solution.py:139
  154.7 28.0 %collective-permute-start.17 = (bf16[512,512]{1,0:T(8,128)(2,1)S(1)}, bf16[512,512]{1,0:T(8,128)(2,1)S(1)}, u32[]{:S(2)}, u32[]{:S(2)}) collective-permute-start(bf16[512,512]{1,0:T(8,128)(2,1)S(1)} %get-tuple-element.66.refs_2_), channel_id=1, source_target_pairs={{0,1},{1,2},{2,3},{4,5},{5,6},{6,7},{8,9},{9,10},{10,11},{12,13},{... | collective-permute-start | bytes 1572872 | tf_op jit(solution)/shard_map/ppermute | solution.py:646
  163.1 19.6 %collective-permute-start.18 = (bf16[512,512]{1,0:T(8,128)(2,1)S(1)}, bf16[512,512]{1,0:T(8,128)(2,1)S(1)}, u32[]{:S(2)}, u32[]{:S(2)}) collective-permute-start(bf16[512,512]{1,0:T(8,128)(2,1)S(1)} %get-tuple-element.67.refs_3_), channel_id=1, source_target_pairs={{3,2},{2,1},{1,0},{7,6},{6,5},{5,4},{11,10},{10,9},{9,8},{15,14},{... | collective-permute-start | bytes 1572872 | tf_op jit(solution)/shard_map/ppermute | solution.py:646
  165.0 15.1 %collective-permute-start.25 = (bf16[1,64,192]{2,1,0:T(8,128)(2,1)S(1)}, bf16[1,64,192]{2,1,0:T(8,128)(2,1)S(1)}, u32[]{:S(2)}, u32[]{:S(2)}) collective-permute-start(bf16[1,64,192]{2,1,0:T(8,128)(2,1)S(1)} %get-tuple-element.79), channel_id=1, source_target_pairs={{0,1},{1,0},{2,3},{3,2},{4,5},{5,4},{6,7},{7,6},{8,9},{9,8},{10,11... | collective-permute-start | bytes 73736 | tf_op jit(solution)/shard_map/ppermute | solution.py:139
  168.2 13.0 %collective-permute-start.28 = (f32[4,192,128]{2,1,0:T(8,128)S(1)}, f32[4,192,128]{2,1,0:T(8,128)S(1)}, u32[]{:S(2)}, u32[]{:S(2)}) collective-permute-start(f32[4,192,128]{2,1,0:T(8,128)S(1)} %pad_maximum_fusion.1.near), channel_id=1, source_target_pairs={{0,16},{16,0},{1,17},{17,1},{2,18},{18,2},{3,19},{19,3},{4,20},{20... | collective-permute-start | bytes 1179656 | tf_op jit(solution)/shard_map/ppermute | solution.py:139
  182.7 1.1 copy-start.14
  (6 other events, 5.4 us)

commit v3 on v2

--- a/solution.py
+++ b/solution.py
@@ -10,10 +10,10 @@
 
 adapter_scaling = 0.5
 MEBIBYTE = 1024 * 1024
-COST = 20
+COST = 1
 HALVES = 2
-COSTS = {"sums": 1, "pair": 1}
-LIMITS = {"low": 6, "sums": 12, "last": 14, "token": 8, "adapter": 12, "small": 4}
+COSTS = {"sums": 1, "pair": 1, "small": 1, "token": 30, "adapter": 20, "last": 480}
+LIMITS = {"low": 6, "sums": 32, "last": 14, "token": 8, "adapter": 12, "small": 4}
 TILE = 512
 STRIP = 256
 QUARTER_ORDER = ((3, 2, 1, 0), (0, 3, 2, 1), (3, 0, 1, 2), (0, 1, 2, 3))
@@ -180,15 +180,6 @@
     return jnp.concatenate([unit[which, :, span] for unit in units], axis=0)
 
 
-def put_in_place(units, here, gate_full, up_full):
-    half = units[0].shape[1]
-    for number, unit in enumerate(units):
-        block = lax.bitwise_xor(here[0], number // 2)
-        row = pl.ds(pl.multiple_of((2 * block + number % 2) * half, half), half)
-        gate_full[row, :] = unit[0]
-        up_full[row, :] = unit[1]
-
-
 def lows_kernel(tokens, cotangent, gate_in, up_in, leave, *refs):
     gate_low, up_low, back_low, turned = refs[-4:]
     rank = leave.shape[0]
@@ -218,29 +209,46 @@
         + [jax.ShapeDtypeStruct((3 * rank, rows), jnp.bfloat16)],
         compiler_params=pltpu.CompilerParams(vmem_limit_bytes=LIMITS["low"] * MEBIBYTE),
         cost_estimate=pl.CostEstimate(
-            flops=24 * COST * rows * width * rank, bytes_accessed=0, transcendentals=0
+            flops=480 * COST * rows * width * rank, bytes_accessed=0, transcendentals=0
         ),
         name="low_rank_values",
     )(tokens, cotangent, *factors, *ahead)
 
 
-def own_kernel(gate, up, down, *units):
+def own_kernel(gate, up, down, *refs):
+    units, (held, sems) = refs[:2], refs[2:]
+    rows = units[0].shape[1]
+    down_copy = pltpu.make_async_copy(down, held, sems.at[0])
+    down_copy.start()
+    copies = []
     for half, unit in enumerate(units):
-        rows = unit.shape[1]
+        for which, ref in enumerate((gate, up)):
+            copies.append(
+                pltpu.make_async_copy(
+                    ref.at[pl.ds(half * rows, rows)], unit.at[which], sems.at[1 + len(copies)]
+                )
+            )
+    for copy in copies:
+        copy.start()
+    down_copy.wait()
+    for half, unit in enumerate(units):
         part = slice(half * rows, (half + 1) * rows)
-        unit[0] = gate[part, :]
-        unit[1] = up[part, :]
-        unit[2] = down[:, part].astype(jnp.float32).T.astype(jnp.bfloat16)
+        unit[2] = held[:, part].astype(jnp.float32).T.astype(jnp.bfloat16)
+    for copy in copies:
+        copy.wait()
 
 
 def own_units(gate, up, down):
     rows, hidden = gate.shape
-    vmem = pl.BlockSpec(memory_space=pltpu.VMEM)
     return pl.pallas_call(
         own_kernel,
-        in_specs=[vmem] * 3,
-        out_specs=[vmem] * 2,
+        in_specs=[pl.BlockSpec(memory_space=pl.ANY)] * 3,
+        out_specs=[pl.BlockSpec(memory_space=pltpu.VMEM)] * 2,
         out_shape=[pltpu.VMEM((3, rows // 2, hidden), jnp.bfloat16)] * 2,
+        scratch_shapes=[
+            pltpu.VMEM((hidden, rows), jnp.bfloat16),
+            pltpu.SemaphoreType.DMA((5,)),
+        ],
         compiler_params=pltpu.CompilerParams(vmem_limit_bytes=LIMITS["low"] * MEBIBYTE),
         cost_estimate=pl.CostEstimate(flops=MEBIBYTE, bytes_accessed=0, transcendentals=0),
         name="own_units",
@@ -267,67 +275,112 @@
     )[0]
 
 
-def single_units(refs):
-    return [
-        part
-        for ref in refs
-        for part in ([ref] if len(ref.shape) == 3 else [ref.at[0], ref.at[1]])
-    ]
-
-
 def sums_kernel(masks, order, n_arrays, last, here, *refs):
-    tokens, cotangent, gate_low, up_low, back_low, gate_out, up_out, down_in = refs[:8]
-    units = single_units(refs[8 : 8 + n_arrays])
+    gate_low, up_low, back_low, gate_out, up_out, down_in, tokens, cotangent = refs[:8]
+    units = []
+    for ref in refs[8 : 8 + n_arrays]:
+        units += [ref] if len(ref.shape) == 3 else [ref.at[0], ref.at[1]]
     units = [units[number] for number in order]
-    sums, rest = refs[-8:-2], refs[-2:]
-    rows = 2 * units[0].shape[1]
-    hidden = units[0].shape[2]
+    outs = refs[8 + n_arrays :]
+    sums, rest, full = outs[: 3 * HALVES], outs[3 * HALVES : 3 * HALVES + 2], outs[-7:-5]
+    held_tokens, held_cotangent, held_down, row_sems, unit_sems = outs[-5:]
+    half_rows, hidden = units[0].shape[1:]
+    rows = 2 * half_rows
     tile = tokens.shape[0] // HALVES
+
+    def unit_copies(which):
+        copies = []
+        for number, unit in enumerate(units):
+            if which == 2:
+                target = held_down.at[pl.ds(number * half_rows, half_rows)]
+            else:
+                block = lax.bitwise_xor(here[0], masks[number // 2])
+                row = pl.multiple_of((2 * block + number % 2) * half_rows, half_rows)
+                target = full[which].at[pl.ds(row, half_rows)]
+            copies.append(
+                pltpu.make_async_copy(
+                    unit.at[which], target, unit_sems.at[which * len(units) + number]
+                )
+            )
+        return copies
+
+    def row_copy(which, half):
+        source, target = ((tokens, held_tokens), (cotangent, held_cotangent))[which]
+        part = pl.ds(half * tile, tile)
+        return pltpu.make_async_copy(
+            source.at[part], target.at[part], row_sems.at[which * HALVES + half]
+        )
+
+    loads = [*unit_copies(0), row_copy(0, 0), *unit_copies(1), row_copy(1, 0), *unit_copies(2)]
+    loads += [row_copy(which, half) for half in range(1, HALVES) for which in range(2)]
+    for load in loads:
+        load.start()
     for half in range(HALVES):
         part = slice(half * tile, (half + 1) * tile)
-        left = width_part(tokens, part, here, masks, rows)
-        back = width_part(cotangent, part, here, masks, rows)
-        for ref, out in zip((tokens, cotangent), rest):
-            out[part, :] = width_part(ref, part, here, last, rows)
-        for column in range(0, hidden, TILE):
-            span = slice(column, column + TILE)
-            for which, (low, factor) in enumerate(
-                ((gate_low, gate_out), (up_low, up_out), (back_low, down_in))
-            ):
+        for which, (low, factor) in enumerate(
+            ((gate_low, gate_out), (up_low, up_out), (back_low, down_in))
+        ):
+            if half == 0:
+                for copy in unit_copies(which):
+                    copy.wait()
+            if which != 1:
+                row_copy(which // 2, half).wait()
+                ref = (held_tokens, held_cotangent)[which // 2]
+                left = width_part(ref, part, here, masks, rows)
+                rest[which // 2][part, :] = width_part(ref, part, here, last, rows)
+            for column in range(0, hidden, TILE):
+                span = slice(column, column + TILE)
+                if which == 2:
+                    right = held_down[:, span]
+                else:
+                    right = jnp.concatenate(
+                        [
+                            full[which][
+                                pl.ds(
+                                    pl.multiple_of(lax.bitwise_xor(here[0], mask) * rows, rows), rows
+                                ),
+                                span,
+                            ]
+                            for mask in masks
+                        ]
+                    )
                 sums[3 * half + which][:, span] = matrix_product(
-                    back if which == 2 else left, stacked(units, which, span)
+                    left, right
                 ) + adapter_scaling * matrix_product(low[part, :], factor[:, span])
 
 
 def width_sums(here, tokens, cotangent, lows, factors, masks, order, arrays, last):
     rows, width = tokens.shape
     _, half, hidden = arrays[0].shape[-3:]
-    outs = vmem_call(
+    vmem, anywhere = pl.BlockSpec(memory_space=pltpu.VMEM), pl.BlockSpec(memory_space=pl.ANY)
+    shapes = [((rows // HALVES, hidden), jnp.float32)] * (3 * HALVES)
+    shapes += [((rows, 2 * half * len(last)), jnp.bfloat16)] * 2
+    shapes += [((width, hidden), jnp.bfloat16)] * 2
+    outs = pl.pallas_call(
         functools.partial(sums_kernel, masks, order, len(arrays), last),
-        [here],
-        [tokens, cotangent, *lows, *factors, *arrays],
-        [],
-        [((rows // HALVES, hidden), jnp.float32)] * (3 * HALVES)
-        + [((rows, 2 * half * len(last)), jnp.bfloat16)] * 2,
-        {},
-        [],
-        LIMITS["sums"],
-        COSTS["sums"],
-        "width_sums",
-    )
-    return outs[:-2], outs[-2:]
-
-
-def last_kernel(half, n_arrays, order, count, here, *refs):
-    left, back, gate_out, up_out = refs[:4]
-    units = single_units(refs[4 : 4 + n_arrays])
-    units = [units[number] for number in order]
-    sums = refs[4 + n_arrays : 7 + n_arrays]
-    outs = refs[-6:] if len(units) > count else refs[-4:]
-    hidden_out, gate_grad_out, up_grad_out, low_out = outs[:4]
-    if len(units) > count:
-        put_in_place(units, here, *outs[4:])
-        units = units[6:8] + units[14:16]
+        in_specs=[pl.BlockSpec(memory_space=pltpu.SMEM)]
+        + [vmem] * 6
+        + [anywhere] * (2 + len(arrays)),
+        out_specs=[vmem] * len(shapes),
+        out_shape=[pltpu.VMEM(shape, kind) for shape, kind in shapes],
+        scratch_shapes=[
+            pltpu.VMEM((rows, width), jnp.bfloat16),
+            pltpu.VMEM((rows, width), jnp.bfloat16),
+            pltpu.VMEM((half * len(order), hidden), jnp.bfloat16),
+            pltpu.SemaphoreType.DMA((2 * HALVES,)),
+            pltpu.SemaphoreType.DMA((3 * len(order),)),
+        ],
+        compiler_params=pltpu.CompilerParams(vmem_limit_bytes=LIMITS["sums"] * MEBIBYTE),
+        cost_estimate=pl.CostEstimate(flops=COSTS["sums"], bytes_accessed=0, transcendentals=0),
+        name="width_sums",
+    )(here, *lows, *factors, tokens, cotangent, *arrays)
+    return outs[: 3 * HALVES], outs[3 * HALVES : -2], outs[-2:]
+
+
+def last_kernel(half, here, left, back, gate_out, up_out, upper, lower, other, *refs):
+    units = [upper, lower, other.at[0], other.at[1]]
+    sums = refs[:3]
+    hidden_out, gate_grad_out, up_grad_out, low_out = refs[-4:]
     rows, hidden = hidden_out.shape
     part = slice(half * rows, (half + 1) * rows)
     gate_low = up_low = 0.0
@@ -348,27 +401,39 @@
     low_out[...] = jnp.concatenate([gate_low, up_low], axis=1)
 
 
-def hidden_and_grads(half, here, parts, factors, order, count, arrays, sums, width, ahead):
+def hidden_and_grads(half, here, parts, factors, tail, sums, ahead):
     rows = parts[0].shape[0] // HALVES
     rank, hidden = factors[0].shape
-    arrays = [*parts, *factors, *arrays, *sums[3 * half : 3 * half + 3]]
-    full = [((width, hidden), jnp.bfloat16)] * 2 if len(order) > count else []
-    outs = vmem_call(
-        functools.partial(last_kernel, half, len(arrays) - 7, order, count),
+    return vmem_call(
+        functools.partial(last_kernel, half),
         [here],
-        arrays,
+        [*parts, *factors, *tail, *sums[3 * half : 3 * half + 3]],
         ahead,
-        [((rows, hidden), jnp.bfloat16)] * 3 + [((rows, 2 * rank), jnp.float32)] + full,
+        [((rows, hidden), jnp.bfloat16)] * 3 + [((rows, 2 * rank), jnp.float32)],
         {},
         [],
         LIMITS["last"],
-        24 * rows * hidden * parts[0].shape[1],
+        COSTS["last"] * rows * hidden * parts[0].shape[1],
         "hidden_and_grads",
     )
-    return outs[:4], outs[4:]
+
+
+def quarter_rows(here, quarter, full, tail, which, columns):
+    upper, lower, other = tail
+    rows = 2 * upper.shape[1]
+    blocks = []
+    for number in range(columns // rows):
+        block = quarter * (columns // rows) + number
+        mask = lax.bitwise_xor(here[0], block)
+        held = full[pl.ds(pl.multiple_of(block * rows, rows), rows), :]
+        near = jnp.concatenate([upper[which], lower[which]])
+        far = jnp.concatenate([other[0, which], other[1, which]])
+        blocks.append(jnp.where(mask == 7, far, jnp.where(mask == 3, near, held)))
+    return jnp.concatenate(blocks)
 
 
 def token_grad_kernel(mode, step, here, gate_grad, up_grad, low, factor, gate, up, *refs):
+    tail, refs = refs[:3], refs[3:]
     came = refs[: {"first": 0, "sum": 1, "both": 3, "last": 2}[mode]]
     outs = refs[-2:] if mode == "both" else refs[-1:]
     columns = outs[0].shape[1]
@@ -376,8 +441,10 @@
         jnp.where(here[1] == place, order[step], 0) for place, order in enumerate(QUARTER_ORDER)
     )
     span = pl.ds(pl.multiple_of(quarter * columns, columns), columns)
-    total = contract_trailing_axis(gate_grad[...], gate[span, :])
-    total += contract_trailing_axis(up_grad[...], up[span, :])
+    total = contract_trailing_axis(
+        gate_grad[...], quarter_rows(here, quarter, gate, tail, 0, columns)
+    )
+    total += contract_trailing_axis(up_grad[...], quarter_rows(here, quarter, up, tail, 1, columns))
     total += matrix_product((adapter_scaling * low[...]).astype(jnp.bfloat16), factor[:, span])
     came = [ref[...].astype(jnp.float32) for ref in came]
     if mode == "both":
@@ -399,7 +466,7 @@
         {},
         [],
         LIMITS["token"],
-        8 * rows * columns * hidden,
+        COSTS["token"] * rows * columns * hidden,
         "token_grad",
     )
     return outs if mode == "both" else outs[0]
@@ -419,7 +486,9 @@
         input_output_aliases={1 + len(arrays): 0} if before else {},
         compiler_params=pltpu.CompilerParams(vmem_limit_bytes=LIMITS["token"] * MEBIBYTE),
         cost_estimate=pl.CostEstimate(
-            flops=8 * COST * rows * columns * hidden, bytes_accessed=0, transcendentals=0
+            flops=COSTS["token"] * COST * rows * columns * hidden,
+            bytes_accessed=0,
+            transcendentals=0,
         ),
         name="last_token_grad",
     )(
@@ -481,7 +550,7 @@
         {},
         [pltpu.VMEM((3 * rank, width), jnp.float32), pltpu.VMEM((3 * rank, hidden), jnp.float32)],
         LIMITS["adapter"],
-        24 * rank * rows * (width + hidden),
+        COSTS["adapter"] * rank * rows * (width + hidden),
         "adapter_grads",
     )
 
@@ -503,54 +572,58 @@
         {},
         [],
         LIMITS["small"],
-        20 * MEBIBYTE,
+        COSTS["small"],
         "halve",
     )
 
 
-def sum_kernel(here, keep, came, out):
-    out[...] = keep[0] + came[0].astype(jnp.float32)
+def sum_kernel(here, keep, *refs):
+    refs[-1][...] = sum((ref[...].astype(jnp.float32) for ref in refs[:-1]), keep[...])
 
 
 def last_sum(here, keep, came):
     return vmem_call(
         sum_kernel,
         [here],
-        [keep, came],
-        [],
-        [(keep.shape[1:], jnp.float32)],
+        [keep, *came],
+        [],
+        [(keep.shape, jnp.float32)],
         {},
         [],
         LIMITS["small"],
-        20 * MEBIBYTE,
+        COSTS["small"],
         "last_sum",
         True,
     )[0]
 
 
-def turn_kernel(wide_columns, here, kept, came, narrow, keep, send, wide):
+def turn_kernel(wide_columns, here, kept, came, narrow, *refs):
+    outs, wide = refs[:-1], refs[-1]
     total = kept[0] + came[0].astype(jnp.float32)
     narrow[...] = total[:, wide_columns:]
     wide[...] = total[:, :wide_columns].T
-    rows = keep.shape[1]
-    for mask in range(4):
+    for mask, out in enumerate(outs):
+        rows = out.shape[0]
         block = pl.ds(pl.multiple_of(lax.bitwise_xor(here[1], mask) * rows, rows), rows)
-        (keep if mask < 2 else send)[mask % 2] = wide[block, :].astype((keep if mask < 2 else send).dtype)
-
-
-def turn(here, keep, came, wide_columns):
+        out[...] = wide[block, :].astype(out.dtype)
+
+
+def turn(here, keep, came, wide_columns, quarters):
     _, rows, columns = keep.shape
     return vmem_call(
         functools.partial(turn_kernel, wide_columns),
         [here],
         [keep, came],
         [],
-        [((rows, columns - wide_columns), keep.dtype)]
-        + [((2, wide_columns // 4, rows), kind) for kind in (jnp.float32, jnp.bfloat16)],
+        [((rows, columns - wide_columns), jnp.float32)]
+        + [
+            ((wide_columns // quarters, rows), jnp.bfloat16 if mask else jnp.float32)
+            for mask in range(quarters)
+        ],
         {},
-        [pltpu.VMEM((wide_columns, rows), keep.dtype)],
+        [pltpu.VMEM((wide_columns, rows), jnp.float32)],
         LIMITS["small"],
-        20 * MEBIBYTE,
+        COSTS["small"],
         "turn",
     )
 
@@ -574,7 +647,7 @@
         {},
         [],
         LIMITS["small"],
-        20 * MEBIBYTE,
+        COSTS["small"],
         "whole",
         True,
     )[0]
@@ -634,41 +707,29 @@
     arrays = [units[key] for key in keys] + [pairs[0], pairs[1]]
     masks = (0, 1, 2, 4, 5, 6)
     order = [placed.index((mask, half)) for mask in masks for half in range(2)]
-    sums, parts = width_sums(
+    sums, parts, full = width_sums(
         here, tokens, cotangent, lows, [gate_out, up_out, down_in], masks, order, arrays, (3, 7)
     )
     tail = [units[3, 0], units[3, 1]]
     tail.append(flip(pair(*tail, [sums[0]]), "cuts", 1))
-    placed = [(3, 0), (3, 1), (7, 0), (7, 1), *placed]
-    order = [placed.index((mask, half)) for mask in range(8) for half in range(2)]
 
     factor = jnp.concatenate([gate_in, up_in])
     shift = lambda array, pairs: lax.ppermute(array, "tp", pairs)
-    states, first, full = [], [], []
+    states, first = [], []
     share = lambda step, half, mode, came=(), ahead=(): token_grad(
         mode,
         step,
         here,
-        [*states[half][1:], factor, *full],
+        [*states[half][1:], factor, *full, *tail],
         width // quarters,
         came,
         ahead,
     )
     both = range(HALVES)
     for half in both:
-        state, placed = hidden_and_grads(
-            half,
-            here,
-            parts,
-            [gate_out, up_out],
-            range(4) if half else order,
-            4,
-            tail if half else tail + arrays,
-            sums,
-            width,
-            first[:],
+        state = hidden_and_grads(
+            half, here, parts, [gate_out, up_out], tail, sums, first[:]
         )
-        full = placed or full
         states.append(state)
         first.append(share(0, half, "first"))
     came = [shift(part, [(0, 1), (3, 2)]) for part in first]
@@ -707,9 +768,10 @@
     )
     keep, send = halve(here, keep, flip(send, "cuts", 1))
     keep, send = halve(here, keep, flip(send, "fsdp", 2))
-    narrow, keep, send = turn(here, keep, flip(send, "fsdp", 1), width // groups)
-    keep, send = halve(here, keep, flip(send, "tp", 2))
-    wide_grads = last_sum(here, keep, flip(send, "tp", 1))
+    narrow, keep, *send = turn(here, keep, flip(send, "fsdp", 1), width // groups, quarters)
+    wide_grads = last_sum(
+        here, keep, [flip(part, "tp", 1 + number) for number, part in enumerate(send)]
+    )
     near = jnp.stack([narrow, flip(narrow, "fsdp", 1)])
     near = jnp.concatenate([near, flip(near, "fsdp", 2)])
     narrow_turned = whole(here, near, flip(near, "cuts", 1))
@@ -722,7 +784,7 @@
                 3,
                 half,
                 here,
-                [*states[half][1:], factor, *full],
+                [*states[half][1:], factor, *full, *tail],
                 width // quarters,
                 [from_left[half], from_right[half]],
                 [wide_grads, narrow_turned] if half else partial[1],

time: 189 us -> 179 us (0.947)
  local copies, waits for them, and re-layouts: 23.7 us -> 13.3 us
  Pallas kernels: 64.1 us -> 71 us
  waiting for transfers between devices: 49.5 us -> 42.8 us
    pallas_call x1 -> x2, Pallas kernels: 1.1 us -> 19.4 us  [the longest x1 18.1 us: width_sums(): pl.pallas_call(functools.partial(sums_kernel, masks, order, len(arrays),...]
    pallas_call x19 -> x17, Pallas kernels: 53.3 us -> 40.1 us  [vmem_call(): pl.pallas_call(kernel, in_specs=[pl.BlockSpec(memory_space=pltpu.SMEM)] *...]
    unnamed x82 -> x62, local copies, waits for them, and re-layouts: 23.7 us -> 13.3 us
    ppermute x19 -> x20, waiting for transfers between devices: 43.4 us -> 35.7 us  [flip(): return lax.ppermute(array, axis, [(i, i ^ bit) for i in range(size)])]
    ppermute x19 -> x20, starting transfers between devices: 20.9 us -> 20.4 us  [flip(): return lax.ppermute(array, axis, [(i, i ^ bit) for i in range(size)])]
  transfers between devices with their start and end apart: 29 -> 30, of which waited for: 12 -> 14; matrix products, arithmetic and copies ran while one was open for 0% -> 0% of each run, Pallas kernels for 24% -> 30%
where the time goes in v3:
time: 179 us; the launch traced here: 178 us
  Pallas kernels  71 us (40%)
  starting transfers between devices  48.7 us (27%)
  waiting for transfers between devices  42.8 us (24%)
  local copies, waits for them, and re-layouts  13.3 us (7%)
    pallas_call x17, Pallas kernels, vmem_call(): pl.pallas_call(kernel, in_specs=[pl.BlockSpec(memory_space=pltpu.SMEM)] *...  40.1 us
    ppermute x20, waiting for transfers between devices, flip(): return lax.ppermute(array, axis, [(i, i ^ bit) for i in range(size)])  35.7 us
    ppermute x10, starting transfers between devices, square_plane(): shift = lambda array, pairs: lax.ppermute(array, 'tp', pairs)  28.2 us
    ppermute x20, starting transfers between devices, flip(): return lax.ppermute(array, axis, [(i, i ^ bit) for i in range(size)])  20.4 us
    pallas_call x1, Pallas kernels, width_sums(): pl.pallas_call(functools.partial(sums_kernel, masks, order, len(arrays),...  18.1 us
    unnamed x62, local copies, waits for them, and re-layouts  13.3 us
    pallas_call x2, Pallas kernels, last_token_grad(): pl.pallas_call(functools.partial(token_grad_kernel, 'last', step), grid=(...  7.43 us
    ppermute x10, waiting for transfers between devices, square_plane(): shift = lambda array, pairs: lax.ppermute(array, 'tp', pairs)  7.11 us
  transfers between devices with their start and end apart: 30, of which 14 were waited for; matrix products, arithmetic and copies ran while one was open for 0% of the time, Pallas kernels for 30%

profile of v3, /device:TPU:0, one launch (start us, length us, event | category | flops | bytes accessed | tf_op | source)
XLA Modules:
  0.0 177.5 jit_solution(10994419438096594269)
XLA Ops:
  0.6 1.0 copy-done.13
  1.7 1.0 copy-done.14
  2.7 1.0 copy-done.15
  3.8 1.2 own_units.1
  5.0 3.0 %collective-permute-start = (bf16[3,128,1024]{2,1,0:T(8,128)(2,1)S(1)}, bf16[3,128,1024]{2,1,0:T(8,128)(2,1)S(1)}, u32[]{:S(2)}, u32[]{:S(2)}) collective-permute-start(bf16[3,128,1024]{2,1,0:T(8,128)(2,1)S(1)} %get-tuple-element.42.refs_8_), channel_id=1, source_target_pairs={{0,4},{4,0},{8,12},{12,8},{1,5},{5,1},{9,13},{13,9},{2,6},{6,2},{1... | collective-permute-start | bytes 2359304 | tf_op jit(solution)/shard_map/ppermute | solution.py:139
  8.0 1.5 collective-permute-start.1
  10.1 16.3 %collective-permute-done.refs_0_.first.refs_10_ = bf16[3,128,1024]{2,1,0:T(8,128)(2,1)S(1)} collective-permute-done((bf16[3,128,1024]{2,1,0:T(8,128)(2,1)S(1)}, bf16[3,128,1024]{2,1,0:T(8,128)(2,1)S(1)}, u32[]{:S(2)}, u32[]{:S(2)}) %collective-permute-start) | collective-permute-done | bytes 786464 | tf_op jit(solution)/shard_map/ppermute | solution.py:139
  26.4 2.3 %collective-permute-done.1.refs_1_.second.refs_13_ = bf16[3,128,1024]{2,1,0:T(8,128)(2,1)S(1)} collective-permute-done((bf16[3,128,1024]{2,1,0:T(8,128)(2,1)}, bf16[3,128,1024]{2,1,0:T(8,128)(2,1)S(1)}, u32[]{:S(2)}, u32[]{:S(2)}) %collective-permute-start.1) | collective-permute-done | bytes 786464 | tf_op jit(solution)/shard_map/ppermute | solution.py:139
  28.7 2.5 %copy-done = bf16[1024,2048]{1,0:T(8,128)(2,1)S(1)} copy-done((bf16[1024,2048]{1,0:T(8,128)(2,1)S(1)}, bf16[1024,2048]{1,0:T(8,128)(2,1)}, u32[]{:S(2)}) %copy-start) | copy-done | bytes 4194328
  31.2 2.2 %copy-done.2 = bf16[1024,2048]{1,0:T(8,128)(2,1)S(1)} copy-done((bf16[1024,2048]{1,0:T(8,128)(2,1)S(1)}, bf16[1024,2048]{1,0:T(8,128)(2,1)}, u32[]{:S(2)}) %copy-start.2) | copy-done | bytes 4194328
  33.4 0.9 copy-done.19
  34.3 0.9 copy-done.21
  35.3 0.9 copy-done.29
  36.2 4.1 %low_rank_values.1 = (bf16[1024,64]{1,0:T(8,128)(2,1)S(1)}, bf16[1024,64]{1,0:T(8,128)(2,1)S(1)}, bf16[1024,64]{1,0:T(8,128)(2,1)S(1)}, bf16[192,1024]{1,0:T(8,128)(2,1)S(1)}) custom-call(bf16[1024,2048]{1,0:T(8,128)(2,1)S(1)} %copy-done, bf16[1024,2048]{1,0:T(8,128)(2,1)S(1)} %copy-done.2, bf16[64,2048]{1,0:T(8,128)(2,1)S(1)} %bitcast.14, ...), custom_call_target="tpu_custom_call" | custom-call | flops 64424509440 | tf_op jit(solution)/shard_map/low_rank_values/pallas_call | solution.py:201
  40.4 1.4 pair.3
  41.8 0.7 collective-permute-done.2.first.refs_11_
  42.4 1.7 collective-permute-done.3.second.refs_12_
  44.1 1.4 pair.4
  46.1 1.5 collective-permute-start.8
  47.7 3.2 %collective-permute-done.4.refs_14_ = bf16[3,128,1024]{2,1,0:T(8,128)(2,1)S(1)} collective-permute-done((bf16[3,128,1024]{2,1,0:T(8,128)(2,1)S(1)}, bf16[3,128,1024]{2,1,0:T(8,128)(2,1)S(1)}, u32[]{:S(2)}, u32[]{:S(2)}) %collective-permute-start.4) | collective-permute-done | bytes 786464 | tf_op jit(solution)/shard_map/ppermute | solution.py:139
  51.8 0.7 pad_add_fusion.here
  52.5 18.1 %width_sums.1 = (f32[512,1024]{1,0:T(8,128)S(1)}, f32[512,1024]{1,0:T(8,128)S(1)}, f32[512,1024]{1,0:T(8,128)S(1)}, f32[512,1024]{1,0:T(8,128)S(1)}, f32[512,102...) custom-call(s32[2]{0:T(128)} %pad_add_fusion.here, ...), custom_call_target="tpu_custom_call" | custom-call | flops 1 | tf_op jit(solution)/shard_map/width_sums/pallas_call | solution.py:359
  70.8 1.7 pair.5
  73.0 3.0 %collective-permute-done.10.other.refs_2_ = bf16[2,3,128,1024]{3,2,1,0:T(8,128)(2,1)S(1)} collective-permute-done((bf16[2,3,128,1024]{3,2,1,0:T(8,128)(2,1)S(1)}, bf16[2,3,128,1024]{3,2,1,0:T(8,128)(2,1)S(1)}, u32[]{:S(2)}, u32[]{:S(2)}) %collective-permute-start.10) | collective-permute-done | bytes 1572896 | tf_op jit(solution)/shard_map/ppermute | solution.py:139
  76.0 4.6 %hidden_and_grads.2 = (bf16[512,1024]{1,0:T(8,128)(2,1)S(1)}, bf16[512,1024]{1,0:T(8,128)(2,1)S(1)}, bf16[512,1024]{1,0:T(8,128)(2,1)S(1)}, f32[512,128]{1,0:T(8,128)S(1)}) custom-call(s32[2]{0:T(128)S(1)} %copy-done.26, bf16[1024,512]{1,0:T(8,128)(2,1)S(1)} %get-tuple-element.48.left, bf16[1024,512]{1,0:T(8,128)(2,1)S(1)} %get-tuple-element.49.back, ...), custom_call_target="tpu_custom_call" | custom-call | flops 128849018880 | tf_op jit(solution)/shard_map/hidden_and_grads/pallas_call | solution.py:147
  80.6 3.0 %token_grad.6.refs_3_.refs_13_ = bf16[512,512]{1,0:T(8,128)(2,1)S(1)} custom-call(s32[2]{0:T(128)S(1)} %copy-done.26, bf16[512,1024]{1,0:T(8,128)(2,1)S(1)} %get-tuple-element.56.gate_grad.refs_2_, bf16[512,1024]{1,0:T(8,128)(2,1)S(1)} %get-tuple-element.57.up_grad.refs_4_, f32[512,128]{1,0:T(8,128)S(1)} %get-tuple-element.58.low.refs_6_, ...), custom_call_target="tpu_custom_call" | custom-call | flops 8053063680 | tf_op jit(solution)/shard_map/token_grad/pallas_call | solution.py:147
  83.6 3.5 %collective-permute-start.12 = (bf16[512,512]{1,0:T(8,128)(2,1)S(1)}, bf16[512,512]{1,0:T(8,128)(2,1)S(1)}, u32[]{:S(2)}, u32[]{:S(2)}) collective-permute-start(bf16[512,512]{1,0:T(8,128)(2,1)S(1)} %token_grad.6.refs_3_.refs_13_), channel_id=1, source_target_pairs={{0,1},{3,2},{4,5},{7,6},{8,9},{11,10},{12,13},{15,14},{16,17},{19,... | collective-permute-start | bytes 1572872 | tf_op jit(solution)/shard_map/ppermute | solution.py:717
  87.2 4.4 %hidden_and_grads.3 = (bf16[512,1024]{1,0:T(8,128)(2,1)S(1)}, bf16[512,1024]{1,0:T(8,128)(2,1)S(1)}, bf16[512,1024]{1,0:T(8,128)(2,1)S(1)}, f32[512,128]{1,0:T(8,128)S(1)}) custom-call(s32[2]{0:T(128)S(1)} %copy-done.26, bf16[1024,512]{1,0:T(8,128)(2,1)S(1)} %get-tuple-element.48.left, bf16[1024,512]{1,0:T(8,128)(2,1)S(1)} %copy-done.28, ...), custom_call_target="tpu_custom_call" | custom-call | flops 128849018880 | tf_op jit(solution)/shard_map/hidden_and_grads/pallas_call | solution.py:147
  91.6 3.1 %token_grad.7.refs_4_.refs_3_.refs_14_ = bf16[512,512]{1,0:T(8,128)(2,1)S(1)} custom-call(s32[2]{0:T(128)S(1)} %copy-done.26, bf16[512,1024]{1,0:T(8,128)(2,1)S(1)} %get-tuple-element.61.gate_grad.refs_3_, bf16[512,1024]{1,0:T(8,128)(2,1)S(1)} %get-tuple-element.62.up_grad.refs_5_, f32[512,128]{1,0:T(8,128)S(1)} %get-tuple-element.63.low.refs_7_, ...), custom_call_target="tpu_custom_call" | custom-call | flops 8053063680 | tf_op jit(solution)/shard_map/token_grad/pallas_call | solution.py:147
  94.7 4.1 %collective-permute-done.12.refs_3_.refs_12_ = bf16[512,512]{1,0:T(8,128)(2,1)S(1)} collective-permute-done((bf16[512,512]{1,0:T(8,128)(2,1)S(1)}, bf16[512,512]{1,0:T(8,128)(2,1)S(1)}, u32[]{:S(2)}, u32[]{:S(2)}) %collective-permute-start.12) | collective-permute-done | bytes 524320 | tf_op jit(solution)/shard_map/ppermute | solution.py:717
  98.8 4.0 %adapter_grads.1 = (f32[4,192,384]{2,1,0:T(8,128)S(1)}, f32[4,192,384]{2,1,0:T(8,128)S(1)}) custom-call(s32[2]{0:T(128)S(1)} %copy-done.26, bf16[512,1024]{1,0:T(8,128)(2,1)S(1)} %get-tuple-element.68.refs_0_, bf16[512,1024]{1,0:T(8,128)(2,1)S(1)} %get-tuple-element.69.refs_1_, bf16[512,1024]{1,0:T(8,128)(2,1)S(1)} %get-tuple-element.56.gate_grad.refs_2_, ...), custom_call_target="tpu_custom_call" | custom-call | flops 4026531840 | tf_op jit(solution)/shard_map/adapter_grads/pallas_call | solution.py:147
  102.9 4.4 %collective-permute-start.11 = (bf16[512,512]{1,0:T(8,128)(2,1)S(1)}, bf16[512,512]{1,0:T(8,128)(2,1)S(1)}, u32[]{:S(2)}, u32[]{:S(2)}) collective-permute-start(bf16[512,512]{1,0:T(8,128)(2,1)S(1)} %token_grad.7.refs_4_.refs_3_.refs_14_), channel_id=1, source_target_pairs={{0,1},{3,2},{4,5},{7,6},{8,9},{11,10},{12,13},{15,14},{16,17},{19,... | collective-permute-start | bytes 1572872 | tf_op jit(solution)/shard_map/ppermute | solution.py:717
  107.4 0.7 halve.2
  108.0 1.6 collective-permute-start.22
  109.6 2.9 %token_grad.8.refs_4_ = bf16[512,512]{1,0:T(8,128)(2,1)S(1)} custom-call(s32[2]{0:T(128)S(1)} %copy-done.26, bf16[512,1024]{1,0:T(8,128)(2,1)S(1)} %get-tuple-element.56.gate_grad.refs_2_, bf16[512,1024]{1,0:T(8,128)(2,1)S(1)} %get-tuple-element.57.up_grad.refs_4_, f32[512,128]{1,0:T(8,128)S(1)} %get-tuple-element.58.low.refs_6_, ...), custom_call_target="tpu_custom_call" | custom-call | flops 8053063680 | tf_op jit(solution)/shard_map/token_grad/pallas_call | solution.py:147
  112.5 2.8 %collective-permute-start.15 = (bf16[512,512]{1,0:T(8,128)(2,1)S(1)}, bf16[512,512]{1,0:T(8,128)(2,1)S(1)}, u32[]{:S(2)}, u32[]{:S(2)}) collective-permute-start(bf16[512,512]{1,0:T(8,128)(2,1)S(1)} %token_grad.8.refs_4_), channel_id=1, source_target_pairs={{0,1},{1,2},{4,5},{5,6},{8,9},{9,10},{12,13},{13,14},{16,17},{17,1... | collective-permute-start | bytes 1572872 | tf_op jit(solution)/shard_map/ppermute | solution.py:717
  115.3 0.7 collective-permute-start.16
  116.0 1.2 collective-permute-done.22.came
  117.8 0.9 collective-permute-start.23
  118.8 0.8 collective-permute-done.11.refs_3_
  119.6 2.9 %token_grad.9.refs_6_ = bf16[512,512]{1,0:T(8,128)(2,1)S(1)} custom-call(s32[2]{0:T(128)S(1)} %copy-done.26, bf16[512,1024]{1,0:T(8,128)(2,1)S(1)} %get-tuple-element.61.gate_grad.refs_3_, bf16[512,1024]{1,0:T(8,128)(2,1)S(1)} %get-tuple-element.62.up_grad.refs_5_, f32[512,128]{1,0:T(8,128)S(1)} %get-tuple-element.63.low.refs_7_, ...), custom_call_target="tpu_custom_call" | custom-call | flops 8053063680 | tf_op jit(solution)/shard_map/token_grad/pallas_call | solution.py:147
  122.5 4.4 %collective-permute-start.13 = (bf16[512,512]{1,0:T(8,128)(2,1)S(1)}, bf16[512,512]{1,0:T(8,128)(2,1)S(1)}, u32[]{:S(2)}, u32[]{:S(2)}) collective-permute-start(bf16[512,512]{1,0:T(8,128)(2,1)S(1)} %token_grad.9.refs_6_), channel_id=1, source_target_pairs={{0,1},{1,2},{4,5},{5,6},{8,9},{9,10},{12,13},{13,14},{16,17},{17,1... | collective-permute-start | bytes 1572872 | tf_op jit(solution)/shard_map/ppermute | solution.py:717
  126.9 0.9 collective-permute-start.14
  127.8 0.7 turn.1
  128.5 0.9 collective-permute-start.27
  129.5 1.3 collective-permute-done.15.refs_4_
  130.8 3.1 %token_grad.10 = (bf16[512,512]{1,0:T(8,128)(2,1)S(1)}, bf16[512,512]{1,0:T(8,128)(2,1)S(1)}) custom-call(s32[2]{0:T(128)S(1)} %copy-done.26, bf16[512,1024]{1,0:T(8,128)(2,1)S(1)} %get-tuple-element.56.gate_grad.refs_2_, bf16[512,1024]{1,0:T(8,128)(2,1)S(1)} %get-tuple-element.57.up_grad.refs_4_, f32[512,128]{1,0:T(8,128)S(1)} %get-tuple-element.58.low.refs_6_, ...), custom_call_target="tpu_custom_call" | custom-call | flops 8053063680 | tf_op jit(solution)/shard_map/token_grad/pallas_call | solution.py:147
  133.9 4.4 %collective-permute-start.19 = (bf16[512,512]{1,0:T(8,128)(2,1)S(1)}, bf16[512,512]{1,0:T(8,128)(2,1)S(1)}, u32[]{:S(2)}, u32[]{:S(2)}) collective-permute-start(bf16[512,512]{1,0:T(8,128)(2,1)S(1)} %get-tuple-element.64.refs_6_), channel_id=1, source_target_pairs={{0,1},{1,2},{2,3},{4,5},{5,6},{6,7},{8,9},{9,10},{10,11},{12,13},{... | collective-permute-start | bytes 1572872 | tf_op jit(solution)/shard_map/ppermute | solution.py:717
  138.3 1.3 collective-permute-start.20
  139.6 1.6 collective-permute-start.28
  141.2 0.9 collective-permute-done.13.refs_4_
  142.0 3.1 %token_grad.11 = (bf16[512,512]{1,0:T(8,128)(2,1)S(1)}, bf16[512,512]{1,0:T(8,128)(2,1)S(1)}) custom-call(s32[2]{0:T(128)S(1)} %copy-done.26, bf16[512,1024]{1,0:T(8,128)(2,1)S(1)} %get-tuple-element.61.gate_grad.refs_3_, bf16[512,1024]{1,0:T(8,128)(2,1)S(1)} %get-tuple-element.62.up_grad.refs_5_, f32[512,128]{1,0:T(8,128)S(1)} %get-tuple-element.63.low.refs_7_, ...), custom_call_target="tpu_custom_call" | custom-call | flops 8053063680 | tf_op jit(solution)/shard_map/token_grad/pallas_call | solution.py:147
  145.1 4.4 %collective-permute-start.17 = (bf16[512,512]{1,0:T(8,128)(2,1)S(1)}, bf16[512,512]{1,0:T(8,128)(2,1)S(1)}, u32[]{:S(2)}, u32[]{:S(2)}) collective-permute-start(bf16[512,512]{1,0:T(8,128)(2,1)S(1)} %get-tuple-element.66.refs_5_), channel_id=1, source_target_pairs={{0,1},{1,2},{2,3},{4,5},{5,6},{6,7},{8,9},{9,10},{10,11},{12,13},{... | collective-permute-start | bytes 1572872 | tf_op jit(solution)/shard_map/ppermute | solution.py:717
  149.5 1.3 collective-permute-start.18
  150.9 2.7 %collective-permute-start.24 = (bf16[64,192]{1,0:T(8,128)(2,1)S(1)}, bf16[64,192]{1,0:T(8,128)(2,1)S(1)}, u32[]{:S(2)}, u32[]{:S(2)}) collective-permute-start(bf16[64,192]{1,0:T(8,128)(2,1)S(1)} %get-tuple-element.77), channel_id=1, source_target_pairs={{0,1},{1,0},{2,3},{3,2},{4,5},{5,4},{6,7},{7,6},{8,9},{9,8},{10,11... | collective-permute-start | bytes 73736 | tf_op jit(solution)/shard_map/ppermute | solution.py:139
  153.6 1.1 collective-permute-start.25
  154.7 3.4 %collective-permute-start.26 = (bf16[64,192]{1,0:T(8,128)(2,1)S(1)}, bf16[64,192]{1,0:T(8,128)(2,1)S(1)}, u32[]{:S(2)}, u32[]{:S(2)}) collective-permute-start(bf16[64,192]{1,0:T(8,128)(2,1)S(1)} %get-tuple-element.79), channel_id=1, source_target_pairs={{0,3},{1,2},{2,1},{3,0},{4,7},{5,6},{6,5},{7,4},{8,11},{9,10},{10,... | collective-permute-start | bytes 73736 | tf_op jit(solution)/shard_map/ppermute | solution.py:139
  158.1 7.2 %collective-permute-done.24.refs_0_ = bf16[64,192]{1,0:T(8,128)(2,1)S(1)} collective-permute-done((bf16[64,192]{1,0:T(8,128)(2,1)S(1)}, bf16[64,192]{1,0:T(8,128)(2,1)S(1)}, u32[]{:S(2)}, u32[]{:S(2)}) %collective-permute-start.24) | collective-permute-done | bytes 24608 | tf_op jit(solution)/shard_map/ppermute | solution.py:139
  165.3 3.7 %last_token_grad.2.refs_5_ = bf16[1024,512]{1,0:T(8,128)(2,1)} custom-call(s32[2]{0:T(128)S(1)} %copy-done.26, bf16[512,1024]{1,0:T(8,128)(2,1)S(1)} %get-tuple-element.56.gate_grad.refs_2_, bf16[512,1024]{1,0:T(8,128)(2,1)S(1)} %get-tuple-element.57.up_grad.refs_4_, f32[512,128]{1,0:T(8,128)S(1)} %get-tuple-element.58.low.refs_6_, ...), custom_call_target="tpu_custom_call" | custom-call | flops 8053063680 | tf_op jit(solution)/shard_map/last_token_grad/pallas_call | solution.py:478
  169.1 1.2 last_sum.1.refs_6_
  170.3 1.5 whole.1.refs_7_
  171.9 1.1 copy-done.11
  173.0 0.8 copy-done.25
  173.8 3.7 %last_token_grad.3 = bf16[1024,512]{1,0:T(8,128)(2,1)} custom-call(s32[2]{0:T(128)S(1)} %copy-done.26, bf16[512,1024]{1,0:T(8,128)(2,1)S(1)} %get-tuple-element.61.gate_grad.refs_3_, bf16[512,1024]{1,0:T(8,128)(2,1)S(1)} %get-tuple-element.62.up_grad.refs_5_, f32[512,128]{1,0:T(8,128)S(1)} %get-tuple-element.63.low.refs_7_, ...), custom_call_target="tpu_custom_call", output_to_operand_aliasing={{}: (12, {})} | custom-call | flops 8053063680 | tf_op jit(solution)/shard_map/last_token_grad/pallas_call | solution.py:478
  (84 shorter events, 3.8 us)
Async XLA Ops:
  0.6 1.0 copy-start.13
  1.7 1.0 copy-start.14
  2.7 1.0 copy-start.15
  5.0 40.5 %copy-start.10 = (bf16[3,128,1024]{2,1,0:T(8,128)(2,1)}, bf16[3,128,1024]{2,1,0:T(8,128)(2,1)S(1)}, u32[]{:S(2)}) copy-start(bf16[3,128,1024]{2,1,0:T(8,128)(2,1)S(1)} %get-tuple-element.42.refs_8_) | copy-start | bytes 2359300
  5.0 21.4 %collective-permute-start = (bf16[3,128,1024]{2,1,0:T(8,128)(2,1)S(1)}, bf16[3,128,1024]{2,1,0:T(8,128)(2,1)S(1)}, u32[]{:S(2)}, u32[]{:S(2)}) collective-permute-start(bf16[3,128,1024]{2,1,0:T(8,128)(2,1)S(1)} %get-tuple-element.42.refs_8_), channel_id=1, source_target_pairs={{0,4},{4,0},{8,12},{12,8},{1,5},{5,1},{9,13},{13,9},{2,6},{6,2},{1... | collective-permute-start | bytes 2359304 | tf_op jit(solution)/shard_map/ppermute | solution.py:139
  8.0 20.7 %collective-permute-start.1 = (bf16[3,128,1024]{2,1,0:T(8,128)(2,1)}, bf16[3,128,1024]{2,1,0:T(8,128)(2,1)S(1)}, u32[]{:S(2)}, u32[]{:S(2)}) collective-permute-start(bf16[3,128,1024]{2,1,0:T(8,128)(2,1)} %get-tuple-element.43.refs_9_), channel_id=1, source_target_pairs={{0,8},{4,12},{8,0},{12,4},{1,9},{5,13},{9,1},{13,5},{2,10},{6,14},... | collective-permute-start | bytes 2359304 | tf_op jit(solution)/shard_map/ppermute | solution.py:139
  9.5 32.9 %collective-permute-start.2 = (bf16[3,128,1024]{2,1,0:T(8,128)(2,1)}, bf16[3,128,1024]{2,1,0:T(8,128)(2,1)S(1)}, u32[]{:S(2)}, u32[]{:S(2)}) collective-permute-start(bf16[3,128,1024]{2,1,0:T(8,128)(2,1)} %get-tuple-element.43.refs_9_), channel_id=1, source_target_pairs={{0,4},{4,0},{8,12},{12,8},{1,5},{5,1},{9,13},{13,9},{2,6},{6,2},{1... | collective-permute-start | bytes 2359304 | tf_op jit(solution)/shard_map/ppermute | solution.py:139
  10.1 34.0 %collective-permute-start.3 = (bf16[3,128,1024]{2,1,0:T(8,128)(2,1)S(1)}, bf16[3,128,1024]{2,1,0:T(8,128)(2,1)S(1)}, u32[]{:S(2)}, u32[]{:S(2)}) collective-permute-start(bf16[3,128,1024]{2,1,0:T(8,128)(2,1)S(1)} %get-tuple-element.42.refs_8_), channel_id=1, source_target_pairs={{0,8},{4,12},{8,0},{12,4},{1,9},{5,13},{9,1},{13,5},{2,10},{6,14},... | collective-permute-start | bytes 2359304 | tf_op jit(solution)/shard_map/ppermute | solution.py:139
  26.4 19.7 %copy-start.6 = (bf16[3,128,1024]{2,1,0:T(8,128)(2,1)}, bf16[3,128,1024]{2,1,0:T(8,128)(2,1)S(1)}, u32[]{:S(2)}) copy-start(bf16[3,128,1024]{2,1,0:T(8,128)(2,1)S(1)} %collective-permute-done.refs_0_.first.refs_10_) | copy-start | bytes 2359300
  28.7 22.1 %copy-start.7 = (bf16[3,128,1024]{2,1,0:T(8,128)(2,1)}, bf16[3,128,1024]{2,1,0:T(8,128)(2,1)S(1)}, u32[]{:S(2)}) copy-start(bf16[3,128,1024]{2,1,0:T(8,128)(2,1)S(1)} %collective-permute-done.1.refs_1_.second.refs_13_) | copy-start | bytes 2359300
  28.7 2.5 %copy-start = (bf16[1024,2048]{1,0:T(8,128)(2,1)S(1)}, bf16[1024,2048]{1,0:T(8,128)(2,1)}, u32[]{:S(2)}) copy-start(bf16[1024,2048]{1,0:T(8,128)(2,1)} %refs_8_.1) | copy-start | bytes 12582916
  31.2 2.2 %copy-start.2 = (bf16[1024,2048]{1,0:T(8,128)(2,1)S(1)}, bf16[1024,2048]{1,0:T(8,128)(2,1)}, u32[]{:S(2)}) copy-start(bf16[1024,2048]{1,0:T(8,128)(2,1)} %refs_9_.1) | copy-start | bytes 12582916
  33.4 0.9 copy-start.19
  34.3 0.9 copy-start.21
  35.3 0.9 copy-start.29
  40.3 5.1 %copy-start.4 = (bf16[192,1024]{1,0:T(8,128)(2,1)}, bf16[192,1024]{1,0:T(8,128)(2,1)S(1)}, u32[]{:S(2)}) copy-start(bf16[192,1024]{1,0:T(8,128)(2,1)S(1)} %get-tuple-element.47.refs_0_.refs_10_) | copy-start | bytes 1179652
  40.4 5.1 %copy-start.16 = (bf16[1024,64]{1,0:T(8,128)(2,1)}, bf16[1024,64]{1,0:T(8,128)(2,1)S(1)}, u32[]{:S(2)}) copy-start(bf16[1024,64]{1,0:T(8,128)(2,1)S(1)} %get-tuple-element.44.refs_0_) | copy-start | bytes 393220
  40.4 5.1 %copy-start.17 = (bf16[1024,64]{1,0:T(8,128)(2,1)}, bf16[1024,64]{1,0:T(8,128)(2,1)S(1)}, u32[]{:S(2)}) copy-start(bf16[1024,64]{1,0:T(8,128)(2,1)S(1)} %get-tuple-element.45.refs_1_) | copy-start | bytes 393220
  40.4 5.1 %copy-start.18 = (bf16[1024,64]{1,0:T(8,128)(2,1)}, bf16[1024,64]{1,0:T(8,128)(2,1)S(1)}, u32[]{:S(2)}) copy-start(bf16[1024,64]{1,0:T(8,128)(2,1)S(1)} %get-tuple-element.46.refs_2_) | copy-start | bytes 393220
  41.7 10.7 %collective-permute-start.6 = (bf16[2,3,128,1024]{3,2,1,0:T(8,128)(2,1)}, bf16[2,3,128,1024]{3,2,1,0:T(8,128)(2,1)}, u32[]{:S(2)}, u32[]{:S(2)}) collective-permute-start(bf16[2,3,128,1024]{3,2,1,0:T(8,128)(2,1)} %pair.3), channel_id=1, source_target_pairs={{0,16},{16,0},{1,17},{17,1},{2,18},{18,2},{3,19},{19,3},{4,20},{20... | collective-permute-start | bytes 4718600 | tf_op jit(solution)/shard_map/ppermute | solution.py:139
  42.4 10.0 %copy-start.8 = (bf16[3,128,1024]{2,1,0:T(8,128)(2,1)}, bf16[3,128,1024]{2,1,0:T(8,128)(2,1)S(1)}, u32[]{:S(2)}) copy-start(bf16[3,128,1024]{2,1,0:T(8,128)(2,1)S(1)} %collective-permute-done.2.first.refs_11_) | copy-start | bytes 2359300
  44.1 8.4 %copy-start.9 = (bf16[3,128,1024]{2,1,0:T(8,128)(2,1)}, bf16[3,128,1024]{2,1,0:T(8,128)(2,1)S(1)}, u32[]{:S(2)}) copy-start(bf16[3,128,1024]{2,1,0:T(8,128)(2,1)S(1)} %collective-permute-done.3.second.refs_12_) | copy-start | bytes 2359300
  45.5 7.0 %collective-permute-start.7 = (bf16[2,3,128,1024]{3,2,1,0:T(8,128)(2,1)}, bf16[2,3,128,1024]{3,2,1,0:T(8,128)(2,1)}, u32[]{:S(2)}, u32[]{:S(2)}) collective-permute-start(bf16[2,3,128,1024]{3,2,1,0:T(8,128)(2,1)} %pair.4), channel_id=1, source_target_pairs={{0,16},{16,0},{1,17},{17,1},{2,18},{18,2},{3,19},{19,3},{4,20},{20... | collective-permute-start | bytes 4718600 | tf_op jit(solution)/shard_map/ppermute | solution.py:139
  45.6 5.3 %collective-permute-start.4 = (bf16[3,128,1024]{2,1,0:T(8,128)(2,1)S(1)}, bf16[3,128,1024]{2,1,0:T(8,128)(2,1)S(1)}, u32[]{:S(2)}, u32[]{:S(2)}) collective-permute-start(bf16[3,128,1024]{2,1,0:T(8,128)(2,1)S(1)} %get-tuple-element.42.refs_8_), channel_id=1, source_target_pairs={{0,16},{16,0},{1,17},{17,1},{2,18},{18,2},{3,19},{19,3},{4,20},{20... | collective-permute-start | bytes 2359304 | tf_op jit(solution)/shard_map/ppermute | solution.py:139
  46.0 6.4 %collective-permute-start.5 = (bf16[3,128,1024]{2,1,0:T(8,128)(2,1)}, bf16[3,128,1024]{2,1,0:T(8,128)(2,1)}, u32[]{:S(2)}, u32[]{:S(2)}) collective-permute-start(bf16[3,128,1024]{2,1,0:T(8,128)(2,1)} %get-tuple-element.43.refs_9_), channel_id=1, source_target_pairs={{0,16},{16,0},{1,17},{17,1},{2,18},{18,2},{3,19},{19,3},{4,20},{20... | collective-permute-start | bytes 2359304 | tf_op jit(solution)/shard_map/ppermute | solution.py:139
  46.1 24.5 %collective-permute-start.8 = (bf16[3,128,1024]{2,1,0:T(8,128)(2,1)S(1)}, bf16[3,128,1024]{2,1,0:T(8,128)(2,1)}, u32[]{:S(2)}, u32[]{:S(2)}) collective-permute-start(bf16[3,128,1024]{2,1,0:T(8,128)(2,1)S(1)} %collective-permute-done.refs_0_.first.refs_10_), channel_id=1, source_target_pairs={{0,8},{4,12},{8,0},{12,4},{1,9},{5,13},{9,1},{13,5},{2,10},{6,14},... | collective-permute-start | bytes 2359304 | tf_op jit(solution)/shard_map/ppermute | solution.py:139
  50.8 0.9 copy-start.30
  50.8 19.9 %collective-permute-start.9 = (bf16[3,128,1024]{2,1,0:T(8,128)(2,1)S(1)}, bf16[3,128,1024]{2,1,0:T(8,128)(2,1)}, u32[]{:S(2)}, u32[]{:S(2)}) collective-permute-start(bf16[3,128,1024]{2,1,0:T(8,128)(2,1)S(1)} %collective-permute-done.1.refs_1_.second.refs_13_), channel_id=1, source_target_pairs={{0,4},{4,0},{8,12},{12,8},{1,5},{5,1},{9,13},{13,9},{2,6},{6,2},{1... | collective-permute-start | bytes 2359304 | tf_op jit(solution)/shard_map/ppermute | solution.py:139
  70.6 5.4 %copy-start.27 = (bf16[1024,512]{1,0:T(8,128)(2,1)}, bf16[1024,512]{1,0:T(8,128)(2,1)S(1)}, u32[]{:S(2)}) copy-start(bf16[1024,512]{1,0:T(8,128)(2,1)S(1)} %get-tuple-element.49.back) | copy-start | bytes 3145732
  70.8 2.2 %copy-start.20 = (bf16[2048,64]{0,1:T(8,128)(2,1)S(1)}, bf16[2048,64]{0,1:T(8,128)(2,1)}, u32[]{:S(2)}) copy-start(bf16[2048,64]{0,1:T(8,128)(2,1)} %param.16) | copy-start | bytes 786436
  70.8 2.2 %copy-start.22 = (bf16[2048,64]{0,1:T(8,128)(2,1)S(1)}, bf16[2048,64]{0,1:T(8,128)(2,1)}, u32[]{:S(2)}) copy-start(bf16[2048,64]{0,1:T(8,128)(2,1)} %param.17) | copy-start | bytes 786436
  70.8 5.3 %copy-start.23 = (bf16[64,1024]{1,0:T(8,128)(2,1)S(1)}, bf16[64,1024]{1,0:T(8,128)(2,1)}, u32[]{:S(2)}) copy-start(bf16[64,1024]{1,0:T(8,128)(2,1)} %gate_out.3) | copy-start | bytes 393220
  70.8 5.3 %copy-start.24 = (bf16[64,1024]{1,0:T(8,128)(2,1)S(1)}, bf16[64,1024]{1,0:T(8,128)(2,1)}, u32[]{:S(2)}) copy-start(bf16[64,1024]{1,0:T(8,128)(2,1)} %up_out.3) | copy-start | bytes 393220
  70.8 5.3 %copy-start.26 = (s32[2]{0:T(128)S(1)}, s32[2]{0:T(128)}, u32[]{:S(2)}) copy-start(s32[2]{0:T(128)} %pad_add_fusion.here) | copy-start | bytes 28
  72.5 3.5 %collective-permute-start.10 = (bf16[2,3,128,1024]{3,2,1,0:T(8,128)(2,1)S(1)}, bf16[2,3,128,1024]{3,2,1,0:T(8,128)(2,1)S(1)}, u32[]{:S(2)}, u32[]{:S(2)}) collective-permute-start(bf16[2,3,128,1024]{3,2,1,0:T(8,128)(2,1)S(1)} %pair.5), channel_id=1, source_target_pairs={{0,16},{16,0},{1,17},{17,1},{2,18},{18,2},{3,19},{19,3},{4,20},{20... | collective-permute-start | bytes 4718600 | tf_op jit(solution)/shard_map/ppermute | solution.py:139
  80.6 6.5 %copy-start.28 = (bf16[1024,512]{1,0:T(8,128)(2,1)S(1)}, bf16[1024,512]{1,0:T(8,128)(2,1)}, u32[]{:S(2)}) copy-start(bf16[1024,512]{1,0:T(8,128)(2,1)} %copy-done.27) | copy-start | bytes 3145732
  83.6 15.2 %collective-permute-start.12 = (bf16[512,512]{1,0:T(8,128)(2,1)S(1)}, bf16[512,512]{1,0:T(8,128)(2,1)S(1)}, u32[]{:S(2)}, u32[]{:S(2)}) collective-permute-start(bf16[512,512]{1,0:T(8,128)(2,1)S(1)} %token_grad.6.refs_3_.refs_13_), channel_id=1, source_target_pairs={{0,1},{3,2},{4,5},{7,6},{8,9},{11,10},{12,13},{15,14},{16,17},{19,... | collective-permute-start | bytes 1572872 | tf_op jit(solution)/shard_map/ppermute | solution.py:717
  91.6 7.2 %copy-start.1 = (bf16[1024,2048]{1,0:T(8,128)(2,1)S(1)}, bf16[1024,2048]{1,0:T(8,128)(2,1)}, u32[]{:S(2)}) copy-start(bf16[1024,2048]{1,0:T(8,128)(2,1)} %refs_8_.1) | copy-start | bytes 12582916
  91.6 7.2 %copy-start.3 = (bf16[1024,2048]{1,0:T(8,128)(2,1)S(1)}, bf16[1024,2048]{1,0:T(8,128)(2,1)}, u32[]{:S(2)}) copy-start(bf16[1024,2048]{1,0:T(8,128)(2,1)} %refs_9_.1) | copy-start | bytes 12582916
  91.6 7.2 %copy-start.5 = (bf16[192,1024]{1,0:T(8,128)(2,1)S(1)}, bf16[192,1024]{1,0:T(8,128)(2,1)}, u32[]{:S(2)}) copy-start(bf16[192,1024]{1,0:T(8,128)(2,1)} %copy-done.4) | copy-start | bytes 1179652
  91.6 7.2 %copy-start.12 = (bf16[1024,64]{0,1:T(8,128)(2,1)S(1)}, bf16[1024,64]{0,1:T(8,128)(2,1)}, u32[]{:S(2)}) copy-start(bf16[1024,64]{0,1:T(8,128)(2,1)} %param.20) | copy-start | bytes 393220
  102.9 4.5 %collective-permute-start.21 = (f32[4,192,384]{2,1,0:T(8,128)S(1)}, f32[4,192,384]{2,1,0:T(8,128)S(1)}, u32[]{:S(2)}, u32[]{:S(2)}) collective-permute-start(f32[4,192,384]{2,1,0:T(8,128)S(1)} %get-tuple-element.71), channel_id=1, source_target_pairs={{0,16},{16,0},{1,17},{17,1},{2,18},{18,2},{3,19},{19,3},{4,20},{20... | collective-permute-start | bytes 3538952 | tf_op jit(solution)/shard_map/ppermute | solution.py:139
  102.9 16.6 %collective-permute-start.11 = (bf16[512,512]{1,0:T(8,128)(2,1)S(1)}, bf16[512,512]{1,0:T(8,128)(2,1)S(1)}, u32[]{:S(2)}, u32[]{:S(2)}) collective-permute-start(bf16[512,512]{1,0:T(8,128)(2,1)S(1)} %token_grad.7.refs_4_.refs_3_.refs_14_), channel_id=1, source_target_pairs={{0,1},{3,2},{4,5},{7,6},{8,9},{11,10},{12,13},{15,14},{16,17},{19,... | collective-permute-start | bytes 1572872 | tf_op jit(solution)/shard_map/ppermute | solution.py:717
  108.0 9.2 %collective-permute-start.22 = (bf16[2,192,384]{2,1,0:T(8,128)(2,1)S(1)}, bf16[2,192,384]{2,1,0:T(8,128)(2,1)S(1)}, u32[]{:S(2)}, u32[]{:S(2)}) collective-permute-start(bf16[2,192,384]{2,1,0:T(8,128)(2,1)S(1)} %get-tuple-element.73), channel_id=1, source_target_pairs={{0,8},{4,12},{8,0},{12,4},{1,9},{5,13},{9,1},{13,5},{2,10},{6,14},... | collective-permute-start | bytes 884744 | tf_op jit(solution)/shard_map/ppermute | solution.py:139
  112.5 18.3 %collective-permute-start.15 = (bf16[512,512]{1,0:T(8,128)(2,1)S(1)}, bf16[512,512]{1,0:T(8,128)(2,1)S(1)}, u32[]{:S(2)}, u32[]{:S(2)}) collective-permute-start(bf16[512,512]{1,0:T(8,128)(2,1)S(1)} %token_grad.8.refs_4_), channel_id=1, source_target_pairs={{0,1},{1,2},{4,5},{5,6},{8,9},{9,10},{12,13},{13,14},{16,17},{17,1... | collective-permute-start | bytes 1572872 | tf_op jit(solution)/shard_map/ppermute | solution.py:717
  115.3 15.5 %collective-permute-start.16 = (bf16[512,512]{1,0:T(8,128)(2,1)S(1)}, bf16[512,512]{1,0:T(8,128)(2,1)S(1)}, u32[]{:S(2)}, u32[]{:S(2)}) collective-permute-start(bf16[512,512]{1,0:T(8,128)(2,1)S(1)} %token_grad.8.refs_4_), channel_id=1, source_target_pairs={{3,2},{2,1},{7,6},{6,5},{11,10},{10,9},{15,14},{14,13},{19,18},{18... | collective-permute-start | bytes 1572872 | tf_op jit(solution)/shard_map/ppermute | solution.py:717
  117.8 10.0 %collective-permute-start.23 = (bf16[1,192,384]{2,1,0:T(8,128)(2,1)S(1)}, bf16[1,192,384]{2,1,0:T(8,128)(2,1)S(1)}, u32[]{:S(2)}, u32[]{:S(2)}) collective-permute-start(bf16[1,192,384]{2,1,0:T(8,128)(2,1)S(1)} %get-tuple-element.75), channel_id=1, source_target_pairs={{0,4},{4,0},{8,12},{12,8},{1,5},{5,1},{9,13},{13,9},{2,6},{6,2},{1... | collective-permute-start | bytes 442376 | tf_op jit(solution)/shard_map/ppermute | solution.py:139
  122.5 19.6 %collective-permute-start.13 = (bf16[512,512]{1,0:T(8,128)(2,1)S(1)}, bf16[512,512]{1,0:T(8,128)(2,1)S(1)}, u32[]{:S(2)}, u32[]{:S(2)}) collective-permute-start(bf16[512,512]{1,0:T(8,128)(2,1)S(1)} %token_grad.9.refs_6_), channel_id=1, source_target_pairs={{0,1},{1,2},{4,5},{5,6},{8,9},{9,10},{12,13},{13,14},{16,17},{17,1... | collective-permute-start | bytes 1572872 | tf_op jit(solution)/shard_map/ppermute | solution.py:717
  126.9 15.1 %collective-permute-start.14 = (bf16[512,512]{1,0:T(8,128)(2,1)S(1)}, bf16[512,512]{1,0:T(8,128)(2,1)S(1)}, u32[]{:S(2)}, u32[]{:S(2)}) collective-permute-start(bf16[512,512]{1,0:T(8,128)(2,1)S(1)} %token_grad.9.refs_6_), channel_id=1, source_target_pairs={{3,2},{2,1},{7,6},{6,5},{11,10},{10,9},{15,14},{14,13},{19,18},{18... | collective-permute-start | bytes 1572872 | tf_op jit(solution)/shard_map/ppermute | solution.py:717
  128.5 11.1 %collective-permute-start.27 = (f32[192,128]{1,0:T(8,128)S(1)}, f32[192,128]{1,0:T(8,128)S(1)}, u32[]{:S(2)}, u32[]{:S(2)}) collective-permute-start(f32[192,128]{1,0:T(8,128)S(1)} %get-tuple-element.80), channel_id=1, source_target_pairs={{0,4},{4,0},{8,12},{12,8},{1,5},{5,1},{9,13},{13,9},{2,6},{6,2},{1... | collective-permute-start | bytes 294920 | tf_op jit(solution)/shard_map/ppermute | solution.py:139
  133.9 19.7 %collective-permute-start.19 = (bf16[512,512]{1,0:T(8,128)(2,1)S(1)}, bf16[512,512]{1,0:T(8,128)(2,1)S(1)}, u32[]{:S(2)}, u32[]{:S(2)}) collective-permute-start(bf16[512,512]{1,0:T(8,128)(2,1)S(1)} %get-tuple-element.64.refs_6_), channel_id=1, source_target_pairs={{0,1},{1,2},{2,3},{4,5},{5,6},{6,7},{8,9},{9,10},{10,11},{12,13},{... | collective-permute-start | bytes 1572872 | tf_op jit(solution)/shard_map/ppermute | solution.py:717
  138.3 16.4 %collective-permute-start.20 = (bf16[512,512]{1,0:T(8,128)(2,1)S(1)}, bf16[512,512]{1,0:T(8,128)(2,1)S(1)}, u32[]{:S(2)}, u32[]{:S(2)}) collective-permute-start(bf16[512,512]{1,0:T(8,128)(2,1)S(1)} %get-tuple-element.65.refs_7_), channel_id=1, source_target_pairs={{3,2},{2,1},{1,0},{7,6},{6,5},{5,4},{11,10},{10,9},{9,8},{15,14},{... | collective-permute-start | bytes 1572872 | tf_op jit(solution)/shard_map/ppermute | solution.py:717
  139.6 11.2 %collective-permute-start.28 = (f32[2,192,128]{2,1,0:T(8,128)S(1)}, f32[2,192,128]{2,1,0:T(8,128)S(1)}, u32[]{:S(2)}, u32[]{:S(2)}) collective-permute-start(f32[2,192,128]{2,1,0:T(8,128)S(1)} %pad_maximum_fusion.2), channel_id=1, source_target_pairs={{0,8},{4,12},{8,0},{12,4},{1,9},{5,13},{9,1},{13,5},{2,10},{6,14},... | collective-permute-start | bytes 589832 | tf_op jit(solution)/shard_map/ppermute | solution.py:139
  145.1 26.7 %collective-permute-start.17 = (bf16[512,512]{1,0:T(8,128)(2,1)S(1)}, bf16[512,512]{1,0:T(8,128)(2,1)S(1)}, u32[]{:S(2)}, u32[]{:S(2)}) collective-permute-start(bf16[512,512]{1,0:T(8,128)(2,1)S(1)} %get-tuple-element.66.refs_5_), channel_id=1, source_target_pairs={{0,1},{1,2},{2,3},{4,5},{5,6},{6,7},{8,9},{9,10},{10,11},{12,13},{... | collective-permute-start | bytes 1572872 | tf_op jit(solution)/shard_map/ppermute | solution.py:717
  149.5 22.3 %collective-permute-start.18 = (bf16[512,512]{1,0:T(8,128)(2,1)S(1)}, bf16[512,512]{1,0:T(8,128)(2,1)S(1)}, u32[]{:S(2)}, u32[]{:S(2)}) collective-permute-start(bf16[512,512]{1,0:T(8,128)(2,1)S(1)} %get-tuple-element.67.refs_6_), channel_id=1, source_target_pairs={{3,2},{2,1},{1,0},{7,6},{6,5},{5,4},{11,10},{10,9},{9,8},{15,14},{... | collective-permute-start | bytes 1572872 | tf_op jit(solution)/shard_map/ppermute | solution.py:717
  150.9 14.5 %collective-permute-start.24 = (bf16[64,192]{1,0:T(8,128)(2,1)S(1)}, bf16[64,192]{1,0:T(8,128)(2,1)S(1)}, u32[]{:S(2)}, u32[]{:S(2)}) collective-permute-start(bf16[64,192]{1,0:T(8,128)(2,1)S(1)} %get-tuple-element.77), channel_id=1, source_target_pairs={{0,1},{1,0},{2,3},{3,2},{4,5},{5,4},{6,7},{7,6},{8,9},{9,8},{10,11... | collective-permute-start | bytes 73736 | tf_op jit(solution)/shard_map/ppermute | solution.py:139
  153.6 15.4 %collective-permute-start.25 = (bf16[64,192]{1,0:T(8,128)(2,1)S(1)}, bf16[64,192]{1,0:T(8,128)(2,1)S(1)}, u32[]{:S(2)}, u32[]{:S(2)}) collective-permute-start(bf16[64,192]{1,0:T(8,128)(2,1)S(1)} %get-tuple-element.78), channel_id=1, source_target_pairs={{0,2},{1,3},{2,0},{3,1},{4,6},{5,7},{6,4},{7,5},{8,10},{9,11},{10,... | collective-permute-start | bytes 73736 | tf_op jit(solution)/shard_map/ppermute | solution.py:139
  154.7 14.4 %collective-permute-start.26 = (bf16[64,192]{1,0:T(8,128)(2,1)S(1)}, bf16[64,192]{1,0:T(8,128)(2,1)S(1)}, u32[]{:S(2)}, u32[]{:S(2)}) collective-permute-start(bf16[64,192]{1,0:T(8,128)(2,1)S(1)} %get-tuple-element.79), channel_id=1, source_target_pairs={{0,3},{1,2},{2,1},{3,0},{4,7},{5,6},{6,5},{7,4},{8,11},{9,10},{10,... | collective-permute-start | bytes 73736 | tf_op jit(solution)/shard_map/ppermute | solution.py:139
  165.3 5.0 %collective-permute-start.29 = (f32[4,192,128]{2,1,0:T(8,128)S(1)}, f32[4,192,128]{2,1,0:T(8,128)S(1)}, u32[]{:S(2)}, u32[]{:S(2)}) collective-permute-start(f32[4,192,128]{2,1,0:T(8,128)S(1)} %pad_maximum_fusion.1.near), channel_id=1, source_target_pairs={{0,16},{16,0},{1,17},{17,1},{2,18},{18,2},{3,19},{19,3},{4,20},{20... | collective-permute-start | bytes 1179656 | tf_op jit(solution)/shard_map/ppermute | solution.py:139
  171.8 1.1 copy-start.11
  173.0 0.8 copy-start.25

commit v4 on v3

--- a/solution.py
+++ b/solution.py
@@ -12,7 +12,7 @@
 MEBIBYTE = 1024 * 1024
 COST = 1
 HALVES = 2
-COSTS = {"sums": 1, "pair": 1, "small": 1, "token": 30, "adapter": 20, "last": 480}
+COSTS = {"sums": 1, "pair": 1, "small": 1, "token": 20 * 10**9, "adapter": 20 * 10**9, "last": 10**11}
 LIMITS = {"low": 6, "sums": 32, "last": 14, "token": 8, "adapter": 12, "small": 4}
 TILE = 512
 STRIP = 256
@@ -252,7 +252,25 @@
         compiler_params=pltpu.CompilerParams(vmem_limit_bytes=LIMITS["low"] * MEBIBYTE),
         cost_estimate=pl.CostEstimate(flops=MEBIBYTE, bytes_accessed=0, transcendentals=0),
         name="own_units",
-    )(gate, up, down)
+    )(*[pltpu.with_memory_space_constraint(array, pltpu.HBM) for array in (gate, up, down)])
+
+
+def nothing_kernel(*refs):
+    pass
+
+
+def hold(arrays, ahead):
+    anywhere = pl.BlockSpec(memory_space=pl.ANY)
+    return pl.pallas_call(
+        nothing_kernel,
+        in_specs=[anywhere] * (len(arrays) + len(ahead)),
+        out_specs=[anywhere] * len(arrays),
+        out_shape=[jax.ShapeDtypeStruct(array.shape, array.dtype) for array in arrays],
+        input_output_aliases={number: number for number in range(len(arrays))},
+        compiler_params=pltpu.CompilerParams(vmem_limit_bytes=MEBIBYTE),
+        cost_estimate=pl.CostEstimate(flops=1, bytes_accessed=1, transcendentals=0),
+        name="hold",
+    )(*arrays, *ahead)
 
 
 def pair_kernel(first, second, *refs):
@@ -377,9 +395,8 @@
     return outs[: 3 * HALVES], outs[3 * HALVES : -2], outs[-2:]
 
 
-def last_kernel(half, here, left, back, gate_out, up_out, upper, lower, other, *refs):
-    units = [upper, lower, other.at[0], other.at[1]]
-    sums = refs[:3]
+def last_kernel(half, here, left, back, gate_out, up_out, *refs):
+    units, sums = refs[:4], refs[4:7]
     hidden_out, gate_grad_out, up_grad_out, low_out = refs[-4:]
     rows, hidden = hidden_out.shape
     part = slice(half * rows, (half + 1) * rows)
@@ -413,27 +430,27 @@
         {},
         [],
         LIMITS["last"],
-        COSTS["last"] * rows * hidden * parts[0].shape[1],
+        COSTS["last"],
         "hidden_and_grads",
     )
 
 
 def quarter_rows(here, quarter, full, tail, which, columns):
-    upper, lower, other = tail
-    rows = 2 * upper.shape[1]
+    rows = 2 * tail[0].shape[1]
     blocks = []
     for number in range(columns // rows):
         block = quarter * (columns // rows) + number
         mask = lax.bitwise_xor(here[0], block)
         held = full[pl.ds(pl.multiple_of(block * rows, rows), rows), :]
-        near = jnp.concatenate([upper[which], lower[which]])
-        far = jnp.concatenate([other[0, which], other[1, which]])
+        near, far = (
+            jnp.concatenate([unit[which] for unit in units]) for units in (tail[:2], tail[2:])
+        )
         blocks.append(jnp.where(mask == 7, far, jnp.where(mask == 3, near, held)))
     return jnp.concatenate(blocks)
 
 
 def token_grad_kernel(mode, step, here, gate_grad, up_grad, low, factor, gate, up, *refs):
-    tail, refs = refs[:3], refs[3:]
+    tail, refs = refs[:4], refs[4:]
     came = refs[: {"first": 0, "sum": 1, "both": 3, "last": 2}[mode]]
     outs = refs[-2:] if mode == "both" else refs[-1:]
     columns = outs[0].shape[1]
@@ -466,7 +483,7 @@
         {},
         [],
         LIMITS["token"],
-        COSTS["token"] * rows * columns * hidden,
+        COSTS["token"],
         "token_grad",
     )
     return outs if mode == "both" else outs[0]
@@ -486,7 +503,7 @@
         input_output_aliases={1 + len(arrays): 0} if before else {},
         compiler_params=pltpu.CompilerParams(vmem_limit_bytes=LIMITS["token"] * MEBIBYTE),
         cost_estimate=pl.CostEstimate(
-            flops=COSTS["token"] * COST * rows * columns * hidden,
+            flops=COSTS["token"],
             bytes_accessed=0,
             transcendentals=0,
         ),
@@ -550,7 +567,7 @@
         {},
         [pltpu.VMEM((3 * rank, width), jnp.float32), pltpu.VMEM((3 * rank, hidden), jnp.float32)],
         LIMITS["adapter"],
-        COSTS["adapter"] * rank * rows * (width + hidden),
+        COSTS["adapter"],
         "adapter_grads",
     )
 
@@ -695,7 +712,7 @@
     for half in range(2):
         units[4, half] = flip(units[0, half], "cuts", 1)
     *lows, turned = low_rank_values(
-        tokens, cotangent, [gate_in, up_in, leave], [units[1, 0], units[2, 1]]
+        tokens, cotangent, [gate_in, up_in, leave], [here, *[units[key] for key in ((1, 0), (2, 1), (4, 0), (4, 1))]]
     )
     pairs = {}
     for number, (one, two, ahead) in enumerate(
@@ -710,8 +727,8 @@
     sums, parts, full = width_sums(
         here, tokens, cotangent, lows, [gate_out, up_out, down_in], masks, order, arrays, (3, 7)
     )
-    tail = [units[3, 0], units[3, 1]]
-    tail.append(flip(pair(*tail, [sums[0]]), "cuts", 1))
+    tail = list(hold([units[3, 0], units[3, 1]], [sums[0]]))
+    tail += [flip(unit, "cuts", 1) for unit in tail]
 
     factor = jnp.concatenate([gate_in, up_in])
     shift = lambda array, pairs: lax.ppermute(array, "tp", pairs)
@@ -739,20 +756,6 @@
     second = partial
     from_left = [shift(part, [(0, 1), (1, 2)]) for part in partial]
     from_right = [shift(part, [(3, 2), (2, 1)]) for part in partial]
-    partial = []
-    for half in both:
-        partial.append(
-            share(
-                2,
-                half,
-                "both",
-                [first[half], from_left[half], from_right[half]],
-                partial[0] if partial else second[1:],
-            )
-        )
-    from_left = [shift(part[0], [(0, 1), (1, 2), (2, 3)]) for part in partial]
-    from_right = [shift(part[1], [(3, 2), (2, 1), (1, 0)]) for part in partial]
-
     keep, send = adapter_grads(
         gradient_scaling,
         here,
@@ -777,6 +780,20 @@
     narrow_turned = whole(here, near, flip(near, "cuts", 1))
     narrow_grads = narrow_turned.T
 
+    partial = []
+    for half in both:
+        partial.append(
+            share(
+                2,
+                half,
+                "both",
+                [first[half], from_left[half], from_right[half]],
+                partial[0][:1] if partial else second[1:],
+            )
+        )
+    from_left = [shift(part[0], [(0, 1), (1, 2), (2, 3)]) for part in partial]
+    from_right = [shift(part[1], [(3, 2), (2, 1), (1, 0)]) for part in partial]
+
     results = []
     for half in both:
         results.append(
@@ -787,7 +804,7 @@
                 [*states[half][1:], factor, *full, *tail],
                 width // quarters,
                 [from_left[half], from_right[half]],
-                [wide_grads, narrow_turned] if half else partial[1],
+                [] if half else partial[1],
                 results[:],
             )
         )

time: 179 us -> 157 us (0.88)
  Pallas kernels: 71 us -> 58.8 us
  waiting for transfers between devices: 42.8 us -> 33.4 us
  starting transfers between devices: 48.7 us -> 53.9 us
  local copies, waits for them, and re-layouts: 13.3 us -> 9.21 us
    pallas_call x17 -> x16, Pallas kernels: 40.1 us -> 28.7 us  [vmem_call(): pl.pallas_call(kernel, in_specs=[pl.BlockSpec(memory_space=pltpu.SMEM)] *...]
    ppermute x20 -> x21, waiting for transfers between devices: 35.7 us -> 25.6 us  [flip(): return lax.ppermute(array, axis, [(i, i ^ bit) for i in range(size)])]
    unnamed x62 -> x52, local copies, waits for them, and re-layouts: 13.3 us -> 9.21 us
    ppermute x20 -> x21, starting transfers between devices: 20.4 us -> 23.2 us  [flip(): return lax.ppermute(array, axis, [(i, i ^ bit) for i in range(size)])]
    ppermute x10, starting transfers between devices: 28.2 us -> 30.7 us  [square_plane(): shift = lambda array, pairs: lax.ppermute(array, 'tp', pairs)]
    pallas_call x2, Pallas kernels: 7.43 us -> 5.63 us  [last_token_grad(): pl.pallas_call(functools.partial(token_grad_kernel, 'last', step), grid=(...]
  transfers between devices with their start and end apart: 30 -> 31, of which waited for: 14 -> 11; matrix products, arithmetic and copies ran while one was open for 0% -> 0% of each run, Pallas kernels for 30% -> 31%
where the time goes in v4:
time: 157 us
  Pallas kernels  58.8 us (37%)
  starting transfers between devices  53.9 us (34%)
  waiting for transfers between devices  33.4 us (21%)
  local copies, waits for them, and re-layouts  9.21 us (6%)
    ppermute x10, starting transfers between devices, square_plane(): shift = lambda array, pairs: lax.ppermute(array, 'tp', pairs)  30.7 us
    pallas_call x16, Pallas kernels, vmem_call(): pl.pallas_call(kernel, in_specs=[pl.BlockSpec(memory_space=pltpu.SMEM)] *...  28.7 us
    ppermute x21, waiting for transfers between devices, flip(): return lax.ppermute(array, axis, [(i, i ^ bit) for i in range(size)])  25.6 us
    ppermute x21, starting transfers between devices, flip(): return lax.ppermute(array, axis, [(i, i ^ bit) for i in range(size)])  23.2 us
    pallas_call x1, Pallas kernels, width_sums(): pl.pallas_call(functools.partial(sums_kernel, masks, order, len(arrays),...  18.1 us
    unnamed x52, local copies, waits for them, and re-layouts  9.21 us
    ppermute x10, waiting for transfers between devices, square_plane(): shift = lambda array, pairs: lax.ppermute(array, 'tp', pairs)  7.86 us
    pallas_call x2, Pallas kernels, last_token_grad(): pl.pallas_call(functools.partial(token_grad_kernel, 'last', step), grid=(...  5.63 us
  transfers between devices with their start and end apart: 31, of which 11 were waited for; matrix products, arithmetic and copies ran while one was open for 0% of the time, Pallas kernels for 31%

profile of v4, /device:TPU:0, one launch (start us, length us, event | category | flops | bytes accessed | tf_op | source)
XLA Modules:
  0.0 156.7 jit_solution(1675399086220741687)
XLA Ops:
  0.6 2.3 %own_units.1 = (bf16[3,128,1024]{2,1,0:T(8,128)(2,1)S(1)}, bf16[3,128,1024]{2,1,0:T(8,128)(2,1)}) custom-call(bf16[256,1024]{1,0:T(8,128)(2,1)} %gate.1, bf16[256,1024]{1,0:T(8,128)(2,1)} %up.1, bf16[1024,256]{1,0:T(8,128)(2,1)} %down.1), custom_call_target="tpu_custom_call" | custom-call | flops 1048576 | tf_op jit(solution)/shard_map/own_units/pallas_call | solution.py:243
  2.9 3.0 %collective-permute-start = (bf16[3,128,1024]{2,1,0:T(8,128)(2,1)S(1)}, bf16[3,128,1024]{2,1,0:T(8,128)(2,1)S(1)}, u32[]{:S(2)}, u32[]{:S(2)}) collective-permute-start(bf16[3,128,1024]{2,1,0:T(8,128)(2,1)S(1)} %get-tuple-element.44.refs_8_), channel_id=1, source_target_pairs={{0,4},{4,0},{8,12},{12,8},{1,5},{5,1},{9,13},{13,9},{2,6},{6,2},{1... | collective-permute-start | bytes 2359304 | tf_op jit(solution)/shard_map/ppermute | solution.py:139
  5.9 1.5 collective-permute-start.1
  7.4 0.5 collective-permute-start.3
  8.0 0.5 collective-permute-start.4
  8.6 15.7 %collective-permute-done.refs_1_.first.refs_10_ = bf16[3,128,1024]{2,1,0:T(8,128)(2,1)S(1)} collective-permute-done((bf16[3,128,1024]{2,1,0:T(8,128)(2,1)S(1)}, bf16[3,128,1024]{2,1,0:T(8,128)(2,1)S(1)}, u32[]{:S(2)}, u32[]{:S(2)}) %collective-permute-start) | collective-permute-done | bytes 786464 | tf_op jit(solution)/shard_map/ppermute | solution.py:139
  24.3 2.1 %collective-permute-start.5 = (bf16[3,128,1024]{2,1,0:T(8,128)(2,1)S(1)}, bf16[3,128,1024]{2,1,0:T(8,128)(2,1)S(1)}, u32[]{:S(2)}, u32[]{:S(2)}) collective-permute-start(bf16[3,128,1024]{2,1,0:T(8,128)(2,1)S(1)} %get-tuple-element.44.refs_8_), channel_id=1, source_target_pairs={{0,8},{4,12},{8,0},{12,4},{1,9},{5,13},{9,1},{13,5},{2,10},{6,14},... | collective-permute-start | bytes 2359304 | tf_op jit(solution)/shard_map/ppermute | solution.py:139
  26.4 2.5 %copy-done = bf16[1024,2048]{1,0:T(8,128)(2,1)S(1)} copy-done((bf16[1024,2048]{1,0:T(8,128)(2,1)S(1)}, bf16[1024,2048]{1,0:T(8,128)(2,1)}, u32[]{:S(2)}) %copy-start) | copy-done | bytes 4194328
  28.9 2.2 %copy-done.2 = bf16[1024,2048]{1,0:T(8,128)(2,1)S(1)} copy-done((bf16[1024,2048]{1,0:T(8,128)(2,1)S(1)}, bf16[1024,2048]{1,0:T(8,128)(2,1)}, u32[]{:S(2)}) %copy-start.2) | copy-done | bytes 4194328
  31.1 0.9 copy-done.14
  32.0 0.9 copy-done.16
  33.0 0.9 copy-done.23
  33.9 4.1 %low_rank_values.1 = (bf16[1024,64]{1,0:T(8,128)(2,1)S(1)}, bf16[1024,64]{1,0:T(8,128)(2,1)S(1)}, bf16[1024,64]{1,0:T(8,128)(2,1)S(1)}, bf16[192,1024]{1,0:T(8,128)(2,1)S(1)}) custom-call(bf16[1024,2048]{1,0:T(8,128)(2,1)S(1)} %copy-done, bf16[1024,2048]{1,0:T(8,128)(2,1)S(1)} %copy-done.2, bf16[64,2048]{1,0:T(8,128)(2,1)S(1)} %bitcast.11, ...), custom_call_target="tpu_custom_call" | custom-call | flops 64424509440 | tf_op jit(solution)/shard_map/low_rank_values/pallas_call | solution.py:201
  38.1 0.1 pair.2
  38.3 2.0 %collective-permute-done.4.first.refs_11_ = bf16[3,128,1024]{2,1,0:T(8,128)(2,1)S(1)} collective-permute-done((bf16[3,128,1024]{2,1,0:T(8,128)(2,1)}, bf16[3,128,1024]{2,1,0:T(8,128)(2,1)S(1)}, u32[]{:S(2)}, u32[]{:S(2)}) %collective-permute-start.4) | collective-permute-done | bytes 786464 | tf_op jit(solution)/shard_map/ppermute | solution.py:139
  40.3 1.9 %collective-permute-done.5.second.refs_12_ = bf16[3,128,1024]{2,1,0:T(8,128)(2,1)S(1)} collective-permute-done((bf16[3,128,1024]{2,1,0:T(8,128)(2,1)S(1)}, bf16[3,128,1024]{2,1,0:T(8,128)(2,1)S(1)}, u32[]{:S(2)}, u32[]{:S(2)}) %collective-permute-start.5) | collective-permute-done | bytes 786464 | tf_op jit(solution)/shard_map/ppermute | solution.py:139
  42.2 0.1 pair.3
  42.4 1.5 collective-permute-start.8
  43.9 1.5 collective-permute-start.9
  45.4 0.4 collective-permute-done.7.refs_17_
  45.8 1.2 copy-done.25
  47.1 18.1 %width_sums.1 = (f32[512,1024]{1,0:T(8,128)S(1)}, f32[512,1024]{1,0:T(8,128)S(1)}, f32[512,1024]{1,0:T(8,128)S(1)}, f32[512,1024]{1,0:T(8,128)S(1)}, f32[512,102...) custom-call(s32[2]{0:T(128)} %copy-done.21, ...), custom_call_target="tpu_custom_call" | custom-call | flops 1 | tf_op jit(solution)/shard_map/width_sums/pallas_call | solution.py:377
  65.3 0.1 collective-permute-start.10
  65.4 0.5 collective-permute-start.11
  65.8 0.3 copy-done.15
  66.3 1.4 collective-permute-done.10.refs_2_
  67.6 1.1 collective-permute-done.11.refs_3_
  68.8 3.8 %hidden_and_grads.2 = (bf16[512,1024]{1,0:T(8,128)(2,1)S(1)}, bf16[512,1024]{1,0:T(8,128)(2,1)S(1)}, bf16[512,1024]{1,0:T(8,128)(2,1)S(1)}, f32[512,128]{1,0:T(8,128)S(1)}) custom-call(s32[2]{0:T(128)S(1)} %copy-done.22, bf16[1024,512]{1,0:T(8,128)(2,1)S(1)} %get-tuple-element.50.left, bf16[1024,512]{1,0:T(8,128)(2,1)S(1)} %get-tuple-element.51.back, ...), custom_call_target="tpu_custom_call" | custom-call | flops 99999997952 | tf_op jit(solution)/shard_map/hidden_and_grads/pallas_call | solution.py:147
  72.5 2.0 %token_grad.6.refs_7_.refs_4_.refs_13_ = bf16[512,512]{1,0:T(8,128)(2,1)S(1)} custom-call(s32[2]{0:T(128)S(1)} %copy-done.22, bf16[512,1024]{1,0:T(8,128)(2,1)S(1)} %get-tuple-element.60.gate_grad.refs_2_, bf16[512,1024]{1,0:T(8,128)(2,1)S(1)} %get-tuple-element.61.up_grad.refs_4_, f32[512,128]{1,0:T(8,128)S(1)} %get-tuple-element.62.low.refs_6_, ...), custom_call_target="tpu_custom_call" | custom-call | flops 20000000000 | tf_op jit(solution)/shard_map/token_grad/pallas_call | solution.py:147
  74.5 3.5 %collective-permute-start.13 = (bf16[512,512]{1,0:T(8,128)(2,1)S(1)}, bf16[512,512]{1,0:T(8,128)(2,1)S(1)}, u32[]{:S(2)}, u32[]{:S(2)}) collective-permute-start(bf16[512,512]{1,0:T(8,128)(2,1)S(1)} %token_grad.6.refs_7_.refs_4_.refs_13_), channel_id=1, source_target_pairs={{0,1},{3,2},{4,5},{7,6},{8,9},{11,10},{12,13},{15,14},{16,17},{19,... | collective-permute-start | bytes 1572872 | tf_op jit(solution)/shard_map/ppermute | solution.py:734
  78.1 3.7 %hidden_and_grads.3 = (bf16[512,1024]{1,0:T(8,128)(2,1)S(1)}, bf16[512,1024]{1,0:T(8,128)(2,1)S(1)}, bf16[512,1024]{1,0:T(8,128)(2,1)S(1)}, f32[512,128]{1,0:T(8,128)S(1)}) custom-call(s32[2]{0:T(128)S(1)} %copy-done.22, bf16[1024,512]{1,0:T(8,128)(2,1)S(1)} %get-tuple-element.50.left, bf16[1024,512]{1,0:T(8,128)(2,1)S(1)} %get-tuple-element.51.back, ...), custom_call_target="tpu_custom_call" | custom-call | flops 99999997952 | tf_op jit(solution)/shard_map/hidden_and_grads/pallas_call | solution.py:147
  81.8 2.0 %token_grad.7.refs_5_.refs_4_.refs_14_ = bf16[512,512]{1,0:T(8,128)(2,1)S(1)} custom-call(s32[2]{0:T(128)S(1)} %copy-done.22, bf16[512,1024]{1,0:T(8,128)(2,1)S(1)} %get-tuple-element.65.gate_grad.refs_3_, bf16[512,1024]{1,0:T(8,128)(2,1)S(1)} %get-tuple-element.66.up_grad.refs_5_, f32[512,128]{1,0:T(8,128)S(1)} %get-tuple-element.67.low.refs_7_, ...), custom_call_target="tpu_custom_call" | custom-call | flops 20000000000 | tf_op jit(solution)/shard_map/token_grad/pallas_call | solution.py:147
  83.8 1.5 collective-permute-start.12
  85.3 5.0 %collective-permute-done.13.refs_4_.refs_12_ = bf16[512,512]{1,0:T(8,128)(2,1)S(1)} collective-permute-done((bf16[512,512]{1,0:T(8,128)(2,1)S(1)}, bf16[512,512]{1,0:T(8,128)(2,1)S(1)}, u32[]{:S(2)}, u32[]{:S(2)}) %collective-permute-start.13) | collective-permute-done | bytes 524320 | tf_op jit(solution)/shard_map/ppermute | solution.py:734
  90.3 4.1 %adapter_grads.1 = (f32[4,192,384]{2,1,0:T(8,128)S(1)}, f32[4,192,384]{2,1,0:T(8,128)S(1)}) custom-call(s32[2]{0:T(128)S(1)} %copy-done.22, bf16[512,1024]{1,0:T(8,128)(2,1)S(1)} %get-tuple-element.72.refs_0_, bf16[512,1024]{1,0:T(8,128)(2,1)S(1)} %get-tuple-element.73.refs_1_, bf16[512,1024]{1,0:T(8,128)(2,1)S(1)} %get-tuple-element.60.gate_grad.refs_2_, ...), custom_call_target="tpu_custom_call" | custom-call | flops 20000000000 | tf_op jit(solution)/shard_map/adapter_grads/pallas_call | solution.py:147
  94.5 2.0 %token_grad.8.refs_5_ = bf16[512,512]{1,0:T(8,128)(2,1)S(1)} custom-call(s32[2]{0:T(128)S(1)} %copy-done.22, bf16[512,1024]{1,0:T(8,128)(2,1)S(1)} %get-tuple-element.60.gate_grad.refs_2_, bf16[512,1024]{1,0:T(8,128)(2,1)S(1)} %get-tuple-element.61.up_grad.refs_4_, f32[512,128]{1,0:T(8,128)S(1)} %get-tuple-element.62.low.refs_6_, ...), custom_call_target="tpu_custom_call" | custom-call | flops 20000000000 | tf_op jit(solution)/shard_map/token_grad/pallas_call | solution.py:147
  96.5 4.4 %collective-permute-start.16 = (bf16[512,512]{1,0:T(8,128)(2,1)S(1)}, bf16[512,512]{1,0:T(8,128)(2,1)S(1)}, u32[]{:S(2)}, u32[]{:S(2)}) collective-permute-start(bf16[512,512]{1,0:T(8,128)(2,1)S(1)} %token_grad.8.refs_5_), channel_id=1, source_target_pairs={{0,1},{1,2},{4,5},{5,6},{8,9},{9,10},{12,13},{13,14},{16,17},{17,1... | collective-permute-start | bytes 1572872 | tf_op jit(solution)/shard_map/ppermute | solution.py:734
  100.9 0.7 collective-permute-start.17
  101.6 0.7 halve.2
  102.3 1.4 collective-permute-start.23
  103.7 2.0 %token_grad.9.refs_7_ = bf16[512,512]{1,0:T(8,128)(2,1)S(1)} custom-call(s32[2]{0:T(128)S(1)} %copy-done.22, bf16[512,1024]{1,0:T(8,128)(2,1)S(1)} %get-tuple-element.65.gate_grad.refs_3_, bf16[512,1024]{1,0:T(8,128)(2,1)S(1)} %get-tuple-element.66.up_grad.refs_5_, f32[512,128]{1,0:T(8,128)S(1)} %get-tuple-element.67.low.refs_7_, ...), custom_call_target="tpu_custom_call" | custom-call | flops 20000000000 | tf_op jit(solution)/shard_map/token_grad/pallas_call | solution.py:147
  105.6 4.1 %collective-permute-start.14 = (bf16[512,512]{1,0:T(8,128)(2,1)S(1)}, bf16[512,512]{1,0:T(8,128)(2,1)S(1)}, u32[]{:S(2)}, u32[]{:S(2)}) collective-permute-start(bf16[512,512]{1,0:T(8,128)(2,1)S(1)} %token_grad.9.refs_7_), channel_id=1, source_target_pairs={{0,1},{1,2},{4,5},{5,6},{8,9},{9,10},{12,13},{13,14},{16,17},{17,1... | collective-permute-start | bytes 1572872 | tf_op jit(solution)/shard_map/ppermute | solution.py:734
  109.8 0.7 collective-permute-start.15
  110.5 1.0 collective-permute-done.23.came
  111.5 0.6 halve.3
  112.1 1.4 collective-permute-start.24
  113.5 2.2 %token_grad.10 = (bf16[512,512]{1,0:T(8,128)(2,1)S(1)}, bf16[512,512]{1,0:T(8,128)(2,1)S(1)}) custom-call(s32[2]{0:T(128)S(1)} %copy-done.22, bf16[512,1024]{1,0:T(8,128)(2,1)S(1)} %get-tuple-element.60.gate_grad.refs_2_, bf16[512,1024]{1,0:T(8,128)(2,1)S(1)} %get-tuple-element.61.up_grad.refs_4_, f32[512,128]{1,0:T(8,128)S(1)} %get-tuple-element.62.low.refs_6_, ...), custom_call_target="tpu_custom_call" | custom-call | flops 20000000000 | tf_op jit(solution)/shard_map/token_grad/pallas_call | solution.py:147
  115.6 7.8 %collective-permute-start.20 = (bf16[512,512]{1,0:T(8,128)(2,1)S(1)}, bf16[512,512]{1,0:T(8,128)(2,1)S(1)}, u32[]{:S(2)}, u32[]{:S(2)}) collective-permute-start(bf16[512,512]{1,0:T(8,128)(2,1)S(1)} %get-tuple-element.68.refs_7_), channel_id=1, source_target_pairs={{0,1},{1,2},{2,3},{4,5},{5,6},{6,7},{8,9},{9,10},{10,11},{12,13},{... | collective-permute-start | bytes 1572872 | tf_op jit(solution)/shard_map/ppermute | solution.py:734
  123.4 1.3 collective-permute-start.21
  124.7 0.7 turn.1
  125.4 1.4 collective-permute-start.28
  126.8 2.1 %token_grad.11 = (bf16[512,512]{1,0:T(8,128)(2,1)S(1)}, bf16[512,512]{1,0:T(8,128)(2,1)S(1)}) custom-call(s32[2]{0:T(128)S(1)} %copy-done.22, bf16[512,1024]{1,0:T(8,128)(2,1)S(1)} %get-tuple-element.65.gate_grad.refs_3_, bf16[512,1024]{1,0:T(8,128)(2,1)S(1)} %get-tuple-element.66.up_grad.refs_5_, f32[512,128]{1,0:T(8,128)S(1)} %get-tuple-element.67.low.refs_7_, ...), custom_call_target="tpu_custom_call" | custom-call | flops 20000000000 | tf_op jit(solution)/shard_map/token_grad/pallas_call | solution.py:147
  129.0 5.4 %collective-permute-start.18 = (bf16[512,512]{1,0:T(8,128)(2,1)S(1)}, bf16[512,512]{1,0:T(8,128)(2,1)S(1)}, u32[]{:S(2)}, u32[]{:S(2)}) collective-permute-start(bf16[512,512]{1,0:T(8,128)(2,1)S(1)} %get-tuple-element.69.refs_6_), channel_id=1, source_target_pairs={{0,1},{1,2},{2,3},{4,5},{5,6},{6,7},{8,9},{9,10},{10,11},{12,13},{... | collective-permute-start | bytes 1572872 | tf_op jit(solution)/shard_map/ppermute | solution.py:734
  134.4 1.3 collective-permute-start.19
  135.8 1.4 collective-permute-start.29
  137.2 0.6 collective-permute-done.21.refs_5_
  137.7 2.8 %last_token_grad.2.refs_6_ = bf16[1024,512]{1,0:T(8,128)(2,1)} custom-call(s32[2]{0:T(128)S(1)} %copy-done.22, bf16[512,1024]{1,0:T(8,128)(2,1)S(1)} %get-tuple-element.60.gate_grad.refs_2_, bf16[512,1024]{1,0:T(8,128)(2,1)S(1)} %get-tuple-element.61.up_grad.refs_4_, f32[512,128]{1,0:T(8,128)S(1)} %get-tuple-element.62.low.refs_6_, ...), custom_call_target="tpu_custom_call" | custom-call | flops 20000000000 | tf_op jit(solution)/shard_map/last_token_grad/pallas_call | solution.py:495
  140.6 3.9 %collective-permute-start.25 = (bf16[64,192]{1,0:T(8,128)(2,1)S(1)}, bf16[64,192]{1,0:T(8,128)(2,1)S(1)}, u32[]{:S(2)}, u32[]{:S(2)}) collective-permute-start(bf16[64,192]{1,0:T(8,128)(2,1)S(1)} %get-tuple-element.81), channel_id=1, source_target_pairs={{0,1},{1,0},{2,3},{3,2},{4,5},{5,4},{6,7},{7,6},{8,9},{9,8},{10,11... | collective-permute-start | bytes 73736 | tf_op jit(solution)/shard_map/ppermute | solution.py:139
  144.4 2.4 %collective-permute-start.27 = (bf16[64,192]{1,0:T(8,128)(2,1)S(1)}, bf16[64,192]{1,0:T(8,128)(2,1)S(1)}, u32[]{:S(2)}, u32[]{:S(2)}) collective-permute-start(bf16[64,192]{1,0:T(8,128)(2,1)S(1)} %get-tuple-element.83), channel_id=1, source_target_pairs={{0,3},{1,2},{2,1},{3,0},{4,7},{5,6},{6,5},{7,4},{8,11},{9,10},{10,... | collective-permute-start | bytes 73736 | tf_op jit(solution)/shard_map/ppermute | solution.py:139
  146.9 2.2 %collective-permute-done.19.refs_5_ = bf16[512,512]{1,0:T(8,128)(2,1)S(1)} collective-permute-done((bf16[512,512]{1,0:T(8,128)(2,1)S(1)}, bf16[512,512]{1,0:T(8,128)(2,1)S(1)}, u32[]{:S(2)}, u32[]{:S(2)}) %collective-permute-start.19) | collective-permute-done | bytes 524320 | tf_op jit(solution)/shard_map/ppermute | solution.py:734
  149.1 2.8 %last_token_grad.3 = bf16[1024,512]{1,0:T(8,128)(2,1)} custom-call(s32[2]{0:T(128)S(1)} %copy-done.22, bf16[512,1024]{1,0:T(8,128)(2,1)S(1)} %get-tuple-element.65.gate_grad.refs_3_, bf16[512,1024]{1,0:T(8,128)(2,1)S(1)} %get-tuple-element.66.up_grad.refs_5_, f32[512,128]{1,0:T(8,128)S(1)} %get-tuple-element.67.low.refs_7_, ...), custom_call_target="tpu_custom_call", output_to_operand_aliasing={{}: (13, {})} | custom-call | flops 20000000000 | tf_op jit(solution)/shard_map/last_token_grad/pallas_call | solution.py:495
  151.9 2.0 %collective-permute-done.26.refs_1_ = bf16[64,192]{1,0:T(8,128)(2,1)S(1)} collective-permute-done((bf16[64,192]{1,0:T(8,128)(2,1)S(1)}, bf16[64,192]{1,0:T(8,128)(2,1)S(1)}, u32[]{:S(2)}, u32[]{:S(2)}) %collective-permute-start.26) | collective-permute-done | bytes 24608 | tf_op jit(solution)/shard_map/ppermute | solution.py:139
  154.0 1.2 last_sum.1
  155.2 1.5 whole.1
  (76 shorter events, 0.7 us)
Async XLA Ops:
  2.9 35.1 %copy-start.10 = (bf16[3,128,1024]{2,1,0:T(8,128)(2,1)}, bf16[3,128,1024]{2,1,0:T(8,128)(2,1)S(1)}, u32[]{:S(2)}) copy-start(bf16[3,128,1024]{2,1,0:T(8,128)(2,1)S(1)} %get-tuple-element.44.refs_8_) | copy-start | bytes 2359300
  2.9 21.4 %collective-permute-start = (bf16[3,128,1024]{2,1,0:T(8,128)(2,1)S(1)}, bf16[3,128,1024]{2,1,0:T(8,128)(2,1)S(1)}, u32[]{:S(2)}, u32[]{:S(2)}) collective-permute-start(bf16[3,128,1024]{2,1,0:T(8,128)(2,1)S(1)} %get-tuple-element.44.refs_8_), channel_id=1, source_target_pairs={{0,4},{4,0},{8,12},{12,8},{1,5},{5,1},{9,13},{13,9},{2,6},{6,2},{1... | collective-permute-start | bytes 2359304 | tf_op jit(solution)/shard_map/ppermute | solution.py:139
  5.9 20.5 %collective-permute-start.1 = (bf16[3,128,1024]{2,1,0:T(8,128)(2,1)}, bf16[3,128,1024]{2,1,0:T(8,128)(2,1)S(1)}, u32[]{:S(2)}, u32[]{:S(2)}) collective-permute-start(bf16[3,128,1024]{2,1,0:T(8,128)(2,1)} %get-tuple-element.45.refs_9_), channel_id=1, source_target_pairs={{0,8},{4,12},{8,0},{12,4},{1,9},{5,13},{9,1},{13,5},{2,10},{6,14},... | collective-permute-start | bytes 2359304 | tf_op jit(solution)/shard_map/ppermute | solution.py:139
  7.4 18.9 %collective-permute-start.2 = (bf16[3,128,1024]{2,1,0:T(8,128)(2,1)S(1)}, bf16[3,128,1024]{2,1,0:T(8,128)(2,1)}, u32[]{:S(2)}, u32[]{:S(2)}) collective-permute-start(bf16[3,128,1024]{2,1,0:T(8,128)(2,1)S(1)} %get-tuple-element.44.refs_8_), channel_id=1, source_target_pairs={{0,16},{16,0},{1,17},{17,1},{2,18},{18,2},{3,19},{19,3},{4,20},{20... | collective-permute-start | bytes 2359304 | tf_op jit(solution)/shard_map/ppermute | solution.py:139
  7.4 18.9 %collective-permute-start.3 = (bf16[3,128,1024]{2,1,0:T(8,128)(2,1)}, bf16[3,128,1024]{2,1,0:T(8,128)(2,1)}, u32[]{:S(2)}, u32[]{:S(2)}) collective-permute-start(bf16[3,128,1024]{2,1,0:T(8,128)(2,1)} %get-tuple-element.45.refs_9_), channel_id=1, source_target_pairs={{0,16},{16,0},{1,17},{17,1},{2,18},{18,2},{3,19},{19,3},{4,20},{20... | collective-permute-start | bytes 2359304 | tf_op jit(solution)/shard_map/ppermute | solution.py:139
  8.0 32.4 %collective-permute-start.4 = (bf16[3,128,1024]{2,1,0:T(8,128)(2,1)}, bf16[3,128,1024]{2,1,0:T(8,128)(2,1)S(1)}, u32[]{:S(2)}, u32[]{:S(2)}) collective-permute-start(bf16[3,128,1024]{2,1,0:T(8,128)(2,1)} %get-tuple-element.45.refs_9_), channel_id=1, source_target_pairs={{0,4},{4,0},{8,12},{12,8},{1,5},{5,1},{9,13},{13,9},{2,6},{6,2},{1... | collective-permute-start | bytes 2359304 | tf_op jit(solution)/shard_map/ppermute | solution.py:139
  8.6 29.5 %copy-start.21 = (s32[2]{0:T(128)}, s32[2]{0:T(128)S(1)}, u32[]{:S(2)}) copy-start(s32[2]{0:T(128)S(1)} %pad_add_fusion.refs_0_.here) | copy-start | bytes 28
  24.3 18.1 %copy-start.4 = (bf16[3,128,1024]{2,1,0:T(8,128)(2,1)}, bf16[3,128,1024]{2,1,0:T(8,128)(2,1)S(1)}, u32[]{:S(2)}) copy-start(bf16[3,128,1024]{2,1,0:T(8,128)(2,1)S(1)} %collective-permute-done.refs_1_.first.refs_10_) | copy-start | bytes 2359300
  24.3 17.9 %collective-permute-start.5 = (bf16[3,128,1024]{2,1,0:T(8,128)(2,1)S(1)}, bf16[3,128,1024]{2,1,0:T(8,128)(2,1)S(1)}, u32[]{:S(2)}, u32[]{:S(2)}) collective-permute-start(bf16[3,128,1024]{2,1,0:T(8,128)(2,1)S(1)} %get-tuple-element.44.refs_8_), channel_id=1, source_target_pairs={{0,8},{4,12},{8,0},{12,4},{1,9},{5,13},{9,1},{13,5},{2,10},{6,14},... | collective-permute-start | bytes 2359304 | tf_op jit(solution)/shard_map/ppermute | solution.py:139
  26.4 17.6 %copy-start.5 = (bf16[3,128,1024]{2,1,0:T(8,128)(2,1)}, bf16[3,128,1024]{2,1,0:T(8,128)(2,1)S(1)}, u32[]{:S(2)}) copy-start(bf16[3,128,1024]{2,1,0:T(8,128)(2,1)S(1)} %collective-permute-done.1.refs_2_.second.refs_13_) | copy-start | bytes 2359300
  26.4 2.5 %copy-start = (bf16[1024,2048]{1,0:T(8,128)(2,1)S(1)}, bf16[1024,2048]{1,0:T(8,128)(2,1)}, u32[]{:S(2)}) copy-start(bf16[1024,2048]{1,0:T(8,128)(2,1)} %refs_8_.1) | copy-start | bytes 12582916
  28.9 2.2 %copy-start.2 = (bf16[1024,2048]{1,0:T(8,128)(2,1)S(1)}, bf16[1024,2048]{1,0:T(8,128)(2,1)}, u32[]{:S(2)}) copy-start(bf16[1024,2048]{1,0:T(8,128)(2,1)} %refs_9_.1) | copy-start | bytes 12582916
  31.1 0.9 copy-start.14
  32.0 0.9 copy-start.16
  33.0 0.9 copy-start.23
  38.1 4.2 %copy-start.8 = (bf16[192,1024]{1,0:T(8,128)(2,1)}, bf16[192,1024]{1,0:T(8,128)(2,1)S(1)}, u32[]{:S(2)}) copy-start(bf16[192,1024]{1,0:T(8,128)(2,1)S(1)} %get-tuple-element.49.refs_0_.refs_10_) | copy-start | bytes 1179652
  38.1 4.2 %copy-start.11 = (bf16[1024,64]{1,0:T(8,128)(2,1)}, bf16[1024,64]{1,0:T(8,128)(2,1)S(1)}, u32[]{:S(2)}) copy-start(bf16[1024,64]{1,0:T(8,128)(2,1)S(1)} %get-tuple-element.46.refs_0_) | copy-start | bytes 393220
  38.1 4.2 %copy-start.12 = (bf16[1024,64]{1,0:T(8,128)(2,1)}, bf16[1024,64]{1,0:T(8,128)(2,1)S(1)}, u32[]{:S(2)}) copy-start(bf16[1024,64]{1,0:T(8,128)(2,1)S(1)} %get-tuple-element.47.refs_1_) | copy-start | bytes 393220
  38.1 4.2 %copy-start.13 = (bf16[1024,64]{1,0:T(8,128)(2,1)}, bf16[1024,64]{1,0:T(8,128)(2,1)S(1)}, u32[]{:S(2)}) copy-start(bf16[1024,64]{1,0:T(8,128)(2,1)S(1)} %get-tuple-element.48.refs_2_) | copy-start | bytes 393220
  38.2 7.2 %collective-permute-start.6 = (bf16[2,3,128,1024]{3,2,1,0:T(8,128)(2,1)S(1)}, bf16[2,3,128,1024]{3,2,1,0:T(8,128)(2,1)S(1)}, u32[]{:S(2)}, u32[]{:S(2)}) collective-permute-start(bf16[2,3,128,1024]{3,2,1,0:T(8,128)(2,1)S(1)} %pair.2), channel_id=1, source_target_pairs={{0,16},{16,0},{1,17},{17,1},{2,18},{18,2},{3,19},{19,3},{4,20},{20... | collective-permute-start | bytes 4718600 | tf_op jit(solution)/shard_map/ppermute | solution.py:139
  40.3 6.8 %copy-start.6 = (bf16[3,128,1024]{2,1,0:T(8,128)(2,1)}, bf16[3,128,1024]{2,1,0:T(8,128)(2,1)S(1)}, u32[]{:S(2)}) copy-start(bf16[3,128,1024]{2,1,0:T(8,128)(2,1)S(1)} %collective-permute-done.4.first.refs_11_) | copy-start | bytes 2359300
  42.2 4.9 %copy-start.7 = (bf16[3,128,1024]{2,1,0:T(8,128)(2,1)}, bf16[3,128,1024]{2,1,0:T(8,128)(2,1)S(1)}, u32[]{:S(2)}) copy-start(bf16[3,128,1024]{2,1,0:T(8,128)(2,1)S(1)} %collective-permute-done.5.second.refs_12_) | copy-start | bytes 2359300
  42.3 3.5 %collective-permute-start.7 = (bf16[2,3,128,1024]{3,2,1,0:T(8,128)(2,1)S(1)}, bf16[2,3,128,1024]{3,2,1,0:T(8,128)(2,1)S(1)}, u32[]{:S(2)}, u32[]{:S(2)}) collective-permute-start(bf16[2,3,128,1024]{3,2,1,0:T(8,128)(2,1)S(1)} %pair.3), channel_id=1, source_target_pairs={{0,16},{16,0},{1,17},{17,1},{2,18},{18,2},{3,19},{19,3},{4,20},{20... | collective-permute-start | bytes 4718600 | tf_op jit(solution)/shard_map/ppermute | solution.py:139
  42.4 22.8 %collective-permute-start.8 = (bf16[3,128,1024]{2,1,0:T(8,128)(2,1)S(1)}, bf16[3,128,1024]{2,1,0:T(8,128)(2,1)S(1)}, u32[]{:S(2)}, u32[]{:S(2)}) collective-permute-start(bf16[3,128,1024]{2,1,0:T(8,128)(2,1)S(1)} %collective-permute-done.refs_1_.first.refs_10_), channel_id=1, source_target_pairs={{0,8},{4,12},{8,0},{12,4},{1,9},{5,13},{9,1},{13,5},{2,10},{6,14},... | collective-permute-start | bytes 2359304 | tf_op jit(solution)/shard_map/ppermute | solution.py:139
  43.9 21.3 %collective-permute-start.9 = (bf16[3,128,1024]{2,1,0:T(8,128)(2,1)S(1)}, bf16[3,128,1024]{2,1,0:T(8,128)(2,1)S(1)}, u32[]{:S(2)}, u32[]{:S(2)}) collective-permute-start(bf16[3,128,1024]{2,1,0:T(8,128)(2,1)S(1)} %collective-permute-done.1.refs_2_.second.refs_13_), channel_id=1, source_target_pairs={{0,4},{4,0},{8,12},{12,8},{1,5},{5,1},{9,13},{13,9},{2,6},{6,2},{1... | collective-permute-start | bytes 2359304 | tf_op jit(solution)/shard_map/ppermute | solution.py:139
  45.4 1.6 %copy-start.24 = (bf16[2,3,128,1024]{3,2,1,0:T(8,128)(2,1)}, bf16[2,3,128,1024]{3,2,1,0:T(8,128)(2,1)S(1)}, u32[]{:S(2)}) copy-start(bf16[2,3,128,1024]{3,2,1,0:T(8,128)(2,1)S(1)} %collective-permute-done.6.refs_16_) | copy-start | bytes 4718596
  45.8 1.2 copy-start.25
  65.2 1.0 copy-start.15
  65.2 1.0 copy-start.17
  65.2 3.5 %copy-start.18 = (bf16[64,1024]{1,0:T(8,128)(2,1)S(1)}, bf16[64,1024]{1,0:T(8,128)(2,1)}, u32[]{:S(2)}) copy-start(bf16[64,1024]{1,0:T(8,128)(2,1)} %gate_out.3) | copy-start | bytes 393220
  65.2 3.5 %copy-start.19 = (bf16[64,1024]{1,0:T(8,128)(2,1)S(1)}, bf16[64,1024]{1,0:T(8,128)(2,1)}, u32[]{:S(2)}) copy-start(bf16[64,1024]{1,0:T(8,128)(2,1)} %up_out.3) | copy-start | bytes 393220
  65.3 3.5 %copy-start.22 = (s32[2]{0:T(128)S(1)}, s32[2]{0:T(128)}, u32[]{:S(2)}) copy-start(s32[2]{0:T(128)} %copy-done.21) | copy-start | bytes 28
  65.3 2.4 %collective-permute-start.10 = (bf16[3,128,1024]{2,1,0:T(8,128)(2,1)S(1)}, bf16[3,128,1024]{2,1,0:T(8,128)(2,1)S(1)}, u32[]{:S(2)}, u32[]{:S(2)}) collective-permute-start(bf16[3,128,1024]{2,1,0:T(8,128)(2,1)S(1)} %get-tuple-element.53.refs_0_), channel_id=1, source_target_pairs={{0,16},{16,0},{1,17},{17,1},{2,18},{18,2},{3,19},{19,3},{4,20},{20... | collective-permute-start | bytes 2359304 | tf_op jit(solution)/shard_map/ppermute | solution.py:139
  65.4 3.4 %collective-permute-start.11 = (bf16[3,128,1024]{2,1,0:T(8,128)(2,1)S(1)}, bf16[3,128,1024]{2,1,0:T(8,128)(2,1)S(1)}, u32[]{:S(2)}, u32[]{:S(2)}) collective-permute-start(bf16[3,128,1024]{2,1,0:T(8,128)(2,1)S(1)} %get-tuple-element.54.refs_1_), channel_id=1, source_target_pairs={{0,16},{16,0},{1,17},{17,1},{2,18},{18,2},{3,19},{19,3},{4,20},{20... | collective-permute-start | bytes 2359304 | tf_op jit(solution)/shard_map/ppermute | solution.py:139
  74.5 15.8 %collective-permute-start.13 = (bf16[512,512]{1,0:T(8,128)(2,1)S(1)}, bf16[512,512]{1,0:T(8,128)(2,1)S(1)}, u32[]{:S(2)}, u32[]{:S(2)}) collective-permute-start(bf16[512,512]{1,0:T(8,128)(2,1)S(1)} %token_grad.6.refs_7_.refs_4_.refs_13_), channel_id=1, source_target_pairs={{0,1},{3,2},{4,5},{7,6},{8,9},{11,10},{12,13},{15,14},{16,17},{19,... | collective-permute-start | bytes 1572872 | tf_op jit(solution)/shard_map/ppermute | solution.py:734
  81.8 8.5 %copy-start.1 = (bf16[1024,2048]{1,0:T(8,128)(2,1)S(1)}, bf16[1024,2048]{1,0:T(8,128)(2,1)}, u32[]{:S(2)}) copy-start(bf16[1024,2048]{1,0:T(8,128)(2,1)} %refs_8_.1) | copy-start | bytes 12582916
  81.8 8.5 %copy-start.3 = (bf16[1024,2048]{1,0:T(8,128)(2,1)S(1)}, bf16[1024,2048]{1,0:T(8,128)(2,1)}, u32[]{:S(2)}) copy-start(bf16[1024,2048]{1,0:T(8,128)(2,1)} %refs_9_.1) | copy-start | bytes 12582916
  81.8 8.5 %copy-start.9 = (bf16[192,1024]{1,0:T(8,128)(2,1)S(1)}, bf16[192,1024]{1,0:T(8,128)(2,1)}, u32[]{:S(2)}) copy-start(bf16[192,1024]{1,0:T(8,128)(2,1)} %copy-done.8) | copy-start | bytes 1179652
  81.8 8.5 %copy-start.20 = (bf16[1024,64]{0,1:T(8,128)(2,1)S(1)}, bf16[1024,64]{0,1:T(8,128)(2,1)}, u32[]{:S(2)}) copy-start(bf16[1024,64]{0,1:T(8,128)(2,1)} %param.20) | copy-start | bytes 393220
  83.8 19.8 %collective-permute-start.12 = (bf16[512,512]{1,0:T(8,128)(2,1)S(1)}, bf16[512,512]{1,0:T(8,128)(2,1)S(1)}, u32[]{:S(2)}, u32[]{:S(2)}) collective-permute-start(bf16[512,512]{1,0:T(8,128)(2,1)S(1)} %token_grad.7.refs_5_.refs_4_.refs_14_), channel_id=1, source_target_pairs={{0,1},{3,2},{4,5},{7,6},{8,9},{11,10},{12,13},{15,14},{16,17},{19,... | collective-permute-start | bytes 1572872 | tf_op jit(solution)/shard_map/ppermute | solution.py:734
  94.4 7.2 %collective-permute-start.22 = (f32[4,192,384]{2,1,0:T(8,128)S(1)}, f32[4,192,384]{2,1,0:T(8,128)S(1)}, u32[]{:S(2)}, u32[]{:S(2)}) collective-permute-start(f32[4,192,384]{2,1,0:T(8,128)S(1)} %get-tuple-element.75), channel_id=1, source_target_pairs={{0,16},{16,0},{1,17},{17,1},{2,18},{18,2},{3,19},{19,3},{4,20},{20... | collective-permute-start | bytes 3538952 | tf_op jit(solution)/shard_map/ppermute | solution.py:139
  96.5 17.0 %collective-permute-start.16 = (bf16[512,512]{1,0:T(8,128)(2,1)S(1)}, bf16[512,512]{1,0:T(8,128)(2,1)S(1)}, u32[]{:S(2)}, u32[]{:S(2)}) collective-permute-start(bf16[512,512]{1,0:T(8,128)(2,1)S(1)} %token_grad.8.refs_5_), channel_id=1, source_target_pairs={{0,1},{1,2},{4,5},{5,6},{8,9},{9,10},{12,13},{13,14},{16,17},{17,1... | collective-permute-start | bytes 1572872 | tf_op jit(solution)/shard_map/ppermute | solution.py:734
  100.9 12.5 %collective-permute-start.17 = (bf16[512,512]{1,0:T(8,128)(2,1)S(1)}, bf16[512,512]{1,0:T(8,128)(2,1)S(1)}, u32[]{:S(2)}, u32[]{:S(2)}) collective-permute-start(bf16[512,512]{1,0:T(8,128)(2,1)S(1)} %token_grad.8.refs_5_), channel_id=1, source_target_pairs={{3,2},{2,1},{7,6},{6,5},{11,10},{10,9},{15,14},{14,13},{19,18},{18... | collective-permute-start | bytes 1572872 | tf_op jit(solution)/shard_map/ppermute | solution.py:734
  102.3 9.2 %collective-permute-start.23 = (bf16[2,192,384]{2,1,0:T(8,128)(2,1)S(1)}, bf16[2,192,384]{2,1,0:T(8,128)(2,1)S(1)}, u32[]{:S(2)}, u32[]{:S(2)}) collective-permute-start(bf16[2,192,384]{2,1,0:T(8,128)(2,1)S(1)} %get-tuple-element.77), channel_id=1, source_target_pairs={{0,8},{4,12},{8,0},{12,4},{1,9},{5,13},{9,1},{13,5},{2,10},{6,14},... | collective-permute-start | bytes 884744 | tf_op jit(solution)/shard_map/ppermute | solution.py:139
  105.6 21.2 %collective-permute-start.14 = (bf16[512,512]{1,0:T(8,128)(2,1)S(1)}, bf16[512,512]{1,0:T(8,128)(2,1)S(1)}, u32[]{:S(2)}, u32[]{:S(2)}) collective-permute-start(bf16[512,512]{1,0:T(8,128)(2,1)S(1)} %token_grad.9.refs_7_), channel_id=1, source_target_pairs={{0,1},{1,2},{4,5},{5,6},{8,9},{9,10},{12,13},{13,14},{16,17},{17,1... | collective-permute-start | bytes 1572872 | tf_op jit(solution)/shard_map/ppermute | solution.py:734
  109.8 17.1 %collective-permute-start.15 = (bf16[512,512]{1,0:T(8,128)(2,1)S(1)}, bf16[512,512]{1,0:T(8,128)(2,1)S(1)}, u32[]{:S(2)}, u32[]{:S(2)}) collective-permute-start(bf16[512,512]{1,0:T(8,128)(2,1)S(1)} %token_grad.9.refs_7_), channel_id=1, source_target_pairs={{3,2},{2,1},{7,6},{6,5},{11,10},{10,9},{15,14},{14,13},{19,18},{18... | collective-permute-start | bytes 1572872 | tf_op jit(solution)/shard_map/ppermute | solution.py:734
  112.1 12.7 %collective-permute-start.24 = (bf16[1,192,384]{2,1,0:T(8,128)(2,1)S(1)}, bf16[1,192,384]{2,1,0:T(8,128)(2,1)S(1)}, u32[]{:S(2)}, u32[]{:S(2)}) collective-permute-start(bf16[1,192,384]{2,1,0:T(8,128)(2,1)S(1)} %get-tuple-element.79), channel_id=1, source_target_pairs={{0,4},{4,0},{8,12},{12,8},{1,5},{5,1},{9,13},{13,9},{2,6},{6,2},{1... | collective-permute-start | bytes 442376 | tf_op jit(solution)/shard_map/ppermute | solution.py:139
  115.6 21.5 %collective-permute-start.20 = (bf16[512,512]{1,0:T(8,128)(2,1)S(1)}, bf16[512,512]{1,0:T(8,128)(2,1)S(1)}, u32[]{:S(2)}, u32[]{:S(2)}) collective-permute-start(bf16[512,512]{1,0:T(8,128)(2,1)S(1)} %get-tuple-element.68.refs_7_), channel_id=1, source_target_pairs={{0,1},{1,2},{2,3},{4,5},{5,6},{6,7},{8,9},{9,10},{10,11},{12,13},{... | collective-permute-start | bytes 1572872 | tf_op jit(solution)/shard_map/ppermute | solution.py:734
  123.4 14.3 %collective-permute-start.21 = (bf16[512,512]{1,0:T(8,128)(2,1)S(1)}, bf16[512,512]{1,0:T(8,128)(2,1)S(1)}, u32[]{:S(2)}, u32[]{:S(2)}) collective-permute-start(bf16[512,512]{1,0:T(8,128)(2,1)S(1)} %get-tuple-element.71), channel_id=1, source_target_pairs={{3,2},{2,1},{1,0},{7,6},{6,5},{5,4},{11,10},{10,9},{9,8},{15,14},{... | collective-permute-start | bytes 1572872 | tf_op jit(solution)/shard_map/ppermute | solution.py:734
  125.4 10.3 %collective-permute-start.28 = (f32[192,128]{1,0:T(8,128)S(1)}, f32[192,128]{1,0:T(8,128)S(1)}, u32[]{:S(2)}, u32[]{:S(2)}) collective-permute-start(f32[192,128]{1,0:T(8,128)S(1)} %get-tuple-element.84), channel_id=1, source_target_pairs={{0,4},{4,0},{8,12},{12,8},{1,5},{5,1},{9,13},{13,9},{2,6},{6,2},{1... | collective-permute-start | bytes 294920 | tf_op jit(solution)/shard_map/ppermute | solution.py:139
  129.0 17.8 %collective-permute-start.18 = (bf16[512,512]{1,0:T(8,128)(2,1)S(1)}, bf16[512,512]{1,0:T(8,128)(2,1)S(1)}, u32[]{:S(2)}, u32[]{:S(2)}) collective-permute-start(bf16[512,512]{1,0:T(8,128)(2,1)S(1)} %get-tuple-element.69.refs_6_), channel_id=1, source_target_pairs={{0,1},{1,2},{2,3},{4,5},{5,6},{6,7},{8,9},{9,10},{10,11},{12,13},{... | collective-permute-start | bytes 1572872 | tf_op jit(solution)/shard_map/ppermute | solution.py:734
  134.4 14.7 %collective-permute-start.19 = (bf16[512,512]{1,0:T(8,128)(2,1)S(1)}, bf16[512,512]{1,0:T(8,128)(2,1)S(1)}, u32[]{:S(2)}, u32[]{:S(2)}) collective-permute-start(bf16[512,512]{1,0:T(8,128)(2,1)S(1)} %get-tuple-element.70.refs_7_), channel_id=1, source_target_pairs={{3,2},{2,1},{1,0},{7,6},{6,5},{5,4},{11,10},{10,9},{9,8},{15,14},{... | collective-permute-start | bytes 1572872 | tf_op jit(solution)/shard_map/ppermute | solution.py:734
  135.8 8.6 %collective-permute-start.29 = (f32[2,192,128]{2,1,0:T(8,128)S(1)}, f32[2,192,128]{2,1,0:T(8,128)S(1)}, u32[]{:S(2)}, u32[]{:S(2)}) collective-permute-start(f32[2,192,128]{2,1,0:T(8,128)S(1)} %pad_maximum_fusion.2), channel_id=1, source_target_pairs={{0,8},{4,12},{8,0},{12,4},{1,9},{5,13},{9,1},{13,5},{2,10},{6,14},... | collective-permute-start | bytes 589832 | tf_op jit(solution)/shard_map/ppermute | solution.py:139
  140.6 11.4 %collective-permute-start.25 = (bf16[64,192]{1,0:T(8,128)(2,1)S(1)}, bf16[64,192]{1,0:T(8,128)(2,1)S(1)}, u32[]{:S(2)}, u32[]{:S(2)}) collective-permute-start(bf16[64,192]{1,0:T(8,128)(2,1)S(1)} %get-tuple-element.81), channel_id=1, source_target_pairs={{0,1},{1,0},{2,3},{3,2},{4,5},{5,4},{6,7},{7,6},{8,9},{9,8},{10,11... | collective-permute-start | bytes 73736 | tf_op jit(solution)/shard_map/ppermute | solution.py:139
  144.4 9.6 %collective-permute-start.26 = (bf16[64,192]{1,0:T(8,128)(2,1)S(1)}, bf16[64,192]{1,0:T(8,128)(2,1)S(1)}, u32[]{:S(2)}, u32[]{:S(2)}) collective-permute-start(bf16[64,192]{1,0:T(8,128)(2,1)S(1)} %get-tuple-element.82), channel_id=1, source_target_pairs={{0,2},{1,3},{2,0},{3,1},{4,6},{5,7},{6,4},{7,5},{8,10},{9,11},{10,... | collective-permute-start | bytes 73736 | tf_op jit(solution)/shard_map/ppermute | solution.py:139
  144.4 9.6 %collective-permute-start.27 = (bf16[64,192]{1,0:T(8,128)(2,1)S(1)}, bf16[64,192]{1,0:T(8,128)(2,1)S(1)}, u32[]{:S(2)}, u32[]{:S(2)}) collective-permute-start(bf16[64,192]{1,0:T(8,128)(2,1)S(1)} %get-tuple-element.83), channel_id=1, source_target_pairs={{0,3},{1,2},{2,1},{3,0},{4,7},{5,6},{6,5},{7,4},{8,11},{9,10},{10,... | collective-permute-start | bytes 73736 | tf_op jit(solution)/shard_map/ppermute | solution.py:139
  146.8 8.4 %collective-permute-start.30 = (f32[4,192,128]{2,1,0:T(8,128)S(1)}, f32[4,192,128]{2,1,0:T(8,128)S(1)}, u32[]{:S(2)}, u32[]{:S(2)}) collective-permute-start(f32[4,192,128]{2,1,0:T(8,128)S(1)} %pad_maximum_fusion.1.near), channel_id=1, source_target_pairs={{0,16},{16,0},{1,17},{17,1},{2,18},{18,2},{3,19},{19,3},{4,20},{20... | collective-permute-start | bytes 1179656 | tf_op jit(solution)/shard_map/ppermute | solution.py:139

commit v5 on v4

--- a/solution.py
+++ b/solution.py
@@ -216,38 +216,42 @@
 
 
 def own_kernel(gate, up, down, *refs):
-    units, (held, sems) = refs[:2], refs[2:]
+    units, both, (held, sems) = refs[:2], refs[2], refs[3:]
     rows = units[0].shape[1]
     down_copy = pltpu.make_async_copy(down, held, sems.at[0])
     down_copy.start()
     copies = []
     for half, unit in enumerate(units):
         for which, ref in enumerate((gate, up)):
-            copies.append(
-                pltpu.make_async_copy(
-                    ref.at[pl.ds(half * rows, rows)], unit.at[which], sems.at[1 + len(copies)]
+            for target in (unit.at[which], both.at[half, which]):
+                copies.append(
+                    pltpu.make_async_copy(
+                        ref.at[pl.ds(half * rows, rows)], target, sems.at[1 + len(copies)]
+                    )
                 )
-            )
     for copy in copies:
         copy.start()
     down_copy.wait()
     for half, unit in enumerate(units):
         part = slice(half * rows, (half + 1) * rows)
-        unit[2] = held[:, part].astype(jnp.float32).T.astype(jnp.bfloat16)
+        turned = held[:, part].astype(jnp.float32).T.astype(jnp.bfloat16)
+        unit[2] = turned
+        both[half, 2] = turned
     for copy in copies:
         copy.wait()
 
 
 def own_units(gate, up, down):
     rows, hidden = gate.shape
+    unit = (3, rows // 2, hidden)
     return pl.pallas_call(
         own_kernel,
         in_specs=[pl.BlockSpec(memory_space=pl.ANY)] * 3,
-        out_specs=[pl.BlockSpec(memory_space=pltpu.VMEM)] * 2,
-        out_shape=[pltpu.VMEM((3, rows // 2, hidden), jnp.bfloat16)] * 2,
+        out_specs=[pl.BlockSpec(memory_space=pltpu.VMEM)] * 3,
+        out_shape=[pltpu.VMEM(shape, jnp.bfloat16) for shape in (unit, unit, (2, *unit))],
         scratch_shapes=[
             pltpu.VMEM((hidden, rows), jnp.bfloat16),
-            pltpu.SemaphoreType.DMA((5,)),
+            pltpu.SemaphoreType.DMA((9,)),
         ],
         compiler_params=pltpu.CompilerParams(vmem_limit_bytes=LIMITS["low"] * MEBIBYTE),
         cost_estimate=pl.CostEstimate(flops=MEBIBYTE, bytes_accessed=0, transcendentals=0),
@@ -700,7 +704,7 @@
     gate_out, up_out = gate_adapter_output_factor, up_adapter_output_factor
 
     units = {}
-    units[0, 0], units[0, 1] = own_units(
+    units[0, 0], units[0, 1], own_pair = own_units(
         gate_frozen_matrix, up_frozen_matrix, down_frozen_matrix
     )
     units[1, 0] = flip(units[0, 0], "fsdp", 1)
@@ -709,19 +713,21 @@
     units[2, 0] = flip(units[0, 0], "fsdp", 2)
     units[3, 0] = flip(units[1, 0], "fsdp", 2)
     units[3, 1] = flip(units[2, 1], "fsdp", 1)
-    for half in range(2):
-        units[4, half] = flip(units[0, half], "cuts", 1)
+    own_pair = flip(own_pair, "cuts", 1)
     *lows, turned = low_rank_values(
-        tokens, cotangent, [gate_in, up_in, leave], [here, *[units[key] for key in ((1, 0), (2, 1), (4, 0), (4, 1))]]
+        tokens,
+        cotangent,
+        [gate_in, up_in, leave],
+        [here, units[1, 0], units[2, 1], own_pair],
     )
     pairs = {}
     for number, (one, two, ahead) in enumerate(
         (((1, 0), (2, 1), [turned]), ((1, 1), (2, 0), [turned]))
     ):
         pairs[number] = flip(pair(units[one], units[two], ahead), "cuts", 1)
-    keys = [(0, 0), (0, 1), (1, 0), (1, 1), (2, 0), (2, 1), (4, 0), (4, 1)]
-    placed = keys + [(5, 0), (6, 1), (5, 1), (6, 0)]
-    arrays = [units[key] for key in keys] + [pairs[0], pairs[1]]
+    placed = [(mask, half) for mask in range(3) for half in range(2)]
+    arrays = [units[key] for key in placed] + [own_pair, pairs[0], pairs[1]]
+    placed += [(4, 0), (4, 1), (5, 0), (6, 1), (5, 1), (6, 0)]
     masks = (0, 1, 2, 4, 5, 6)
     order = [placed.index((mask, half)) for mask in masks for half in range(2)]
     sums, parts, full = width_sums(
@@ -767,7 +773,7 @@
             turned,
             down_in,
         ],
-        [came[0], *first],
+        first,
     )
     keep, send = halve(here, keep, flip(send, "cuts", 1))
     keep, send = halve(here, keep, flip(send, "fsdp", 2))

time: 157 us -> 156 us (level)
  starting transfers between devices: 53.9 us -> 44.6 us
  waiting for transfers between devices: 33.4 us -> 40 us
    ppermute x21 -> x20, starting transfers between devices: 23.2 us -> 17.8 us  [flip(): return lax.ppermute(array, axis, [(i, i ^ bit) for i in range(size)])]
    ppermute x10, waiting for transfers between devices: 7.86 us -> 12.2 us  [square_plane(): shift = lambda array, pairs: lax.ppermute(array, 'tp', pairs)]
    ppermute x10, starting transfers between devices: 30.7 us -> 26.8 us  [square_plane(): shift = lambda array, pairs: lax.ppermute(array, 'tp', pairs)]
    ppermute x21 -> x20, waiting for transfers between devices: 25.6 us -> 27.8 us  [flip(): return lax.ppermute(array, axis, [(i, i ^ bit) for i in range(size)])]
    unnamed x52 -> x50, local copies, waits for them, and re-layouts: 9.21 us -> 9.15 us
  transfers between devices with their start and end apart: 31 -> 30, of which waited for: 11 -> 14; matrix products, arithmetic and copies ran while one was open for 0% -> 0% of each run, Pallas kernels for 31% -> 32%
where the time goes in v5:
time: 156 us; the launch traced here: 155 us
  Pallas kernels  59.9 us (38%)
  starting transfers between devices  44.6 us (29%)
  waiting for transfers between devices  40 us (26%)
  local copies, waits for them, and re-layouts  9.15 us (6%)
    pallas_call x16, Pallas kernels, vmem_call(): pl.pallas_call(kernel, in_specs=[pl.BlockSpec(memory_space=pltpu.SMEM)] *...  28.7 us
    ppermute x20, waiting for transfers between devices, flip(): return lax.ppermute(array, axis, [(i, i ^ bit) for i in range(size)])  27.8 us
    ppermute x10, starting transfers between devices, square_plane(): shift = lambda array, pairs: lax.ppermute(array, 'tp', pairs)  26.8 us
    pallas_call x1, Pallas kernels, width_sums(): pl.pallas_call(functools.partial(sums_kernel, masks, order, len(arrays),...  18 us
    ppermute x20, starting transfers between devices, flip(): return lax.ppermute(array, axis, [(i, i ^ bit) for i in range(size)])  17.8 us
    ppermute x10, waiting for transfers between devices, square_plane(): shift = lambda array, pairs: lax.ppermute(array, 'tp', pairs)  12.2 us
    unnamed x50, local copies, waits for them, and re-layouts  9.15 us
    pallas_call x2, Pallas kernels, last_token_grad(): pl.pallas_call(functools.partial(token_grad_kernel, 'last', step), grid=(...  5.61 us
  transfers between devices with their start and end apart: 30, of which 14 were waited for; matrix products, arithmetic and copies ran while one was open for 0% of the time, Pallas kernels for 32%

profile of v5, /device:TPU:0, one launch (start us, length us, event | category | flops | bytes accessed | tf_op | source)
XLA Modules:
  0.0 155.0 jit_solution(5155420067230094713)
XLA Ops:
  0.6 3.5 %own_units.1 = (bf16[3,128,1024]{2,1,0:T(8,128)(2,1)}, bf16[3,128,1024]{2,1,0:T(8,128)(2,1)}, bf16[2,3,128,1024]{3,2,1,0:T(8,128)(2,1)}) custom-call(bf16[256,1024]{1,0:T(8,128)(2,1)} %gate.1, bf16[256,1024]{1,0:T(8,128)(2,1)} %up.1, bf16[1024,256]{1,0:T(8,128)(2,1)} %down.1), custom_call_target="tpu_custom_call" | custom-call | flops 1048576 | tf_op jit(solution)/shard_map/own_units/pallas_call | solution.py:247
  4.1 0.5 collective-permute-start.2
  4.6 2.6 %collective-permute-start = (bf16[3,128,1024]{2,1,0:T(8,128)(2,1)}, bf16[3,128,1024]{2,1,0:T(8,128)(2,1)S(1)}, u32[]{:S(2)}, u32[]{:S(2)}) collective-permute-start(bf16[3,128,1024]{2,1,0:T(8,128)(2,1)} %get-tuple-element.45.refs_8_), channel_id=1, source_target_pairs={{0,4},{4,0},{8,12},{12,8},{1,5},{5,1},{9,13},{13,9},{2,6},{6,2},{1... | collective-permute-start | bytes 2359304 | tf_op jit(solution)/shard_map/ppermute | solution.py:139
  7.2 1.5 collective-permute-start.1
  8.7 0.5 collective-permute-start.3
  9.4 16.4 %collective-permute-done.refs_1_.first.refs_10_ = bf16[3,128,1024]{2,1,0:T(8,128)(2,1)S(1)} collective-permute-done((bf16[3,128,1024]{2,1,0:T(8,128)(2,1)}, bf16[3,128,1024]{2,1,0:T(8,128)(2,1)S(1)}, u32[]{:S(2)}, u32[]{:S(2)}) %collective-permute-start) | collective-permute-done | bytes 786464 | tf_op jit(solution)/shard_map/ppermute | solution.py:139
  25.8 2.0 %collective-permute-done.1.refs_2_.second.refs_13_ = bf16[3,128,1024]{2,1,0:T(8,128)(2,1)S(1)} collective-permute-done((bf16[3,128,1024]{2,1,0:T(8,128)(2,1)}, bf16[3,128,1024]{2,1,0:T(8,128)(2,1)S(1)}, u32[]{:S(2)}, u32[]{:S(2)}) %collective-permute-start.1) | collective-permute-done | bytes 786464 | tf_op jit(solution)/shard_map/ppermute | solution.py:139
  27.8 2.5 %copy-done = bf16[1024,2048]{1,0:T(8,128)(2,1)S(1)} copy-done((bf16[1024,2048]{1,0:T(8,128)(2,1)S(1)}, bf16[1024,2048]{1,0:T(8,128)(2,1)}, u32[]{:S(2)}) %copy-start) | copy-done | bytes 4194328
  30.3 2.2 %copy-done.2 = bf16[1024,2048]{1,0:T(8,128)(2,1)S(1)} copy-done((bf16[1024,2048]{1,0:T(8,128)(2,1)S(1)}, bf16[1024,2048]{1,0:T(8,128)(2,1)}, u32[]{:S(2)}) %copy-start.2) | copy-done | bytes 4194328
  32.5 0.9 copy-done.13
  33.4 0.9 copy-done.15
  34.4 0.9 copy-done.22
  35.3 4.1 %low_rank_values.1 = (bf16[1024,64]{1,0:T(8,128)(2,1)S(1)}, bf16[1024,64]{1,0:T(8,128)(2,1)S(1)}, bf16[1024,64]{1,0:T(8,128)(2,1)S(1)}, bf16[192,1024]{1,0:T(8,128)(2,1)S(1)}) custom-call(bf16[1024,2048]{1,0:T(8,128)(2,1)S(1)} %copy-done, bf16[1024,2048]{1,0:T(8,128)(2,1)S(1)} %copy-done.2, bf16[64,2048]{1,0:T(8,128)(2,1)S(1)} %bitcast.11, ...), custom_call_target="tpu_custom_call" | custom-call | flops 64424509440 | tf_op jit(solution)/shard_map/low_rank_values/pallas_call | solution.py:201
  39.7 2.7 %collective-permute-done.3.first.refs_11_ = bf16[3,128,1024]{2,1,0:T(8,128)(2,1)S(1)} collective-permute-done((bf16[3,128,1024]{2,1,0:T(8,128)(2,1)}, bf16[3,128,1024]{2,1,0:T(8,128)(2,1)S(1)}, u32[]{:S(2)}, u32[]{:S(2)}) %collective-permute-start.3) | collective-permute-done | bytes 786464 | tf_op jit(solution)/shard_map/ppermute | solution.py:139
  42.4 1.5 collective-permute-done.4.second.refs_12_
  44.1 1.6 %collective-permute-start.7 = (bf16[3,128,1024]{2,1,0:T(8,128)(2,1)S(1)}, bf16[3,128,1024]{2,1,0:T(8,128)(2,1)S(1)}, u32[]{:S(2)}, u32[]{:S(2)}) collective-permute-start(bf16[3,128,1024]{2,1,0:T(8,128)(2,1)S(1)} %collective-permute-done.refs_1_.first.refs_10_), channel_id=1, source_target_pairs={{0,8},{4,12},{8,0},{12,4},{1,9},{5,13},{9,1},{13,5},{2,10},{6,14},... | collective-permute-start | bytes 2359304 | tf_op jit(solution)/shard_map/ppermute | solution.py:139
  45.7 0.5 collective-permute-start.8
  46.2 1.3 collective-permute-done.6.refs_16_
  47.5 1.2 copy-done.24
  48.7 18.0 %width_sums.1 = (f32[512,1024]{1,0:T(8,128)S(1)}, f32[512,1024]{1,0:T(8,128)S(1)}, f32[512,1024]{1,0:T(8,128)S(1)}, f32[512,1024]{1,0:T(8,128)S(1)}, f32[512,102...) custom-call(s32[2]{0:T(128)} %copy-done.20, ...), custom_call_target="tpu_custom_call" | custom-call | flops 1 | tf_op jit(solution)/shard_map/width_sums/pallas_call | solution.py:381
  67.0 0.4 collective-permute-start.9
  67.4 0.3 copy-done.14
  67.8 1.4 collective-permute-done.10.refs_3_
  69.2 1.1 collective-permute-done.9.refs_2_
  70.3 3.8 %hidden_and_grads.2 = (bf16[512,1024]{1,0:T(8,128)(2,1)S(1)}, bf16[512,1024]{1,0:T(8,128)(2,1)S(1)}, bf16[512,1024]{1,0:T(8,128)(2,1)S(1)}, f32[512,128]{1,0:T(8,128)S(1)}) custom-call(s32[2]{0:T(128)S(1)} %copy-done.21, bf16[1024,512]{1,0:T(8,128)(2,1)S(1)} %get-tuple-element.52.left, bf16[1024,512]{1,0:T(8,128)(2,1)S(1)} %get-tuple-element.53.back, ...), custom_call_target="tpu_custom_call" | custom-call | flops 99999997952 | tf_op jit(solution)/shard_map/hidden_and_grads/pallas_call | solution.py:147
  74.1 2.0 %token_grad.6.refs_7_.refs_4_.refs_12_ = bf16[512,512]{1,0:T(8,128)(2,1)S(1)} custom-call(s32[2]{0:T(128)S(1)} %copy-done.21, bf16[512,1024]{1,0:T(8,128)(2,1)S(1)} %get-tuple-element.62.gate_grad.refs_2_, bf16[512,1024]{1,0:T(8,128)(2,1)S(1)} %get-tuple-element.63.up_grad.refs_4_, f32[512,128]{1,0:T(8,128)S(1)} %get-tuple-element.64.low.refs_6_, ...), custom_call_target="tpu_custom_call" | custom-call | flops 20000000000 | tf_op jit(solution)/shard_map/token_grad/pallas_call | solution.py:147
  76.1 3.5 %collective-permute-start.12 = (bf16[512,512]{1,0:T(8,128)(2,1)S(1)}, bf16[512,512]{1,0:T(8,128)(2,1)S(1)}, u32[]{:S(2)}, u32[]{:S(2)}) collective-permute-start(bf16[512,512]{1,0:T(8,128)(2,1)S(1)} %token_grad.6.refs_7_.refs_4_.refs_12_), channel_id=1, source_target_pairs={{0,1},{3,2},{4,5},{7,6},{8,9},{11,10},{12,13},{15,14},{16,17},{19,... | collective-permute-start | bytes 1572872 | tf_op jit(solution)/shard_map/ppermute | solution.py:740
  79.6 3.7 %hidden_and_grads.3 = (bf16[512,1024]{1,0:T(8,128)(2,1)S(1)}, bf16[512,1024]{1,0:T(8,128)(2,1)S(1)}, bf16[512,1024]{1,0:T(8,128)(2,1)S(1)}, f32[512,128]{1,0:T(8,128)S(1)}) custom-call(s32[2]{0:T(128)S(1)} %copy-done.21, bf16[1024,512]{1,0:T(8,128)(2,1)S(1)} %get-tuple-element.52.left, bf16[1024,512]{1,0:T(8,128)(2,1)S(1)} %get-tuple-element.53.back, ...), custom_call_target="tpu_custom_call" | custom-call | flops 99999997952 | tf_op jit(solution)/shard_map/hidden_and_grads/pallas_call | solution.py:147
  83.4 2.0 %token_grad.7.refs_5_.refs_4_.refs_13_ = bf16[512,512]{1,0:T(8,128)(2,1)S(1)} custom-call(s32[2]{0:T(128)S(1)} %copy-done.21, bf16[512,1024]{1,0:T(8,128)(2,1)S(1)} %get-tuple-element.67.gate_grad.refs_3_, bf16[512,1024]{1,0:T(8,128)(2,1)S(1)} %get-tuple-element.68.up_grad.refs_5_, f32[512,128]{1,0:T(8,128)S(1)} %get-tuple-element.69.low.refs_7_, ...), custom_call_target="tpu_custom_call" | custom-call | flops 20000000000 | tf_op jit(solution)/shard_map/token_grad/pallas_call | solution.py:147
  85.4 1.5 collective-permute-start.11
  86.9 4.1 %adapter_grads.1 = (f32[4,192,384]{2,1,0:T(8,128)S(1)}, f32[4,192,384]{2,1,0:T(8,128)S(1)}) custom-call(s32[2]{0:T(128)S(1)} %copy-done.21, bf16[512,1024]{1,0:T(8,128)(2,1)S(1)} %get-tuple-element.74.refs_0_, bf16[512,1024]{1,0:T(8,128)(2,1)S(1)} %get-tuple-element.75.refs_1_, bf16[512,1024]{1,0:T(8,128)(2,1)S(1)} %get-tuple-element.62.gate_grad.refs_2_, ...), custom_call_target="tpu_custom_call" | custom-call | flops 20000000000 | tf_op jit(solution)/shard_map/adapter_grads/pallas_call | solution.py:147
  91.0 0.8 collective-permute-done.12.refs_4_
  91.8 2.0 %token_grad.8.refs_5_ = bf16[512,512]{1,0:T(8,128)(2,1)S(1)} custom-call(s32[2]{0:T(128)S(1)} %copy-done.21, bf16[512,1024]{1,0:T(8,128)(2,1)S(1)} %get-tuple-element.62.gate_grad.refs_2_, bf16[512,1024]{1,0:T(8,128)(2,1)S(1)} %get-tuple-element.63.up_grad.refs_4_, f32[512,128]{1,0:T(8,128)S(1)} %get-tuple-element.64.low.refs_6_, ...), custom_call_target="tpu_custom_call" | custom-call | flops 20000000000 | tf_op jit(solution)/shard_map/token_grad/pallas_call | solution.py:147
  93.8 4.4 %collective-permute-start.15 = (bf16[512,512]{1,0:T(8,128)(2,1)S(1)}, bf16[512,512]{1,0:T(8,128)(2,1)S(1)}, u32[]{:S(2)}, u32[]{:S(2)}) collective-permute-start(bf16[512,512]{1,0:T(8,128)(2,1)S(1)} %token_grad.8.refs_5_), channel_id=1, source_target_pairs={{0,1},{1,2},{4,5},{5,6},{8,9},{9,10},{12,13},{13,14},{16,17},{17,1... | collective-permute-start | bytes 1572872 | tf_op jit(solution)/shard_map/ppermute | solution.py:740
  98.3 0.7 collective-permute-start.16
  99.0 0.7 halve.2
  99.6 1.6 %collective-permute-start.22 = (bf16[2,192,384]{2,1,0:T(8,128)(2,1)S(1)}, bf16[2,192,384]{2,1,0:T(8,128)(2,1)S(1)}, u32[]{:S(2)}, u32[]{:S(2)}) collective-permute-start(bf16[2,192,384]{2,1,0:T(8,128)(2,1)S(1)} %get-tuple-element.79), channel_id=1, source_target_pairs={{0,8},{4,12},{8,0},{12,4},{1,9},{5,13},{9,1},{13,5},{2,10},{6,14},... | collective-permute-start | bytes 884744 | tf_op jit(solution)/shard_map/ppermute | solution.py:139
  101.2 1.9 %collective-permute-done.11.refs_4_ = bf16[512,512]{1,0:T(8,128)(2,1)S(1)} collective-permute-done((bf16[512,512]{1,0:T(8,128)(2,1)S(1)}, bf16[512,512]{1,0:T(8,128)(2,1)S(1)}, u32[]{:S(2)}, u32[]{:S(2)}) %collective-permute-start.11) | collective-permute-done | bytes 524320 | tf_op jit(solution)/shard_map/ppermute | solution.py:740
  103.1 2.0 %token_grad.9.refs_7_ = bf16[512,512]{1,0:T(8,128)(2,1)S(1)} custom-call(s32[2]{0:T(128)S(1)} %copy-done.21, bf16[512,1024]{1,0:T(8,128)(2,1)S(1)} %get-tuple-element.67.gate_grad.refs_3_, bf16[512,1024]{1,0:T(8,128)(2,1)S(1)} %get-tuple-element.68.up_grad.refs_5_, f32[512,128]{1,0:T(8,128)S(1)} %get-tuple-element.69.low.refs_7_, ...), custom_call_target="tpu_custom_call" | custom-call | flops 20000000000 | tf_op jit(solution)/shard_map/token_grad/pallas_call | solution.py:147
  105.1 4.4 %collective-permute-start.13 = (bf16[512,512]{1,0:T(8,128)(2,1)S(1)}, bf16[512,512]{1,0:T(8,128)(2,1)S(1)}, u32[]{:S(2)}, u32[]{:S(2)}) collective-permute-start(bf16[512,512]{1,0:T(8,128)(2,1)S(1)} %token_grad.9.refs_7_), channel_id=1, source_target_pairs={{0,1},{1,2},{4,5},{5,6},{8,9},{9,10},{12,13},{13,14},{16,17},{17,1... | collective-permute-start | bytes 1572872 | tf_op jit(solution)/shard_map/ppermute | solution.py:740
  109.5 0.7 collective-permute-start.14
  110.2 0.6 halve.3
  110.8 0.8 collective-permute-start.23
  111.6 2.7 %collective-permute-done.15.refs_5_ = bf16[512,512]{1,0:T(8,128)(2,1)S(1)} collective-permute-done((bf16[512,512]{1,0:T(8,128)(2,1)S(1)}, bf16[512,512]{1,0:T(8,128)(2,1)S(1)}, u32[]{:S(2)}, u32[]{:S(2)}) %collective-permute-start.15) | collective-permute-done | bytes 524320 | tf_op jit(solution)/shard_map/ppermute | solution.py:740
  114.3 2.2 %token_grad.10 = (bf16[512,512]{1,0:T(8,128)(2,1)S(1)}, bf16[512,512]{1,0:T(8,128)(2,1)S(1)}) custom-call(s32[2]{0:T(128)S(1)} %copy-done.21, bf16[512,1024]{1,0:T(8,128)(2,1)S(1)} %get-tuple-element.62.gate_grad.refs_2_, bf16[512,1024]{1,0:T(8,128)(2,1)S(1)} %get-tuple-element.63.up_grad.refs_4_, f32[512,128]{1,0:T(8,128)S(1)} %get-tuple-element.64.low.refs_6_, ...), custom_call_target="tpu_custom_call" | custom-call | flops 20000000000 | tf_op jit(solution)/shard_map/token_grad/pallas_call | solution.py:147
  116.5 4.6 %collective-permute-start.19 = (bf16[512,512]{1,0:T(8,128)(2,1)S(1)}, bf16[512,512]{1,0:T(8,128)(2,1)S(1)}, u32[]{:S(2)}, u32[]{:S(2)}) collective-permute-start(bf16[512,512]{1,0:T(8,128)(2,1)S(1)} %get-tuple-element.70.refs_7_), channel_id=1, source_target_pairs={{0,1},{1,2},{2,3},{4,5},{5,6},{6,7},{8,9},{9,10},{10,11},{12,13},{... | collective-permute-start | bytes 1572872 | tf_op jit(solution)/shard_map/ppermute | solution.py:740
  121.1 1.3 collective-permute-start.20
  122.4 0.7 turn.1
  123.1 0.8 collective-permute-start.27
  124.0 1.6 %collective-permute-done.13.refs_5_ = bf16[512,512]{1,0:T(8,128)(2,1)S(1)} collective-permute-done((bf16[512,512]{1,0:T(8,128)(2,1)S(1)}, bf16[512,512]{1,0:T(8,128)(2,1)S(1)}, u32[]{:S(2)}, u32[]{:S(2)}) %collective-permute-start.13) | collective-permute-done | bytes 524320 | tf_op jit(solution)/shard_map/ppermute | solution.py:740
  125.6 2.1 %token_grad.11 = (bf16[512,512]{1,0:T(8,128)(2,1)S(1)}, bf16[512,512]{1,0:T(8,128)(2,1)S(1)}) custom-call(s32[2]{0:T(128)S(1)} %copy-done.21, bf16[512,1024]{1,0:T(8,128)(2,1)S(1)} %get-tuple-element.67.gate_grad.refs_3_, bf16[512,1024]{1,0:T(8,128)(2,1)S(1)} %get-tuple-element.68.up_grad.refs_5_, f32[512,128]{1,0:T(8,128)S(1)} %get-tuple-element.69.low.refs_7_, ...), custom_call_target="tpu_custom_call" | custom-call | flops 20000000000 | tf_op jit(solution)/shard_map/token_grad/pallas_call | solution.py:147
  127.7 4.4 %collective-permute-start.17 = (bf16[512,512]{1,0:T(8,128)(2,1)S(1)}, bf16[512,512]{1,0:T(8,128)(2,1)S(1)}, u32[]{:S(2)}, u32[]{:S(2)}) collective-permute-start(bf16[512,512]{1,0:T(8,128)(2,1)S(1)} %get-tuple-element.71.refs_6_), channel_id=1, source_target_pairs={{0,1},{1,2},{2,3},{4,5},{5,6},{6,7},{8,9},{9,10},{10,11},{12,13},{... | collective-permute-start | bytes 1572872 | tf_op jit(solution)/shard_map/ppermute | solution.py:740
  132.1 1.3 collective-permute-start.18
  133.5 1.6 %collective-permute-start.28 = (f32[2,192,128]{2,1,0:T(8,128)S(1)}, f32[2,192,128]{2,1,0:T(8,128)S(1)}, u32[]{:S(2)}, u32[]{:S(2)}) collective-permute-start(f32[2,192,128]{2,1,0:T(8,128)S(1)} %pad_maximum_fusion.2), channel_id=1, source_target_pairs={{0,8},{4,12},{8,0},{12,4},{1,9},{5,13},{9,1},{13,5},{2,10},{6,14},... | collective-permute-start | bytes 589832 | tf_op jit(solution)/shard_map/ppermute | solution.py:139
  135.0 1.8 %collective-permute-done.19.refs_4_ = bf16[512,512]{1,0:T(8,128)(2,1)S(1)} collective-permute-done((bf16[512,512]{1,0:T(8,128)(2,1)S(1)}, bf16[512,512]{1,0:T(8,128)(2,1)S(1)}, u32[]{:S(2)}, u32[]{:S(2)}) %collective-permute-start.19) | collective-permute-done | bytes 524320 | tf_op jit(solution)/shard_map/ppermute | solution.py:740
  136.8 2.8 %last_token_grad.2.refs_6_ = bf16[1024,512]{1,0:T(8,128)(2,1)} custom-call(s32[2]{0:T(128)S(1)} %copy-done.21, bf16[512,1024]{1,0:T(8,128)(2,1)S(1)} %get-tuple-element.62.gate_grad.refs_2_, bf16[512,1024]{1,0:T(8,128)(2,1)S(1)} %get-tuple-element.63.up_grad.refs_4_, f32[512,128]{1,0:T(8,128)S(1)} %get-tuple-element.64.low.refs_6_, ...), custom_call_target="tpu_custom_call" | custom-call | flops 20000000000 | tf_op jit(solution)/shard_map/last_token_grad/pallas_call | solution.py:499
  139.6 2.5 %collective-permute-start.24 = (bf16[64,192]{1,0:T(8,128)(2,1)S(1)}, bf16[64,192]{1,0:T(8,128)(2,1)S(1)}, u32[]{:S(2)}, u32[]{:S(2)}) collective-permute-start(bf16[64,192]{1,0:T(8,128)(2,1)S(1)} %get-tuple-element.83), channel_id=1, source_target_pairs={{0,1},{1,0},{2,3},{3,2},{4,5},{5,4},{6,7},{7,6},{8,9},{9,8},{10,11... | collective-permute-start | bytes 73736 | tf_op jit(solution)/shard_map/ppermute | solution.py:139
  142.1 1.0 collective-permute-start.25
  143.1 1.5 collective-permute-start.26
  144.6 3.4 %collective-permute-done.17.refs_4_ = bf16[512,512]{1,0:T(8,128)(2,1)S(1)} collective-permute-done((bf16[512,512]{1,0:T(8,128)(2,1)S(1)}, bf16[512,512]{1,0:T(8,128)(2,1)S(1)}, u32[]{:S(2)}, u32[]{:S(2)}) %collective-permute-start.17) | collective-permute-done | bytes 524320 | tf_op jit(solution)/shard_map/ppermute | solution.py:740
  148.0 2.8 %last_token_grad.3 = bf16[1024,512]{1,0:T(8,128)(2,1)} custom-call(s32[2]{0:T(128)S(1)} %copy-done.21, bf16[512,1024]{1,0:T(8,128)(2,1)S(1)} %get-tuple-element.67.gate_grad.refs_3_, bf16[512,1024]{1,0:T(8,128)(2,1)S(1)} %get-tuple-element.68.up_grad.refs_5_, f32[512,128]{1,0:T(8,128)S(1)} %get-tuple-element.69.low.refs_7_, ...), custom_call_target="tpu_custom_call", output_to_operand_aliasing={{}: (13, {})} | custom-call | flops 20000000000 | tf_op jit(solution)/shard_map/last_token_grad/pallas_call | solution.py:499
  150.8 1.4 collective-permute-done.26.refs_2_
  152.3 1.2 last_sum.1
  153.4 1.5 whole.1
  (72 shorter events, 1.0 us)
Async XLA Ops:
  4.1 23.7 %collective-permute-start.2 = (bf16[2,3,128,1024]{3,2,1,0:T(8,128)(2,1)}, bf16[2,3,128,1024]{3,2,1,0:T(8,128)(2,1)}, u32[]{:S(2)}, u32[]{:S(2)}) collective-permute-start(bf16[2,3,128,1024]{3,2,1,0:T(8,128)(2,1)} %get-tuple-element.47), channel_id=1, source_target_pairs={{0,16},{16,0},{1,17},{17,1},{2,18},{18,2},{3,19},{19,3},{4,20},{20... | collective-permute-start | bytes 4718600 | tf_op jit(solution)/shard_map/ppermute | solution.py:139
  4.6 21.2 %collective-permute-start = (bf16[3,128,1024]{2,1,0:T(8,128)(2,1)}, bf16[3,128,1024]{2,1,0:T(8,128)(2,1)S(1)}, u32[]{:S(2)}, u32[]{:S(2)}) collective-permute-start(bf16[3,128,1024]{2,1,0:T(8,128)(2,1)} %get-tuple-element.45.refs_8_), channel_id=1, source_target_pairs={{0,4},{4,0},{8,12},{12,8},{1,5},{5,1},{9,13},{13,9},{2,6},{6,2},{1... | collective-permute-start | bytes 2359304 | tf_op jit(solution)/shard_map/ppermute | solution.py:139
  7.2 20.6 %collective-permute-start.1 = (bf16[3,128,1024]{2,1,0:T(8,128)(2,1)}, bf16[3,128,1024]{2,1,0:T(8,128)(2,1)S(1)}, u32[]{:S(2)}, u32[]{:S(2)}) collective-permute-start(bf16[3,128,1024]{2,1,0:T(8,128)(2,1)} %get-tuple-element.46.refs_9_), channel_id=1, source_target_pairs={{0,8},{4,12},{8,0},{12,4},{1,9},{5,13},{9,1},{13,5},{2,10},{6,14},... | collective-permute-start | bytes 2359304 | tf_op jit(solution)/shard_map/ppermute | solution.py:139
  8.7 33.7 %collective-permute-start.3 = (bf16[3,128,1024]{2,1,0:T(8,128)(2,1)}, bf16[3,128,1024]{2,1,0:T(8,128)(2,1)S(1)}, u32[]{:S(2)}, u32[]{:S(2)}) collective-permute-start(bf16[3,128,1024]{2,1,0:T(8,128)(2,1)} %get-tuple-element.46.refs_9_), channel_id=1, source_target_pairs={{0,4},{4,0},{8,12},{12,8},{1,5},{5,1},{9,13},{13,9},{2,6},{6,2},{1... | collective-permute-start | bytes 2359304 | tf_op jit(solution)/shard_map/ppermute | solution.py:139
  9.3 34.6 %collective-permute-start.4 = (bf16[3,128,1024]{2,1,0:T(8,128)(2,1)}, bf16[3,128,1024]{2,1,0:T(8,128)(2,1)S(1)}, u32[]{:S(2)}, u32[]{:S(2)}) collective-permute-start(bf16[3,128,1024]{2,1,0:T(8,128)(2,1)} %get-tuple-element.45.refs_8_), channel_id=1, source_target_pairs={{0,8},{4,12},{8,0},{12,4},{1,9},{5,13},{9,1},{13,5},{2,10},{6,14},... | collective-permute-start | bytes 2359304 | tf_op jit(solution)/shard_map/ppermute | solution.py:139
  9.4 30.1 %copy-start.20 = (s32[2]{0:T(128)}, s32[2]{0:T(128)S(1)}, u32[]{:S(2)}) copy-start(s32[2]{0:T(128)S(1)} %pad_add_fusion.refs_0_.here) | copy-start | bytes 28
  25.8 18.3 %copy-start.4 = (bf16[3,128,1024]{2,1,0:T(8,128)(2,1)}, bf16[3,128,1024]{2,1,0:T(8,128)(2,1)S(1)}, u32[]{:S(2)}) copy-start(bf16[3,128,1024]{2,1,0:T(8,128)(2,1)S(1)} %collective-permute-done.refs_1_.first.refs_10_) | copy-start | bytes 2359300
  27.8 17.9 %copy-start.5 = (bf16[3,128,1024]{2,1,0:T(8,128)(2,1)}, bf16[3,128,1024]{2,1,0:T(8,128)(2,1)S(1)}, u32[]{:S(2)}) copy-start(bf16[3,128,1024]{2,1,0:T(8,128)(2,1)S(1)} %collective-permute-done.1.refs_2_.second.refs_13_) | copy-start | bytes 2359300
  27.8 2.5 %copy-start = (bf16[1024,2048]{1,0:T(8,128)(2,1)S(1)}, bf16[1024,2048]{1,0:T(8,128)(2,1)}, u32[]{:S(2)}) copy-start(bf16[1024,2048]{1,0:T(8,128)(2,1)} %refs_8_.1) | copy-start | bytes 12582916
  30.3 2.2 %copy-start.2 = (bf16[1024,2048]{1,0:T(8,128)(2,1)S(1)}, bf16[1024,2048]{1,0:T(8,128)(2,1)}, u32[]{:S(2)}) copy-start(bf16[1024,2048]{1,0:T(8,128)(2,1)} %refs_9_.1) | copy-start | bytes 12582916
  32.5 0.9 copy-start.13
  33.4 0.9 copy-start.15
  34.4 0.9 copy-start.22
  39.4 4.5 %copy-start.8 = (bf16[192,1024]{1,0:T(8,128)(2,1)}, bf16[192,1024]{1,0:T(8,128)(2,1)S(1)}, u32[]{:S(2)}) copy-start(bf16[192,1024]{1,0:T(8,128)(2,1)S(1)} %get-tuple-element.51.refs_0_.refs_10_) | copy-start | bytes 1179652
  39.5 4.5 %copy-start.10 = (bf16[1024,64]{1,0:T(8,128)(2,1)}, bf16[1024,64]{1,0:T(8,128)(2,1)S(1)}, u32[]{:S(2)}) copy-start(bf16[1024,64]{1,0:T(8,128)(2,1)S(1)} %get-tuple-element.48.refs_0_) | copy-start | bytes 393220
  39.5 4.5 %copy-start.11 = (bf16[1024,64]{1,0:T(8,128)(2,1)}, bf16[1024,64]{1,0:T(8,128)(2,1)S(1)}, u32[]{:S(2)}) copy-start(bf16[1024,64]{1,0:T(8,128)(2,1)S(1)} %get-tuple-element.49.refs_1_) | copy-start | bytes 393220
  39.5 4.5 %copy-start.12 = (bf16[1024,64]{1,0:T(8,128)(2,1)}, bf16[1024,64]{1,0:T(8,128)(2,1)S(1)}, u32[]{:S(2)}) copy-start(bf16[1024,64]{1,0:T(8,128)(2,1)S(1)} %get-tuple-element.50.refs_2_) | copy-start | bytes 393220
  39.6 6.6 %collective-permute-start.5 = (bf16[2,3,128,1024]{3,2,1,0:T(8,128)(2,1)S(1)}, bf16[2,3,128,1024]{3,2,1,0:T(8,128)(2,1)S(1)}, u32[]{:S(2)}, u32[]{:S(2)}) collective-permute-start(bf16[2,3,128,1024]{3,2,1,0:T(8,128)(2,1)S(1)} %pair.2), channel_id=1, source_target_pairs={{0,16},{16,0},{1,17},{17,1},{2,18},{18,2},{3,19},{19,3},{4,20},{20... | collective-permute-start | bytes 4718600 | tf_op jit(solution)/shard_map/ppermute | solution.py:139
  42.4 5.1 %copy-start.6 = (bf16[3,128,1024]{2,1,0:T(8,128)(2,1)}, bf16[3,128,1024]{2,1,0:T(8,128)(2,1)S(1)}, u32[]{:S(2)}) copy-start(bf16[3,128,1024]{2,1,0:T(8,128)(2,1)S(1)} %collective-permute-done.3.first.refs_11_) | copy-start | bytes 2359300
  43.9 3.6 %copy-start.7 = (bf16[3,128,1024]{2,1,0:T(8,128)(2,1)}, bf16[3,128,1024]{2,1,0:T(8,128)(2,1)S(1)}, u32[]{:S(2)}) copy-start(bf16[3,128,1024]{2,1,0:T(8,128)(2,1)S(1)} %collective-permute-done.4.second.refs_12_) | copy-start | bytes 2359300
  44.0 3.5 %collective-permute-start.6 = (bf16[2,3,128,1024]{3,2,1,0:T(8,128)(2,1)S(1)}, bf16[2,3,128,1024]{3,2,1,0:T(8,128)(2,1)S(1)}, u32[]{:S(2)}, u32[]{:S(2)}) collective-permute-start(bf16[2,3,128,1024]{3,2,1,0:T(8,128)(2,1)S(1)} %pair.3), channel_id=1, source_target_pairs={{0,16},{16,0},{1,17},{17,1},{2,18},{18,2},{3,19},{19,3},{4,20},{20... | collective-permute-start | bytes 4718600 | tf_op jit(solution)/shard_map/ppermute | solution.py:139
  44.1 22.6 %collective-permute-start.7 = (bf16[3,128,1024]{2,1,0:T(8,128)(2,1)S(1)}, bf16[3,128,1024]{2,1,0:T(8,128)(2,1)S(1)}, u32[]{:S(2)}, u32[]{:S(2)}) collective-permute-start(bf16[3,128,1024]{2,1,0:T(8,128)(2,1)S(1)} %collective-permute-done.refs_1_.first.refs_10_), channel_id=1, source_target_pairs={{0,8},{4,12},{8,0},{12,4},{1,9},{5,13},{9,1},{13,5},{2,10},{6,14},... | collective-permute-start | bytes 2359304 | tf_op jit(solution)/shard_map/ppermute | solution.py:139
  45.7 21.1 %collective-permute-start.8 = (bf16[3,128,1024]{2,1,0:T(8,128)(2,1)S(1)}, bf16[3,128,1024]{2,1,0:T(8,128)(2,1)S(1)}, u32[]{:S(2)}, u32[]{:S(2)}) collective-permute-start(bf16[3,128,1024]{2,1,0:T(8,128)(2,1)S(1)} %collective-permute-done.1.refs_2_.second.refs_13_), channel_id=1, source_target_pairs={{0,4},{4,0},{8,12},{12,8},{1,5},{5,1},{9,13},{13,9},{2,6},{6,2},{1... | collective-permute-start | bytes 2359304 | tf_op jit(solution)/shard_map/ppermute | solution.py:139
  46.2 1.3 copy-start.23
  47.5 1.2 copy-start.24
  66.7 1.0 copy-start.14
  66.7 1.0 copy-start.16
  66.8 3.5 %copy-start.17 = (bf16[64,1024]{1,0:T(8,128)(2,1)S(1)}, bf16[64,1024]{1,0:T(8,128)(2,1)}, u32[]{:S(2)}) copy-start(bf16[64,1024]{1,0:T(8,128)(2,1)} %gate_out.3) | copy-start | bytes 393220
  66.8 3.5 %copy-start.18 = (bf16[64,1024]{1,0:T(8,128)(2,1)S(1)}, bf16[64,1024]{1,0:T(8,128)(2,1)}, u32[]{:S(2)}) copy-start(bf16[64,1024]{1,0:T(8,128)(2,1)} %up_out.3) | copy-start | bytes 393220
  66.8 3.5 %copy-start.21 = (s32[2]{0:T(128)S(1)}, s32[2]{0:T(128)}, u32[]{:S(2)}) copy-start(s32[2]{0:T(128)} %copy-done.20) | copy-start | bytes 28
  66.8 2.4 %collective-permute-start.10 = (bf16[3,128,1024]{2,1,0:T(8,128)(2,1)S(1)}, bf16[3,128,1024]{2,1,0:T(8,128)(2,1)S(1)}, u32[]{:S(2)}, u32[]{:S(2)}) collective-permute-start(bf16[3,128,1024]{2,1,0:T(8,128)(2,1)S(1)} %get-tuple-element.56.refs_1_), channel_id=1, source_target_pairs={{0,16},{16,0},{1,17},{17,1},{2,18},{18,2},{3,19},{19,3},{4,20},{20... | collective-permute-start | bytes 2359304 | tf_op jit(solution)/shard_map/ppermute | solution.py:139
  67.0 3.3 %collective-permute-start.9 = (bf16[3,128,1024]{2,1,0:T(8,128)(2,1)S(1)}, bf16[3,128,1024]{2,1,0:T(8,128)(2,1)S(1)}, u32[]{:S(2)}, u32[]{:S(2)}) collective-permute-start(bf16[3,128,1024]{2,1,0:T(8,128)(2,1)S(1)} %get-tuple-element.55.refs_0_), channel_id=1, source_target_pairs={{0,16},{16,0},{1,17},{17,1},{2,18},{18,2},{3,19},{19,3},{4,20},{20... | collective-permute-start | bytes 2359304 | tf_op jit(solution)/shard_map/ppermute | solution.py:139
  76.1 15.7 %collective-permute-start.12 = (bf16[512,512]{1,0:T(8,128)(2,1)S(1)}, bf16[512,512]{1,0:T(8,128)(2,1)S(1)}, u32[]{:S(2)}, u32[]{:S(2)}) collective-permute-start(bf16[512,512]{1,0:T(8,128)(2,1)S(1)} %token_grad.6.refs_7_.refs_4_.refs_12_), channel_id=1, source_target_pairs={{0,1},{3,2},{4,5},{7,6},{8,9},{11,10},{12,13},{15,14},{16,17},{19,... | collective-permute-start | bytes 1572872 | tf_op jit(solution)/shard_map/ppermute | solution.py:740
  83.4 3.5 %copy-start.1 = (bf16[1024,2048]{1,0:T(8,128)(2,1)S(1)}, bf16[1024,2048]{1,0:T(8,128)(2,1)}, u32[]{:S(2)}) copy-start(bf16[1024,2048]{1,0:T(8,128)(2,1)} %refs_8_.1) | copy-start | bytes 12582916
  83.4 3.5 %copy-start.3 = (bf16[1024,2048]{1,0:T(8,128)(2,1)S(1)}, bf16[1024,2048]{1,0:T(8,128)(2,1)}, u32[]{:S(2)}) copy-start(bf16[1024,2048]{1,0:T(8,128)(2,1)} %refs_9_.1) | copy-start | bytes 12582916
  83.4 3.5 %copy-start.9 = (bf16[192,1024]{1,0:T(8,128)(2,1)S(1)}, bf16[192,1024]{1,0:T(8,128)(2,1)}, u32[]{:S(2)}) copy-start(bf16[192,1024]{1,0:T(8,128)(2,1)} %copy-done.8) | copy-start | bytes 1179652
  83.4 3.5 %copy-start.19 = (bf16[1024,64]{0,1:T(8,128)(2,1)S(1)}, bf16[1024,64]{0,1:T(8,128)(2,1)}, u32[]{:S(2)}) copy-start(bf16[1024,64]{0,1:T(8,128)(2,1)} %param.20) | copy-start | bytes 393220
  85.4 17.7 %collective-permute-start.11 = (bf16[512,512]{1,0:T(8,128)(2,1)S(1)}, bf16[512,512]{1,0:T(8,128)(2,1)S(1)}, u32[]{:S(2)}, u32[]{:S(2)}) collective-permute-start(bf16[512,512]{1,0:T(8,128)(2,1)S(1)} %token_grad.7.refs_5_.refs_4_.refs_13_), channel_id=1, source_target_pairs={{0,1},{3,2},{4,5},{7,6},{8,9},{11,10},{12,13},{15,14},{16,17},{19,... | collective-permute-start | bytes 1572872 | tf_op jit(solution)/shard_map/ppermute | solution.py:740
  91.0 8.0 %collective-permute-start.21 = (f32[4,192,384]{2,1,0:T(8,128)S(1)}, f32[4,192,384]{2,1,0:T(8,128)S(1)}, u32[]{:S(2)}, u32[]{:S(2)}) collective-permute-start(f32[4,192,384]{2,1,0:T(8,128)S(1)} %get-tuple-element.77), channel_id=1, source_target_pairs={{0,16},{16,0},{1,17},{17,1},{2,18},{18,2},{3,19},{19,3},{4,20},{20... | collective-permute-start | bytes 3538952 | tf_op jit(solution)/shard_map/ppermute | solution.py:139
  93.8 20.5 %collective-permute-start.15 = (bf16[512,512]{1,0:T(8,128)(2,1)S(1)}, bf16[512,512]{1,0:T(8,128)(2,1)S(1)}, u32[]{:S(2)}, u32[]{:S(2)}) collective-permute-start(bf16[512,512]{1,0:T(8,128)(2,1)S(1)} %token_grad.8.refs_5_), channel_id=1, source_target_pairs={{0,1},{1,2},{4,5},{5,6},{8,9},{9,10},{12,13},{13,14},{16,17},{17,1... | collective-permute-start | bytes 1572872 | tf_op jit(solution)/shard_map/ppermute | solution.py:740
  98.3 16.0 %collective-permute-start.16 = (bf16[512,512]{1,0:T(8,128)(2,1)S(1)}, bf16[512,512]{1,0:T(8,128)(2,1)S(1)}, u32[]{:S(2)}, u32[]{:S(2)}) collective-permute-start(bf16[512,512]{1,0:T(8,128)(2,1)S(1)} %token_grad.8.refs_5_), channel_id=1, source_target_pairs={{3,2},{2,1},{7,6},{6,5},{11,10},{10,9},{15,14},{14,13},{19,18},{18... | collective-permute-start | bytes 1572872 | tf_op jit(solution)/shard_map/ppermute | solution.py:740
  99.6 10.6 %collective-permute-start.22 = (bf16[2,192,384]{2,1,0:T(8,128)(2,1)S(1)}, bf16[2,192,384]{2,1,0:T(8,128)(2,1)S(1)}, u32[]{:S(2)}, u32[]{:S(2)}) collective-permute-start(bf16[2,192,384]{2,1,0:T(8,128)(2,1)S(1)} %get-tuple-element.79), channel_id=1, source_target_pairs={{0,8},{4,12},{8,0},{12,4},{1,9},{5,13},{9,1},{13,5},{2,10},{6,14},... | collective-permute-start | bytes 884744 | tf_op jit(solution)/shard_map/ppermute | solution.py:139
  105.1 20.5 %collective-permute-start.13 = (bf16[512,512]{1,0:T(8,128)(2,1)S(1)}, bf16[512,512]{1,0:T(8,128)(2,1)S(1)}, u32[]{:S(2)}, u32[]{:S(2)}) collective-permute-start(bf16[512,512]{1,0:T(8,128)(2,1)S(1)} %token_grad.9.refs_7_), channel_id=1, source_target_pairs={{0,1},{1,2},{4,5},{5,6},{8,9},{9,10},{12,13},{13,14},{16,17},{17,1... | collective-permute-start | bytes 1572872 | tf_op jit(solution)/shard_map/ppermute | solution.py:740
  109.5 16.1 %collective-permute-start.14 = (bf16[512,512]{1,0:T(8,128)(2,1)S(1)}, bf16[512,512]{1,0:T(8,128)(2,1)S(1)}, u32[]{:S(2)}, u32[]{:S(2)}) collective-permute-start(bf16[512,512]{1,0:T(8,128)(2,1)S(1)} %token_grad.9.refs_7_), channel_id=1, source_target_pairs={{3,2},{2,1},{7,6},{6,5},{11,10},{10,9},{15,14},{14,13},{19,18},{18... | collective-permute-start | bytes 1572872 | tf_op jit(solution)/shard_map/ppermute | solution.py:740
  110.8 11.6 %collective-permute-start.23 = (bf16[1,192,384]{2,1,0:T(8,128)(2,1)S(1)}, bf16[1,192,384]{2,1,0:T(8,128)(2,1)S(1)}, u32[]{:S(2)}, u32[]{:S(2)}) collective-permute-start(bf16[1,192,384]{2,1,0:T(8,128)(2,1)S(1)} %get-tuple-element.81), channel_id=1, source_target_pairs={{0,4},{4,0},{8,12},{12,8},{1,5},{5,1},{9,13},{13,9},{2,6},{6,2},{1... | collective-permute-start | bytes 442376 | tf_op jit(solution)/shard_map/ppermute | solution.py:139
  116.5 20.3 %collective-permute-start.19 = (bf16[512,512]{1,0:T(8,128)(2,1)S(1)}, bf16[512,512]{1,0:T(8,128)(2,1)S(1)}, u32[]{:S(2)}, u32[]{:S(2)}) collective-permute-start(bf16[512,512]{1,0:T(8,128)(2,1)S(1)} %get-tuple-element.70.refs_7_), channel_id=1, source_target_pairs={{0,1},{1,2},{2,3},{4,5},{5,6},{6,7},{8,9},{9,10},{10,11},{12,13},{... | collective-permute-start | bytes 1572872 | tf_op jit(solution)/shard_map/ppermute | solution.py:740
  121.1 15.7 %collective-permute-start.20 = (bf16[512,512]{1,0:T(8,128)(2,1)S(1)}, bf16[512,512]{1,0:T(8,128)(2,1)S(1)}, u32[]{:S(2)}, u32[]{:S(2)}) collective-permute-start(bf16[512,512]{1,0:T(8,128)(2,1)S(1)} %get-tuple-element.73), channel_id=1, source_target_pairs={{3,2},{2,1},{1,0},{7,6},{6,5},{5,4},{11,10},{10,9},{9,8},{15,14},{... | collective-permute-start | bytes 1572872 | tf_op jit(solution)/shard_map/ppermute | solution.py:740
  123.1 10.3 %collective-permute-start.27 = (f32[192,128]{1,0:T(8,128)S(1)}, f32[192,128]{1,0:T(8,128)S(1)}, u32[]{:S(2)}, u32[]{:S(2)}) collective-permute-start(f32[192,128]{1,0:T(8,128)S(1)} %get-tuple-element.86), channel_id=1, source_target_pairs={{0,4},{4,0},{8,12},{12,8},{1,5},{5,1},{9,13},{13,9},{2,6},{6,2},{1... | collective-permute-start | bytes 294920 | tf_op jit(solution)/shard_map/ppermute | solution.py:139
  127.7 20.3 %collective-permute-start.17 = (bf16[512,512]{1,0:T(8,128)(2,1)S(1)}, bf16[512,512]{1,0:T(8,128)(2,1)S(1)}, u32[]{:S(2)}, u32[]{:S(2)}) collective-permute-start(bf16[512,512]{1,0:T(8,128)(2,1)S(1)} %get-tuple-element.71.refs_6_), channel_id=1, source_target_pairs={{0,1},{1,2},{2,3},{4,5},{5,6},{6,7},{8,9},{9,10},{10,11},{12,13},{... | collective-permute-start | bytes 1572872 | tf_op jit(solution)/shard_map/ppermute | solution.py:740
  132.1 15.9 %collective-permute-start.18 = (bf16[512,512]{1,0:T(8,128)(2,1)S(1)}, bf16[512,512]{1,0:T(8,128)(2,1)S(1)}, u32[]{:S(2)}, u32[]{:S(2)}) collective-permute-start(bf16[512,512]{1,0:T(8,128)(2,1)S(1)} %get-tuple-element.72.refs_7_), channel_id=1, source_target_pairs={{3,2},{2,1},{1,0},{7,6},{6,5},{5,4},{11,10},{10,9},{9,8},{15,14},{... | collective-permute-start | bytes 1572872 | tf_op jit(solution)/shard_map/ppermute | solution.py:740
  133.5 9.6 %collective-permute-start.28 = (f32[2,192,128]{2,1,0:T(8,128)S(1)}, f32[2,192,128]{2,1,0:T(8,128)S(1)}, u32[]{:S(2)}, u32[]{:S(2)}) collective-permute-start(f32[2,192,128]{2,1,0:T(8,128)S(1)} %pad_maximum_fusion.2), channel_id=1, source_target_pairs={{0,8},{4,12},{8,0},{12,4},{1,9},{5,13},{9,1},{13,5},{2,10},{6,14},... | collective-permute-start | bytes 589832 | tf_op jit(solution)/shard_map/ppermute | solution.py:139
  139.6 11.2 %collective-permute-start.24 = (bf16[64,192]{1,0:T(8,128)(2,1)S(1)}, bf16[64,192]{1,0:T(8,128)(2,1)S(1)}, u32[]{:S(2)}, u32[]{:S(2)}) collective-permute-start(bf16[64,192]{1,0:T(8,128)(2,1)S(1)} %get-tuple-element.83), channel_id=1, source_target_pairs={{0,1},{1,0},{2,3},{3,2},{4,5},{5,4},{6,7},{7,6},{8,9},{9,8},{10,11... | collective-permute-start | bytes 73736 | tf_op jit(solution)/shard_map/ppermute | solution.py:139
  142.1 8.7 %collective-permute-start.25 = (bf16[64,192]{1,0:T(8,128)(2,1)S(1)}, bf16[64,192]{1,0:T(8,128)(2,1)S(1)}, u32[]{:S(2)}, u32[]{:S(2)}) collective-permute-start(bf16[64,192]{1,0:T(8,128)(2,1)S(1)} %get-tuple-element.84), channel_id=1, source_target_pairs={{0,2},{1,3},{2,0},{3,1},{4,6},{5,7},{6,4},{7,5},{8,10},{9,11},{10,... | collective-permute-start | bytes 73736 | tf_op jit(solution)/shard_map/ppermute | solution.py:139
  143.1 9.2 %collective-permute-start.26 = (bf16[64,192]{1,0:T(8,128)(2,1)S(1)}, bf16[64,192]{1,0:T(8,128)(2,1)S(1)}, u32[]{:S(2)}, u32[]{:S(2)}) collective-permute-start(bf16[64,192]{1,0:T(8,128)(2,1)S(1)} %get-tuple-element.85), channel_id=1, source_target_pairs={{0,3},{1,2},{2,1},{3,0},{4,7},{5,6},{6,5},{7,4},{8,11},{9,10},{10,... | collective-permute-start | bytes 73736 | tf_op jit(solution)/shard_map/ppermute | solution.py:139
  148.0 5.4 %collective-permute-start.29 = (f32[4,192,128]{2,1,0:T(8,128)S(1)}, f32[4,192,128]{2,1,0:T(8,128)S(1)}, u32[]{:S(2)}, u32[]{:S(2)}) collective-permute-start(f32[4,192,128]{2,1,0:T(8,128)S(1)} %pad_maximum_fusion.1.near), channel_id=1, source_target_pairs={{0,16},{16,0},{1,17},{17,1},{2,18},{18,2},{3,19},{19,3},{4,20},{20... | collective-permute-start | bytes 1179656 | tf_op jit(solution)/shard_map/ppermute | solution.py:139

commit v6 on v5

--- a/solution.py
+++ b/solution.py
@@ -13,7 +13,7 @@
 COST = 1
 HALVES = 2
 COSTS = {"sums": 1, "pair": 1, "small": 1, "token": 20 * 10**9, "adapter": 20 * 10**9, "last": 10**11}
-LIMITS = {"low": 6, "sums": 32, "last": 14, "token": 8, "adapter": 12, "small": 4}
+LIMITS = {"low": 6, "sums": 24, "last": 14, "half": 24, "token": 8, "adapter": 12, "small": 4}
 TILE = 512
 STRIP = 256
 QUARTER_ORDER = ((3, 2, 1, 0), (0, 3, 2, 1), (3, 0, 1, 2), (0, 1, 2, 3))
@@ -304,11 +304,11 @@
         units += [ref] if len(ref.shape) == 3 else [ref.at[0], ref.at[1]]
     units = [units[number] for number in order]
     outs = refs[8 + n_arrays :]
-    sums, rest, full = outs[: 3 * HALVES], outs[3 * HALVES : 3 * HALVES + 2], outs[-7:-5]
-    held_tokens, held_cotangent, held_down, row_sems, unit_sems = outs[-5:]
+    sums, rest, full, held_down = outs[:3], outs[3:5], outs[5:7], outs[7]
+    held_tokens, held_cotangent, row_sems, unit_sems = outs[8:]
     half_rows, hidden = units[0].shape[1:]
     rows = 2 * half_rows
-    tile = tokens.shape[0] // HALVES
+    tile = rest[0].shape[0]
 
     def unit_copies(which):
         copies = []
@@ -326,58 +326,51 @@
             )
         return copies
 
-    def row_copy(which, half):
+    def row_copy(which):
         source, target = ((tokens, held_tokens), (cotangent, held_cotangent))[which]
-        part = pl.ds(half * tile, tile)
-        return pltpu.make_async_copy(
-            source.at[part], target.at[part], row_sems.at[which * HALVES + half]
-        )
-
-    loads = [*unit_copies(0), row_copy(0, 0), *unit_copies(1), row_copy(1, 0), *unit_copies(2)]
-    loads += [row_copy(which, half) for half in range(1, HALVES) for which in range(2)]
-    for load in loads:
+        return pltpu.make_async_copy(source.at[pl.ds(0, tile)], target, row_sems.at[which])
+
+    for load in [*unit_copies(0), row_copy(0), *unit_copies(1), row_copy(1), *unit_copies(2)]:
         load.start()
-    for half in range(HALVES):
-        part = slice(half * tile, (half + 1) * tile)
-        for which, (low, factor) in enumerate(
-            ((gate_low, gate_out), (up_low, up_out), (back_low, down_in))
-        ):
-            if half == 0:
-                for copy in unit_copies(which):
-                    copy.wait()
-            if which != 1:
-                row_copy(which // 2, half).wait()
-                ref = (held_tokens, held_cotangent)[which // 2]
-                left = width_part(ref, part, here, masks, rows)
-                rest[which // 2][part, :] = width_part(ref, part, here, last, rows)
-            for column in range(0, hidden, TILE):
-                span = slice(column, column + TILE)
-                if which == 2:
-                    right = held_down[:, span]
-                else:
-                    right = jnp.concatenate(
-                        [
-                            full[which][
-                                pl.ds(
-                                    pl.multiple_of(lax.bitwise_xor(here[0], mask) * rows, rows), rows
-                                ),
-                                span,
-                            ]
-                            for mask in masks
-                        ]
-                    )
-                sums[3 * half + which][:, span] = matrix_product(
-                    left, right
-                ) + adapter_scaling * matrix_product(low[part, :], factor[:, span])
+    part = slice(0, tile)
+    for which, (low, factor) in enumerate(
+        ((gate_low, gate_out), (up_low, up_out), (back_low, down_in))
+    ):
+        for copy in unit_copies(which):
+            copy.wait()
+        if which != 1:
+            row_copy(which // 2).wait()
+            ref = (held_tokens, held_cotangent)[which // 2]
+            left = width_part(ref, part, here, masks, rows)
+            rest[which // 2][...] = width_part(ref, part, here, last, rows)
+        for column in range(0, hidden, TILE):
+            span = slice(column, column + TILE)
+            if which == 2:
+                right = held_down[:, span]
+            else:
+                right = block_rows(here, full[which], masks, rows, span)
+            sums[which][:, span] = matrix_product(left, right) + adapter_scaling * matrix_product(
+                low[part, :], factor[:, span]
+            )
+
+
+def block_rows(here, ref, masks, rows, span):
+    return jnp.concatenate(
+        [
+            ref[pl.ds(pl.multiple_of(lax.bitwise_xor(here[0], mask) * rows, rows), rows), span]
+            for mask in masks
+        ]
+    )
 
 
 def width_sums(here, tokens, cotangent, lows, factors, masks, order, arrays, last):
     rows, width = tokens.shape
     _, half, hidden = arrays[0].shape[-3:]
     vmem, anywhere = pl.BlockSpec(memory_space=pltpu.VMEM), pl.BlockSpec(memory_space=pl.ANY)
-    shapes = [((rows // HALVES, hidden), jnp.float32)] * (3 * HALVES)
-    shapes += [((rows, 2 * half * len(last)), jnp.bfloat16)] * 2
+    shapes = [((rows // HALVES, hidden), jnp.float32)] * 3
+    shapes += [((rows // HALVES, 2 * half * len(last)), jnp.bfloat16)] * 2
     shapes += [((width, hidden), jnp.bfloat16)] * 2
+    shapes += [((half * len(order), hidden), jnp.bfloat16)]
     outs = pl.pallas_call(
         functools.partial(sums_kernel, masks, order, len(arrays), last),
         in_specs=[pl.BlockSpec(memory_space=pltpu.SMEM)]
@@ -386,56 +379,129 @@
         out_specs=[vmem] * len(shapes),
         out_shape=[pltpu.VMEM(shape, kind) for shape, kind in shapes],
         scratch_shapes=[
-            pltpu.VMEM((rows, width), jnp.bfloat16),
-            pltpu.VMEM((rows, width), jnp.bfloat16),
-            pltpu.VMEM((half * len(order), hidden), jnp.bfloat16),
-            pltpu.SemaphoreType.DMA((2 * HALVES,)),
+            pltpu.VMEM((rows // HALVES, width), jnp.bfloat16),
+            pltpu.VMEM((rows // HALVES, width), jnp.bfloat16),
+            pltpu.SemaphoreType.DMA((2,)),
             pltpu.SemaphoreType.DMA((3 * len(order),)),
         ],
         compiler_params=pltpu.CompilerParams(vmem_limit_bytes=LIMITS["sums"] * MEBIBYTE),
         cost_estimate=pl.CostEstimate(flops=COSTS["sums"], bytes_accessed=0, transcendentals=0),
         name="width_sums",
     )(here, *lows, *factors, tokens, cotangent, *arrays)
-    return outs[: 3 * HALVES], outs[3 * HALVES : -2], outs[-2:]
-
-
-def last_kernel(half, here, left, back, gate_out, up_out, *refs):
-    units, sums = refs[:4], refs[4:7]
-    hidden_out, gate_grad_out, up_grad_out, low_out = refs[-4:]
-    rows, hidden = hidden_out.shape
-    part = slice(half * rows, (half + 1) * rows)
-    gate_low = up_low = 0.0
+    return outs[:3], outs[3:5], outs[5:7], outs[7]
+
+
+def finish(outs, gate_out, up_out, gate, up, hidden_grad, span, lows):
+    hidden_out, gate_grad_out, up_grad_out = outs[:3]
+    sig = 1.0 / (1.0 + jnp.exp(-gate))
+    gated = gate * sig
+    hidden_out[:, span] = (gated * up).astype(jnp.bfloat16)
+    gate_grad = (hidden_grad * up * sig * (1.0 + gate * (1.0 - sig))).astype(jnp.bfloat16)
+    up_grad = (hidden_grad * gated).astype(jnp.bfloat16)
+    gate_grad_out[:, span] = gate_grad
+    up_grad_out[:, span] = up_grad
+    return (
+        lows[0] + contract_trailing_axis(gate_grad, gate_out[:, span]),
+        lows[1] + contract_trailing_axis(up_grad, up_out[:, span]),
+    )
+
+
+def last_kernel(here, left, back, gate_out, up_out, *refs):
+    units, sums, outs = refs[:4], refs[4:7], refs[-4:]
+    hidden = outs[0].shape[1]
+    lows = (0.0, 0.0)
     for column in range(0, hidden, STRIP):
         span = slice(column, column + STRIP)
-        gate = sums[0][:, span] + matrix_product(left[part, :], stacked(units, 0, span))
-        up = sums[1][:, span] + matrix_product(left[part, :], stacked(units, 1, span))
-        hidden_grad = sums[2][:, span] + matrix_product(back[part, :], stacked(units, 2, span))
-        sig = 1.0 / (1.0 + jnp.exp(-gate))
-        gated = gate * sig
-        hidden_out[:, span] = (gated * up).astype(jnp.bfloat16)
-        gate_grad = (hidden_grad * up * sig * (1.0 + gate * (1.0 - sig))).astype(jnp.bfloat16)
-        up_grad = (hidden_grad * gated).astype(jnp.bfloat16)
-        gate_grad_out[:, span] = gate_grad
-        up_grad_out[:, span] = up_grad
-        gate_low += contract_trailing_axis(gate_grad, gate_out[:, span])
-        up_low += contract_trailing_axis(up_grad, up_out[:, span])
-    low_out[...] = jnp.concatenate([gate_low, up_low], axis=1)
-
-
-def hidden_and_grads(half, here, parts, factors, tail, sums, ahead):
-    rows = parts[0].shape[0] // HALVES
+        gate = sums[0][:, span] + matrix_product(left[...], stacked(units, 0, span))
+        up = sums[1][:, span] + matrix_product(left[...], stacked(units, 1, span))
+        hidden_grad = sums[2][:, span] + matrix_product(back[...], stacked(units, 2, span))
+        lows = finish(outs, gate_out, up_out, gate, up, hidden_grad, span, lows)
+    outs[3][...] = jnp.concatenate(lows, axis=1)
+
+
+def first_half(here, parts, factors, tail, sums):
+    rows = parts[0].shape[0]
     rank, hidden = factors[0].shape
     return vmem_call(
-        functools.partial(last_kernel, half),
+        last_kernel,
         [here],
-        [*parts, *factors, *tail, *sums[3 * half : 3 * half + 3]],
-        ahead,
+        [*parts, *factors, *tail, *sums],
+        [],
         [((rows, hidden), jnp.bfloat16)] * 3 + [((rows, 2 * rank), jnp.float32)],
         {},
         [],
         LIMITS["last"],
         COSTS["last"],
         "hidden_and_grads",
+    )
+
+
+def whole_kernel_half(masks, last, here, *refs):
+    lows, factors, units, full, down_rows = refs[:3], refs[3:6], refs[6:10], refs[10:12], refs[12]
+    tokens, cotangent = refs[13:15]
+    outs, (held_tokens, held_cotangent, sems) = refs[-7:-3], refs[-3:]
+    tile, hidden = outs[0].shape
+    part = slice(tokens.shape[0] - tile, tokens.shape[0])
+    copies = [
+        pltpu.make_async_copy(ref.at[pl.ds(tokens.shape[0] - tile, tile)], held, sems.at[number])
+        for number, (ref, held) in enumerate(((tokens, held_tokens), (cotangent, held_cotangent)))
+    ]
+    for copy in copies:
+        copy.start()
+    for copy in copies:
+        copy.wait()
+    rows = 2 * units[0].shape[1]
+    every = slice(None)
+    left, back, left_last, back_last = (
+        width_part(ref, every, here, group, rows)
+        for group in (masks, last)
+        for ref in (held_tokens, held_cotangent)
+    )
+    back_lows = (0.0, 0.0)
+    for column in range(0, hidden, STRIP):
+        span = slice(column, column + STRIP)
+        values = []
+        for which, (low, factor) in enumerate(zip(lows, factors)):
+            if which == 2:
+                right = down_rows[:, span]
+            else:
+                right = block_rows(here, full[which], masks, rows, span)
+            values.append(
+                matrix_product(back if which == 2 else left, right)
+                + matrix_product(
+                    back_last if which == 2 else left_last, stacked(units, which, span)
+                )
+                + adapter_scaling * matrix_product(low[part, :], factor[:, span])
+            )
+        back_lows = finish(outs, factors[0], factors[1], *values, span, back_lows)
+    outs[3][...] = jnp.concatenate(back_lows, axis=1)
+
+
+def second_half(here, tokens, cotangent, lows, factors, tail, full, down_rows, masks, last, ahead):
+    rows, width = tokens.shape
+    rank, hidden = factors[0].shape
+    tile = rows // HALVES
+    vmem, anywhere = pl.BlockSpec(memory_space=pltpu.VMEM), pl.BlockSpec(memory_space=pl.ANY)
+    arrays = [*lows, *factors, *tail, *full, down_rows]
+    shapes = [((tile, hidden), jnp.bfloat16)] * 3 + [((tile, 2 * rank), jnp.float32)]
+    return pl.pallas_call(
+        functools.partial(whole_kernel_half, masks, last),
+        in_specs=[pl.BlockSpec(memory_space=pltpu.SMEM)]
+        + [vmem] * len(arrays)
+        + [anywhere] * (2 + len(ahead)),
+        out_specs=[vmem] * len(shapes),
+        out_shape=[pltpu.VMEM(shape, kind) for shape, kind in shapes],
+        scratch_shapes=[pltpu.VMEM((tile, width), jnp.bfloat16)] * 2
+        + [pltpu.SemaphoreType.DMA((2,))],
+        compiler_params=pltpu.CompilerParams(vmem_limit_bytes=LIMITS["half"] * MEBIBYTE),
+        cost_estimate=pl.CostEstimate(flops=COSTS["last"], bytes_accessed=0, transcendentals=0),
+        name="second_half",
+    )(
+        here,
+        *[pltpu.with_memory_space_constraint(array, pltpu.VMEM) for array in arrays],
+        tokens,
+        cotangent,
+        *ahead,
     )
 
 
@@ -730,7 +796,7 @@
     placed += [(4, 0), (4, 1), (5, 0), (6, 1), (5, 1), (6, 0)]
     masks = (0, 1, 2, 4, 5, 6)
     order = [placed.index((mask, half)) for mask in masks for half in range(2)]
-    sums, parts, full = width_sums(
+    sums, parts, full, down_rows = width_sums(
         here, tokens, cotangent, lows, [gate_out, up_out, down_in], masks, order, arrays, (3, 7)
     )
     tail = list(hold([units[3, 0], units[3, 1]], [sums[0]]))
@@ -750,9 +816,22 @@
     )
     both = range(HALVES)
     for half in both:
-        state = hidden_and_grads(
-            half, here, parts, [gate_out, up_out], tail, sums, first[:]
-        )
+        if half == 0:
+            state = first_half(here, parts, [gate_out, up_out], tail, sums)
+        else:
+            state = second_half(
+                here,
+                tokens,
+                cotangent,
+                lows,
+                [gate_out, up_out, down_in],
+                tail,
+                full,
+                down_rows,
+                masks,
+                (3, 7),
+                first[:],
+            )
         states.append(state)
         first.append(share(0, half, "first"))
     came = [shift(part, [(0, 1), (3, 2)]) for part in first]

time: 156 us -> 162 us (1.038)
  waiting for transfers between devices: 40 us -> 49.2 us
  starting transfers between devices: 44.6 us -> 40.3 us
  local copies, waits for them, and re-layouts: 9.15 us -> 12.8 us
  Pallas kernels: 59.9 us -> 57.6 us
    pallas_call x0 -> x1, Pallas kernels: none -> 10.2 us  [second_half(): pl.pallas_call(functools.partial(whole_kernel_half, masks, last), in_spec...]
    pallas_call x1, Pallas kernels: 18 us -> 9.29 us  [width_sums(): pl.pallas_call(functools.partial(sums_kernel, masks, order, len(arrays),...]
    ppermute x20, waiting for transfers between devices: 27.8 us -> 35.8 us  [flip(): return lax.ppermute(array, axis, [(i, i ^ bit) for i in range(size)])]
    pallas_call x16 -> x15, Pallas kernels: 28.7 us -> 24.9 us  [vmem_call(): pl.pallas_call(kernel, in_specs=[pl.BlockSpec(memory_space=pltpu.SMEM)] *...]
    unnamed x50 -> x46, local copies, waits for them, and re-layouts: 9.15 us -> 12.8 us
    ppermute x20, starting transfers between devices: 17.8 us -> 15.4 us  [flip(): return lax.ppermute(array, axis, [(i, i ^ bit) for i in range(size)])]
    ppermute x10, starting transfers between devices: 26.8 us -> 24.9 us  [square_plane(): shift = lambda array, pairs: lax.ppermute(array, 'tp', pairs)]
  transfers between devices with their start and end apart: 30 -> 30, of which waited for: 14 -> 15; matrix products, arithmetic and copies ran while one was open for 0% -> 0% of each run, Pallas kernels for 32% -> 29%
where the time goes in v6:
time: 162 us; the launch traced here: 161 us
  Pallas kernels  57.6 us (36%)
  waiting for transfers between devices  49.2 us (30%)
  starting transfers between devices  40.3 us (25%)
  local copies, waits for them, and re-layouts  12.8 us (8%)
    ppermute x20, waiting for transfers between devices, flip(): return lax.ppermute(array, axis, [(i, i ^ bit) for i in range(size)])  35.8 us
    ppermute x10, starting transfers between devices, square_plane(): shift = lambda array, pairs: lax.ppermute(array, 'tp', pairs)  24.9 us
    pallas_call x15, Pallas kernels, vmem_call(): pl.pallas_call(kernel, in_specs=[pl.BlockSpec(memory_space=pltpu.SMEM)] *...  24.9 us
    ppermute x20, starting transfers between devices, flip(): return lax.ppermute(array, axis, [(i, i ^ bit) for i in range(size)])  15.4 us
    ppermute x10, waiting for transfers between devices, square_plane(): shift = lambda array, pairs: lax.ppermute(array, 'tp', pairs)  13.4 us
    unnamed x46, local copies, waits for them, and re-layouts  12.8 us
    pallas_call x1, Pallas kernels, second_half(): pl.pallas_call(functools.partial(whole_kernel_half, masks, last), in_spec...  10.2 us
    pallas_call x1, Pallas kernels, width_sums(): pl.pallas_call(functools.partial(sums_kernel, masks, order, len(arrays),...  9.29 us
  transfers between devices with their start and end apart: 30, of which 15 were waited for; matrix products, arithmetic and copies ran while one was open for 0% of the time, Pallas kernels for 29%

profile of v6, /device:TPU:0, one launch (start us, length us, event | category | flops | bytes accessed | tf_op | source)
XLA Modules:
  0.0 161.3 jit_solution(454242609169271052)
XLA Ops:
  0.6 3.5 %own_units.1 = (bf16[3,128,1024]{2,1,0:T(8,128)(2,1)}, bf16[3,128,1024]{2,1,0:T(8,128)(2,1)}, bf16[2,3,128,1024]{3,2,1,0:T(8,128)(2,1)}) custom-call(bf16[256,1024]{1,0:T(8,128)(2,1)} %gate.1, bf16[256,1024]{1,0:T(8,128)(2,1)} %up.1, bf16[1024,256]{1,0:T(8,128)(2,1)} %down.1), custom_call_target="tpu_custom_call" | custom-call | flops 1048576 | tf_op jit(solution)/shard_map/own_units/pallas_call | solution.py:247
  4.2 0.5 collective-permute-start.2
  4.7 2.6 %collective-permute-start = (bf16[3,128,1024]{2,1,0:T(8,128)(2,1)}, bf16[3,128,1024]{2,1,0:T(8,128)(2,1)S(1)}, u32[]{:S(2)}, u32[]{:S(2)}) collective-permute-start(bf16[3,128,1024]{2,1,0:T(8,128)(2,1)} %get-tuple-element.43.refs_8_), channel_id=1, source_target_pairs={{0,4},{4,0},{8,12},{12,8},{1,5},{5,1},{9,13},{13,9},{2,6},{6,2},{1... | collective-permute-start | bytes 2359304 | tf_op jit(solution)/shard_map/ppermute | solution.py:139
  7.3 1.5 collective-permute-start.1
  8.8 0.5 collective-permute-start.5
  9.4 16.4 %collective-permute-done.refs_1_.first.refs_10_ = bf16[3,128,1024]{2,1,0:T(8,128)(2,1)S(1)} collective-permute-done((bf16[3,128,1024]{2,1,0:T(8,128)(2,1)}, bf16[3,128,1024]{2,1,0:T(8,128)(2,1)S(1)}, u32[]{:S(2)}, u32[]{:S(2)}) %collective-permute-start) | collective-permute-done | bytes 786464 | tf_op jit(solution)/shard_map/ppermute | solution.py:139
  25.9 2.0 %collective-permute-done.1.refs_2_.second.refs_13_ = bf16[3,128,1024]{2,1,0:T(8,128)(2,1)S(1)} collective-permute-done((bf16[3,128,1024]{2,1,0:T(8,128)(2,1)}, bf16[3,128,1024]{2,1,0:T(8,128)(2,1)S(1)}, u32[]{:S(2)}, u32[]{:S(2)}) %collective-permute-start.1) | collective-permute-done | bytes 786464 | tf_op jit(solution)/shard_map/ppermute | solution.py:139
  27.9 2.2 %copy-done = bf16[1024,2048]{1,0:T(8,128)(2,1)S(1)} copy-done((bf16[1024,2048]{1,0:T(8,128)(2,1)S(1)}, bf16[1024,2048]{1,0:T(8,128)(2,1)}, u32[]{:S(2)}) %copy-start) | copy-done | bytes 4194328
  30.1 2.2 %copy-done.2 = bf16[1024,2048]{1,0:T(8,128)(2,1)S(1)} copy-done((bf16[1024,2048]{1,0:T(8,128)(2,1)S(1)}, bf16[1024,2048]{1,0:T(8,128)(2,1)}, u32[]{:S(2)}) %copy-start.2) | copy-done | bytes 4194328
  32.2 0.9 copy-done.7
  33.2 0.9 copy-done.20
  34.1 4.1 %low_rank_values.1 = (bf16[1024,64]{1,0:T(8,128)(2,1)S(1)}, bf16[1024,64]{1,0:T(8,128)(2,1)S(1)}, bf16[1024,64]{1,0:T(8,128)(2,1)S(1)}, bf16[192,1024]{1,0:T(8,128)(2,1)S(1)}) custom-call(bf16[1024,2048]{1,0:T(8,128)(2,1)S(1)} %copy-done, bf16[1024,2048]{1,0:T(8,128)(2,1)S(1)} %copy-done.2, bf16[64,2048]{1,0:T(8,128)(2,1)S(1)} %bitcast.11, ...), custom_call_target="tpu_custom_call" | custom-call | flops 64424509440 | tf_op jit(solution)/shard_map/low_rank_values/pallas_call | solution.py:201
  38.5 4.0 %collective-permute-done.5.first.refs_11_ = bf16[3,128,1024]{2,1,0:T(8,128)(2,1)S(1)} collective-permute-done((bf16[3,128,1024]{2,1,0:T(8,128)(2,1)}, bf16[3,128,1024]{2,1,0:T(8,128)(2,1)S(1)}, u32[]{:S(2)}, u32[]{:S(2)}) %collective-permute-start.5) | collective-permute-done | bytes 786464 | tf_op jit(solution)/shard_map/ppermute | solution.py:139
  42.5 1.5 collective-permute-done.6.second.refs_12_
  44.1 1.6 collective-permute-start.3
  45.7 0.5 collective-permute-start.4
  46.3 1.3 collective-permute-done.8.refs_16_
  47.5 9.3 %width_sums.1 = (f32[512,1024]{1,0:T(8,128)S(1)}, f32[512,1024]{1,0:T(8,128)S(1)}, f32[512,1024]{1,0:T(8,128)S(1)}, bf16[512,512]{1,0:T(8,128)(2,1)S(1)}, bf16[5...) custom-call(s32[2]{0:T(128)S(1)} %pad_add_fusion.refs_0_.here, ...), custom_call_target="tpu_custom_call" | custom-call | flops 1 | tf_op jit(solution)/shard_map/width_sums/pallas_call | solution.py:374
  56.8 1.6 %copy-done.18 = bf16[1536,1024]{1,0:T(8,128)(2,1)} copy-done((bf16[1536,1024]{1,0:T(8,128)(2,1)}, bf16[1536,1024]{1,0:T(8,128)(2,1)S(1)}, u32[]{:S(2)}) %copy-start.18) | copy-done | bytes 3145752
  58.5 5.6 %collective-permute-done.3.refs_0_ = bf16[3,128,1024]{2,1,0:T(8,128)(2,1)S(1)} collective-permute-done((bf16[3,128,1024]{2,1,0:T(8,128)(2,1)S(1)}, bf16[3,128,1024]{2,1,0:T(8,128)(2,1)S(1)}, u32[]{:S(2)}, u32[]{:S(2)}) %collective-permute-start.3) | collective-permute-done | bytes 786464 | tf_op jit(solution)/shard_map/ppermute | solution.py:139
  64.1 1.2 collective-permute-done.4.refs_1_
  66.3 1.3 collective-permute-done.10.refs_3_.refs_9_
  67.6 1.1 collective-permute-done.9.refs_2_.refs_8_
  68.7 3.8 %hidden_and_grads.1 = (bf16[512,1024]{1,0:T(8,128)(2,1)S(1)}, bf16[512,1024]{1,0:T(8,128)(2,1)S(1)}, bf16[512,1024]{1,0:T(8,128)(2,1)S(1)}, f32[512,128]{1,0:T(8,128)S(1)}) custom-call(s32[2]{0:T(128)S(1)} %pad_add_fusion.refs_0_.here, bf16[512,512]{1,0:T(8,128)(2,1)S(1)} %get-tuple-element.56.left, bf16[512,512]{1,0:T(8,128)(2,1)S(1)} %get-tuple-element.57.back, ...), custom_call_target="tpu_custom_call" | custom-call | flops 99999997952 | tf_op jit(solution)/shard_map/hidden_and_grads/pallas_call | solution.py:147
  72.6 2.0 %token_grad.6.refs_15_.refs_4_.refs_12_ = bf16[512,512]{1,0:T(8,128)(2,1)S(1)} custom-call(s32[2]{0:T(128)S(1)} %pad_add_fusion.refs_0_.here, bf16[512,1024]{1,0:T(8,128)(2,1)S(1)} %get-tuple-element.60.gate_grad.refs_2_, bf16[512,1024]{1,0:T(8,128)(2,1)S(1)} %get-tuple-element.61.up_grad.refs_4_, f32[512,128]{1,0:T(8,128)S(1)} %get-tuple-element.62.low.refs_6_, ...), custom_call_target="tpu_custom_call" | custom-call | flops 20000000000 | tf_op jit(solution)/shard_map/token_grad/pallas_call | solution.py:147
  74.6 3.9 %collective-permute-start.12 = (bf16[512,512]{1,0:T(8,128)(2,1)S(1)}, bf16[512,512]{1,0:T(8,128)(2,1)S(1)}, u32[]{:S(2)}, u32[]{:S(2)}) collective-permute-start(bf16[512,512]{1,0:T(8,128)(2,1)S(1)} %token_grad.6.refs_15_.refs_4_.refs_12_), channel_id=1, source_target_pairs={{0,1},{3,2},{4,5},{7,6},{8,9},{11,10},{12,13},{15,14},{16,17},{19,... | collective-permute-start | bytes 1572872 | tf_op jit(solution)/shard_map/ppermute | solution.py:806
  78.6 2.2 %copy-done.13 = bf16[2048,1024]{1,0:T(8,128)(2,1)S(1)} copy-done((bf16[2048,1024]{1,0:T(8,128)(2,1)S(1)}, bf16[2048,1024]{1,0:T(8,128)(2,1)}, u32[]{:S(2)}) %copy-start.13) | copy-done | bytes 4194328
  80.8 2.2 %copy-done.16 = bf16[2048,1024]{1,0:T(8,128)(2,1)S(1)} copy-done((bf16[2048,1024]{1,0:T(8,128)(2,1)S(1)}, bf16[2048,1024]{1,0:T(8,128)(2,1)}, u32[]{:S(2)}) %copy-start.16) | copy-done | bytes 4194328
  83.0 10.2 %second_half.1 = (bf16[512,1024]{1,0:T(8,128)(2,1)S(1)}, bf16[512,1024]{1,0:T(8,128)(2,1)S(1)}, bf16[512,1024]{1,0:T(8,128)(2,1)S(1)}, f32[512,128]{1,0:T(8,128)S(1)}) custom-call(s32[2]{0:T(128)S(1)} %pad_add_fusion.refs_0_.here, bf16[1024,64]{1,0:T(8,128)(2,1)S(1)} %get-tuple-element.46.refs_0_, bf16[1024,64]{1,0:T(8,128)(2,1)S(1)} %get-tuple-element.47.refs_1_, ...), custom_call_target="tpu_custom_call" | custom-call | flops 99999997952 | tf_op jit(solution)/shard_map/second_half/pallas_call | solution.py:487
  93.2 2.0 %token_grad.7.refs_5_.refs_4_.refs_13_ = bf16[512,512]{1,0:T(8,128)(2,1)S(1)} custom-call(s32[2]{0:T(128)S(1)} %pad_add_fusion.refs_0_.here, bf16[512,1024]{1,0:T(8,128)(2,1)S(1)} %get-tuple-element.63.gate_grad.refs_3_, bf16[512,1024]{1,0:T(8,128)(2,1)S(1)} %get-tuple-element.64.up_grad.refs_5_, f32[512,128]{1,0:T(8,128)S(1)} %get-tuple-element.65.low.refs_7_, ...), custom_call_target="tpu_custom_call" | custom-call | flops 20000000000 | tf_op jit(solution)/shard_map/token_grad/pallas_call | solution.py:147
  95.2 2.1 %collective-permute-start.11 = (bf16[512,512]{1,0:T(8,128)(2,1)S(1)}, bf16[512,512]{1,0:T(8,128)(2,1)S(1)}, u32[]{:S(2)}, u32[]{:S(2)}) collective-permute-start(bf16[512,512]{1,0:T(8,128)(2,1)S(1)} %token_grad.7.refs_5_.refs_4_.refs_13_), channel_id=1, source_target_pairs={{0,1},{3,2},{4,5},{7,6},{8,9},{11,10},{12,13},{15,14},{16,17},{19,... | collective-permute-start | bytes 1572872 | tf_op jit(solution)/shard_map/ppermute | solution.py:806
  97.4 4.0 %adapter_grads.1 = (f32[4,192,384]{2,1,0:T(8,128)S(1)}, f32[4,192,384]{2,1,0:T(8,128)S(1)}) custom-call(s32[2]{0:T(128)S(1)} %pad_add_fusion.refs_0_.here, bf16[512,1024]{1,0:T(8,128)(2,1)S(1)} %get-tuple-element.70.refs_0_, bf16[512,1024]{1,0:T(8,128)(2,1)S(1)} %get-tuple-element.71.refs_1_, bf16[512,1024]{1,0:T(8,128)(2,1)S(1)} %get-tuple-element.60.gate_grad.refs_2_, ...), custom_call_target="tpu_custom_call" | custom-call | flops 20000000000 | tf_op jit(solution)/shard_map/adapter_grads/pallas_call | solution.py:147
  101.6 2.0 %token_grad.8.refs_5_ = bf16[512,512]{1,0:T(8,128)(2,1)S(1)} custom-call(s32[2]{0:T(128)S(1)} %pad_add_fusion.refs_0_.here, bf16[512,1024]{1,0:T(8,128)(2,1)S(1)} %get-tuple-element.60.gate_grad.refs_2_, bf16[512,1024]{1,0:T(8,128)(2,1)S(1)} %get-tuple-element.61.up_grad.refs_4_, f32[512,128]{1,0:T(8,128)S(1)} %copy-done.22, ...), custom_call_target="tpu_custom_call" | custom-call | flops 20000000000 | tf_op jit(solution)/shard_map/token_grad/pallas_call | solution.py:147
  103.5 1.4 collective-permute-start.15
  105.0 0.7 collective-permute-start.16
  105.7 0.7 halve.2
  106.3 0.6 collective-permute-start.22
  106.9 2.4 %collective-permute-done.11.refs_4_ = bf16[512,512]{1,0:T(8,128)(2,1)S(1)} collective-permute-done((bf16[512,512]{1,0:T(8,128)(2,1)S(1)}, bf16[512,512]{1,0:T(8,128)(2,1)S(1)}, u32[]{:S(2)}, u32[]{:S(2)}) %collective-permute-start.11) | collective-permute-done | bytes 524320 | tf_op jit(solution)/shard_map/ppermute | solution.py:806
  109.4 2.0 %token_grad.9.refs_7_ = bf16[512,512]{1,0:T(8,128)(2,1)S(1)} custom-call(s32[2]{0:T(128)S(1)} %pad_add_fusion.refs_0_.here, bf16[512,1024]{1,0:T(8,128)(2,1)S(1)} %get-tuple-element.63.gate_grad.refs_3_, bf16[512,1024]{1,0:T(8,128)(2,1)S(1)} %get-tuple-element.64.up_grad.refs_5_, f32[512,128]{1,0:T(8,128)S(1)} %get-tuple-element.65.low.refs_7_, ...), custom_call_target="tpu_custom_call" | custom-call | flops 20000000000 | tf_op jit(solution)/shard_map/token_grad/pallas_call | solution.py:147
  111.3 4.4 %collective-permute-start.13 = (bf16[512,512]{1,0:T(8,128)(2,1)S(1)}, bf16[512,512]{1,0:T(8,128)(2,1)S(1)}, u32[]{:S(2)}, u32[]{:S(2)}) collective-permute-start(bf16[512,512]{1,0:T(8,128)(2,1)S(1)} %token_grad.9.refs_7_), channel_id=1, source_target_pairs={{0,1},{1,2},{4,5},{5,6},{8,9},{9,10},{12,13},{13,14},{16,17},{17,1... | collective-permute-start | bytes 1572872 | tf_op jit(solution)/shard_map/ppermute | solution.py:806
  115.8 0.7 collective-permute-start.14
  116.5 0.6 halve.3
  117.1 0.6 collective-permute-start.23
  117.7 2.9 %collective-permute-done.15.refs_5_ = bf16[512,512]{1,0:T(8,128)(2,1)S(1)} collective-permute-done((bf16[512,512]{1,0:T(8,128)(2,1)S(1)}, bf16[512,512]{1,0:T(8,128)(2,1)S(1)}, u32[]{:S(2)}, u32[]{:S(2)}) %collective-permute-start.15) | collective-permute-done | bytes 524320 | tf_op jit(solution)/shard_map/ppermute | solution.py:806
  120.6 2.1 %token_grad.10 = (bf16[512,512]{1,0:T(8,128)(2,1)S(1)}, bf16[512,512]{1,0:T(8,128)(2,1)S(1)}) custom-call(s32[2]{0:T(128)S(1)} %pad_add_fusion.refs_0_.here, bf16[512,1024]{1,0:T(8,128)(2,1)S(1)} %get-tuple-element.60.gate_grad.refs_2_, bf16[512,1024]{1,0:T(8,128)(2,1)S(1)} %get-tuple-element.61.up_grad.refs_4_, f32[512,128]{1,0:T(8,128)S(1)} %copy-done.22, ...), custom_call_target="tpu_custom_call" | custom-call | flops 20000000000 | tf_op jit(solution)/shard_map/token_grad/pallas_call | solution.py:147
  122.7 4.5 %collective-permute-start.19 = (bf16[512,512]{1,0:T(8,128)(2,1)S(1)}, bf16[512,512]{1,0:T(8,128)(2,1)S(1)}, u32[]{:S(2)}, u32[]{:S(2)}) collective-permute-start(bf16[512,512]{1,0:T(8,128)(2,1)S(1)} %get-tuple-element.66.refs_7_), channel_id=1, source_target_pairs={{0,1},{1,2},{2,3},{4,5},{5,6},{6,7},{8,9},{9,10},{10,11},{12,13},{... | collective-permute-start | bytes 1572872 | tf_op jit(solution)/shard_map/ppermute | solution.py:806
  127.3 1.3 collective-permute-start.20
  128.6 0.7 turn.1
  129.3 0.6 collective-permute-start.27
  129.9 1.9 %collective-permute-done.13.refs_5_ = bf16[512,512]{1,0:T(8,128)(2,1)S(1)} collective-permute-done((bf16[512,512]{1,0:T(8,128)(2,1)S(1)}, bf16[512,512]{1,0:T(8,128)(2,1)S(1)}, u32[]{:S(2)}, u32[]{:S(2)}) %collective-permute-start.13) | collective-permute-done | bytes 524320 | tf_op jit(solution)/shard_map/ppermute | solution.py:806
  131.8 2.1 %token_grad.11 = (bf16[512,512]{1,0:T(8,128)(2,1)S(1)}, bf16[512,512]{1,0:T(8,128)(2,1)S(1)}) custom-call(s32[2]{0:T(128)S(1)} %pad_add_fusion.refs_0_.here, bf16[512,1024]{1,0:T(8,128)(2,1)S(1)} %get-tuple-element.63.gate_grad.refs_3_, bf16[512,1024]{1,0:T(8,128)(2,1)S(1)} %get-tuple-element.64.up_grad.refs_5_, ...), custom_call_target="tpu_custom_call" | custom-call | flops 20000000000 | tf_op jit(solution)/shard_map/token_grad/pallas_call | solution.py:147
  134.0 4.5 %collective-permute-start.17 = (bf16[512,512]{1,0:T(8,128)(2,1)S(1)}, bf16[512,512]{1,0:T(8,128)(2,1)S(1)}, u32[]{:S(2)}, u32[]{:S(2)}) collective-permute-start(bf16[512,512]{1,0:T(8,128)(2,1)S(1)} %get-tuple-element.67.refs_6_), channel_id=1, source_target_pairs={{0,1},{1,2},{2,3},{4,5},{5,6},{6,7},{8,9},{9,10},{10,11},{12,13},{... | collective-permute-start | bytes 1572872 | tf_op jit(solution)/shard_map/ppermute | solution.py:806
  138.5 1.3 collective-permute-start.18
  139.8 0.6 collective-permute-start.28
  140.4 2.7 %collective-permute-done.19.refs_4_ = bf16[512,512]{1,0:T(8,128)(2,1)S(1)} collective-permute-done((bf16[512,512]{1,0:T(8,128)(2,1)S(1)}, bf16[512,512]{1,0:T(8,128)(2,1)S(1)}, u32[]{:S(2)}, u32[]{:S(2)}) %collective-permute-start.19) | collective-permute-done | bytes 524320 | tf_op jit(solution)/shard_map/ppermute | solution.py:806
  143.1 2.8 %last_token_grad.2.refs_6_ = bf16[1024,512]{1,0:T(8,128)(2,1)} custom-call(s32[2]{0:T(128)S(1)} %pad_add_fusion.refs_0_.here, bf16[512,1024]{1,0:T(8,128)(2,1)S(1)} %get-tuple-element.60.gate_grad.refs_2_, bf16[512,1024]{1,0:T(8,128)(2,1)S(1)} %get-tuple-element.61.up_grad.refs_4_, f32[512,128]{1,0:T(8,128)S(1)} %copy-done.22, ...), custom_call_target="tpu_custom_call" | custom-call | flops 20000000000 | tf_op jit(solution)/shard_map/last_token_grad/pallas_call | solution.py:565
  145.9 2.6 %collective-permute-start.24 = (bf16[64,192]{1,0:T(8,128)(2,1)S(1)}, bf16[64,192]{1,0:T(8,128)(2,1)S(1)}, u32[]{:S(2)}, u32[]{:S(2)}) collective-permute-start(bf16[64,192]{1,0:T(8,128)(2,1)S(1)} %get-tuple-element.79), channel_id=1, source_target_pairs={{0,1},{1,0},{2,3},{3,2},{4,5},{5,4},{6,7},{7,6},{8,9},{9,8},{10,11... | collective-permute-start | bytes 73736 | tf_op jit(solution)/shard_map/ppermute | solution.py:139
  148.5 0.9 collective-permute-start.25
  149.4 1.5 collective-permute-start.26
  150.9 3.4 %collective-permute-done.17.refs_4_ = bf16[512,512]{1,0:T(8,128)(2,1)S(1)} collective-permute-done((bf16[512,512]{1,0:T(8,128)(2,1)S(1)}, bf16[512,512]{1,0:T(8,128)(2,1)S(1)}, u32[]{:S(2)}, u32[]{:S(2)}) %collective-permute-start.17) | collective-permute-done | bytes 524320 | tf_op jit(solution)/shard_map/ppermute | solution.py:806
  154.3 2.8 %last_token_grad.3 = bf16[1024,512]{1,0:T(8,128)(2,1)} custom-call(s32[2]{0:T(128)S(1)} %pad_add_fusion.refs_0_.here, bf16[512,1024]{1,0:T(8,128)(2,1)S(1)} %get-tuple-element.63.gate_grad.refs_3_, bf16[512,1024]{1,0:T(8,128)(2,1)S(1)} %get-tuple-element.64.up_grad.refs_5_, ...), custom_call_target="tpu_custom_call", output_to_operand_aliasing={{}: (13, {})} | custom-call | flops 20000000000 | tf_op jit(solution)/shard_map/last_token_grad/pallas_call | solution.py:565
  157.1 1.4 collective-permute-done.26.refs_2_
  158.6 1.2 last_sum.1
  159.7 1.5 whole.1
  (68 shorter events, 1.7 us)
Async XLA Ops:
  0.6 27.2 %copy-start.6 = (bf16[2048,64]{0,1:T(8,128)(2,1)S(1)}, bf16[2048,64]{0,1:T(8,128)(2,1)}, u32[]{:S(2)}) copy-start(bf16[2048,64]{0,1:T(8,128)(2,1)} %param.16) | copy-start | bytes 786436
  4.2 23.7 %collective-permute-start.2 = (bf16[2,3,128,1024]{3,2,1,0:T(8,128)(2,1)}, bf16[2,3,128,1024]{3,2,1,0:T(8,128)(2,1)}, u32[]{:S(2)}, u32[]{:S(2)}) collective-permute-start(bf16[2,3,128,1024]{3,2,1,0:T(8,128)(2,1)} %get-tuple-element.45), channel_id=1, source_target_pairs={{0,16},{16,0},{1,17},{17,1},{2,18},{18,2},{3,19},{19,3},{4,20},{20... | collective-permute-start | bytes 4718600 | tf_op jit(solution)/shard_map/ppermute | solution.py:139
  4.7 21.2 %collective-permute-start = (bf16[3,128,1024]{2,1,0:T(8,128)(2,1)}, bf16[3,128,1024]{2,1,0:T(8,128)(2,1)S(1)}, u32[]{:S(2)}, u32[]{:S(2)}) collective-permute-start(bf16[3,128,1024]{2,1,0:T(8,128)(2,1)} %get-tuple-element.43.refs_8_), channel_id=1, source_target_pairs={{0,4},{4,0},{8,12},{12,8},{1,5},{5,1},{9,13},{13,9},{2,6},{6,2},{1... | collective-permute-start | bytes 2359304 | tf_op jit(solution)/shard_map/ppermute | solution.py:139
  7.3 20.6 %collective-permute-start.1 = (bf16[3,128,1024]{2,1,0:T(8,128)(2,1)}, bf16[3,128,1024]{2,1,0:T(8,128)(2,1)S(1)}, u32[]{:S(2)}, u32[]{:S(2)}) collective-permute-start(bf16[3,128,1024]{2,1,0:T(8,128)(2,1)} %get-tuple-element.44.refs_9_), channel_id=1, source_target_pairs={{0,8},{4,12},{8,0},{12,4},{1,9},{5,13},{9,1},{13,5},{2,10},{6,14},... | collective-permute-start | bytes 2359304 | tf_op jit(solution)/shard_map/ppermute | solution.py:139
  8.8 33.7 %collective-permute-start.5 = (bf16[3,128,1024]{2,1,0:T(8,128)(2,1)}, bf16[3,128,1024]{2,1,0:T(8,128)(2,1)S(1)}, u32[]{:S(2)}, u32[]{:S(2)}) collective-permute-start(bf16[3,128,1024]{2,1,0:T(8,128)(2,1)} %get-tuple-element.44.refs_9_), channel_id=1, source_target_pairs={{0,4},{4,0},{8,12},{12,8},{1,5},{5,1},{9,13},{13,9},{2,6},{6,2},{1... | collective-permute-start | bytes 2359304 | tf_op jit(solution)/shard_map/ppermute | solution.py:139
  9.3 34.6 %collective-permute-start.6 = (bf16[3,128,1024]{2,1,0:T(8,128)(2,1)}, bf16[3,128,1024]{2,1,0:T(8,128)(2,1)S(1)}, u32[]{:S(2)}, u32[]{:S(2)}) collective-permute-start(bf16[3,128,1024]{2,1,0:T(8,128)(2,1)} %get-tuple-element.43.refs_8_), channel_id=1, source_target_pairs={{0,8},{4,12},{8,0},{12,4},{1,9},{5,13},{9,1},{13,5},{2,10},{6,14},... | collective-permute-start | bytes 2359304 | tf_op jit(solution)/shard_map/ppermute | solution.py:139
  27.9 2.2 %copy-start = (bf16[1024,2048]{1,0:T(8,128)(2,1)S(1)}, bf16[1024,2048]{1,0:T(8,128)(2,1)}, u32[]{:S(2)}) copy-start(bf16[1024,2048]{1,0:T(8,128)(2,1)} %refs_8_.1) | copy-start | bytes 12582916
  30.1 2.2 %copy-start.2 = (bf16[1024,2048]{1,0:T(8,128)(2,1)S(1)}, bf16[1024,2048]{1,0:T(8,128)(2,1)}, u32[]{:S(2)}) copy-start(bf16[1024,2048]{1,0:T(8,128)(2,1)} %refs_9_.1) | copy-start | bytes 12582916
  32.2 0.9 copy-start.7
  33.2 0.9 copy-start.20
  38.3 5.7 %copy-start.4 = (bf16[192,1024]{1,0:T(8,128)(2,1)}, bf16[192,1024]{1,0:T(8,128)(2,1)S(1)}, u32[]{:S(2)}) copy-start(bf16[192,1024]{1,0:T(8,128)(2,1)S(1)} %get-tuple-element.49.refs_0_.refs_10_) | copy-start | bytes 1179652
  38.4 9.1 %copy-start.9 = (bf16[64,1024]{1,0:T(8,128)(2,1)S(1)}, bf16[64,1024]{1,0:T(8,128)(2,1)}, u32[]{:S(2)}) copy-start(bf16[64,1024]{1,0:T(8,128)(2,1)} %refs_3_.3) | copy-start | bytes 393220
  38.4 9.1 %copy-start.10 = (bf16[64,1024]{1,0:T(8,128)(2,1)S(1)}, bf16[64,1024]{1,0:T(8,128)(2,1)}, u32[]{:S(2)}) copy-start(bf16[64,1024]{1,0:T(8,128)(2,1)} %refs_4_.3) | copy-start | bytes 393220
  38.4 9.1 %copy-start.11 = (bf16[1024,64]{0,1:T(8,128)(2,1)S(1)}, bf16[1024,64]{0,1:T(8,128)(2,1)}, u32[]{:S(2)}) copy-start(bf16[1024,64]{0,1:T(8,128)(2,1)} %param.20) | copy-start | bytes 393220
  38.4 7.8 %collective-permute-start.7 = (bf16[2,3,128,1024]{3,2,1,0:T(8,128)(2,1)S(1)}, bf16[2,3,128,1024]{3,2,1,0:T(8,128)(2,1)S(1)}, u32[]{:S(2)}, u32[]{:S(2)}) collective-permute-start(bf16[2,3,128,1024]{3,2,1,0:T(8,128)(2,1)S(1)} %pair.2), channel_id=1, source_target_pairs={{0,16},{16,0},{1,17},{17,1},{2,18},{18,2},{3,19},{19,3},{4,20},{20... | collective-permute-start | bytes 4718600 | tf_op jit(solution)/shard_map/ppermute | solution.py:139
  44.0 3.5 %collective-permute-start.8 = (bf16[2,3,128,1024]{3,2,1,0:T(8,128)(2,1)S(1)}, bf16[2,3,128,1024]{3,2,1,0:T(8,128)(2,1)S(1)}, u32[]{:S(2)}, u32[]{:S(2)}) collective-permute-start(bf16[2,3,128,1024]{3,2,1,0:T(8,128)(2,1)S(1)} %pair.3), channel_id=1, source_target_pairs={{0,16},{16,0},{1,17},{17,1},{2,18},{18,2},{3,19},{19,3},{4,20},{20... | collective-permute-start | bytes 4718600 | tf_op jit(solution)/shard_map/ppermute | solution.py:139
  44.1 20.0 %collective-permute-start.3 = (bf16[3,128,1024]{2,1,0:T(8,128)(2,1)S(1)}, bf16[3,128,1024]{2,1,0:T(8,128)(2,1)S(1)}, u32[]{:S(2)}, u32[]{:S(2)}) collective-permute-start(bf16[3,128,1024]{2,1,0:T(8,128)(2,1)S(1)} %collective-permute-done.refs_1_.first.refs_10_), channel_id=1, source_target_pairs={{0,8},{4,12},{8,0},{12,4},{1,9},{5,13},{9,1},{13,5},{2,10},{6,14},... | collective-permute-start | bytes 2359304 | tf_op jit(solution)/shard_map/ppermute | solution.py:139
  45.7 19.6 %collective-permute-start.4 = (bf16[3,128,1024]{2,1,0:T(8,128)(2,1)S(1)}, bf16[3,128,1024]{2,1,0:T(8,128)(2,1)S(1)}, u32[]{:S(2)}, u32[]{:S(2)}) collective-permute-start(bf16[3,128,1024]{2,1,0:T(8,128)(2,1)S(1)} %collective-permute-done.1.refs_2_.second.refs_13_), channel_id=1, source_target_pairs={{0,4},{4,0},{8,12},{12,8},{1,5},{5,1},{9,13},{13,9},{2,6},{6,2},{1... | collective-permute-start | bytes 2359304 | tf_op jit(solution)/shard_map/ppermute | solution.py:139
  56.8 1.6 %copy-start.18 = (bf16[1536,1024]{1,0:T(8,128)(2,1)}, bf16[1536,1024]{1,0:T(8,128)(2,1)S(1)}, u32[]{:S(2)}) copy-start(bf16[1536,1024]{1,0:T(8,128)(2,1)S(1)} %get-tuple-element.55.refs_12_) | copy-start | bytes 9437188
  58.5 14.1 %copy-start.12 = (bf16[2048,1024]{1,0:T(8,128)(2,1)}, bf16[2048,1024]{1,0:T(8,128)(2,1)S(1)}, u32[]{:S(2)}) copy-start(bf16[2048,1024]{1,0:T(8,128)(2,1)S(1)} %get-tuple-element.53.gate.refs_10_) | copy-start | bytes 12582916
  58.5 14.1 %copy-start.15 = (bf16[2048,1024]{1,0:T(8,128)(2,1)}, bf16[2048,1024]{1,0:T(8,128)(2,1)S(1)}, u32[]{:S(2)}) copy-start(bf16[2048,1024]{1,0:T(8,128)(2,1)S(1)} %get-tuple-element.54.up.refs_11_) | copy-start | bytes 12582916
  65.3 1.0 copy-start.8
  65.3 2.3 %collective-permute-start.10 = (bf16[3,128,1024]{2,1,0:T(8,128)(2,1)S(1)}, bf16[3,128,1024]{2,1,0:T(8,128)(2,1)S(1)}, u32[]{:S(2)}, u32[]{:S(2)}) collective-permute-start(bf16[3,128,1024]{2,1,0:T(8,128)(2,1)S(1)} %get-tuple-element.52.refs_1_.refs_7_), channel_id=1, source_target_pairs={{0,16},{16,0},{1,17},{17,1},{2,18},{18,2},{3,19},{19,3},{4,20},{20... | collective-permute-start | bytes 2359304 | tf_op jit(solution)/shard_map/ppermute | solution.py:139
  65.3 3.4 %collective-permute-start.9 = (bf16[3,128,1024]{2,1,0:T(8,128)(2,1)S(1)}, bf16[3,128,1024]{2,1,0:T(8,128)(2,1)S(1)}, u32[]{:S(2)}, u32[]{:S(2)}) collective-permute-start(bf16[3,128,1024]{2,1,0:T(8,128)(2,1)S(1)} %get-tuple-element.51.refs_0_.refs_6_), channel_id=1, source_target_pairs={{0,16},{16,0},{1,17},{17,1},{2,18},{18,2},{3,19},{19,3},{4,20},{20... | collective-permute-start | bytes 2359304 | tf_op jit(solution)/shard_map/ppermute | solution.py:139
  72.5 2.1 %copy-start.21 = (f32[512,128]{1,0:T(8,128)}, f32[512,128]{1,0:T(8,128)S(1)}, u32[]{:S(2)}) copy-start(f32[512,128]{1,0:T(8,128)S(1)} %get-tuple-element.62.low.refs_6_) | copy-start | bytes 786436
  72.6 6.0 %copy-start.1 = (bf16[1024,2048]{1,0:T(8,128)(2,1)S(1)}, bf16[1024,2048]{1,0:T(8,128)(2,1)}, u32[]{:S(2)}) copy-start(bf16[1024,2048]{1,0:T(8,128)(2,1)} %refs_8_.1) | copy-start | bytes 12582916
  72.6 6.0 %copy-start.3 = (bf16[1024,2048]{1,0:T(8,128)(2,1)S(1)}, bf16[1024,2048]{1,0:T(8,128)(2,1)}, u32[]{:S(2)}) copy-start(bf16[1024,2048]{1,0:T(8,128)(2,1)} %refs_9_.1) | copy-start | bytes 12582916
  72.6 6.0 %copy-start.19 = (bf16[1536,1024]{1,0:T(8,128)(2,1)S(1)}, bf16[1536,1024]{1,0:T(8,128)(2,1)}, u32[]{:S(2)}) copy-start(bf16[1536,1024]{1,0:T(8,128)(2,1)} %copy-done.18) | copy-start | bytes 9437188
  74.6 26.9 %collective-permute-start.12 = (bf16[512,512]{1,0:T(8,128)(2,1)S(1)}, bf16[512,512]{1,0:T(8,128)(2,1)S(1)}, u32[]{:S(2)}, u32[]{:S(2)}) collective-permute-start(bf16[512,512]{1,0:T(8,128)(2,1)S(1)} %token_grad.6.refs_15_.refs_4_.refs_12_), channel_id=1, source_target_pairs={{0,1},{3,2},{4,5},{7,6},{8,9},{11,10},{12,13},{15,14},{16,17},{19,... | collective-permute-start | bytes 1572872 | tf_op jit(solution)/shard_map/ppermute | solution.py:806
  78.6 2.2 %copy-start.13 = (bf16[2048,1024]{1,0:T(8,128)(2,1)S(1)}, bf16[2048,1024]{1,0:T(8,128)(2,1)}, u32[]{:S(2)}) copy-start(bf16[2048,1024]{1,0:T(8,128)(2,1)} %copy-done.12) | copy-start | bytes 12582916
  80.8 2.2 %copy-start.16 = (bf16[2048,1024]{1,0:T(8,128)(2,1)S(1)}, bf16[2048,1024]{1,0:T(8,128)(2,1)}, u32[]{:S(2)}) copy-start(bf16[2048,1024]{1,0:T(8,128)(2,1)} %copy-done.15) | copy-start | bytes 12582916
  93.2 4.2 %copy-start.5 = (bf16[192,1024]{1,0:T(8,128)(2,1)S(1)}, bf16[192,1024]{1,0:T(8,128)(2,1)}, u32[]{:S(2)}) copy-start(bf16[192,1024]{1,0:T(8,128)(2,1)} %copy-done.4) | copy-start | bytes 1179652
  93.2 4.2 %copy-start.22 = (f32[512,128]{1,0:T(8,128)S(1)}, f32[512,128]{1,0:T(8,128)}, u32[]{:S(2)}) copy-start(f32[512,128]{1,0:T(8,128)} %copy-done.21) | copy-start | bytes 786436
  95.2 14.2 %collective-permute-start.11 = (bf16[512,512]{1,0:T(8,128)(2,1)S(1)}, bf16[512,512]{1,0:T(8,128)(2,1)S(1)}, u32[]{:S(2)}, u32[]{:S(2)}) collective-permute-start(bf16[512,512]{1,0:T(8,128)(2,1)S(1)} %token_grad.7.refs_5_.refs_4_.refs_13_), channel_id=1, source_target_pairs={{0,1},{3,2},{4,5},{7,6},{8,9},{11,10},{12,13},{15,14},{16,17},{19,... | collective-permute-start | bytes 1572872 | tf_op jit(solution)/shard_map/ppermute | solution.py:806
  97.4 4.2 %copy-start.14 = (bf16[2048,1024]{1,0:T(8,128)(2,1)S(1)}, bf16[2048,1024]{1,0:T(8,128)(2,1)}, u32[]{:S(2)}) copy-start(bf16[2048,1024]{1,0:T(8,128)(2,1)} %copy-done.12) | copy-start | bytes 12582916
  97.4 4.2 %copy-start.17 = (bf16[2048,1024]{1,0:T(8,128)(2,1)S(1)}, bf16[2048,1024]{1,0:T(8,128)(2,1)}, u32[]{:S(2)}) copy-start(bf16[2048,1024]{1,0:T(8,128)(2,1)} %copy-done.15) | copy-start | bytes 12582916
  101.4 4.2 %collective-permute-start.21 = (f32[4,192,384]{2,1,0:T(8,128)S(1)}, f32[4,192,384]{2,1,0:T(8,128)S(1)}, u32[]{:S(2)}, u32[]{:S(2)}) collective-permute-start(f32[4,192,384]{2,1,0:T(8,128)S(1)} %get-tuple-element.73), channel_id=1, source_target_pairs={{0,16},{16,0},{1,17},{17,1},{2,18},{18,2},{3,19},{19,3},{4,20},{20... | collective-permute-start | bytes 3538952 | tf_op jit(solution)/shard_map/ppermute | solution.py:139
  103.5 17.1 %collective-permute-start.15 = (bf16[512,512]{1,0:T(8,128)(2,1)S(1)}, bf16[512,512]{1,0:T(8,128)(2,1)S(1)}, u32[]{:S(2)}, u32[]{:S(2)}) collective-permute-start(bf16[512,512]{1,0:T(8,128)(2,1)S(1)} %token_grad.8.refs_5_), channel_id=1, source_target_pairs={{0,1},{1,2},{4,5},{5,6},{8,9},{9,10},{12,13},{13,14},{16,17},{17,1... | collective-permute-start | bytes 1572872 | tf_op jit(solution)/shard_map/ppermute | solution.py:806
  105.0 15.6 %collective-permute-start.16 = (bf16[512,512]{1,0:T(8,128)(2,1)S(1)}, bf16[512,512]{1,0:T(8,128)(2,1)S(1)}, u32[]{:S(2)}, u32[]{:S(2)}) collective-permute-start(bf16[512,512]{1,0:T(8,128)(2,1)S(1)} %token_grad.8.refs_5_), channel_id=1, source_target_pairs={{3,2},{2,1},{7,6},{6,5},{11,10},{10,9},{15,14},{14,13},{19,18},{18... | collective-permute-start | bytes 1572872 | tf_op jit(solution)/shard_map/ppermute | solution.py:806
  106.3 10.1 %collective-permute-start.22 = (bf16[2,192,384]{2,1,0:T(8,128)(2,1)S(1)}, bf16[2,192,384]{2,1,0:T(8,128)(2,1)S(1)}, u32[]{:S(2)}, u32[]{:S(2)}) collective-permute-start(bf16[2,192,384]{2,1,0:T(8,128)(2,1)S(1)} %get-tuple-element.75), channel_id=1, source_target_pairs={{0,8},{4,12},{8,0},{12,4},{1,9},{5,13},{9,1},{13,5},{2,10},{6,14},... | collective-permute-start | bytes 884744 | tf_op jit(solution)/shard_map/ppermute | solution.py:139
  111.3 20.5 %collective-permute-start.13 = (bf16[512,512]{1,0:T(8,128)(2,1)S(1)}, bf16[512,512]{1,0:T(8,128)(2,1)S(1)}, u32[]{:S(2)}, u32[]{:S(2)}) collective-permute-start(bf16[512,512]{1,0:T(8,128)(2,1)S(1)} %token_grad.9.refs_7_), channel_id=1, source_target_pairs={{0,1},{1,2},{4,5},{5,6},{8,9},{9,10},{12,13},{13,14},{16,17},{17,1... | collective-permute-start | bytes 1572872 | tf_op jit(solution)/shard_map/ppermute | solution.py:806
  115.8 16.1 %collective-permute-start.14 = (bf16[512,512]{1,0:T(8,128)(2,1)S(1)}, bf16[512,512]{1,0:T(8,128)(2,1)S(1)}, u32[]{:S(2)}, u32[]{:S(2)}) collective-permute-start(bf16[512,512]{1,0:T(8,128)(2,1)S(1)} %token_grad.9.refs_7_), channel_id=1, source_target_pairs={{3,2},{2,1},{7,6},{6,5},{11,10},{10,9},{15,14},{14,13},{19,18},{18... | collective-permute-start | bytes 1572872 | tf_op jit(solution)/shard_map/ppermute | solution.py:806
  117.1 11.5 %collective-permute-start.23 = (bf16[1,192,384]{2,1,0:T(8,128)(2,1)S(1)}, bf16[1,192,384]{2,1,0:T(8,128)(2,1)S(1)}, u32[]{:S(2)}, u32[]{:S(2)}) collective-permute-start(bf16[1,192,384]{2,1,0:T(8,128)(2,1)S(1)} %get-tuple-element.77), channel_id=1, source_target_pairs={{0,4},{4,0},{8,12},{12,8},{1,5},{5,1},{9,13},{13,9},{2,6},{6,2},{1... | collective-permute-start | bytes 442376 | tf_op jit(solution)/shard_map/ppermute | solution.py:139
  122.7 20.3 %collective-permute-start.19 = (bf16[512,512]{1,0:T(8,128)(2,1)S(1)}, bf16[512,512]{1,0:T(8,128)(2,1)S(1)}, u32[]{:S(2)}, u32[]{:S(2)}) collective-permute-start(bf16[512,512]{1,0:T(8,128)(2,1)S(1)} %get-tuple-element.66.refs_7_), channel_id=1, source_target_pairs={{0,1},{1,2},{2,3},{4,5},{5,6},{6,7},{8,9},{9,10},{10,11},{12,13},{... | collective-permute-start | bytes 1572872 | tf_op jit(solution)/shard_map/ppermute | solution.py:806
  127.3 15.8 %collective-permute-start.20 = (bf16[512,512]{1,0:T(8,128)(2,1)S(1)}, bf16[512,512]{1,0:T(8,128)(2,1)S(1)}, u32[]{:S(2)}, u32[]{:S(2)}) collective-permute-start(bf16[512,512]{1,0:T(8,128)(2,1)S(1)} %get-tuple-element.69), channel_id=1, source_target_pairs={{3,2},{2,1},{1,0},{7,6},{6,5},{5,4},{11,10},{10,9},{9,8},{15,14},{... | collective-permute-start | bytes 1572872 | tf_op jit(solution)/shard_map/ppermute | solution.py:806
  129.3 10.5 %collective-permute-start.27 = (f32[192,128]{1,0:T(8,128)S(1)}, f32[192,128]{1,0:T(8,128)S(1)}, u32[]{:S(2)}, u32[]{:S(2)}) collective-permute-start(f32[192,128]{1,0:T(8,128)S(1)} %get-tuple-element.82), channel_id=1, source_target_pairs={{0,4},{4,0},{8,12},{12,8},{1,5},{5,1},{9,13},{13,9},{2,6},{6,2},{1... | collective-permute-start | bytes 294920 | tf_op jit(solution)/shard_map/ppermute | solution.py:139
  134.0 20.3 %collective-permute-start.17 = (bf16[512,512]{1,0:T(8,128)(2,1)S(1)}, bf16[512,512]{1,0:T(8,128)(2,1)S(1)}, u32[]{:S(2)}, u32[]{:S(2)}) collective-permute-start(bf16[512,512]{1,0:T(8,128)(2,1)S(1)} %get-tuple-element.67.refs_6_), channel_id=1, source_target_pairs={{0,1},{1,2},{2,3},{4,5},{5,6},{6,7},{8,9},{9,10},{10,11},{12,13},{... | collective-permute-start | bytes 1572872 | tf_op jit(solution)/shard_map/ppermute | solution.py:806
  138.5 15.8 %collective-permute-start.18 = (bf16[512,512]{1,0:T(8,128)(2,1)S(1)}, bf16[512,512]{1,0:T(8,128)(2,1)S(1)}, u32[]{:S(2)}, u32[]{:S(2)}) collective-permute-start(bf16[512,512]{1,0:T(8,128)(2,1)S(1)} %get-tuple-element.68.refs_7_), channel_id=1, source_target_pairs={{3,2},{2,1},{1,0},{7,6},{6,5},{5,4},{11,10},{10,9},{9,8},{15,14},{... | collective-permute-start | bytes 1572872 | tf_op jit(solution)/shard_map/ppermute | solution.py:806
  139.8 9.5 %collective-permute-start.28 = (f32[2,192,128]{2,1,0:T(8,128)S(1)}, f32[2,192,128]{2,1,0:T(8,128)S(1)}, u32[]{:S(2)}, u32[]{:S(2)}) collective-permute-start(f32[2,192,128]{2,1,0:T(8,128)S(1)} %pad_maximum_fusion.2), channel_id=1, source_target_pairs={{0,8},{4,12},{8,0},{12,4},{1,9},{5,13},{9,1},{13,5},{2,10},{6,14},... | collective-permute-start | bytes 589832 | tf_op jit(solution)/shard_map/ppermute | solution.py:139
  145.9 11.2 %collective-permute-start.24 = (bf16[64,192]{1,0:T(8,128)(2,1)S(1)}, bf16[64,192]{1,0:T(8,128)(2,1)S(1)}, u32[]{:S(2)}, u32[]{:S(2)}) collective-permute-start(bf16[64,192]{1,0:T(8,128)(2,1)S(1)} %get-tuple-element.79), channel_id=1, source_target_pairs={{0,1},{1,0},{2,3},{3,2},{4,5},{5,4},{6,7},{7,6},{8,9},{9,8},{10,11... | collective-permute-start | bytes 73736 | tf_op jit(solution)/shard_map/ppermute | solution.py:139
  148.5 8.7 %collective-permute-start.25 = (bf16[64,192]{1,0:T(8,128)(2,1)S(1)}, bf16[64,192]{1,0:T(8,128)(2,1)S(1)}, u32[]{:S(2)}, u32[]{:S(2)}) collective-permute-start(bf16[64,192]{1,0:T(8,128)(2,1)S(1)} %get-tuple-element.80), channel_id=1, source_target_pairs={{0,2},{1,3},{2,0},{3,1},{4,6},{5,7},{6,4},{7,5},{8,10},{9,11},{10,... | collective-permute-start | bytes 73736 | tf_op jit(solution)/shard_map/ppermute | solution.py:139
  149.4 9.2 %collective-permute-start.26 = (bf16[64,192]{1,0:T(8,128)(2,1)S(1)}, bf16[64,192]{1,0:T(8,128)(2,1)S(1)}, u32[]{:S(2)}, u32[]{:S(2)}) collective-permute-start(bf16[64,192]{1,0:T(8,128)(2,1)S(1)} %get-tuple-element.81), channel_id=1, source_target_pairs={{0,3},{1,2},{2,1},{3,0},{4,7},{5,6},{6,5},{7,4},{8,11},{9,10},{10,... | collective-permute-start | bytes 73736 | tf_op jit(solution)/shard_map/ppermute | solution.py:139
  154.3 5.4 %collective-permute-start.29 = (f32[4,192,128]{2,1,0:T(8,128)S(1)}, f32[4,192,128]{2,1,0:T(8,128)S(1)}, u32[]{:S(2)}, u32[]{:S(2)}) collective-permute-start(f32[4,192,128]{2,1,0:T(8,128)S(1)} %pad_maximum_fusion.1.near), channel_id=1, source_target_pairs={{0,16},{16,0},{1,17},{17,1},{2,18},{18,2},{3,19},{19,3},{4,20},{20... | collective-permute-start | bytes 1179656 | tf_op jit(solution)/shard_map/ppermute | solution.py:139

commit v7 on v4

--- a/solution.py
+++ b/solution.py
@@ -12,8 +12,8 @@
 MEBIBYTE = 1024 * 1024
 COST = 1
 HALVES = 2
-COSTS = {"sums": 1, "pair": 1, "small": 1, "token": 20 * 10**9, "adapter": 20 * 10**9, "last": 10**11}
-LIMITS = {"low": 6, "sums": 32, "last": 14, "token": 8, "adapter": 12, "small": 4}
+COSTS = {"sums": 1, "pair": 1, "small": 10**10, "token": 20 * 10**9, "adapter": 20 * 10**9, "last": 10**11}
+LIMITS = {"low": 6, "sums": 25, "last": 14, "token": 8, "adapter": 12, "small": 4}
 TILE = 512
 STRIP = 256
 QUARTER_ORDER = ((3, 2, 1, 0), (0, 3, 2, 1), (3, 0, 1, 2), (0, 1, 2, 3))
@@ -767,7 +767,7 @@
             turned,
             down_in,
         ],
-        [came[0], *first],
+        first,
     )
     keep, send = halve(here, keep, flip(send, "cuts", 1))
     keep, send = halve(here, keep, flip(send, "fsdp", 2))
@@ -804,7 +804,7 @@
                 [*states[half][1:], factor, *full, *tail],
                 width // quarters,
                 [from_left[half], from_right[half]],
-                [] if half else partial[1],
+                [narrow_turned] if half else partial[1],
                 results[:],
             )
         )

time: 157 us -> 156 us (level)
  waiting for transfers between devices: 33.4 us -> 40.6 us
  starting transfers between devices: 53.9 us -> 47.5 us
  Pallas kernels: 58.8 us -> 56.9 us
    ppermute x21, waiting for transfers between devices: 25.6 us -> 31.8 us  [flip(): return lax.ppermute(array, axis, [(i, i ^ bit) for i in range(size)])]
    ppermute x10, starting transfers between devices: 30.7 us -> 26.9 us  [square_plane(): shift = lambda array, pairs: lax.ppermute(array, 'tp', pairs)]
    pallas_call x1, Pallas kernels: 18.1 us -> 15.4 us  [width_sums(): pl.pallas_call(functools.partial(sums_kernel, masks, order, len(arrays),...]
    ppermute x21, starting transfers between devices: 23.2 us -> 20.6 us  [flip(): return lax.ppermute(array, axis, [(i, i ^ bit) for i in range(size)])]
    unnamed x52 -> x36, local copies, waits for them, and re-layouts: 9.21 us -> 9.65 us
  transfers between devices with their start and end apart: 31 -> 31, of which waited for: 11 -> 15; matrix products, arithmetic and copies ran while one was open for 0% -> 0% of each run, Pallas kernels for 31% -> 29%
where the time goes in v7:
time: 156 us
  Pallas kernels  56.9 us (36%)
  starting transfers between devices  47.5 us (30%)
  waiting for transfers between devices  40.6 us (26%)
  local copies, waits for them, and re-layouts  9.65 us (6%)
    ppermute x21, waiting for transfers between devices, flip(): return lax.ppermute(array, axis, [(i, i ^ bit) for i in range(size)])  31.8 us
    pallas_call x16, Pallas kernels, vmem_call(): pl.pallas_call(kernel, in_specs=[pl.BlockSpec(memory_space=pltpu.SMEM)] *...  29.4 us
    ppermute x10, starting transfers between devices, square_plane(): shift = lambda array, pairs: lax.ppermute(array, 'tp', pairs)  26.9 us
    ppermute x21, starting transfers between devices, flip(): return lax.ppermute(array, axis, [(i, i ^ bit) for i in range(size)])  20.6 us
    pallas_call x1, Pallas kernels, width_sums(): pl.pallas_call(functools.partial(sums_kernel, masks, order, len(arrays),...  15.4 us
    unnamed x36, local copies, waits for them, and re-layouts  9.65 us
    ppermute x10, waiting for transfers between devices, square_plane(): shift = lambda array, pairs: lax.ppermute(array, 'tp', pairs)  8.84 us
    pallas_call x2, Pallas kernels, last_token_grad(): pl.pallas_call(functools.partial(token_grad_kernel, 'last', step), grid=(...  5.72 us
  transfers between devices with their start and end apart: 31, of which 15 were waited for; matrix products, arithmetic and copies ran while one was open for 0% of the time, Pallas kernels for 29%

profile of v7, /device:TPU:0, one launch (start us, length us, event | category | flops | bytes accessed | tf_op | source)
XLA Modules:
  0.0 155.9 jit_solution(11357383904687601948)
XLA Ops:
  0.6 2.3 %own_units.1 = (bf16[3,128,1024]{2,1,0:T(8,128)(2,1)S(1)}, bf16[3,128,1024]{2,1,0:T(8,128)(2,1)}) custom-call(bf16[256,1024]{1,0:T(8,128)(2,1)} %gate.1, bf16[256,1024]{1,0:T(8,128)(2,1)} %up.1, bf16[1024,256]{1,0:T(8,128)(2,1)} %down.1), custom_call_target="tpu_custom_call" | custom-call | flops 1048576 | tf_op jit(solution)/shard_map/own_units/pallas_call | solution.py:243
  2.9 3.0 %collective-permute-start = (bf16[3,128,1024]{2,1,0:T(8,128)(2,1)S(1)}, bf16[3,128,1024]{2,1,0:T(8,128)(2,1)S(1)}, u32[]{:S(2)}, u32[]{:S(2)}) collective-permute-start(bf16[3,128,1024]{2,1,0:T(8,128)(2,1)S(1)} %get-tuple-element.44.refs_8_), channel_id=1, source_target_pairs={{0,4},{4,0},{8,12},{12,8},{1,5},{5,1},{9,13},{13,9},{2,6},{6,2},{1... | collective-permute-start | bytes 2359304 | tf_op jit(solution)/shard_map/ppermute | solution.py:139
  5.9 1.5 collective-permute-start.1
  7.4 0.5 collective-permute-start.3
  7.9 0.5 collective-permute-start.4
  8.6 15.7 %collective-permute-done.refs_1_.first.refs_10_ = bf16[3,128,1024]{2,1,0:T(8,128)(2,1)S(1)} collective-permute-done((bf16[3,128,1024]{2,1,0:T(8,128)(2,1)S(1)}, bf16[3,128,1024]{2,1,0:T(8,128)(2,1)S(1)}, u32[]{:S(2)}, u32[]{:S(2)}) %collective-permute-start) | collective-permute-done | bytes 786464 | tf_op jit(solution)/shard_map/ppermute | solution.py:139
  24.3 2.1 %collective-permute-start.5 = (bf16[3,128,1024]{2,1,0:T(8,128)(2,1)S(1)}, bf16[3,128,1024]{2,1,0:T(8,128)(2,1)S(1)}, u32[]{:S(2)}, u32[]{:S(2)}) collective-permute-start(bf16[3,128,1024]{2,1,0:T(8,128)(2,1)S(1)} %get-tuple-element.44.refs_8_), channel_id=1, source_target_pairs={{0,8},{4,12},{8,0},{12,4},{1,9},{5,13},{9,1},{13,5},{2,10},{6,14},... | collective-permute-start | bytes 2359304 | tf_op jit(solution)/shard_map/ppermute | solution.py:139
  26.4 2.2 %copy-done = bf16[1024,2048]{1,0:T(8,128)(2,1)S(1)} copy-done((bf16[1024,2048]{1,0:T(8,128)(2,1)S(1)}, bf16[1024,2048]{1,0:T(8,128)(2,1)}, u32[]{:S(2)}) %copy-start) | copy-done | bytes 4194328
  28.6 2.2 %copy-done.2 = bf16[1024,2048]{1,0:T(8,128)(2,1)S(1)} copy-done((bf16[1024,2048]{1,0:T(8,128)(2,1)S(1)}, bf16[1024,2048]{1,0:T(8,128)(2,1)}, u32[]{:S(2)}) %copy-start.2) | copy-done | bytes 4194328
  30.8 0.9 copy-done.6
  31.7 0.9 copy-done.8
  32.7 0.9 copy-done.14
  33.6 4.1 %low_rank_values.1 = (bf16[1024,64]{1,0:T(8,128)(2,1)S(1)}, bf16[1024,64]{1,0:T(8,128)(2,1)S(1)}, bf16[1024,64]{1,0:T(8,128)(2,1)S(1)}, bf16[192,1024]{1,0:T(8,128)(2,1)S(1)}) custom-call(bf16[1024,2048]{1,0:T(8,128)(2,1)S(1)} %copy-done, bf16[1024,2048]{1,0:T(8,128)(2,1)S(1)} %copy-done.2, bf16[64,2048]{1,0:T(8,128)(2,1)S(1)} %bitcast.11, ...), custom_call_target="tpu_custom_call" | custom-call | flops 64424509440 | tf_op jit(solution)/shard_map/low_rank_values/pallas_call | solution.py:201
  38.0 2.3 %collective-permute-done.4.first.refs_11_ = bf16[3,128,1024]{2,1,0:T(8,128)(2,1)S(1)} collective-permute-done((bf16[3,128,1024]{2,1,0:T(8,128)(2,1)}, bf16[3,128,1024]{2,1,0:T(8,128)(2,1)S(1)}, u32[]{:S(2)}, u32[]{:S(2)}) %collective-permute-start.4) | collective-permute-done | bytes 786464 | tf_op jit(solution)/shard_map/ppermute | solution.py:139
  40.3 1.9 %collective-permute-done.5.second.refs_12_ = bf16[3,128,1024]{2,1,0:T(8,128)(2,1)S(1)} collective-permute-done((bf16[3,128,1024]{2,1,0:T(8,128)(2,1)S(1)}, bf16[3,128,1024]{2,1,0:T(8,128)(2,1)S(1)}, u32[]{:S(2)}, u32[]{:S(2)}) %collective-permute-start.5) | collective-permute-done | bytes 786464 | tf_op jit(solution)/shard_map/ppermute | solution.py:139
  42.4 1.5 collective-permute-start.8
  43.9 1.5 collective-permute-start.9
  45.8 0.8 copy-done.16
  47.0 15.4 %width_sums.1 = (f32[512,1024]{1,0:T(8,128)S(1)}, f32[512,1024]{1,0:T(8,128)S(1)}, f32[512,1024]{1,0:T(8,128)S(1)}, f32[512,1024]{1,0:T(8,128)S(1)}, f32[512,102...) custom-call(s32[2]{0:T(128)S(1)} %pad_add_fusion.refs_0_.here, ...), custom_call_target="tpu_custom_call" | custom-call | flops 1 | tf_op jit(solution)/shard_map/width_sums/pallas_call | solution.py:377
  62.5 1.0 collective-permute-done.9.refs_1_
  63.5 0.5 collective-permute-start.11
  64.1 1.7 %collective-permute-done.10.refs_2_ = bf16[3,128,1024]{2,1,0:T(8,128)(2,1)S(1)} collective-permute-done((bf16[3,128,1024]{2,1,0:T(8,128)(2,1)S(1)}, bf16[3,128,1024]{2,1,0:T(8,128)(2,1)S(1)}, u32[]{:S(2)}, u32[]{:S(2)}) %collective-permute-start.10) | collective-permute-done | bytes 786464 | tf_op jit(solution)/shard_map/ppermute | solution.py:139
  65.8 1.1 collective-permute-done.11.refs_3_
  66.9 3.8 %hidden_and_grads.2 = (bf16[512,1024]{1,0:T(8,128)(2,1)S(1)}, bf16[512,1024]{1,0:T(8,128)(2,1)S(1)}, bf16[512,1024]{1,0:T(8,128)(2,1)S(1)}, f32[512,128]{1,0:T(8,128)S(1)}) custom-call(s32[2]{0:T(128)S(1)} %pad_add_fusion.refs_0_.here, bf16[1024,512]{1,0:T(8,128)(2,1)S(1)} %get-tuple-element.50.left, bf16[1024,512]{1,0:T(8,128)(2,1)S(1)} %get-tuple-element.51.back, ...), custom_call_target="tpu_custom_call" | custom-call | flops 99999997952 | tf_op jit(solution)/shard_map/hidden_and_grads/pallas_call | solution.py:147
  70.8 2.3 %token_grad.6.refs_7_.refs_4_.refs_12_ = bf16[512,512]{1,0:T(8,128)(2,1)S(1)} custom-call(s32[2]{0:T(128)S(1)} %pad_add_fusion.refs_0_.here, bf16[512,1024]{1,0:T(8,128)(2,1)S(1)} %get-tuple-element.60.gate_grad.refs_2_, bf16[512,1024]{1,0:T(8,128)(2,1)S(1)} %get-tuple-element.61.up_grad.refs_4_, f32[512,128]{1,0:T(8,128)S(1)} %get-tuple-element.62.low.refs_6_, ...), custom_call_target="tpu_custom_call" | custom-call | flops 20000000000 | tf_op jit(solution)/shard_map/token_grad/pallas_call | solution.py:147
  73.1 3.5 %collective-permute-start.13 = (bf16[512,512]{1,0:T(8,128)(2,1)S(1)}, bf16[512,512]{1,0:T(8,128)(2,1)S(1)}, u32[]{:S(2)}, u32[]{:S(2)}) collective-permute-start(bf16[512,512]{1,0:T(8,128)(2,1)S(1)} %token_grad.6.refs_7_.refs_4_.refs_12_), channel_id=1, source_target_pairs={{0,1},{3,2},{4,5},{7,6},{8,9},{11,10},{12,13},{15,14},{16,17},{19,... | collective-permute-start | bytes 1572872 | tf_op jit(solution)/shard_map/ppermute | solution.py:734
  76.6 3.9 %hidden_and_grads.3 = (bf16[512,1024]{1,0:T(8,128)(2,1)S(1)}, bf16[512,1024]{1,0:T(8,128)(2,1)S(1)}, bf16[512,1024]{1,0:T(8,128)(2,1)S(1)}, f32[512,128]{1,0:T(8,128)S(1)}) custom-call(s32[2]{0:T(128)S(1)} %pad_add_fusion.refs_0_.here, bf16[1024,512]{1,0:T(8,128)(2,1)S(1)} %get-tuple-element.50.left, bf16[1024,512]{1,0:T(8,128)(2,1)S(1)} %get-tuple-element.51.back, ...), custom_call_target="tpu_custom_call" | custom-call | flops 99999997952 | tf_op jit(solution)/shard_map/hidden_and_grads/pallas_call | solution.py:147
  80.5 2.0 %token_grad.7.refs_5_.refs_4_.refs_13_ = bf16[512,512]{1,0:T(8,128)(2,1)S(1)} custom-call(s32[2]{0:T(128)S(1)} %pad_add_fusion.refs_0_.here, bf16[512,1024]{1,0:T(8,128)(2,1)S(1)} %get-tuple-element.65.gate_grad.refs_3_, bf16[512,1024]{1,0:T(8,128)(2,1)S(1)} %get-tuple-element.66.up_grad.refs_5_, f32[512,128]{1,0:T(8,128)S(1)} %get-tuple-element.67.low.refs_7_, ...), custom_call_target="tpu_custom_call" | custom-call | flops 20000000000 | tf_op jit(solution)/shard_map/token_grad/pallas_call | solution.py:147
  82.5 1.5 collective-permute-start.12
  84.0 4.1 %adapter_grads.1 = (f32[4,192,384]{2,1,0:T(8,128)S(1)}, f32[4,192,384]{2,1,0:T(8,128)S(1)}) custom-call(s32[2]{0:T(128)S(1)} %pad_add_fusion.refs_0_.here, bf16[512,1024]{1,0:T(8,128)(2,1)S(1)} %get-tuple-element.72.refs_0_, bf16[512,1024]{1,0:T(8,128)(2,1)S(1)} %get-tuple-element.73.refs_1_, bf16[512,1024]{1,0:T(8,128)(2,1)S(1)} %get-tuple-element.60.gate_grad.refs_2_, ...), custom_call_target="tpu_custom_call" | custom-call | flops 20000000000 | tf_op jit(solution)/shard_map/adapter_grads/pallas_call | solution.py:147
  88.2 0.7 collective-permute-done.13.refs_4_
  88.8 2.1 %token_grad.8.refs_5_ = bf16[512,512]{1,0:T(8,128)(2,1)S(1)} custom-call(s32[2]{0:T(128)S(1)} %pad_add_fusion.refs_0_.here, bf16[512,1024]{1,0:T(8,128)(2,1)S(1)} %get-tuple-element.60.gate_grad.refs_2_, bf16[512,1024]{1,0:T(8,128)(2,1)S(1)} %get-tuple-element.61.up_grad.refs_4_, f32[512,128]{1,0:T(8,128)S(1)} %get-tuple-element.62.low.refs_6_, ...), custom_call_target="tpu_custom_call" | custom-call | flops 20000000000 | tf_op jit(solution)/shard_map/token_grad/pallas_call | solution.py:147
  90.9 4.4 %collective-permute-start.16 = (bf16[512,512]{1,0:T(8,128)(2,1)S(1)}, bf16[512,512]{1,0:T(8,128)(2,1)S(1)}, u32[]{:S(2)}, u32[]{:S(2)}) collective-permute-start(bf16[512,512]{1,0:T(8,128)(2,1)S(1)} %token_grad.8.refs_5_), channel_id=1, source_target_pairs={{0,1},{1,2},{4,5},{5,6},{8,9},{9,10},{12,13},{13,14},{16,17},{17,1... | collective-permute-start | bytes 1572872 | tf_op jit(solution)/shard_map/ppermute | solution.py:734
  95.3 0.7 collective-permute-start.17
  96.0 0.7 halve.2
  96.7 0.6 collective-permute-start.23
  97.3 2.8 %collective-permute-done.12.refs_4_ = bf16[512,512]{1,0:T(8,128)(2,1)S(1)} collective-permute-done((bf16[512,512]{1,0:T(8,128)(2,1)S(1)}, bf16[512,512]{1,0:T(8,128)(2,1)S(1)}, u32[]{:S(2)}, u32[]{:S(2)}) %collective-permute-start.12) | collective-permute-done | bytes 524320 | tf_op jit(solution)/shard_map/ppermute | solution.py:734
  100.1 2.0 %token_grad.9.refs_7_ = bf16[512,512]{1,0:T(8,128)(2,1)S(1)} custom-call(s32[2]{0:T(128)S(1)} %pad_add_fusion.refs_0_.here, bf16[512,1024]{1,0:T(8,128)(2,1)S(1)} %get-tuple-element.65.gate_grad.refs_3_, bf16[512,1024]{1,0:T(8,128)(2,1)S(1)} %get-tuple-element.66.up_grad.refs_5_, f32[512,128]{1,0:T(8,128)S(1)} %get-tuple-element.67.low.refs_7_, ...), custom_call_target="tpu_custom_call" | custom-call | flops 20000000000 | tf_op jit(solution)/shard_map/token_grad/pallas_call | solution.py:147
  102.1 4.4 %collective-permute-start.14 = (bf16[512,512]{1,0:T(8,128)(2,1)S(1)}, bf16[512,512]{1,0:T(8,128)(2,1)S(1)}, u32[]{:S(2)}, u32[]{:S(2)}) collective-permute-start(bf16[512,512]{1,0:T(8,128)(2,1)S(1)} %token_grad.9.refs_7_), channel_id=1, source_target_pairs={{0,1},{1,2},{4,5},{5,6},{8,9},{9,10},{12,13},{13,14},{16,17},{17,1... | collective-permute-start | bytes 1572872 | tf_op jit(solution)/shard_map/ppermute | solution.py:734
  106.5 0.7 collective-permute-start.15
  107.2 0.6 halve.3
  107.8 1.6 %collective-permute-start.24 = (bf16[1,192,384]{2,1,0:T(8,128)(2,1)S(1)}, bf16[1,192,384]{2,1,0:T(8,128)(2,1)S(1)}, u32[]{:S(2)}, u32[]{:S(2)}) collective-permute-start(bf16[1,192,384]{2,1,0:T(8,128)(2,1)S(1)} %get-tuple-element.79), channel_id=1, source_target_pairs={{0,4},{4,0},{8,12},{12,8},{1,5},{5,1},{9,13},{13,9},{2,6},{6,2},{1... | collective-permute-start | bytes 442376 | tf_op jit(solution)/shard_map/ppermute | solution.py:139
  109.4 1.9 %collective-permute-done.16.refs_5_ = bf16[512,512]{1,0:T(8,128)(2,1)S(1)} collective-permute-done((bf16[512,512]{1,0:T(8,128)(2,1)S(1)}, bf16[512,512]{1,0:T(8,128)(2,1)S(1)}, u32[]{:S(2)}, u32[]{:S(2)}) %collective-permute-start.16) | collective-permute-done | bytes 524320 | tf_op jit(solution)/shard_map/ppermute | solution.py:734
  111.3 2.2 %token_grad.10 = (bf16[512,512]{1,0:T(8,128)(2,1)S(1)}, bf16[512,512]{1,0:T(8,128)(2,1)S(1)}) custom-call(s32[2]{0:T(128)S(1)} %pad_add_fusion.refs_0_.here, bf16[512,1024]{1,0:T(8,128)(2,1)S(1)} %get-tuple-element.60.gate_grad.refs_2_, bf16[512,1024]{1,0:T(8,128)(2,1)S(1)} %get-tuple-element.61.up_grad.refs_4_, ...), custom_call_target="tpu_custom_call" | custom-call | flops 20000000000 | tf_op jit(solution)/shard_map/token_grad/pallas_call | solution.py:147
  113.5 4.4 %collective-permute-start.20 = (bf16[512,512]{1,0:T(8,128)(2,1)S(1)}, bf16[512,512]{1,0:T(8,128)(2,1)S(1)}, u32[]{:S(2)}, u32[]{:S(2)}) collective-permute-start(bf16[512,512]{1,0:T(8,128)(2,1)S(1)} %get-tuple-element.68.refs_7_), channel_id=1, source_target_pairs={{0,1},{1,2},{2,3},{4,5},{5,6},{6,7},{8,9},{9,10},{10,11},{12,13},{... | collective-permute-start | bytes 1572872 | tf_op jit(solution)/shard_map/ppermute | solution.py:734
  117.9 1.6 collective-permute-start.21
  119.5 0.7 turn.1
  120.2 1.6 collective-permute-start.25
  121.8 0.8 collective-permute-done.14.refs_5_
  122.5 2.2 %token_grad.11 = (bf16[512,512]{1,0:T(8,128)(2,1)S(1)}, bf16[512,512]{1,0:T(8,128)(2,1)S(1)}) custom-call(s32[2]{0:T(128)S(1)} %pad_add_fusion.refs_0_.here, bf16[512,1024]{1,0:T(8,128)(2,1)S(1)} %get-tuple-element.65.gate_grad.refs_3_, bf16[512,1024]{1,0:T(8,128)(2,1)S(1)} %get-tuple-element.66.up_grad.refs_5_, ...), custom_call_target="tpu_custom_call" | custom-call | flops 20000000000 | tf_op jit(solution)/shard_map/token_grad/pallas_call | solution.py:147
  124.7 4.4 %collective-permute-start.18 = (bf16[512,512]{1,0:T(8,128)(2,1)S(1)}, bf16[512,512]{1,0:T(8,128)(2,1)S(1)}, u32[]{:S(2)}, u32[]{:S(2)}) collective-permute-start(bf16[512,512]{1,0:T(8,128)(2,1)S(1)} %get-tuple-element.69.refs_6_), channel_id=1, source_target_pairs={{0,1},{1,2},{2,3},{4,5},{5,6},{6,7},{8,9},{9,10},{10,11},{12,13},{... | collective-permute-start | bytes 1572872 | tf_op jit(solution)/shard_map/ppermute | solution.py:734
  129.1 1.3 collective-permute-start.19
  130.5 0.6 collective-permute-start.26
  131.0 2.7 %collective-permute-done.20.refs_4_ = bf16[512,512]{1,0:T(8,128)(2,1)S(1)} collective-permute-done((bf16[512,512]{1,0:T(8,128)(2,1)S(1)}, bf16[512,512]{1,0:T(8,128)(2,1)S(1)}, u32[]{:S(2)}, u32[]{:S(2)}) %collective-permute-start.20) | collective-permute-done | bytes 524320 | tf_op jit(solution)/shard_map/ppermute | solution.py:734
  133.8 2.9 %last_token_grad.2.refs_6_ = bf16[1024,512]{1,0:T(8,128)(2,1)} custom-call(s32[2]{0:T(128)S(1)} %pad_add_fusion.refs_0_.here, bf16[512,1024]{1,0:T(8,128)(2,1)S(1)} %get-tuple-element.60.gate_grad.refs_2_, bf16[512,1024]{1,0:T(8,128)(2,1)S(1)} %get-tuple-element.61.up_grad.refs_4_, f32[512,128]{1,0:T(8,128)S(1)} %get-tuple-element.62.low.refs_6_, ...), custom_call_target="tpu_custom_call" | custom-call | flops 20000000000 | tf_op jit(solution)/shard_map/last_token_grad/pallas_call | solution.py:495
  136.6 2.5 %collective-permute-start.28 = (bf16[64,192]{1,0:T(8,128)(2,1)S(1)}, bf16[64,192]{1,0:T(8,128)(2,1)S(1)}, u32[]{:S(2)}, u32[]{:S(2)}) collective-permute-start(bf16[64,192]{1,0:T(8,128)(2,1)S(1)} %get-tuple-element.82), channel_id=1, source_target_pairs={{0,1},{1,0},{2,3},{3,2},{4,5},{5,4},{6,7},{7,6},{8,9},{9,8},{10,11... | collective-permute-start | bytes 73736 | tf_op jit(solution)/shard_map/ppermute | solution.py:139
  139.1 1.0 collective-permute-start.29
  140.1 1.5 collective-permute-start.30
  141.6 4.0 %collective-permute-done.28.refs_0_ = bf16[64,192]{1,0:T(8,128)(2,1)S(1)} collective-permute-done((bf16[64,192]{1,0:T(8,128)(2,1)S(1)}, bf16[64,192]{1,0:T(8,128)(2,1)S(1)}, u32[]{:S(2)}, u32[]{:S(2)}) %collective-permute-start.28) | collective-permute-done | bytes 24608 | tf_op jit(solution)/shard_map/ppermute | solution.py:139
  145.9 3.3 %collective-permute-done.30.refs_2_ = bf16[64,192]{1,0:T(8,128)(2,1)S(1)} collective-permute-done((bf16[64,192]{1,0:T(8,128)(2,1)S(1)}, bf16[64,192]{1,0:T(8,128)(2,1)S(1)}, u32[]{:S(2)}, u32[]{:S(2)}) %collective-permute-start.30) | collective-permute-done | bytes 24608 | tf_op jit(solution)/shard_map/ppermute | solution.py:139
  149.2 1.2 last_sum.1
  150.4 1.5 whole.1.refs_7_
  151.9 1.1 copy-done.15
  153.1 2.8 %last_token_grad.3 = bf16[1024,512]{1,0:T(8,128)(2,1)} custom-call(s32[2]{0:T(128)S(1)} %pad_add_fusion.refs_0_.here, bf16[512,1024]{1,0:T(8,128)(2,1)S(1)} %get-tuple-element.65.gate_grad.refs_3_, bf16[512,1024]{1,0:T(8,128)(2,1)S(1)} %get-tuple-element.66.up_grad.refs_5_, ...), custom_call_target="tpu_custom_call", output_to_operand_aliasing={{}: (13, {})} | custom-call | flops 20000000000 | tf_op jit(solution)/shard_map/last_token_grad/pallas_call | solution.py:495
  (60 shorter events, 1.9 us)
Async XLA Ops:
  2.9 21.4 %collective-permute-start = (bf16[3,128,1024]{2,1,0:T(8,128)(2,1)S(1)}, bf16[3,128,1024]{2,1,0:T(8,128)(2,1)S(1)}, u32[]{:S(2)}, u32[]{:S(2)}) collective-permute-start(bf16[3,128,1024]{2,1,0:T(8,128)(2,1)S(1)} %get-tuple-element.44.refs_8_), channel_id=1, source_target_pairs={{0,4},{4,0},{8,12},{12,8},{1,5},{5,1},{9,13},{13,9},{2,6},{6,2},{1... | collective-permute-start | bytes 2359304 | tf_op jit(solution)/shard_map/ppermute | solution.py:139
  5.9 20.5 %collective-permute-start.1 = (bf16[3,128,1024]{2,1,0:T(8,128)(2,1)}, bf16[3,128,1024]{2,1,0:T(8,128)(2,1)S(1)}, u32[]{:S(2)}, u32[]{:S(2)}) collective-permute-start(bf16[3,128,1024]{2,1,0:T(8,128)(2,1)} %get-tuple-element.45.refs_9_), channel_id=1, source_target_pairs={{0,8},{4,12},{8,0},{12,4},{1,9},{5,13},{9,1},{13,5},{2,10},{6,14},... | collective-permute-start | bytes 2359304 | tf_op jit(solution)/shard_map/ppermute | solution.py:139
  7.4 18.9 %collective-permute-start.2 = (bf16[3,128,1024]{2,1,0:T(8,128)(2,1)S(1)}, bf16[3,128,1024]{2,1,0:T(8,128)(2,1)}, u32[]{:S(2)}, u32[]{:S(2)}) collective-permute-start(bf16[3,128,1024]{2,1,0:T(8,128)(2,1)S(1)} %get-tuple-element.44.refs_8_), channel_id=1, source_target_pairs={{0,16},{16,0},{1,17},{17,1},{2,18},{18,2},{3,19},{19,3},{4,20},{20... | collective-permute-start | bytes 2359304 | tf_op jit(solution)/shard_map/ppermute | solution.py:139
  7.4 18.9 %collective-permute-start.3 = (bf16[3,128,1024]{2,1,0:T(8,128)(2,1)}, bf16[3,128,1024]{2,1,0:T(8,128)(2,1)}, u32[]{:S(2)}, u32[]{:S(2)}) collective-permute-start(bf16[3,128,1024]{2,1,0:T(8,128)(2,1)} %get-tuple-element.45.refs_9_), channel_id=1, source_target_pairs={{0,16},{16,0},{1,17},{17,1},{2,18},{18,2},{3,19},{19,3},{4,20},{20... | collective-permute-start | bytes 2359304 | tf_op jit(solution)/shard_map/ppermute | solution.py:139
  7.9 32.4 %collective-permute-start.4 = (bf16[3,128,1024]{2,1,0:T(8,128)(2,1)}, bf16[3,128,1024]{2,1,0:T(8,128)(2,1)S(1)}, u32[]{:S(2)}, u32[]{:S(2)}) collective-permute-start(bf16[3,128,1024]{2,1,0:T(8,128)(2,1)} %get-tuple-element.45.refs_9_), channel_id=1, source_target_pairs={{0,4},{4,0},{8,12},{12,8},{1,5},{5,1},{9,13},{13,9},{2,6},{6,2},{1... | collective-permute-start | bytes 2359304 | tf_op jit(solution)/shard_map/ppermute | solution.py:139
  24.3 17.9 %collective-permute-start.5 = (bf16[3,128,1024]{2,1,0:T(8,128)(2,1)S(1)}, bf16[3,128,1024]{2,1,0:T(8,128)(2,1)S(1)}, u32[]{:S(2)}, u32[]{:S(2)}) collective-permute-start(bf16[3,128,1024]{2,1,0:T(8,128)(2,1)S(1)} %get-tuple-element.44.refs_8_), channel_id=1, source_target_pairs={{0,8},{4,12},{8,0},{12,4},{1,9},{5,13},{9,1},{13,5},{2,10},{6,14},... | collective-permute-start | bytes 2359304 | tf_op jit(solution)/shard_map/ppermute | solution.py:139
  26.4 2.2 %copy-start = (bf16[1024,2048]{1,0:T(8,128)(2,1)S(1)}, bf16[1024,2048]{1,0:T(8,128)(2,1)}, u32[]{:S(2)}) copy-start(bf16[1024,2048]{1,0:T(8,128)(2,1)} %refs_8_.1) | copy-start | bytes 12582916
  28.6 2.2 %copy-start.2 = (bf16[1024,2048]{1,0:T(8,128)(2,1)S(1)}, bf16[1024,2048]{1,0:T(8,128)(2,1)}, u32[]{:S(2)}) copy-start(bf16[1024,2048]{1,0:T(8,128)(2,1)} %refs_9_.1) | copy-start | bytes 12582916
  30.8 0.9 copy-start.6
  31.7 0.9 copy-start.8
  32.7 0.9 copy-start.14
  37.7 4.6 %copy-start.4 = (bf16[192,1024]{1,0:T(8,128)(2,1)}, bf16[192,1024]{1,0:T(8,128)(2,1)S(1)}, u32[]{:S(2)}) copy-start(bf16[192,1024]{1,0:T(8,128)(2,1)S(1)} %get-tuple-element.49.refs_0_.refs_10_) | copy-start | bytes 1179652
  37.9 9.2 %copy-start.10 = (bf16[64,1024]{1,0:T(8,128)(2,1)S(1)}, bf16[64,1024]{1,0:T(8,128)(2,1)}, u32[]{:S(2)}) copy-start(bf16[64,1024]{1,0:T(8,128)(2,1)} %gate_out.3) | copy-start | bytes 393220
  37.9 9.1 %copy-start.11 = (bf16[64,1024]{1,0:T(8,128)(2,1)S(1)}, bf16[64,1024]{1,0:T(8,128)(2,1)}, u32[]{:S(2)}) copy-start(bf16[64,1024]{1,0:T(8,128)(2,1)} %up_out.3) | copy-start | bytes 393220
  37.9 9.1 %copy-start.12 = (bf16[1024,64]{0,1:T(8,128)(2,1)S(1)}, bf16[1024,64]{0,1:T(8,128)(2,1)}, u32[]{:S(2)}) copy-start(bf16[1024,64]{0,1:T(8,128)(2,1)} %param.20) | copy-start | bytes 393220
  37.9 7.5 %collective-permute-start.6 = (bf16[2,3,128,1024]{3,2,1,0:T(8,128)(2,1)S(1)}, bf16[2,3,128,1024]{3,2,1,0:T(8,128)(2,1)S(1)}, u32[]{:S(2)}, u32[]{:S(2)}) collective-permute-start(bf16[2,3,128,1024]{3,2,1,0:T(8,128)(2,1)S(1)} %pair.2), channel_id=1, source_target_pairs={{0,16},{16,0},{1,17},{17,1},{2,18},{18,2},{3,19},{19,3},{4,20},{20... | collective-permute-start | bytes 4718600 | tf_op jit(solution)/shard_map/ppermute | solution.py:139
  42.3 3.5 %collective-permute-start.7 = (bf16[2,3,128,1024]{3,2,1,0:T(8,128)(2,1)S(1)}, bf16[2,3,128,1024]{3,2,1,0:T(8,128)(2,1)S(1)}, u32[]{:S(2)}, u32[]{:S(2)}) collective-permute-start(bf16[2,3,128,1024]{3,2,1,0:T(8,128)(2,1)S(1)} %pair.3), channel_id=1, source_target_pairs={{0,16},{16,0},{1,17},{17,1},{2,18},{18,2},{3,19},{19,3},{4,20},{20... | collective-permute-start | bytes 4718600 | tf_op jit(solution)/shard_map/ppermute | solution.py:139
  42.4 20.1 %collective-permute-start.8 = (bf16[3,128,1024]{2,1,0:T(8,128)(2,1)S(1)}, bf16[3,128,1024]{2,1,0:T(8,128)(2,1)S(1)}, u32[]{:S(2)}, u32[]{:S(2)}) collective-permute-start(bf16[3,128,1024]{2,1,0:T(8,128)(2,1)S(1)} %collective-permute-done.refs_1_.first.refs_10_), channel_id=1, source_target_pairs={{0,8},{4,12},{8,0},{12,4},{1,9},{5,13},{9,1},{13,5},{2,10},{6,14},... | collective-permute-start | bytes 2359304 | tf_op jit(solution)/shard_map/ppermute | solution.py:139
  43.9 19.6 %collective-permute-start.9 = (bf16[3,128,1024]{2,1,0:T(8,128)(2,1)S(1)}, bf16[3,128,1024]{2,1,0:T(8,128)(2,1)S(1)}, u32[]{:S(2)}, u32[]{:S(2)}) collective-permute-start(bf16[3,128,1024]{2,1,0:T(8,128)(2,1)S(1)} %collective-permute-done.1.refs_2_.second.refs_13_), channel_id=1, source_target_pairs={{0,4},{4,0},{8,12},{12,8},{1,5},{5,1},{9,13},{13,9},{2,6},{6,2},{1... | collective-permute-start | bytes 2359304 | tf_op jit(solution)/shard_map/ppermute | solution.py:139
  45.4 1.2 copy-start.16
  45.8 1.2 copy-start.17
  62.5 1.6 copy-start.7
  62.5 1.5 copy-start.9
  63.5 2.3 %collective-permute-start.10 = (bf16[3,128,1024]{2,1,0:T(8,128)(2,1)S(1)}, bf16[3,128,1024]{2,1,0:T(8,128)(2,1)S(1)}, u32[]{:S(2)}, u32[]{:S(2)}) collective-permute-start(bf16[3,128,1024]{2,1,0:T(8,128)(2,1)S(1)} %get-tuple-element.53.refs_0_), channel_id=1, source_target_pairs={{0,16},{16,0},{1,17},{17,1},{2,18},{18,2},{3,19},{19,3},{4,20},{20... | collective-permute-start | bytes 2359304 | tf_op jit(solution)/shard_map/ppermute | solution.py:139
  63.5 3.4 %collective-permute-start.11 = (bf16[3,128,1024]{2,1,0:T(8,128)(2,1)S(1)}, bf16[3,128,1024]{2,1,0:T(8,128)(2,1)S(1)}, u32[]{:S(2)}, u32[]{:S(2)}) collective-permute-start(bf16[3,128,1024]{2,1,0:T(8,128)(2,1)S(1)} %get-tuple-element.54.refs_1_), channel_id=1, source_target_pairs={{0,16},{16,0},{1,17},{17,1},{2,18},{18,2},{3,19},{19,3},{4,20},{20... | collective-permute-start | bytes 2359304 | tf_op jit(solution)/shard_map/ppermute | solution.py:139
  73.1 15.8 %collective-permute-start.13 = (bf16[512,512]{1,0:T(8,128)(2,1)S(1)}, bf16[512,512]{1,0:T(8,128)(2,1)S(1)}, u32[]{:S(2)}, u32[]{:S(2)}) collective-permute-start(bf16[512,512]{1,0:T(8,128)(2,1)S(1)} %token_grad.6.refs_7_.refs_4_.refs_12_), channel_id=1, source_target_pairs={{0,1},{3,2},{4,5},{7,6},{8,9},{11,10},{12,13},{15,14},{16,17},{19,... | collective-permute-start | bytes 1572872 | tf_op jit(solution)/shard_map/ppermute | solution.py:734
  80.4 3.6 %copy-start.1 = (bf16[1024,2048]{1,0:T(8,128)(2,1)S(1)}, bf16[1024,2048]{1,0:T(8,128)(2,1)}, u32[]{:S(2)}) copy-start(bf16[1024,2048]{1,0:T(8,128)(2,1)} %refs_8_.1) | copy-start | bytes 12582916
  80.4 3.6 %copy-start.3 = (bf16[1024,2048]{1,0:T(8,128)(2,1)S(1)}, bf16[1024,2048]{1,0:T(8,128)(2,1)}, u32[]{:S(2)}) copy-start(bf16[1024,2048]{1,0:T(8,128)(2,1)} %refs_9_.1) | copy-start | bytes 12582916
  80.5 3.5 %copy-start.5 = (bf16[192,1024]{1,0:T(8,128)(2,1)S(1)}, bf16[192,1024]{1,0:T(8,128)(2,1)}, u32[]{:S(2)}) copy-start(bf16[192,1024]{1,0:T(8,128)(2,1)} %copy-done.4) | copy-start | bytes 1179652
  80.5 3.5 %copy-start.13 = (bf16[1024,64]{0,1:T(8,128)(2,1)S(1)}, bf16[1024,64]{0,1:T(8,128)(2,1)}, u32[]{:S(2)}) copy-start(bf16[1024,64]{0,1:T(8,128)(2,1)} %param.20) | copy-start | bytes 393220
  82.5 17.5 %collective-permute-start.12 = (bf16[512,512]{1,0:T(8,128)(2,1)S(1)}, bf16[512,512]{1,0:T(8,128)(2,1)S(1)}, u32[]{:S(2)}, u32[]{:S(2)}) collective-permute-start(bf16[512,512]{1,0:T(8,128)(2,1)S(1)} %token_grad.7.refs_5_.refs_4_.refs_13_), channel_id=1, source_target_pairs={{0,1},{3,2},{4,5},{7,6},{8,9},{11,10},{12,13},{15,14},{16,17},{19,... | collective-permute-start | bytes 1572872 | tf_op jit(solution)/shard_map/ppermute | solution.py:734
  88.1 7.9 %collective-permute-start.22 = (f32[4,192,384]{2,1,0:T(8,128)S(1)}, f32[4,192,384]{2,1,0:T(8,128)S(1)}, u32[]{:S(2)}, u32[]{:S(2)}) collective-permute-start(f32[4,192,384]{2,1,0:T(8,128)S(1)} %get-tuple-element.75), channel_id=1, source_target_pairs={{0,16},{16,0},{1,17},{17,1},{2,18},{18,2},{3,19},{19,3},{4,20},{20... | collective-permute-start | bytes 3538952 | tf_op jit(solution)/shard_map/ppermute | solution.py:139
  90.9 20.4 %collective-permute-start.16 = (bf16[512,512]{1,0:T(8,128)(2,1)S(1)}, bf16[512,512]{1,0:T(8,128)(2,1)S(1)}, u32[]{:S(2)}, u32[]{:S(2)}) collective-permute-start(bf16[512,512]{1,0:T(8,128)(2,1)S(1)} %token_grad.8.refs_5_), channel_id=1, source_target_pairs={{0,1},{1,2},{4,5},{5,6},{8,9},{9,10},{12,13},{13,14},{16,17},{17,1... | collective-permute-start | bytes 1572872 | tf_op jit(solution)/shard_map/ppermute | solution.py:734
  95.3 16.0 %collective-permute-start.17 = (bf16[512,512]{1,0:T(8,128)(2,1)S(1)}, bf16[512,512]{1,0:T(8,128)(2,1)S(1)}, u32[]{:S(2)}, u32[]{:S(2)}) collective-permute-start(bf16[512,512]{1,0:T(8,128)(2,1)S(1)} %token_grad.8.refs_5_), channel_id=1, source_target_pairs={{3,2},{2,1},{7,6},{6,5},{11,10},{10,9},{15,14},{14,13},{19,18},{18... | collective-permute-start | bytes 1572872 | tf_op jit(solution)/shard_map/ppermute | solution.py:734
  96.7 10.5 %collective-permute-start.23 = (bf16[2,192,384]{2,1,0:T(8,128)(2,1)S(1)}, bf16[2,192,384]{2,1,0:T(8,128)(2,1)S(1)}, u32[]{:S(2)}, u32[]{:S(2)}) collective-permute-start(bf16[2,192,384]{2,1,0:T(8,128)(2,1)S(1)} %get-tuple-element.77), channel_id=1, source_target_pairs={{0,8},{4,12},{8,0},{12,4},{1,9},{5,13},{9,1},{13,5},{2,10},{6,14},... | collective-permute-start | bytes 884744 | tf_op jit(solution)/shard_map/ppermute | solution.py:139
  102.1 20.4 %collective-permute-start.14 = (bf16[512,512]{1,0:T(8,128)(2,1)S(1)}, bf16[512,512]{1,0:T(8,128)(2,1)S(1)}, u32[]{:S(2)}, u32[]{:S(2)}) collective-permute-start(bf16[512,512]{1,0:T(8,128)(2,1)S(1)} %token_grad.9.refs_7_), channel_id=1, source_target_pairs={{0,1},{1,2},{4,5},{5,6},{8,9},{9,10},{12,13},{13,14},{16,17},{17,1... | collective-permute-start | bytes 1572872 | tf_op jit(solution)/shard_map/ppermute | solution.py:734
  106.5 16.0 %collective-permute-start.15 = (bf16[512,512]{1,0:T(8,128)(2,1)S(1)}, bf16[512,512]{1,0:T(8,128)(2,1)S(1)}, u32[]{:S(2)}, u32[]{:S(2)}) collective-permute-start(bf16[512,512]{1,0:T(8,128)(2,1)S(1)} %token_grad.9.refs_7_), channel_id=1, source_target_pairs={{3,2},{2,1},{7,6},{6,5},{11,10},{10,9},{15,14},{14,13},{19,18},{18... | collective-permute-start | bytes 1572872 | tf_op jit(solution)/shard_map/ppermute | solution.py:734
  107.8 11.7 %collective-permute-start.24 = (bf16[1,192,384]{2,1,0:T(8,128)(2,1)S(1)}, bf16[1,192,384]{2,1,0:T(8,128)(2,1)S(1)}, u32[]{:S(2)}, u32[]{:S(2)}) collective-permute-start(bf16[1,192,384]{2,1,0:T(8,128)(2,1)S(1)} %get-tuple-element.79), channel_id=1, source_target_pairs={{0,4},{4,0},{8,12},{12,8},{1,5},{5,1},{9,13},{13,9},{2,6},{6,2},{1... | collective-permute-start | bytes 442376 | tf_op jit(solution)/shard_map/ppermute | solution.py:139
  113.5 20.2 %collective-permute-start.20 = (bf16[512,512]{1,0:T(8,128)(2,1)S(1)}, bf16[512,512]{1,0:T(8,128)(2,1)S(1)}, u32[]{:S(2)}, u32[]{:S(2)}) collective-permute-start(bf16[512,512]{1,0:T(8,128)(2,1)S(1)} %get-tuple-element.68.refs_7_), channel_id=1, source_target_pairs={{0,1},{1,2},{2,3},{4,5},{5,6},{6,7},{8,9},{9,10},{10,11},{12,13},{... | collective-permute-start | bytes 1572872 | tf_op jit(solution)/shard_map/ppermute | solution.py:734
  117.9 15.8 %collective-permute-start.21 = (bf16[512,512]{1,0:T(8,128)(2,1)S(1)}, bf16[512,512]{1,0:T(8,128)(2,1)S(1)}, u32[]{:S(2)}, u32[]{:S(2)}) collective-permute-start(bf16[512,512]{1,0:T(8,128)(2,1)S(1)} %get-tuple-element.71), channel_id=1, source_target_pairs={{3,2},{2,1},{1,0},{7,6},{6,5},{5,4},{11,10},{10,9},{9,8},{15,14},{... | collective-permute-start | bytes 1572872 | tf_op jit(solution)/shard_map/ppermute | solution.py:734
  120.2 10.2 %collective-permute-start.25 = (f32[192,128]{1,0:T(8,128)S(1)}, f32[192,128]{1,0:T(8,128)S(1)}, u32[]{:S(2)}, u32[]{:S(2)}) collective-permute-start(f32[192,128]{1,0:T(8,128)S(1)} %get-tuple-element.80), channel_id=1, source_target_pairs={{0,4},{4,0},{8,12},{12,8},{1,5},{5,1},{9,13},{13,9},{2,6},{6,2},{1... | collective-permute-start | bytes 294920 | tf_op jit(solution)/shard_map/ppermute | solution.py:139
  124.7 27.2 %collective-permute-start.18 = (bf16[512,512]{1,0:T(8,128)(2,1)S(1)}, bf16[512,512]{1,0:T(8,128)(2,1)S(1)}, u32[]{:S(2)}, u32[]{:S(2)}) collective-permute-start(bf16[512,512]{1,0:T(8,128)(2,1)S(1)} %get-tuple-element.69.refs_6_), channel_id=1, source_target_pairs={{0,1},{1,2},{2,3},{4,5},{5,6},{6,7},{8,9},{9,10},{10,11},{12,13},{... | collective-permute-start | bytes 1572872 | tf_op jit(solution)/shard_map/ppermute | solution.py:734
  129.1 22.8 %collective-permute-start.19 = (bf16[512,512]{1,0:T(8,128)(2,1)S(1)}, bf16[512,512]{1,0:T(8,128)(2,1)S(1)}, u32[]{:S(2)}, u32[]{:S(2)}) collective-permute-start(bf16[512,512]{1,0:T(8,128)(2,1)S(1)} %get-tuple-element.70.refs_7_), channel_id=1, source_target_pairs={{3,2},{2,1},{1,0},{7,6},{6,5},{5,4},{11,10},{10,9},{9,8},{15,14},{... | collective-permute-start | bytes 1572872 | tf_op jit(solution)/shard_map/ppermute | solution.py:734
  130.5 9.7 %collective-permute-start.26 = (f32[2,192,128]{2,1,0:T(8,128)S(1)}, f32[2,192,128]{2,1,0:T(8,128)S(1)}, u32[]{:S(2)}, u32[]{:S(2)}) collective-permute-start(f32[2,192,128]{2,1,0:T(8,128)S(1)} %pad_maximum_fusion.2), channel_id=1, source_target_pairs={{0,8},{4,12},{8,0},{12,4},{1,9},{5,13},{9,1},{13,5},{2,10},{6,14},... | collective-permute-start | bytes 589832 | tf_op jit(solution)/shard_map/ppermute | solution.py:139
  136.6 9.0 %collective-permute-start.28 = (bf16[64,192]{1,0:T(8,128)(2,1)S(1)}, bf16[64,192]{1,0:T(8,128)(2,1)S(1)}, u32[]{:S(2)}, u32[]{:S(2)}) collective-permute-start(bf16[64,192]{1,0:T(8,128)(2,1)S(1)} %get-tuple-element.82), channel_id=1, source_target_pairs={{0,1},{1,0},{2,3},{3,2},{4,5},{5,4},{6,7},{7,6},{8,9},{9,8},{10,11... | collective-permute-start | bytes 73736 | tf_op jit(solution)/shard_map/ppermute | solution.py:139
  139.1 6.8 %collective-permute-start.29 = (bf16[64,192]{1,0:T(8,128)(2,1)S(1)}, bf16[64,192]{1,0:T(8,128)(2,1)S(1)}, u32[]{:S(2)}, u32[]{:S(2)}) collective-permute-start(bf16[64,192]{1,0:T(8,128)(2,1)S(1)} %get-tuple-element.83), channel_id=1, source_target_pairs={{0,2},{1,3},{2,0},{3,1},{4,6},{5,7},{6,4},{7,5},{8,10},{9,11},{10,... | collective-permute-start | bytes 73736 | tf_op jit(solution)/shard_map/ppermute | solution.py:139
  140.1 9.1 %collective-permute-start.30 = (bf16[64,192]{1,0:T(8,128)(2,1)S(1)}, bf16[64,192]{1,0:T(8,128)(2,1)S(1)}, u32[]{:S(2)}, u32[]{:S(2)}) collective-permute-start(bf16[64,192]{1,0:T(8,128)(2,1)S(1)} %get-tuple-element.84), channel_id=1, source_target_pairs={{0,3},{1,2},{2,1},{3,0},{4,7},{5,6},{6,5},{7,4},{8,11},{9,10},{10,... | collective-permute-start | bytes 73736 | tf_op jit(solution)/shard_map/ppermute | solution.py:139
  145.6 4.8 %collective-permute-start.27 = (f32[4,192,128]{2,1,0:T(8,128)S(1)}, f32[4,192,128]{2,1,0:T(8,128)S(1)}, u32[]{:S(2)}, u32[]{:S(2)}) collective-permute-start(f32[4,192,128]{2,1,0:T(8,128)S(1)} %pad_maximum_fusion.1.near), channel_id=1, source_target_pairs={{0,16},{16,0},{1,17},{17,1},{2,18},{18,2},{3,19},{19,3},{4,20},{20... | collective-permute-start | bytes 1179656 | tf_op jit(solution)/shard_map/ppermute | solution.py:139
  151.9 1.1 copy-start.15

commit v8 on v7

--- a/solution.py
+++ b/solution.py
@@ -12,7 +12,7 @@
 MEBIBYTE = 1024 * 1024
 COST = 1
 HALVES = 2
-COSTS = {"sums": 1, "pair": 1, "small": 10**10, "token": 20 * 10**9, "adapter": 20 * 10**9, "last": 10**11}
+COSTS = {"sums": 1, "pair": 1, "small": 1, "token": 20 * 10**9, "adapter": 20 * 10**9, "last": 10**11}
 LIMITS = {"low": 6, "sums": 25, "last": 14, "token": 8, "adapter": 12, "small": 4}
 TILE = 512
 STRIP = 256
@@ -804,7 +804,7 @@
                 [*states[half][1:], factor, *full, *tail],
                 width // quarters,
                 [from_left[half], from_right[half]],
-                [narrow_turned] if half else partial[1],
+                [] if half else partial[1],
                 results[:],
             )
         )

time: 156 us -> 152 us (0.974)
  waiting for transfers between devices: 40.6 us -> 37.6 us
    ppermute x21, waiting for transfers between devices: 31.8 us -> 25.5 us  [flip(): return lax.ppermute(array, axis, [(i, i ^ bit) for i in range(size)])]
    ppermute x10, waiting for transfers between devices: 8.84 us -> 12.1 us  [square_plane(): shift = lambda array, pairs: lax.ppermute(array, 'tp', pairs)]
    unnamed x36 -> x34, local copies, waits for them, and re-layouts: 9.65 us -> 8.53 us
  transfers between devices with their start and end apart: 31 -> 31, of which waited for: 15 -> 14; matrix products, arithmetic and copies ran while one was open for 0% -> 0% of each run, Pallas kernels for 29% -> 31%
where the time goes in v8:
time: 152 us
  Pallas kernels  57.1 us (38%)
  starting transfers between devices  47.5 us (31%)
  waiting for transfers between devices  37.6 us (25%)
  local copies, waits for them, and re-layouts  8.53 us (6%)
    pallas_call x16, Pallas kernels, vmem_call(): pl.pallas_call(kernel, in_specs=[pl.BlockSpec(memory_space=pltpu.SMEM)] *...  29.5 us
    ppermute x10, starting transfers between devices, square_plane(): shift = lambda array, pairs: lax.ppermute(array, 'tp', pairs)  26.9 us
    ppermute x21, waiting for transfers between devices, flip(): return lax.ppermute(array, axis, [(i, i ^ bit) for i in range(size)])  25.5 us
    ppermute x21, starting transfers between devices, flip(): return lax.ppermute(array, axis, [(i, i ^ bit) for i in range(size)])  20.6 us
    pallas_call x1, Pallas kernels, width_sums(): pl.pallas_call(functools.partial(sums_kernel, masks, order, len(arrays),...  15.4 us
    ppermute x10, waiting for transfers between devices, square_plane(): shift = lambda array, pairs: lax.ppermute(array, 'tp', pairs)  12.1 us
    unnamed x34, local copies, waits for them, and re-layouts  8.53 us
    pallas_call x2, Pallas kernels, last_token_grad(): pl.pallas_call(functools.partial(token_grad_kernel, 'last', step), grid=(...  5.76 us
  transfers between devices with their start and end apart: 31, of which 14 were waited for; matrix products, arithmetic and copies ran while one was open for 0% of the time, Pallas kernels for 31%

profile of v8, /device:TPU:0, one launch (start us, length us, event | category | flops | bytes accessed | tf_op | source)
XLA Modules:
  0.0 151.9 jit_solution(13002665668138847742)
XLA Ops:
  0.6 2.3 %own_units.1 = (bf16[3,128,1024]{2,1,0:T(8,128)(2,1)S(1)}, bf16[3,128,1024]{2,1,0:T(8,128)(2,1)}) custom-call(bf16[256,1024]{1,0:T(8,128)(2,1)} %gate.1, bf16[256,1024]{1,0:T(8,128)(2,1)} %up.1, bf16[1024,256]{1,0:T(8,128)(2,1)} %down.1), custom_call_target="tpu_custom_call" | custom-call | flops 1048576 | tf_op jit(solution)/shard_map/own_units/pallas_call | solution.py:243
  2.9 3.0 %collective-permute-start = (bf16[3,128,1024]{2,1,0:T(8,128)(2,1)S(1)}, bf16[3,128,1024]{2,1,0:T(8,128)(2,1)S(1)}, u32[]{:S(2)}, u32[]{:S(2)}) collective-permute-start(bf16[3,128,1024]{2,1,0:T(8,128)(2,1)S(1)} %get-tuple-element.44.refs_8_), channel_id=1, source_target_pairs={{0,4},{4,0},{8,12},{12,8},{1,5},{5,1},{9,13},{13,9},{2,6},{6,2},{1... | collective-permute-start | bytes 2359304 | tf_op jit(solution)/shard_map/ppermute | solution.py:139
  5.9 1.5 %collective-permute-start.1 = (bf16[3,128,1024]{2,1,0:T(8,128)(2,1)}, bf16[3,128,1024]{2,1,0:T(8,128)(2,1)S(1)}, u32[]{:S(2)}, u32[]{:S(2)}) collective-permute-start(bf16[3,128,1024]{2,1,0:T(8,128)(2,1)} %get-tuple-element.45.refs_9_), channel_id=1, source_target_pairs={{0,8},{4,12},{8,0},{12,4},{1,9},{5,13},{9,1},{13,5},{2,10},{6,14},... | collective-permute-start | bytes 2359304 | tf_op jit(solution)/shard_map/ppermute | solution.py:139
  7.4 0.5 collective-permute-start.3
  7.9 0.5 collective-permute-start.4
  8.6 15.7 %collective-permute-done.refs_1_.first.refs_10_ = bf16[3,128,1024]{2,1,0:T(8,128)(2,1)S(1)} collective-permute-done((bf16[3,128,1024]{2,1,0:T(8,128)(2,1)S(1)}, bf16[3,128,1024]{2,1,0:T(8,128)(2,1)S(1)}, u32[]{:S(2)}, u32[]{:S(2)}) %collective-permute-start) | collective-permute-done | bytes 786464 | tf_op jit(solution)/shard_map/ppermute | solution.py:139
  24.3 2.1 %collective-permute-start.5 = (bf16[3,128,1024]{2,1,0:T(8,128)(2,1)S(1)}, bf16[3,128,1024]{2,1,0:T(8,128)(2,1)S(1)}, u32[]{:S(2)}, u32[]{:S(2)}) collective-permute-start(bf16[3,128,1024]{2,1,0:T(8,128)(2,1)S(1)} %get-tuple-element.44.refs_8_), channel_id=1, source_target_pairs={{0,8},{4,12},{8,0},{12,4},{1,9},{5,13},{9,1},{13,5},{2,10},{6,14},... | collective-permute-start | bytes 2359304 | tf_op jit(solution)/shard_map/ppermute | solution.py:139
  26.4 2.2 %copy-done = bf16[1024,2048]{1,0:T(8,128)(2,1)S(1)} copy-done((bf16[1024,2048]{1,0:T(8,128)(2,1)S(1)}, bf16[1024,2048]{1,0:T(8,128)(2,1)}, u32[]{:S(2)}) %copy-start) | copy-done | bytes 4194328
  28.6 2.2 %copy-done.2 = bf16[1024,2048]{1,0:T(8,128)(2,1)S(1)} copy-done((bf16[1024,2048]{1,0:T(8,128)(2,1)S(1)}, bf16[1024,2048]{1,0:T(8,128)(2,1)}, u32[]{:S(2)}) %copy-start.2) | copy-done | bytes 4194328
  30.8 0.9 copy-done.6
  31.7 0.9 copy-done.8
  32.7 0.9 copy-done.14
  33.6 4.1 %low_rank_values.1 = (bf16[1024,64]{1,0:T(8,128)(2,1)S(1)}, bf16[1024,64]{1,0:T(8,128)(2,1)S(1)}, bf16[1024,64]{1,0:T(8,128)(2,1)S(1)}, bf16[192,1024]{1,0:T(8,128)(2,1)S(1)}) custom-call(bf16[1024,2048]{1,0:T(8,128)(2,1)S(1)} %copy-done, bf16[1024,2048]{1,0:T(8,128)(2,1)S(1)} %copy-done.2, bf16[64,2048]{1,0:T(8,128)(2,1)S(1)} %bitcast.11, ...), custom_call_target="tpu_custom_call" | custom-call | flops 64424509440 | tf_op jit(solution)/shard_map/low_rank_values/pallas_call | solution.py:201
  38.0 2.3 %collective-permute-done.4.first.refs_11_ = bf16[3,128,1024]{2,1,0:T(8,128)(2,1)S(1)} collective-permute-done((bf16[3,128,1024]{2,1,0:T(8,128)(2,1)}, bf16[3,128,1024]{2,1,0:T(8,128)(2,1)S(1)}, u32[]{:S(2)}, u32[]{:S(2)}) %collective-permute-start.4) | collective-permute-done | bytes 786464 | tf_op jit(solution)/shard_map/ppermute | solution.py:139
  40.3 1.9 %collective-permute-done.5.second.refs_12_ = bf16[3,128,1024]{2,1,0:T(8,128)(2,1)S(1)} collective-permute-done((bf16[3,128,1024]{2,1,0:T(8,128)(2,1)S(1)}, bf16[3,128,1024]{2,1,0:T(8,128)(2,1)S(1)}, u32[]{:S(2)}, u32[]{:S(2)}) %collective-permute-start.5) | collective-permute-done | bytes 786464 | tf_op jit(solution)/shard_map/ppermute | solution.py:139
  42.4 1.5 collective-permute-start.8
  43.9 1.5 collective-permute-start.9
  45.8 0.8 copy-done.15
  46.6 0.5 copy-done.16
  47.0 15.4 %width_sums.1 = (f32[512,1024]{1,0:T(8,128)S(1)}, f32[512,1024]{1,0:T(8,128)S(1)}, f32[512,1024]{1,0:T(8,128)S(1)}, f32[512,1024]{1,0:T(8,128)S(1)}, f32[512,102...) custom-call(s32[2]{0:T(128)S(1)} %pad_add_fusion.refs_0_.here, ...), custom_call_target="tpu_custom_call" | custom-call | flops 1 | tf_op jit(solution)/shard_map/width_sums/pallas_call | solution.py:377
  62.5 1.0 collective-permute-done.9.refs_1_
  63.5 0.5 collective-permute-start.11
  64.1 1.7 %collective-permute-done.10.refs_2_ = bf16[3,128,1024]{2,1,0:T(8,128)(2,1)S(1)} collective-permute-done((bf16[3,128,1024]{2,1,0:T(8,128)(2,1)S(1)}, bf16[3,128,1024]{2,1,0:T(8,128)(2,1)S(1)}, u32[]{:S(2)}, u32[]{:S(2)}) %collective-permute-start.10) | collective-permute-done | bytes 786464 | tf_op jit(solution)/shard_map/ppermute | solution.py:139
  65.8 1.1 collective-permute-done.11.refs_3_
  66.9 3.8 %hidden_and_grads.2 = (bf16[512,1024]{1,0:T(8,128)(2,1)S(1)}, bf16[512,1024]{1,0:T(8,128)(2,1)S(1)}, bf16[512,1024]{1,0:T(8,128)(2,1)S(1)}, f32[512,128]{1,0:T(8,128)S(1)}) custom-call(s32[2]{0:T(128)S(1)} %pad_add_fusion.refs_0_.here, bf16[1024,512]{1,0:T(8,128)(2,1)S(1)} %get-tuple-element.50.left, bf16[1024,512]{1,0:T(8,128)(2,1)S(1)} %get-tuple-element.51.back, ...), custom_call_target="tpu_custom_call" | custom-call | flops 99999997952 | tf_op jit(solution)/shard_map/hidden_and_grads/pallas_call | solution.py:147
  70.8 2.3 %token_grad.6.refs_7_.refs_4_.refs_12_ = bf16[512,512]{1,0:T(8,128)(2,1)S(1)} custom-call(s32[2]{0:T(128)S(1)} %pad_add_fusion.refs_0_.here, bf16[512,1024]{1,0:T(8,128)(2,1)S(1)} %get-tuple-element.60.gate_grad.refs_2_, bf16[512,1024]{1,0:T(8,128)(2,1)S(1)} %get-tuple-element.61.up_grad.refs_4_, f32[512,128]{1,0:T(8,128)S(1)} %get-tuple-element.62.low.refs_6_, ...), custom_call_target="tpu_custom_call" | custom-call | flops 20000000000 | tf_op jit(solution)/shard_map/token_grad/pallas_call | solution.py:147
  73.1 3.5 %collective-permute-start.13 = (bf16[512,512]{1,0:T(8,128)(2,1)S(1)}, bf16[512,512]{1,0:T(8,128)(2,1)S(1)}, u32[]{:S(2)}, u32[]{:S(2)}) collective-permute-start(bf16[512,512]{1,0:T(8,128)(2,1)S(1)} %token_grad.6.refs_7_.refs_4_.refs_12_), channel_id=1, source_target_pairs={{0,1},{3,2},{4,5},{7,6},{8,9},{11,10},{12,13},{15,14},{16,17},{19,... | collective-permute-start | bytes 1572872 | tf_op jit(solution)/shard_map/ppermute | solution.py:734
  76.6 3.8 %hidden_and_grads.3 = (bf16[512,1024]{1,0:T(8,128)(2,1)S(1)}, bf16[512,1024]{1,0:T(8,128)(2,1)S(1)}, bf16[512,1024]{1,0:T(8,128)(2,1)S(1)}, f32[512,128]{1,0:T(8,128)S(1)}) custom-call(s32[2]{0:T(128)S(1)} %pad_add_fusion.refs_0_.here, bf16[1024,512]{1,0:T(8,128)(2,1)S(1)} %get-tuple-element.50.left, bf16[1024,512]{1,0:T(8,128)(2,1)S(1)} %get-tuple-element.51.back, ...), custom_call_target="tpu_custom_call" | custom-call | flops 99999997952 | tf_op jit(solution)/shard_map/hidden_and_grads/pallas_call | solution.py:147
  80.5 2.1 %token_grad.7.refs_5_.refs_4_.refs_13_ = bf16[512,512]{1,0:T(8,128)(2,1)S(1)} custom-call(s32[2]{0:T(128)S(1)} %pad_add_fusion.refs_0_.here, bf16[512,1024]{1,0:T(8,128)(2,1)S(1)} %get-tuple-element.65.gate_grad.refs_3_, bf16[512,1024]{1,0:T(8,128)(2,1)S(1)} %get-tuple-element.66.up_grad.refs_5_, f32[512,128]{1,0:T(8,128)S(1)} %get-tuple-element.67.low.refs_7_, ...), custom_call_target="tpu_custom_call" | custom-call | flops 20000000000 | tf_op jit(solution)/shard_map/token_grad/pallas_call | solution.py:147
  82.6 1.5 collective-permute-start.12
  84.1 4.1 %adapter_grads.1 = (f32[4,192,384]{2,1,0:T(8,128)S(1)}, f32[4,192,384]{2,1,0:T(8,128)S(1)}) custom-call(s32[2]{0:T(128)S(1)} %pad_add_fusion.refs_0_.here, bf16[512,1024]{1,0:T(8,128)(2,1)S(1)} %get-tuple-element.72.refs_0_, bf16[512,1024]{1,0:T(8,128)(2,1)S(1)} %get-tuple-element.73.refs_1_, bf16[512,1024]{1,0:T(8,128)(2,1)S(1)} %get-tuple-element.60.gate_grad.refs_2_, ...), custom_call_target="tpu_custom_call" | custom-call | flops 20000000000 | tf_op jit(solution)/shard_map/adapter_grads/pallas_call | solution.py:147
  88.2 0.6 collective-permute-done.13.refs_4_
  88.8 2.1 %token_grad.8.refs_5_ = bf16[512,512]{1,0:T(8,128)(2,1)S(1)} custom-call(s32[2]{0:T(128)S(1)} %pad_add_fusion.refs_0_.here, bf16[512,1024]{1,0:T(8,128)(2,1)S(1)} %get-tuple-element.60.gate_grad.refs_2_, bf16[512,1024]{1,0:T(8,128)(2,1)S(1)} %get-tuple-element.61.up_grad.refs_4_, f32[512,128]{1,0:T(8,128)S(1)} %get-tuple-element.62.low.refs_6_, ...), custom_call_target="tpu_custom_call" | custom-call | flops 20000000000 | tf_op jit(solution)/shard_map/token_grad/pallas_call | solution.py:147
  90.9 4.4 %collective-permute-start.16 = (bf16[512,512]{1,0:T(8,128)(2,1)S(1)}, bf16[512,512]{1,0:T(8,128)(2,1)S(1)}, u32[]{:S(2)}, u32[]{:S(2)}) collective-permute-start(bf16[512,512]{1,0:T(8,128)(2,1)S(1)} %token_grad.8.refs_5_), channel_id=1, source_target_pairs={{0,1},{1,2},{4,5},{5,6},{8,9},{9,10},{12,13},{13,14},{16,17},{17,1... | collective-permute-start | bytes 1572872 | tf_op jit(solution)/shard_map/ppermute | solution.py:734
  95.3 0.7 collective-permute-start.17
  96.0 0.7 halve.2
  96.7 0.6 collective-permute-start.23
  97.3 2.8 %collective-permute-done.12.refs_4_ = bf16[512,512]{1,0:T(8,128)(2,1)S(1)} collective-permute-done((bf16[512,512]{1,0:T(8,128)(2,1)S(1)}, bf16[512,512]{1,0:T(8,128)(2,1)S(1)}, u32[]{:S(2)}, u32[]{:S(2)}) %collective-permute-start.12) | collective-permute-done | bytes 524320 | tf_op jit(solution)/shard_map/ppermute | solution.py:734
  100.1 2.1 %token_grad.9.refs_7_ = bf16[512,512]{1,0:T(8,128)(2,1)S(1)} custom-call(s32[2]{0:T(128)S(1)} %pad_add_fusion.refs_0_.here, bf16[512,1024]{1,0:T(8,128)(2,1)S(1)} %get-tuple-element.65.gate_grad.refs_3_, bf16[512,1024]{1,0:T(8,128)(2,1)S(1)} %get-tuple-element.66.up_grad.refs_5_, f32[512,128]{1,0:T(8,128)S(1)} %get-tuple-element.67.low.refs_7_, ...), custom_call_target="tpu_custom_call" | custom-call | flops 20000000000 | tf_op jit(solution)/shard_map/token_grad/pallas_call | solution.py:147
  102.1 4.4 %collective-permute-start.14 = (bf16[512,512]{1,0:T(8,128)(2,1)S(1)}, bf16[512,512]{1,0:T(8,128)(2,1)S(1)}, u32[]{:S(2)}, u32[]{:S(2)}) collective-permute-start(bf16[512,512]{1,0:T(8,128)(2,1)S(1)} %token_grad.9.refs_7_), channel_id=1, source_target_pairs={{0,1},{1,2},{4,5},{5,6},{8,9},{9,10},{12,13},{13,14},{16,17},{17,1... | collective-permute-start | bytes 1572872 | tf_op jit(solution)/shard_map/ppermute | solution.py:734
  106.5 0.7 collective-permute-start.15
  107.3 0.6 halve.3
  107.9 1.6 %collective-permute-start.24 = (bf16[1,192,384]{2,1,0:T(8,128)(2,1)S(1)}, bf16[1,192,384]{2,1,0:T(8,128)(2,1)S(1)}, u32[]{:S(2)}, u32[]{:S(2)}) collective-permute-start(bf16[1,192,384]{2,1,0:T(8,128)(2,1)S(1)} %get-tuple-element.79), channel_id=1, source_target_pairs={{0,4},{4,0},{8,12},{12,8},{1,5},{5,1},{9,13},{13,9},{2,6},{6,2},{1... | collective-permute-start | bytes 442376 | tf_op jit(solution)/shard_map/ppermute | solution.py:139
  109.4 1.9 %collective-permute-done.16.refs_5_ = bf16[512,512]{1,0:T(8,128)(2,1)S(1)} collective-permute-done((bf16[512,512]{1,0:T(8,128)(2,1)S(1)}, bf16[512,512]{1,0:T(8,128)(2,1)S(1)}, u32[]{:S(2)}, u32[]{:S(2)}) %collective-permute-start.16) | collective-permute-done | bytes 524320 | tf_op jit(solution)/shard_map/ppermute | solution.py:734
  111.3 2.2 %token_grad.10 = (bf16[512,512]{1,0:T(8,128)(2,1)S(1)}, bf16[512,512]{1,0:T(8,128)(2,1)S(1)}) custom-call(s32[2]{0:T(128)S(1)} %pad_add_fusion.refs_0_.here, bf16[512,1024]{1,0:T(8,128)(2,1)S(1)} %get-tuple-element.60.gate_grad.refs_2_, bf16[512,1024]{1,0:T(8,128)(2,1)S(1)} %get-tuple-element.61.up_grad.refs_4_, ...), custom_call_target="tpu_custom_call" | custom-call | flops 20000000000 | tf_op jit(solution)/shard_map/token_grad/pallas_call | solution.py:147
  113.5 4.4 %collective-permute-start.20 = (bf16[512,512]{1,0:T(8,128)(2,1)S(1)}, bf16[512,512]{1,0:T(8,128)(2,1)S(1)}, u32[]{:S(2)}, u32[]{:S(2)}) collective-permute-start(bf16[512,512]{1,0:T(8,128)(2,1)S(1)} %get-tuple-element.68.refs_7_), channel_id=1, source_target_pairs={{0,1},{1,2},{2,3},{4,5},{5,6},{6,7},{8,9},{9,10},{10,11},{12,13},{... | collective-permute-start | bytes 1572872 | tf_op jit(solution)/shard_map/ppermute | solution.py:734
  117.9 1.6 %collective-permute-start.21 = (bf16[512,512]{1,0:T(8,128)(2,1)S(1)}, bf16[512,512]{1,0:T(8,128)(2,1)S(1)}, u32[]{:S(2)}, u32[]{:S(2)}) collective-permute-start(bf16[512,512]{1,0:T(8,128)(2,1)S(1)} %get-tuple-element.71), channel_id=1, source_target_pairs={{3,2},{2,1},{1,0},{7,6},{6,5},{5,4},{11,10},{10,9},{9,8},{15,14},{... | collective-permute-start | bytes 1572872 | tf_op jit(solution)/shard_map/ppermute | solution.py:734
  119.5 0.7 turn.1
  120.2 1.6 %collective-permute-start.28 = (f32[192,128]{1,0:T(8,128)S(1)}, f32[192,128]{1,0:T(8,128)S(1)}, u32[]{:S(2)}, u32[]{:S(2)}) collective-permute-start(f32[192,128]{1,0:T(8,128)S(1)} %get-tuple-element.84), channel_id=1, source_target_pairs={{0,4},{4,0},{8,12},{12,8},{1,5},{5,1},{9,13},{13,9},{2,6},{6,2},{1... | collective-permute-start | bytes 294920 | tf_op jit(solution)/shard_map/ppermute | solution.py:139
  121.8 0.8 collective-permute-done.14.refs_5_
  122.5 2.2 %token_grad.11 = (bf16[512,512]{1,0:T(8,128)(2,1)S(1)}, bf16[512,512]{1,0:T(8,128)(2,1)S(1)}) custom-call(s32[2]{0:T(128)S(1)} %pad_add_fusion.refs_0_.here, bf16[512,1024]{1,0:T(8,128)(2,1)S(1)} %get-tuple-element.65.gate_grad.refs_3_, bf16[512,1024]{1,0:T(8,128)(2,1)S(1)} %get-tuple-element.66.up_grad.refs_5_, ...), custom_call_target="tpu_custom_call" | custom-call | flops 20000000000 | tf_op jit(solution)/shard_map/token_grad/pallas_call | solution.py:147
  124.7 4.4 %collective-permute-start.18 = (bf16[512,512]{1,0:T(8,128)(2,1)S(1)}, bf16[512,512]{1,0:T(8,128)(2,1)S(1)}, u32[]{:S(2)}, u32[]{:S(2)}) collective-permute-start(bf16[512,512]{1,0:T(8,128)(2,1)S(1)} %get-tuple-element.69.refs_6_), channel_id=1, source_target_pairs={{0,1},{1,2},{2,3},{4,5},{5,6},{6,7},{8,9},{9,10},{10,11},{12,13},{... | collective-permute-start | bytes 1572872 | tf_op jit(solution)/shard_map/ppermute | solution.py:734
  129.2 1.3 collective-permute-start.19
  130.5 0.6 collective-permute-start.29
  131.1 2.7 %collective-permute-done.20.refs_4_ = bf16[512,512]{1,0:T(8,128)(2,1)S(1)} collective-permute-done((bf16[512,512]{1,0:T(8,128)(2,1)S(1)}, bf16[512,512]{1,0:T(8,128)(2,1)S(1)}, u32[]{:S(2)}, u32[]{:S(2)}) %collective-permute-start.20) | collective-permute-done | bytes 524320 | tf_op jit(solution)/shard_map/ppermute | solution.py:734
  133.8 2.9 %last_token_grad.2.refs_6_ = bf16[1024,512]{1,0:T(8,128)(2,1)} custom-call(s32[2]{0:T(128)S(1)} %pad_add_fusion.refs_0_.here, bf16[512,1024]{1,0:T(8,128)(2,1)S(1)} %get-tuple-element.60.gate_grad.refs_2_, bf16[512,1024]{1,0:T(8,128)(2,1)S(1)} %get-tuple-element.61.up_grad.refs_4_, f32[512,128]{1,0:T(8,128)S(1)} %get-tuple-element.62.low.refs_6_, ...), custom_call_target="tpu_custom_call" | custom-call | flops 20000000000 | tf_op jit(solution)/shard_map/last_token_grad/pallas_call | solution.py:495
  136.6 2.5 %collective-permute-start.25 = (bf16[64,192]{1,0:T(8,128)(2,1)S(1)}, bf16[64,192]{1,0:T(8,128)(2,1)S(1)}, u32[]{:S(2)}, u32[]{:S(2)}) collective-permute-start(bf16[64,192]{1,0:T(8,128)(2,1)S(1)} %get-tuple-element.81), channel_id=1, source_target_pairs={{0,1},{1,0},{2,3},{3,2},{4,5},{5,4},{6,7},{7,6},{8,9},{9,8},{10,11... | collective-permute-start | bytes 73736 | tf_op jit(solution)/shard_map/ppermute | solution.py:139
  139.1 1.0 collective-permute-start.26
  140.1 1.5 collective-permute-start.27
  141.6 3.4 %collective-permute-done.18.refs_4_ = bf16[512,512]{1,0:T(8,128)(2,1)S(1)} collective-permute-done((bf16[512,512]{1,0:T(8,128)(2,1)S(1)}, bf16[512,512]{1,0:T(8,128)(2,1)S(1)}, u32[]{:S(2)}, u32[]{:S(2)}) %collective-permute-start.18) | collective-permute-done | bytes 524320 | tf_op jit(solution)/shard_map/ppermute | solution.py:734
  145.0 2.9 %last_token_grad.3 = bf16[1024,512]{1,0:T(8,128)(2,1)} custom-call(s32[2]{0:T(128)S(1)} %pad_add_fusion.refs_0_.here, bf16[512,1024]{1,0:T(8,128)(2,1)S(1)} %get-tuple-element.65.gate_grad.refs_3_, bf16[512,1024]{1,0:T(8,128)(2,1)S(1)} %get-tuple-element.66.up_grad.refs_5_, ...), custom_call_target="tpu_custom_call", output_to_operand_aliasing={{}: (13, {})} | custom-call | flops 20000000000 | tf_op jit(solution)/shard_map/last_token_grad/pallas_call | solution.py:495
  147.9 1.3 collective-permute-done.27.refs_2_
  149.2 1.2 last_sum.1
  150.4 1.5 whole.1
  (58 shorter events, 1.1 us)
Async XLA Ops:
  2.9 21.4 %collective-permute-start = (bf16[3,128,1024]{2,1,0:T(8,128)(2,1)S(1)}, bf16[3,128,1024]{2,1,0:T(8,128)(2,1)S(1)}, u32[]{:S(2)}, u32[]{:S(2)}) collective-permute-start(bf16[3,128,1024]{2,1,0:T(8,128)(2,1)S(1)} %get-tuple-element.44.refs_8_), channel_id=1, source_target_pairs={{0,4},{4,0},{8,12},{12,8},{1,5},{5,1},{9,13},{13,9},{2,6},{6,2},{1... | collective-permute-start | bytes 2359304 | tf_op jit(solution)/shard_map/ppermute | solution.py:139
  5.9 20.5 %collective-permute-start.1 = (bf16[3,128,1024]{2,1,0:T(8,128)(2,1)}, bf16[3,128,1024]{2,1,0:T(8,128)(2,1)S(1)}, u32[]{:S(2)}, u32[]{:S(2)}) collective-permute-start(bf16[3,128,1024]{2,1,0:T(8,128)(2,1)} %get-tuple-element.45.refs_9_), channel_id=1, source_target_pairs={{0,8},{4,12},{8,0},{12,4},{1,9},{5,13},{9,1},{13,5},{2,10},{6,14},... | collective-permute-start | bytes 2359304 | tf_op jit(solution)/shard_map/ppermute | solution.py:139
  7.4 18.9 %collective-permute-start.2 = (bf16[3,128,1024]{2,1,0:T(8,128)(2,1)S(1)}, bf16[3,128,1024]{2,1,0:T(8,128)(2,1)}, u32[]{:S(2)}, u32[]{:S(2)}) collective-permute-start(bf16[3,128,1024]{2,1,0:T(8,128)(2,1)S(1)} %get-tuple-element.44.refs_8_), channel_id=1, source_target_pairs={{0,16},{16,0},{1,17},{17,1},{2,18},{18,2},{3,19},{19,3},{4,20},{20... | collective-permute-start | bytes 2359304 | tf_op jit(solution)/shard_map/ppermute | solution.py:139
  7.4 18.9 %collective-permute-start.3 = (bf16[3,128,1024]{2,1,0:T(8,128)(2,1)}, bf16[3,128,1024]{2,1,0:T(8,128)(2,1)}, u32[]{:S(2)}, u32[]{:S(2)}) collective-permute-start(bf16[3,128,1024]{2,1,0:T(8,128)(2,1)} %get-tuple-element.45.refs_9_), channel_id=1, source_target_pairs={{0,16},{16,0},{1,17},{17,1},{2,18},{18,2},{3,19},{19,3},{4,20},{20... | collective-permute-start | bytes 2359304 | tf_op jit(solution)/shard_map/ppermute | solution.py:139
  7.9 32.4 %collective-permute-start.4 = (bf16[3,128,1024]{2,1,0:T(8,128)(2,1)}, bf16[3,128,1024]{2,1,0:T(8,128)(2,1)S(1)}, u32[]{:S(2)}, u32[]{:S(2)}) collective-permute-start(bf16[3,128,1024]{2,1,0:T(8,128)(2,1)} %get-tuple-element.45.refs_9_), channel_id=1, source_target_pairs={{0,4},{4,0},{8,12},{12,8},{1,5},{5,1},{9,13},{13,9},{2,6},{6,2},{1... | collective-permute-start | bytes 2359304 | tf_op jit(solution)/shard_map/ppermute | solution.py:139
  24.3 17.9 %collective-permute-start.5 = (bf16[3,128,1024]{2,1,0:T(8,128)(2,1)S(1)}, bf16[3,128,1024]{2,1,0:T(8,128)(2,1)S(1)}, u32[]{:S(2)}, u32[]{:S(2)}) collective-permute-start(bf16[3,128,1024]{2,1,0:T(8,128)(2,1)S(1)} %get-tuple-element.44.refs_8_), channel_id=1, source_target_pairs={{0,8},{4,12},{8,0},{12,4},{1,9},{5,13},{9,1},{13,5},{2,10},{6,14},... | collective-permute-start | bytes 2359304 | tf_op jit(solution)/shard_map/ppermute | solution.py:139
  26.4 2.2 %copy-start = (bf16[1024,2048]{1,0:T(8,128)(2,1)S(1)}, bf16[1024,2048]{1,0:T(8,128)(2,1)}, u32[]{:S(2)}) copy-start(bf16[1024,2048]{1,0:T(8,128)(2,1)} %refs_8_.1) | copy-start | bytes 12582916
  28.6 2.2 %copy-start.2 = (bf16[1024,2048]{1,0:T(8,128)(2,1)S(1)}, bf16[1024,2048]{1,0:T(8,128)(2,1)}, u32[]{:S(2)}) copy-start(bf16[1024,2048]{1,0:T(8,128)(2,1)} %refs_9_.1) | copy-start | bytes 12582916
  30.8 0.9 copy-start.6
  31.7 0.9 copy-start.8
  32.7 0.9 copy-start.14
  37.7 4.6 %copy-start.4 = (bf16[192,1024]{1,0:T(8,128)(2,1)}, bf16[192,1024]{1,0:T(8,128)(2,1)S(1)}, u32[]{:S(2)}) copy-start(bf16[192,1024]{1,0:T(8,128)(2,1)S(1)} %get-tuple-element.49.refs_0_.refs_10_) | copy-start | bytes 1179652
  37.9 9.2 %copy-start.10 = (bf16[64,1024]{1,0:T(8,128)(2,1)S(1)}, bf16[64,1024]{1,0:T(8,128)(2,1)}, u32[]{:S(2)}) copy-start(bf16[64,1024]{1,0:T(8,128)(2,1)} %gate_out.3) | copy-start | bytes 393220
  37.9 9.2 %copy-start.11 = (bf16[64,1024]{1,0:T(8,128)(2,1)S(1)}, bf16[64,1024]{1,0:T(8,128)(2,1)}, u32[]{:S(2)}) copy-start(bf16[64,1024]{1,0:T(8,128)(2,1)} %up_out.3) | copy-start | bytes 393220
  37.9 9.1 %copy-start.12 = (bf16[1024,64]{0,1:T(8,128)(2,1)S(1)}, bf16[1024,64]{0,1:T(8,128)(2,1)}, u32[]{:S(2)}) copy-start(bf16[1024,64]{0,1:T(8,128)(2,1)} %param.20) | copy-start | bytes 393220
  37.9 7.5 %collective-permute-start.6 = (bf16[2,3,128,1024]{3,2,1,0:T(8,128)(2,1)S(1)}, bf16[2,3,128,1024]{3,2,1,0:T(8,128)(2,1)S(1)}, u32[]{:S(2)}, u32[]{:S(2)}) collective-permute-start(bf16[2,3,128,1024]{3,2,1,0:T(8,128)(2,1)S(1)} %pair.2), channel_id=1, source_target_pairs={{0,16},{16,0},{1,17},{17,1},{2,18},{18,2},{3,19},{19,3},{4,20},{20... | collective-permute-start | bytes 4718600 | tf_op jit(solution)/shard_map/ppermute | solution.py:139
  42.3 3.5 %collective-permute-start.7 = (bf16[2,3,128,1024]{3,2,1,0:T(8,128)(2,1)S(1)}, bf16[2,3,128,1024]{3,2,1,0:T(8,128)(2,1)S(1)}, u32[]{:S(2)}, u32[]{:S(2)}) collective-permute-start(bf16[2,3,128,1024]{3,2,1,0:T(8,128)(2,1)S(1)} %pair.3), channel_id=1, source_target_pairs={{0,16},{16,0},{1,17},{17,1},{2,18},{18,2},{3,19},{19,3},{4,20},{20... | collective-permute-start | bytes 4718600 | tf_op jit(solution)/shard_map/ppermute | solution.py:139
  42.4 20.1 %collective-permute-start.8 = (bf16[3,128,1024]{2,1,0:T(8,128)(2,1)S(1)}, bf16[3,128,1024]{2,1,0:T(8,128)(2,1)S(1)}, u32[]{:S(2)}, u32[]{:S(2)}) collective-permute-start(bf16[3,128,1024]{2,1,0:T(8,128)(2,1)S(1)} %collective-permute-done.refs_1_.first.refs_10_), channel_id=1, source_target_pairs={{0,8},{4,12},{8,0},{12,4},{1,9},{5,13},{9,1},{13,5},{2,10},{6,14},... | collective-permute-start | bytes 2359304 | tf_op jit(solution)/shard_map/ppermute | solution.py:139
  43.9 19.6 %collective-permute-start.9 = (bf16[3,128,1024]{2,1,0:T(8,128)(2,1)S(1)}, bf16[3,128,1024]{2,1,0:T(8,128)(2,1)S(1)}, u32[]{:S(2)}, u32[]{:S(2)}) collective-permute-start(bf16[3,128,1024]{2,1,0:T(8,128)(2,1)S(1)} %collective-permute-done.1.refs_2_.second.refs_13_), channel_id=1, source_target_pairs={{0,4},{4,0},{8,12},{12,8},{1,5},{5,1},{9,13},{13,9},{2,6},{6,2},{1... | collective-permute-start | bytes 2359304 | tf_op jit(solution)/shard_map/ppermute | solution.py:139
  45.4 1.2 copy-start.15
  45.8 1.2 copy-start.16
  62.5 1.6 %copy-start.7 = (bf16[2048,64]{0,1:T(8,128)(2,1)S(1)}, bf16[2048,64]{0,1:T(8,128)(2,1)}, u32[]{:S(2)}) copy-start(bf16[2048,64]{0,1:T(8,128)(2,1)} %param.16) | copy-start | bytes 786436
  62.5 1.5 %copy-start.9 = (bf16[2048,64]{0,1:T(8,128)(2,1)S(1)}, bf16[2048,64]{0,1:T(8,128)(2,1)}, u32[]{:S(2)}) copy-start(bf16[2048,64]{0,1:T(8,128)(2,1)} %param.17) | copy-start | bytes 786436
  63.5 2.3 %collective-permute-start.10 = (bf16[3,128,1024]{2,1,0:T(8,128)(2,1)S(1)}, bf16[3,128,1024]{2,1,0:T(8,128)(2,1)S(1)}, u32[]{:S(2)}, u32[]{:S(2)}) collective-permute-start(bf16[3,128,1024]{2,1,0:T(8,128)(2,1)S(1)} %get-tuple-element.53.refs_0_), channel_id=1, source_target_pairs={{0,16},{16,0},{1,17},{17,1},{2,18},{18,2},{3,19},{19,3},{4,20},{20... | collective-permute-start | bytes 2359304 | tf_op jit(solution)/shard_map/ppermute | solution.py:139
  63.5 3.4 %collective-permute-start.11 = (bf16[3,128,1024]{2,1,0:T(8,128)(2,1)S(1)}, bf16[3,128,1024]{2,1,0:T(8,128)(2,1)S(1)}, u32[]{:S(2)}, u32[]{:S(2)}) collective-permute-start(bf16[3,128,1024]{2,1,0:T(8,128)(2,1)S(1)} %get-tuple-element.54.refs_1_), channel_id=1, source_target_pairs={{0,16},{16,0},{1,17},{17,1},{2,18},{18,2},{3,19},{19,3},{4,20},{20... | collective-permute-start | bytes 2359304 | tf_op jit(solution)/shard_map/ppermute | solution.py:139
  73.1 15.7 %collective-permute-start.13 = (bf16[512,512]{1,0:T(8,128)(2,1)S(1)}, bf16[512,512]{1,0:T(8,128)(2,1)S(1)}, u32[]{:S(2)}, u32[]{:S(2)}) collective-permute-start(bf16[512,512]{1,0:T(8,128)(2,1)S(1)} %token_grad.6.refs_7_.refs_4_.refs_12_), channel_id=1, source_target_pairs={{0,1},{3,2},{4,5},{7,6},{8,9},{11,10},{12,13},{15,14},{16,17},{19,... | collective-permute-start | bytes 1572872 | tf_op jit(solution)/shard_map/ppermute | solution.py:734
  80.4 3.6 %copy-start.1 = (bf16[1024,2048]{1,0:T(8,128)(2,1)S(1)}, bf16[1024,2048]{1,0:T(8,128)(2,1)}, u32[]{:S(2)}) copy-start(bf16[1024,2048]{1,0:T(8,128)(2,1)} %refs_8_.1) | copy-start | bytes 12582916
  80.4 3.6 %copy-start.3 = (bf16[1024,2048]{1,0:T(8,128)(2,1)S(1)}, bf16[1024,2048]{1,0:T(8,128)(2,1)}, u32[]{:S(2)}) copy-start(bf16[1024,2048]{1,0:T(8,128)(2,1)} %refs_9_.1) | copy-start | bytes 12582916
  80.5 3.6 %copy-start.5 = (bf16[192,1024]{1,0:T(8,128)(2,1)S(1)}, bf16[192,1024]{1,0:T(8,128)(2,1)}, u32[]{:S(2)}) copy-start(bf16[192,1024]{1,0:T(8,128)(2,1)} %copy-done.4) | copy-start | bytes 1179652
  80.5 3.6 %copy-start.13 = (bf16[1024,64]{0,1:T(8,128)(2,1)S(1)}, bf16[1024,64]{0,1:T(8,128)(2,1)}, u32[]{:S(2)}) copy-start(bf16[1024,64]{0,1:T(8,128)(2,1)} %param.20) | copy-start | bytes 393220
  82.6 17.5 %collective-permute-start.12 = (bf16[512,512]{1,0:T(8,128)(2,1)S(1)}, bf16[512,512]{1,0:T(8,128)(2,1)S(1)}, u32[]{:S(2)}, u32[]{:S(2)}) collective-permute-start(bf16[512,512]{1,0:T(8,128)(2,1)S(1)} %token_grad.7.refs_5_.refs_4_.refs_13_), channel_id=1, source_target_pairs={{0,1},{3,2},{4,5},{7,6},{8,9},{11,10},{12,13},{15,14},{16,17},{19,... | collective-permute-start | bytes 1572872 | tf_op jit(solution)/shard_map/ppermute | solution.py:734
  88.1 7.9 %collective-permute-start.22 = (f32[4,192,384]{2,1,0:T(8,128)S(1)}, f32[4,192,384]{2,1,0:T(8,128)S(1)}, u32[]{:S(2)}, u32[]{:S(2)}) collective-permute-start(f32[4,192,384]{2,1,0:T(8,128)S(1)} %get-tuple-element.75), channel_id=1, source_target_pairs={{0,16},{16,0},{1,17},{17,1},{2,18},{18,2},{3,19},{19,3},{4,20},{20... | collective-permute-start | bytes 3538952 | tf_op jit(solution)/shard_map/ppermute | solution.py:139
  90.9 20.4 %collective-permute-start.16 = (bf16[512,512]{1,0:T(8,128)(2,1)S(1)}, bf16[512,512]{1,0:T(8,128)(2,1)S(1)}, u32[]{:S(2)}, u32[]{:S(2)}) collective-permute-start(bf16[512,512]{1,0:T(8,128)(2,1)S(1)} %token_grad.8.refs_5_), channel_id=1, source_target_pairs={{0,1},{1,2},{4,5},{5,6},{8,9},{9,10},{12,13},{13,14},{16,17},{17,1... | collective-permute-start | bytes 1572872 | tf_op jit(solution)/shard_map/ppermute | solution.py:734
  95.3 16.0 %collective-permute-start.17 = (bf16[512,512]{1,0:T(8,128)(2,1)S(1)}, bf16[512,512]{1,0:T(8,128)(2,1)S(1)}, u32[]{:S(2)}, u32[]{:S(2)}) collective-permute-start(bf16[512,512]{1,0:T(8,128)(2,1)S(1)} %token_grad.8.refs_5_), channel_id=1, source_target_pairs={{3,2},{2,1},{7,6},{6,5},{11,10},{10,9},{15,14},{14,13},{19,18},{18... | collective-permute-start | bytes 1572872 | tf_op jit(solution)/shard_map/ppermute | solution.py:734
  96.7 10.6 %collective-permute-start.23 = (bf16[2,192,384]{2,1,0:T(8,128)(2,1)S(1)}, bf16[2,192,384]{2,1,0:T(8,128)(2,1)S(1)}, u32[]{:S(2)}, u32[]{:S(2)}) collective-permute-start(bf16[2,192,384]{2,1,0:T(8,128)(2,1)S(1)} %get-tuple-element.77), channel_id=1, source_target_pairs={{0,8},{4,12},{8,0},{12,4},{1,9},{5,13},{9,1},{13,5},{2,10},{6,14},... | collective-permute-start | bytes 884744 | tf_op jit(solution)/shard_map/ppermute | solution.py:139
  102.1 20.4 %collective-permute-start.14 = (bf16[512,512]{1,0:T(8,128)(2,1)S(1)}, bf16[512,512]{1,0:T(8,128)(2,1)S(1)}, u32[]{:S(2)}, u32[]{:S(2)}) collective-permute-start(bf16[512,512]{1,0:T(8,128)(2,1)S(1)} %token_grad.9.refs_7_), channel_id=1, source_target_pairs={{0,1},{1,2},{4,5},{5,6},{8,9},{9,10},{12,13},{13,14},{16,17},{17,1... | collective-permute-start | bytes 1572872 | tf_op jit(solution)/shard_map/ppermute | solution.py:734
  106.5 16.0 %collective-permute-start.15 = (bf16[512,512]{1,0:T(8,128)(2,1)S(1)}, bf16[512,512]{1,0:T(8,128)(2,1)S(1)}, u32[]{:S(2)}, u32[]{:S(2)}) collective-permute-start(bf16[512,512]{1,0:T(8,128)(2,1)S(1)} %token_grad.9.refs_7_), channel_id=1, source_target_pairs={{3,2},{2,1},{7,6},{6,5},{11,10},{10,9},{15,14},{14,13},{19,18},{18... | collective-permute-start | bytes 1572872 | tf_op jit(solution)/shard_map/ppermute | solution.py:734
  107.9 11.6 %collective-permute-start.24 = (bf16[1,192,384]{2,1,0:T(8,128)(2,1)S(1)}, bf16[1,192,384]{2,1,0:T(8,128)(2,1)S(1)}, u32[]{:S(2)}, u32[]{:S(2)}) collective-permute-start(bf16[1,192,384]{2,1,0:T(8,128)(2,1)S(1)} %get-tuple-element.79), channel_id=1, source_target_pairs={{0,4},{4,0},{8,12},{12,8},{1,5},{5,1},{9,13},{13,9},{2,6},{6,2},{1... | collective-permute-start | bytes 442376 | tf_op jit(solution)/shard_map/ppermute | solution.py:139
  113.5 20.2 %collective-permute-start.20 = (bf16[512,512]{1,0:T(8,128)(2,1)S(1)}, bf16[512,512]{1,0:T(8,128)(2,1)S(1)}, u32[]{:S(2)}, u32[]{:S(2)}) collective-permute-start(bf16[512,512]{1,0:T(8,128)(2,1)S(1)} %get-tuple-element.68.refs_7_), channel_id=1, source_target_pairs={{0,1},{1,2},{2,3},{4,5},{5,6},{6,7},{8,9},{9,10},{10,11},{12,13},{... | collective-permute-start | bytes 1572872 | tf_op jit(solution)/shard_map/ppermute | solution.py:734
  117.9 15.8 %collective-permute-start.21 = (bf16[512,512]{1,0:T(8,128)(2,1)S(1)}, bf16[512,512]{1,0:T(8,128)(2,1)S(1)}, u32[]{:S(2)}, u32[]{:S(2)}) collective-permute-start(bf16[512,512]{1,0:T(8,128)(2,1)S(1)} %get-tuple-element.71), channel_id=1, source_target_pairs={{3,2},{2,1},{1,0},{7,6},{6,5},{5,4},{11,10},{10,9},{9,8},{15,14},{... | collective-permute-start | bytes 1572872 | tf_op jit(solution)/shard_map/ppermute | solution.py:734
  120.2 10.3 %collective-permute-start.28 = (f32[192,128]{1,0:T(8,128)S(1)}, f32[192,128]{1,0:T(8,128)S(1)}, u32[]{:S(2)}, u32[]{:S(2)}) collective-permute-start(f32[192,128]{1,0:T(8,128)S(1)} %get-tuple-element.84), channel_id=1, source_target_pairs={{0,4},{4,0},{8,12},{12,8},{1,5},{5,1},{9,13},{13,9},{2,6},{6,2},{1... | collective-permute-start | bytes 294920 | tf_op jit(solution)/shard_map/ppermute | solution.py:139
  124.7 20.2 %collective-permute-start.18 = (bf16[512,512]{1,0:T(8,128)(2,1)S(1)}, bf16[512,512]{1,0:T(8,128)(2,1)S(1)}, u32[]{:S(2)}, u32[]{:S(2)}) collective-permute-start(bf16[512,512]{1,0:T(8,128)(2,1)S(1)} %get-tuple-element.69.refs_6_), channel_id=1, source_target_pairs={{0,1},{1,2},{2,3},{4,5},{5,6},{6,7},{8,9},{9,10},{10,11},{12,13},{... | collective-permute-start | bytes 1572872 | tf_op jit(solution)/shard_map/ppermute | solution.py:734
  129.2 15.8 %collective-permute-start.19 = (bf16[512,512]{1,0:T(8,128)(2,1)S(1)}, bf16[512,512]{1,0:T(8,128)(2,1)S(1)}, u32[]{:S(2)}, u32[]{:S(2)}) collective-permute-start(bf16[512,512]{1,0:T(8,128)(2,1)S(1)} %get-tuple-element.70.refs_7_), channel_id=1, source_target_pairs={{3,2},{2,1},{1,0},{7,6},{6,5},{5,4},{11,10},{10,9},{9,8},{15,14},{... | collective-permute-start | bytes 1572872 | tf_op jit(solution)/shard_map/ppermute | solution.py:734
  130.5 9.6 %collective-permute-start.29 = (f32[2,192,128]{2,1,0:T(8,128)S(1)}, f32[2,192,128]{2,1,0:T(8,128)S(1)}, u32[]{:S(2)}, u32[]{:S(2)}) collective-permute-start(f32[2,192,128]{2,1,0:T(8,128)S(1)} %pad_maximum_fusion.2), channel_id=1, source_target_pairs={{0,8},{4,12},{8,0},{12,4},{1,9},{5,13},{9,1},{13,5},{2,10},{6,14},... | collective-permute-start | bytes 589832 | tf_op jit(solution)/shard_map/ppermute | solution.py:139
  136.6 11.2 %collective-permute-start.25 = (bf16[64,192]{1,0:T(8,128)(2,1)S(1)}, bf16[64,192]{1,0:T(8,128)(2,1)S(1)}, u32[]{:S(2)}, u32[]{:S(2)}) collective-permute-start(bf16[64,192]{1,0:T(8,128)(2,1)S(1)} %get-tuple-element.81), channel_id=1, source_target_pairs={{0,1},{1,0},{2,3},{3,2},{4,5},{5,4},{6,7},{7,6},{8,9},{9,8},{10,11... | collective-permute-start | bytes 73736 | tf_op jit(solution)/shard_map/ppermute | solution.py:139
  139.1 8.8 %collective-permute-start.26 = (bf16[64,192]{1,0:T(8,128)(2,1)S(1)}, bf16[64,192]{1,0:T(8,128)(2,1)S(1)}, u32[]{:S(2)}, u32[]{:S(2)}) collective-permute-start(bf16[64,192]{1,0:T(8,128)(2,1)S(1)} %get-tuple-element.82), channel_id=1, source_target_pairs={{0,2},{1,3},{2,0},{3,1},{4,6},{5,7},{6,4},{7,5},{8,10},{9,11},{10,... | collective-permute-start | bytes 73736 | tf_op jit(solution)/shard_map/ppermute | solution.py:139
  140.1 9.1 %collective-permute-start.27 = (bf16[64,192]{1,0:T(8,128)(2,1)S(1)}, bf16[64,192]{1,0:T(8,128)(2,1)S(1)}, u32[]{:S(2)}, u32[]{:S(2)}) collective-permute-start(bf16[64,192]{1,0:T(8,128)(2,1)S(1)} %get-tuple-element.83), channel_id=1, source_target_pairs={{0,3},{1,2},{2,1},{3,0},{4,7},{5,6},{6,5},{7,4},{8,11},{9,10},{10,... | collective-permute-start | bytes 73736 | tf_op jit(solution)/shard_map/ppermute | solution.py:139
  145.0 5.4 %collective-permute-start.30 = (f32[4,192,128]{2,1,0:T(8,128)S(1)}, f32[4,192,128]{2,1,0:T(8,128)S(1)}, u32[]{:S(2)}, u32[]{:S(2)}) collective-permute-start(f32[4,192,128]{2,1,0:T(8,128)S(1)} %pad_maximum_fusion.1.near), channel_id=1, source_target_pairs={{0,16},{16,0},{1,17},{17,1},{2,18},{18,2},{3,19},{19,3},{4,20},{20... | collective-permute-start | bytes 1179656 | tf_op jit(solution)/shard_map/ppermute | solution.py:139

commit v9 on v8

--- a/solution.py
+++ b/solution.py
@@ -13,7 +13,7 @@
 COST = 1
 HALVES = 2
 COSTS = {"sums": 1, "pair": 1, "small": 1, "token": 20 * 10**9, "adapter": 20 * 10**9, "last": 10**11}
-LIMITS = {"low": 6, "sums": 25, "last": 14, "token": 8, "adapter": 12, "small": 4}
+LIMITS = {"low": 6, "sums": 23, "last": 14, "token": 8, "adapter": 12, "small": 4}
 TILE = 512
 STRIP = 256
 QUARTER_ORDER = ((3, 2, 1, 0), (0, 3, 2, 1), (3, 0, 1, 2), (0, 1, 2, 3))

time: 152 us -> 152 us (level)
    unnamed x34 -> x32, local copies, waits for them, and re-layouts: 8.53 us -> 8.46 us
  transfers between devices with their start and end apart: 31 -> 31, of which waited for: 14 -> 15; matrix products, arithmetic and copies ran while one was open for 0% -> 0% of each run, Pallas kernels for 31% -> 31%
where the time goes in v9:
time: 152 us
  Pallas kernels  56.5 us (37%)
  starting transfers between devices  47.5 us (31%)
  waiting for transfers between devices  38.2 us (25%)
  local copies, waits for them, and re-layouts  8.46 us (6%)
    pallas_call x16, Pallas kernels, vmem_call(): pl.pallas_call(kernel, in_specs=[pl.BlockSpec(memory_space=pltpu.SMEM)] *...  29.2 us
    ppermute x10, starting transfers between devices, square_plane(): shift = lambda array, pairs: lax.ppermute(array, 'tp', pairs)  26.9 us
    ppermute x21, waiting for transfers between devices, flip(): return lax.ppermute(array, axis, [(i, i ^ bit) for i in range(size)])  25.8 us
    ppermute x21, starting transfers between devices, flip(): return lax.ppermute(array, axis, [(i, i ^ bit) for i in range(size)])  20.6 us
    pallas_call x1, Pallas kernels, width_sums(): pl.pallas_call(functools.partial(sums_kernel, masks, order, len(arrays),...  15.3 us
    ppermute x10, waiting for transfers between devices, square_plane(): shift = lambda array, pairs: lax.ppermute(array, 'tp', pairs)  12.4 us
    unnamed x32, local copies, waits for them, and re-layouts  8.46 us
    pallas_call x2, Pallas kernels, last_token_grad(): pl.pallas_call(functools.partial(token_grad_kernel, 'last', step), grid=(...  5.68 us
  transfers between devices with their start and end apart: 31, of which 15 were waited for; matrix products, arithmetic and copies ran while one was open for 0% of the time, Pallas kernels for 31%

profile of v9, /device:TPU:0, one launch (start us, length us, event | category | flops | bytes accessed | tf_op | source)
XLA Modules:
  0.0 151.9 jit_solution(13673916447326109756)
XLA Ops:
  0.6 2.3 %own_units.1 = (bf16[3,128,1024]{2,1,0:T(8,128)(2,1)S(1)}, bf16[3,128,1024]{2,1,0:T(8,128)(2,1)}) custom-call(bf16[256,1024]{1,0:T(8,128)(2,1)} %gate.1, bf16[256,1024]{1,0:T(8,128)(2,1)} %up.1, bf16[1024,256]{1,0:T(8,128)(2,1)} %down.1), custom_call_target="tpu_custom_call" | custom-call | flops 1048576 | tf_op jit(solution)/shard_map/own_units/pallas_call | solution.py:243
  2.9 3.0 %collective-permute-start = (bf16[3,128,1024]{2,1,0:T(8,128)(2,1)S(1)}, bf16[3,128,1024]{2,1,0:T(8,128)(2,1)S(1)}, u32[]{:S(2)}, u32[]{:S(2)}) collective-permute-start(bf16[3,128,1024]{2,1,0:T(8,128)(2,1)S(1)} %get-tuple-element.44.refs_8_), channel_id=1, source_target_pairs={{0,4},{4,0},{8,12},{12,8},{1,5},{5,1},{9,13},{13,9},{2,6},{6,2},{1... | collective-permute-start | bytes 2359304 | tf_op jit(solution)/shard_map/ppermute | solution.py:139
  5.9 1.5 %collective-permute-start.1 = (bf16[3,128,1024]{2,1,0:T(8,128)(2,1)}, bf16[3,128,1024]{2,1,0:T(8,128)(2,1)S(1)}, u32[]{:S(2)}, u32[]{:S(2)}) collective-permute-start(bf16[3,128,1024]{2,1,0:T(8,128)(2,1)} %get-tuple-element.45.refs_9_), channel_id=1, source_target_pairs={{0,8},{4,12},{8,0},{12,4},{1,9},{5,13},{9,1},{13,5},{2,10},{6,14},... | collective-permute-start | bytes 2359304 | tf_op jit(solution)/shard_map/ppermute | solution.py:139
  7.4 0.5 collective-permute-start.3
  7.9 0.5 collective-permute-start.4
  8.6 15.7 %collective-permute-done.refs_1_.first.refs_10_ = bf16[3,128,1024]{2,1,0:T(8,128)(2,1)S(1)} collective-permute-done((bf16[3,128,1024]{2,1,0:T(8,128)(2,1)S(1)}, bf16[3,128,1024]{2,1,0:T(8,128)(2,1)S(1)}, u32[]{:S(2)}, u32[]{:S(2)}) %collective-permute-start) | collective-permute-done | bytes 786464 | tf_op jit(solution)/shard_map/ppermute | solution.py:139
  24.3 2.1 %collective-permute-start.5 = (bf16[3,128,1024]{2,1,0:T(8,128)(2,1)S(1)}, bf16[3,128,1024]{2,1,0:T(8,128)(2,1)S(1)}, u32[]{:S(2)}, u32[]{:S(2)}) collective-permute-start(bf16[3,128,1024]{2,1,0:T(8,128)(2,1)S(1)} %get-tuple-element.44.refs_8_), channel_id=1, source_target_pairs={{0,8},{4,12},{8,0},{12,4},{1,9},{5,13},{9,1},{13,5},{2,10},{6,14},... | collective-permute-start | bytes 2359304 | tf_op jit(solution)/shard_map/ppermute | solution.py:139
  26.4 2.2 %copy-done = bf16[1024,2048]{1,0:T(8,128)(2,1)S(1)} copy-done((bf16[1024,2048]{1,0:T(8,128)(2,1)S(1)}, bf16[1024,2048]{1,0:T(8,128)(2,1)}, u32[]{:S(2)}) %copy-start) | copy-done | bytes 4194328
  28.6 2.2 %copy-done.2 = bf16[1024,2048]{1,0:T(8,128)(2,1)S(1)} copy-done((bf16[1024,2048]{1,0:T(8,128)(2,1)S(1)}, bf16[1024,2048]{1,0:T(8,128)(2,1)}, u32[]{:S(2)}) %copy-start.2) | copy-done | bytes 4194328
  30.8 0.9 copy-done.6
  31.7 0.9 copy-done.8
  32.7 0.9 copy-done.14
  33.6 4.1 %low_rank_values.1 = (bf16[1024,64]{1,0:T(8,128)(2,1)S(1)}, bf16[1024,64]{1,0:T(8,128)(2,1)S(1)}, bf16[1024,64]{1,0:T(8,128)(2,1)S(1)}, bf16[192,1024]{1,0:T(8,128)(2,1)S(1)}) custom-call(bf16[1024,2048]{1,0:T(8,128)(2,1)S(1)} %copy-done, bf16[1024,2048]{1,0:T(8,128)(2,1)S(1)} %copy-done.2, bf16[64,2048]{1,0:T(8,128)(2,1)S(1)} %bitcast.11, ...), custom_call_target="tpu_custom_call" | custom-call | flops 64424509440 | tf_op jit(solution)/shard_map/low_rank_values/pallas_call | solution.py:201
  38.0 2.3 %collective-permute-done.4.first.refs_11_ = bf16[3,128,1024]{2,1,0:T(8,128)(2,1)S(1)} collective-permute-done((bf16[3,128,1024]{2,1,0:T(8,128)(2,1)}, bf16[3,128,1024]{2,1,0:T(8,128)(2,1)S(1)}, u32[]{:S(2)}, u32[]{:S(2)}) %collective-permute-start.4) | collective-permute-done | bytes 786464 | tf_op jit(solution)/shard_map/ppermute | solution.py:139
  40.3 1.9 %collective-permute-done.5.second.refs_12_ = bf16[3,128,1024]{2,1,0:T(8,128)(2,1)S(1)} collective-permute-done((bf16[3,128,1024]{2,1,0:T(8,128)(2,1)S(1)}, bf16[3,128,1024]{2,1,0:T(8,128)(2,1)S(1)}, u32[]{:S(2)}, u32[]{:S(2)}) %collective-permute-start.5) | collective-permute-done | bytes 786464 | tf_op jit(solution)/shard_map/ppermute | solution.py:139
  42.4 1.5 collective-permute-start.8
  43.9 1.5 collective-permute-start.9
  45.4 0.4 collective-permute-done.7.refs_17_
  45.8 1.2 copy-done.15
  47.0 15.3 %width_sums.1 = (f32[512,1024]{1,0:T(8,128)S(1)}, f32[512,1024]{1,0:T(8,128)S(1)}, f32[512,1024]{1,0:T(8,128)S(1)}, f32[512,1024]{1,0:T(8,128)S(1)}, f32[512,102...) custom-call(s32[2]{0:T(128)S(1)} %pad_add_fusion.refs_0_.here, ...), custom_call_target="tpu_custom_call" | custom-call | flops 1 | tf_op jit(solution)/shard_map/width_sums/pallas_call | solution.py:377
  62.3 1.2 collective-permute-done.9.refs_1_
  63.5 0.5 collective-permute-start.11
  64.1 1.7 %collective-permute-done.10.refs_2_ = bf16[3,128,1024]{2,1,0:T(8,128)(2,1)S(1)} collective-permute-done((bf16[3,128,1024]{2,1,0:T(8,128)(2,1)S(1)}, bf16[3,128,1024]{2,1,0:T(8,128)(2,1)S(1)}, u32[]{:S(2)}, u32[]{:S(2)}) %collective-permute-start.10) | collective-permute-done | bytes 786464 | tf_op jit(solution)/shard_map/ppermute | solution.py:139
  65.8 1.1 collective-permute-done.11.refs_3_
  66.9 3.8 %hidden_and_grads.2 = (bf16[512,1024]{1,0:T(8,128)(2,1)S(1)}, bf16[512,1024]{1,0:T(8,128)(2,1)S(1)}, bf16[512,1024]{1,0:T(8,128)(2,1)S(1)}, f32[512,128]{1,0:T(8,128)S(1)}) custom-call(s32[2]{0:T(128)S(1)} %pad_add_fusion.refs_0_.here, bf16[1024,512]{1,0:T(8,128)(2,1)S(1)} %get-tuple-element.50.left, bf16[1024,512]{1,0:T(8,128)(2,1)S(1)} %get-tuple-element.51.back, ...), custom_call_target="tpu_custom_call" | custom-call | flops 99999997952 | tf_op jit(solution)/shard_map/hidden_and_grads/pallas_call | solution.py:147
  70.8 2.3 %token_grad.6.refs_7_.refs_4_.refs_12_ = bf16[512,512]{1,0:T(8,128)(2,1)S(1)} custom-call(s32[2]{0:T(128)S(1)} %pad_add_fusion.refs_0_.here, bf16[512,1024]{1,0:T(8,128)(2,1)S(1)} %get-tuple-element.60.gate_grad.refs_2_, bf16[512,1024]{1,0:T(8,128)(2,1)S(1)} %get-tuple-element.61.up_grad.refs_4_, f32[512,128]{1,0:T(8,128)S(1)} %get-tuple-element.62.low.refs_6_, ...), custom_call_target="tpu_custom_call" | custom-call | flops 20000000000 | tf_op jit(solution)/shard_map/token_grad/pallas_call | solution.py:147
  73.1 3.5 %collective-permute-start.13 = (bf16[512,512]{1,0:T(8,128)(2,1)S(1)}, bf16[512,512]{1,0:T(8,128)(2,1)S(1)}, u32[]{:S(2)}, u32[]{:S(2)}) collective-permute-start(bf16[512,512]{1,0:T(8,128)(2,1)S(1)} %token_grad.6.refs_7_.refs_4_.refs_12_), channel_id=1, source_target_pairs={{0,1},{3,2},{4,5},{7,6},{8,9},{11,10},{12,13},{15,14},{16,17},{19,... | collective-permute-start | bytes 1572872 | tf_op jit(solution)/shard_map/ppermute | solution.py:734
  76.6 3.8 %hidden_and_grads.3 = (bf16[512,1024]{1,0:T(8,128)(2,1)S(1)}, bf16[512,1024]{1,0:T(8,128)(2,1)S(1)}, bf16[512,1024]{1,0:T(8,128)(2,1)S(1)}, f32[512,128]{1,0:T(8,128)S(1)}) custom-call(s32[2]{0:T(128)S(1)} %pad_add_fusion.refs_0_.here, bf16[1024,512]{1,0:T(8,128)(2,1)S(1)} %get-tuple-element.50.left, bf16[1024,512]{1,0:T(8,128)(2,1)S(1)} %get-tuple-element.51.back, ...), custom_call_target="tpu_custom_call" | custom-call | flops 99999997952 | tf_op jit(solution)/shard_map/hidden_and_grads/pallas_call | solution.py:147
  80.5 2.0 %token_grad.7.refs_5_.refs_4_.refs_13_ = bf16[512,512]{1,0:T(8,128)(2,1)S(1)} custom-call(s32[2]{0:T(128)S(1)} %pad_add_fusion.refs_0_.here, bf16[512,1024]{1,0:T(8,128)(2,1)S(1)} %get-tuple-element.65.gate_grad.refs_3_, bf16[512,1024]{1,0:T(8,128)(2,1)S(1)} %get-tuple-element.66.up_grad.refs_5_, f32[512,128]{1,0:T(8,128)S(1)} %get-tuple-element.67.low.refs_7_, ...), custom_call_target="tpu_custom_call" | custom-call | flops 20000000000 | tf_op jit(solution)/shard_map/token_grad/pallas_call | solution.py:147
  82.4 1.5 collective-permute-start.12
  83.9 4.0 %adapter_grads.1 = (f32[4,192,384]{2,1,0:T(8,128)S(1)}, f32[4,192,384]{2,1,0:T(8,128)S(1)}) custom-call(s32[2]{0:T(128)S(1)} %pad_add_fusion.refs_0_.here, bf16[512,1024]{1,0:T(8,128)(2,1)S(1)} %get-tuple-element.72.refs_0_, bf16[512,1024]{1,0:T(8,128)(2,1)S(1)} %get-tuple-element.73.refs_1_, bf16[512,1024]{1,0:T(8,128)(2,1)S(1)} %get-tuple-element.60.gate_grad.refs_2_, ...), custom_call_target="tpu_custom_call" | custom-call | flops 20000000000 | tf_op jit(solution)/shard_map/adapter_grads/pallas_call | solution.py:147
  88.1 0.7 collective-permute-done.13.refs_4_
  88.8 2.1 %token_grad.8.refs_5_ = bf16[512,512]{1,0:T(8,128)(2,1)S(1)} custom-call(s32[2]{0:T(128)S(1)} %pad_add_fusion.refs_0_.here, bf16[512,1024]{1,0:T(8,128)(2,1)S(1)} %get-tuple-element.60.gate_grad.refs_2_, bf16[512,1024]{1,0:T(8,128)(2,1)S(1)} %get-tuple-element.61.up_grad.refs_4_, f32[512,128]{1,0:T(8,128)S(1)} %get-tuple-element.62.low.refs_6_, ...), custom_call_target="tpu_custom_call" | custom-call | flops 20000000000 | tf_op jit(solution)/shard_map/token_grad/pallas_call | solution.py:147
  90.9 4.4 %collective-permute-start.16 = (bf16[512,512]{1,0:T(8,128)(2,1)S(1)}, bf16[512,512]{1,0:T(8,128)(2,1)S(1)}, u32[]{:S(2)}, u32[]{:S(2)}) collective-permute-start(bf16[512,512]{1,0:T(8,128)(2,1)S(1)} %token_grad.8.refs_5_), channel_id=1, source_target_pairs={{0,1},{1,2},{4,5},{5,6},{8,9},{9,10},{12,13},{13,14},{16,17},{17,1... | collective-permute-start | bytes 1572872 | tf_op jit(solution)/shard_map/ppermute | solution.py:734
  95.3 0.7 collective-permute-start.17
  96.0 0.7 halve.2
  96.7 0.6 collective-permute-start.23
  97.3 2.8 %collective-permute-done.12.refs_4_ = bf16[512,512]{1,0:T(8,128)(2,1)S(1)} collective-permute-done((bf16[512,512]{1,0:T(8,128)(2,1)S(1)}, bf16[512,512]{1,0:T(8,128)(2,1)S(1)}, u32[]{:S(2)}, u32[]{:S(2)}) %collective-permute-start.12) | collective-permute-done | bytes 524320 | tf_op jit(solution)/shard_map/ppermute | solution.py:734
  100.1 2.0 %token_grad.9.refs_7_ = bf16[512,512]{1,0:T(8,128)(2,1)S(1)} custom-call(s32[2]{0:T(128)S(1)} %pad_add_fusion.refs_0_.here, bf16[512,1024]{1,0:T(8,128)(2,1)S(1)} %get-tuple-element.65.gate_grad.refs_3_, bf16[512,1024]{1,0:T(8,128)(2,1)S(1)} %get-tuple-element.66.up_grad.refs_5_, f32[512,128]{1,0:T(8,128)S(1)} %get-tuple-element.67.low.refs_7_, ...), custom_call_target="tpu_custom_call" | custom-call | flops 20000000000 | tf_op jit(solution)/shard_map/token_grad/pallas_call | solution.py:147
  102.0 4.4 %collective-permute-start.14 = (bf16[512,512]{1,0:T(8,128)(2,1)S(1)}, bf16[512,512]{1,0:T(8,128)(2,1)S(1)}, u32[]{:S(2)}, u32[]{:S(2)}) collective-permute-start(bf16[512,512]{1,0:T(8,128)(2,1)S(1)} %token_grad.9.refs_7_), channel_id=1, source_target_pairs={{0,1},{1,2},{4,5},{5,6},{8,9},{9,10},{12,13},{13,14},{16,17},{17,1... | collective-permute-start | bytes 1572872 | tf_op jit(solution)/shard_map/ppermute | solution.py:734
  106.5 0.7 collective-permute-start.15
  107.2 0.6 halve.3
  107.8 1.6 %collective-permute-start.24 = (bf16[1,192,384]{2,1,0:T(8,128)(2,1)S(1)}, bf16[1,192,384]{2,1,0:T(8,128)(2,1)S(1)}, u32[]{:S(2)}, u32[]{:S(2)}) collective-permute-start(bf16[1,192,384]{2,1,0:T(8,128)(2,1)S(1)} %get-tuple-element.79), channel_id=1, source_target_pairs={{0,4},{4,0},{8,12},{12,8},{1,5},{5,1},{9,13},{13,9},{2,6},{6,2},{1... | collective-permute-start | bytes 442376 | tf_op jit(solution)/shard_map/ppermute | solution.py:139
  109.3 2.0 %collective-permute-done.16.refs_5_ = bf16[512,512]{1,0:T(8,128)(2,1)S(1)} collective-permute-done((bf16[512,512]{1,0:T(8,128)(2,1)S(1)}, bf16[512,512]{1,0:T(8,128)(2,1)S(1)}, u32[]{:S(2)}, u32[]{:S(2)}) %collective-permute-start.16) | collective-permute-done | bytes 524320 | tf_op jit(solution)/shard_map/ppermute | solution.py:734
  111.3 2.2 %token_grad.10 = (bf16[512,512]{1,0:T(8,128)(2,1)S(1)}, bf16[512,512]{1,0:T(8,128)(2,1)S(1)}) custom-call(s32[2]{0:T(128)S(1)} %pad_add_fusion.refs_0_.here, bf16[512,1024]{1,0:T(8,128)(2,1)S(1)} %get-tuple-element.60.gate_grad.refs_2_, bf16[512,1024]{1,0:T(8,128)(2,1)S(1)} %get-tuple-element.61.up_grad.refs_4_, ...), custom_call_target="tpu_custom_call" | custom-call | flops 20000000000 | tf_op jit(solution)/shard_map/token_grad/pallas_call | solution.py:147
  113.5 4.4 %collective-permute-start.20 = (bf16[512,512]{1,0:T(8,128)(2,1)S(1)}, bf16[512,512]{1,0:T(8,128)(2,1)S(1)}, u32[]{:S(2)}, u32[]{:S(2)}) collective-permute-start(bf16[512,512]{1,0:T(8,128)(2,1)S(1)} %get-tuple-element.68.refs_7_), channel_id=1, source_target_pairs={{0,1},{1,2},{2,3},{4,5},{5,6},{6,7},{8,9},{9,10},{10,11},{12,13},{... | collective-permute-start | bytes 1572872 | tf_op jit(solution)/shard_map/ppermute | solution.py:734
  117.9 1.6 %collective-permute-start.21 = (bf16[512,512]{1,0:T(8,128)(2,1)S(1)}, bf16[512,512]{1,0:T(8,128)(2,1)S(1)}, u32[]{:S(2)}, u32[]{:S(2)}) collective-permute-start(bf16[512,512]{1,0:T(8,128)(2,1)S(1)} %get-tuple-element.71), channel_id=1, source_target_pairs={{3,2},{2,1},{1,0},{7,6},{6,5},{5,4},{11,10},{10,9},{9,8},{15,14},{... | collective-permute-start | bytes 1572872 | tf_op jit(solution)/shard_map/ppermute | solution.py:734
  119.5 0.7 turn.1
  120.2 1.6 %collective-permute-start.28 = (f32[192,128]{1,0:T(8,128)S(1)}, f32[192,128]{1,0:T(8,128)S(1)}, u32[]{:S(2)}, u32[]{:S(2)}) collective-permute-start(f32[192,128]{1,0:T(8,128)S(1)} %get-tuple-element.84), channel_id=1, source_target_pairs={{0,4},{4,0},{8,12},{12,8},{1,5},{5,1},{9,13},{13,9},{2,6},{6,2},{1... | collective-permute-start | bytes 294920 | tf_op jit(solution)/shard_map/ppermute | solution.py:139
  121.8 0.8 collective-permute-done.14.refs_5_
  122.5 2.1 %token_grad.11 = (bf16[512,512]{1,0:T(8,128)(2,1)S(1)}, bf16[512,512]{1,0:T(8,128)(2,1)S(1)}) custom-call(s32[2]{0:T(128)S(1)} %pad_add_fusion.refs_0_.here, bf16[512,1024]{1,0:T(8,128)(2,1)S(1)} %get-tuple-element.65.gate_grad.refs_3_, bf16[512,1024]{1,0:T(8,128)(2,1)S(1)} %get-tuple-element.66.up_grad.refs_5_, ...), custom_call_target="tpu_custom_call" | custom-call | flops 20000000000 | tf_op jit(solution)/shard_map/token_grad/pallas_call | solution.py:147
  124.7 4.4 %collective-permute-start.18 = (bf16[512,512]{1,0:T(8,128)(2,1)S(1)}, bf16[512,512]{1,0:T(8,128)(2,1)S(1)}, u32[]{:S(2)}, u32[]{:S(2)}) collective-permute-start(bf16[512,512]{1,0:T(8,128)(2,1)S(1)} %get-tuple-element.69.refs_6_), channel_id=1, source_target_pairs={{0,1},{1,2},{2,3},{4,5},{5,6},{6,7},{8,9},{9,10},{10,11},{12,13},{... | collective-permute-start | bytes 1572872 | tf_op jit(solution)/shard_map/ppermute | solution.py:734
  129.1 1.3 collective-permute-start.19
  130.4 0.6 collective-permute-start.29
  131.0 2.8 %collective-permute-done.20.refs_4_ = bf16[512,512]{1,0:T(8,128)(2,1)S(1)} collective-permute-done((bf16[512,512]{1,0:T(8,128)(2,1)S(1)}, bf16[512,512]{1,0:T(8,128)(2,1)S(1)}, u32[]{:S(2)}, u32[]{:S(2)}) %collective-permute-start.20) | collective-permute-done | bytes 524320 | tf_op jit(solution)/shard_map/ppermute | solution.py:734
  133.8 2.9 %last_token_grad.2.refs_6_ = bf16[1024,512]{1,0:T(8,128)(2,1)} custom-call(s32[2]{0:T(128)S(1)} %pad_add_fusion.refs_0_.here, bf16[512,1024]{1,0:T(8,128)(2,1)S(1)} %get-tuple-element.60.gate_grad.refs_2_, bf16[512,1024]{1,0:T(8,128)(2,1)S(1)} %get-tuple-element.61.up_grad.refs_4_, f32[512,128]{1,0:T(8,128)S(1)} %get-tuple-element.62.low.refs_6_, ...), custom_call_target="tpu_custom_call" | custom-call | flops 20000000000 | tf_op jit(solution)/shard_map/last_token_grad/pallas_call | solution.py:495
  136.6 2.5 %collective-permute-start.25 = (bf16[64,192]{1,0:T(8,128)(2,1)S(1)}, bf16[64,192]{1,0:T(8,128)(2,1)S(1)}, u32[]{:S(2)}, u32[]{:S(2)}) collective-permute-start(bf16[64,192]{1,0:T(8,128)(2,1)S(1)} %get-tuple-element.81), channel_id=1, source_target_pairs={{0,1},{1,0},{2,3},{3,2},{4,5},{5,4},{6,7},{7,6},{8,9},{9,8},{10,11... | collective-permute-start | bytes 73736 | tf_op jit(solution)/shard_map/ppermute | solution.py:139
  139.1 1.0 collective-permute-start.26
  140.1 1.5 collective-permute-start.27
  141.6 3.4 %collective-permute-done.18.refs_4_ = bf16[512,512]{1,0:T(8,128)(2,1)S(1)} collective-permute-done((bf16[512,512]{1,0:T(8,128)(2,1)S(1)}, bf16[512,512]{1,0:T(8,128)(2,1)S(1)}, u32[]{:S(2)}, u32[]{:S(2)}) %collective-permute-start.18) | collective-permute-done | bytes 524320 | tf_op jit(solution)/shard_map/ppermute | solution.py:734
  145.0 2.8 %last_token_grad.3 = bf16[1024,512]{1,0:T(8,128)(2,1)} custom-call(s32[2]{0:T(128)S(1)} %pad_add_fusion.refs_0_.here, bf16[512,1024]{1,0:T(8,128)(2,1)S(1)} %get-tuple-element.65.gate_grad.refs_3_, bf16[512,1024]{1,0:T(8,128)(2,1)S(1)} %get-tuple-element.66.up_grad.refs_5_, ...), custom_call_target="tpu_custom_call", output_to_operand_aliasing={{}: (13, {})} | custom-call | flops 20000000000 | tf_op jit(solution)/shard_map/last_token_grad/pallas_call | solution.py:495
  147.8 1.4 collective-permute-done.27.refs_2_
  149.2 1.2 last_sum.1
  150.4 1.5 whole.1
  (56 shorter events, 0.8 us)
Async XLA Ops:
  2.9 21.4 %collective-permute-start = (bf16[3,128,1024]{2,1,0:T(8,128)(2,1)S(1)}, bf16[3,128,1024]{2,1,0:T(8,128)(2,1)S(1)}, u32[]{:S(2)}, u32[]{:S(2)}) collective-permute-start(bf16[3,128,1024]{2,1,0:T(8,128)(2,1)S(1)} %get-tuple-element.44.refs_8_), channel_id=1, source_target_pairs={{0,4},{4,0},{8,12},{12,8},{1,5},{5,1},{9,13},{13,9},{2,6},{6,2},{1... | collective-permute-start | bytes 2359304 | tf_op jit(solution)/shard_map/ppermute | solution.py:139
  5.9 20.5 %collective-permute-start.1 = (bf16[3,128,1024]{2,1,0:T(8,128)(2,1)}, bf16[3,128,1024]{2,1,0:T(8,128)(2,1)S(1)}, u32[]{:S(2)}, u32[]{:S(2)}) collective-permute-start(bf16[3,128,1024]{2,1,0:T(8,128)(2,1)} %get-tuple-element.45.refs_9_), channel_id=1, source_target_pairs={{0,8},{4,12},{8,0},{12,4},{1,9},{5,13},{9,1},{13,5},{2,10},{6,14},... | collective-permute-start | bytes 2359304 | tf_op jit(solution)/shard_map/ppermute | solution.py:139
  7.4 18.9 %collective-permute-start.2 = (bf16[3,128,1024]{2,1,0:T(8,128)(2,1)S(1)}, bf16[3,128,1024]{2,1,0:T(8,128)(2,1)}, u32[]{:S(2)}, u32[]{:S(2)}) collective-permute-start(bf16[3,128,1024]{2,1,0:T(8,128)(2,1)S(1)} %get-tuple-element.44.refs_8_), channel_id=1, source_target_pairs={{0,16},{16,0},{1,17},{17,1},{2,18},{18,2},{3,19},{19,3},{4,20},{20... | collective-permute-start | bytes 2359304 | tf_op jit(solution)/shard_map/ppermute | solution.py:139
  7.4 18.9 %collective-permute-start.3 = (bf16[3,128,1024]{2,1,0:T(8,128)(2,1)}, bf16[3,128,1024]{2,1,0:T(8,128)(2,1)}, u32[]{:S(2)}, u32[]{:S(2)}) collective-permute-start(bf16[3,128,1024]{2,1,0:T(8,128)(2,1)} %get-tuple-element.45.refs_9_), channel_id=1, source_target_pairs={{0,16},{16,0},{1,17},{17,1},{2,18},{18,2},{3,19},{19,3},{4,20},{20... | collective-permute-start | bytes 2359304 | tf_op jit(solution)/shard_map/ppermute | solution.py:139
  7.9 32.4 %collective-permute-start.4 = (bf16[3,128,1024]{2,1,0:T(8,128)(2,1)}, bf16[3,128,1024]{2,1,0:T(8,128)(2,1)S(1)}, u32[]{:S(2)}, u32[]{:S(2)}) collective-permute-start(bf16[3,128,1024]{2,1,0:T(8,128)(2,1)} %get-tuple-element.45.refs_9_), channel_id=1, source_target_pairs={{0,4},{4,0},{8,12},{12,8},{1,5},{5,1},{9,13},{13,9},{2,6},{6,2},{1... | collective-permute-start | bytes 2359304 | tf_op jit(solution)/shard_map/ppermute | solution.py:139
  24.3 17.9 %collective-permute-start.5 = (bf16[3,128,1024]{2,1,0:T(8,128)(2,1)S(1)}, bf16[3,128,1024]{2,1,0:T(8,128)(2,1)S(1)}, u32[]{:S(2)}, u32[]{:S(2)}) collective-permute-start(bf16[3,128,1024]{2,1,0:T(8,128)(2,1)S(1)} %get-tuple-element.44.refs_8_), channel_id=1, source_target_pairs={{0,8},{4,12},{8,0},{12,4},{1,9},{5,13},{9,1},{13,5},{2,10},{6,14},... | collective-permute-start | bytes 2359304 | tf_op jit(solution)/shard_map/ppermute | solution.py:139
  26.4 2.2 %copy-start = (bf16[1024,2048]{1,0:T(8,128)(2,1)S(1)}, bf16[1024,2048]{1,0:T(8,128)(2,1)}, u32[]{:S(2)}) copy-start(bf16[1024,2048]{1,0:T(8,128)(2,1)} %refs_8_.1) | copy-start | bytes 12582916
  28.6 2.2 %copy-start.2 = (bf16[1024,2048]{1,0:T(8,128)(2,1)S(1)}, bf16[1024,2048]{1,0:T(8,128)(2,1)}, u32[]{:S(2)}) copy-start(bf16[1024,2048]{1,0:T(8,128)(2,1)} %refs_9_.1) | copy-start | bytes 12582916
  30.8 0.9 copy-start.6
  31.7 0.9 copy-start.8
  32.7 0.9 copy-start.14
  37.7 4.6 %copy-start.4 = (bf16[192,1024]{1,0:T(8,128)(2,1)}, bf16[192,1024]{1,0:T(8,128)(2,1)S(1)}, u32[]{:S(2)}) copy-start(bf16[192,1024]{1,0:T(8,128)(2,1)S(1)} %get-tuple-element.49.refs_0_.refs_10_) | copy-start | bytes 1179652
  37.9 9.1 %copy-start.10 = (bf16[64,1024]{1,0:T(8,128)(2,1)S(1)}, bf16[64,1024]{1,0:T(8,128)(2,1)}, u32[]{:S(2)}) copy-start(bf16[64,1024]{1,0:T(8,128)(2,1)} %gate_out.3) | copy-start | bytes 393220
  37.9 9.1 %copy-start.11 = (bf16[64,1024]{1,0:T(8,128)(2,1)S(1)}, bf16[64,1024]{1,0:T(8,128)(2,1)}, u32[]{:S(2)}) copy-start(bf16[64,1024]{1,0:T(8,128)(2,1)} %up_out.3) | copy-start | bytes 393220
  37.9 9.1 %copy-start.12 = (bf16[1024,64]{0,1:T(8,128)(2,1)S(1)}, bf16[1024,64]{0,1:T(8,128)(2,1)}, u32[]{:S(2)}) copy-start(bf16[1024,64]{0,1:T(8,128)(2,1)} %param.20) | copy-start | bytes 393220
  37.9 7.5 %collective-permute-start.6 = (bf16[2,3,128,1024]{3,2,1,0:T(8,128)(2,1)S(1)}, bf16[2,3,128,1024]{3,2,1,0:T(8,128)(2,1)S(1)}, u32[]{:S(2)}, u32[]{:S(2)}) collective-permute-start(bf16[2,3,128,1024]{3,2,1,0:T(8,128)(2,1)S(1)} %pair.2), channel_id=1, source_target_pairs={{0,16},{16,0},{1,17},{17,1},{2,18},{18,2},{3,19},{19,3},{4,20},{20... | collective-permute-start | bytes 4718600 | tf_op jit(solution)/shard_map/ppermute | solution.py:139
  42.3 3.5 %collective-permute-start.7 = (bf16[2,3,128,1024]{3,2,1,0:T(8,128)(2,1)S(1)}, bf16[2,3,128,1024]{3,2,1,0:T(8,128)(2,1)S(1)}, u32[]{:S(2)}, u32[]{:S(2)}) collective-permute-start(bf16[2,3,128,1024]{3,2,1,0:T(8,128)(2,1)S(1)} %pair.3), channel_id=1, source_target_pairs={{0,16},{16,0},{1,17},{17,1},{2,18},{18,2},{3,19},{19,3},{4,20},{20... | collective-permute-start | bytes 4718600 | tf_op jit(solution)/shard_map/ppermute | solution.py:139
  42.4 20.0 %collective-permute-start.8 = (bf16[3,128,1024]{2,1,0:T(8,128)(2,1)S(1)}, bf16[3,128,1024]{2,1,0:T(8,128)(2,1)S(1)}, u32[]{:S(2)}, u32[]{:S(2)}) collective-permute-start(bf16[3,128,1024]{2,1,0:T(8,128)(2,1)S(1)} %collective-permute-done.refs_1_.first.refs_10_), channel_id=1, source_target_pairs={{0,8},{4,12},{8,0},{12,4},{1,9},{5,13},{9,1},{13,5},{2,10},{6,14},... | collective-permute-start | bytes 2359304 | tf_op jit(solution)/shard_map/ppermute | solution.py:139
  43.9 19.6 %collective-permute-start.9 = (bf16[3,128,1024]{2,1,0:T(8,128)(2,1)S(1)}, bf16[3,128,1024]{2,1,0:T(8,128)(2,1)S(1)}, u32[]{:S(2)}, u32[]{:S(2)}) collective-permute-start(bf16[3,128,1024]{2,1,0:T(8,128)(2,1)S(1)} %collective-permute-done.1.refs_2_.second.refs_13_), channel_id=1, source_target_pairs={{0,4},{4,0},{8,12},{12,8},{1,5},{5,1},{9,13},{13,9},{2,6},{6,2},{1... | collective-permute-start | bytes 2359304 | tf_op jit(solution)/shard_map/ppermute | solution.py:139
  45.8 1.2 copy-start.15
  62.2 1.8 %copy-start.7 = (bf16[2048,64]{0,1:T(8,128)(2,1)S(1)}, bf16[2048,64]{0,1:T(8,128)(2,1)}, u32[]{:S(2)}) copy-start(bf16[2048,64]{0,1:T(8,128)(2,1)} %param.16) | copy-start | bytes 786436
  62.3 1.8 %copy-start.9 = (bf16[2048,64]{0,1:T(8,128)(2,1)S(1)}, bf16[2048,64]{0,1:T(8,128)(2,1)}, u32[]{:S(2)}) copy-start(bf16[2048,64]{0,1:T(8,128)(2,1)} %param.17) | copy-start | bytes 786436
  63.5 2.3 %collective-permute-start.10 = (bf16[3,128,1024]{2,1,0:T(8,128)(2,1)S(1)}, bf16[3,128,1024]{2,1,0:T(8,128)(2,1)S(1)}, u32[]{:S(2)}, u32[]{:S(2)}) collective-permute-start(bf16[3,128,1024]{2,1,0:T(8,128)(2,1)S(1)} %get-tuple-element.53.refs_0_), channel_id=1, source_target_pairs={{0,16},{16,0},{1,17},{17,1},{2,18},{18,2},{3,19},{19,3},{4,20},{20... | collective-permute-start | bytes 2359304 | tf_op jit(solution)/shard_map/ppermute | solution.py:139
  63.5 3.4 %collective-permute-start.11 = (bf16[3,128,1024]{2,1,0:T(8,128)(2,1)S(1)}, bf16[3,128,1024]{2,1,0:T(8,128)(2,1)S(1)}, u32[]{:S(2)}, u32[]{:S(2)}) collective-permute-start(bf16[3,128,1024]{2,1,0:T(8,128)(2,1)S(1)} %get-tuple-element.54.refs_1_), channel_id=1, source_target_pairs={{0,16},{16,0},{1,17},{17,1},{2,18},{18,2},{3,19},{19,3},{4,20},{20... | collective-permute-start | bytes 2359304 | tf_op jit(solution)/shard_map/ppermute | solution.py:139
  73.1 15.8 %collective-permute-start.13 = (bf16[512,512]{1,0:T(8,128)(2,1)S(1)}, bf16[512,512]{1,0:T(8,128)(2,1)S(1)}, u32[]{:S(2)}, u32[]{:S(2)}) collective-permute-start(bf16[512,512]{1,0:T(8,128)(2,1)S(1)} %token_grad.6.refs_7_.refs_4_.refs_12_), channel_id=1, source_target_pairs={{0,1},{3,2},{4,5},{7,6},{8,9},{11,10},{12,13},{15,14},{16,17},{19,... | collective-permute-start | bytes 1572872 | tf_op jit(solution)/shard_map/ppermute | solution.py:734
  80.4 3.5 %copy-start.1 = (bf16[1024,2048]{1,0:T(8,128)(2,1)S(1)}, bf16[1024,2048]{1,0:T(8,128)(2,1)}, u32[]{:S(2)}) copy-start(bf16[1024,2048]{1,0:T(8,128)(2,1)} %refs_8_.1) | copy-start | bytes 12582916
  80.4 3.5 %copy-start.3 = (bf16[1024,2048]{1,0:T(8,128)(2,1)S(1)}, bf16[1024,2048]{1,0:T(8,128)(2,1)}, u32[]{:S(2)}) copy-start(bf16[1024,2048]{1,0:T(8,128)(2,1)} %refs_9_.1) | copy-start | bytes 12582916
  80.4 3.5 %copy-start.5 = (bf16[192,1024]{1,0:T(8,128)(2,1)S(1)}, bf16[192,1024]{1,0:T(8,128)(2,1)}, u32[]{:S(2)}) copy-start(bf16[192,1024]{1,0:T(8,128)(2,1)} %copy-done.4) | copy-start | bytes 1179652
  80.4 3.5 %copy-start.13 = (bf16[1024,64]{0,1:T(8,128)(2,1)S(1)}, bf16[1024,64]{0,1:T(8,128)(2,1)}, u32[]{:S(2)}) copy-start(bf16[1024,64]{0,1:T(8,128)(2,1)} %param.20) | copy-start | bytes 393220
  82.4 17.6 %collective-permute-start.12 = (bf16[512,512]{1,0:T(8,128)(2,1)S(1)}, bf16[512,512]{1,0:T(8,128)(2,1)S(1)}, u32[]{:S(2)}, u32[]{:S(2)}) collective-permute-start(bf16[512,512]{1,0:T(8,128)(2,1)S(1)} %token_grad.7.refs_5_.refs_4_.refs_13_), channel_id=1, source_target_pairs={{0,1},{3,2},{4,5},{7,6},{8,9},{11,10},{12,13},{15,14},{16,17},{19,... | collective-permute-start | bytes 1572872 | tf_op jit(solution)/shard_map/ppermute | solution.py:734
  88.0 8.0 %collective-permute-start.22 = (f32[4,192,384]{2,1,0:T(8,128)S(1)}, f32[4,192,384]{2,1,0:T(8,128)S(1)}, u32[]{:S(2)}, u32[]{:S(2)}) collective-permute-start(f32[4,192,384]{2,1,0:T(8,128)S(1)} %get-tuple-element.75), channel_id=1, source_target_pairs={{0,16},{16,0},{1,17},{17,1},{2,18},{18,2},{3,19},{19,3},{4,20},{20... | collective-permute-start | bytes 3538952 | tf_op jit(solution)/shard_map/ppermute | solution.py:139
  90.9 20.4 %collective-permute-start.16 = (bf16[512,512]{1,0:T(8,128)(2,1)S(1)}, bf16[512,512]{1,0:T(8,128)(2,1)S(1)}, u32[]{:S(2)}, u32[]{:S(2)}) collective-permute-start(bf16[512,512]{1,0:T(8,128)(2,1)S(1)} %token_grad.8.refs_5_), channel_id=1, source_target_pairs={{0,1},{1,2},{4,5},{5,6},{8,9},{9,10},{12,13},{13,14},{16,17},{17,1... | collective-permute-start | bytes 1572872 | tf_op jit(solution)/shard_map/ppermute | solution.py:734
  95.3 16.0 %collective-permute-start.17 = (bf16[512,512]{1,0:T(8,128)(2,1)S(1)}, bf16[512,512]{1,0:T(8,128)(2,1)S(1)}, u32[]{:S(2)}, u32[]{:S(2)}) collective-permute-start(bf16[512,512]{1,0:T(8,128)(2,1)S(1)} %token_grad.8.refs_5_), channel_id=1, source_target_pairs={{3,2},{2,1},{7,6},{6,5},{11,10},{10,9},{15,14},{14,13},{19,18},{18... | collective-permute-start | bytes 1572872 | tf_op jit(solution)/shard_map/ppermute | solution.py:734
  96.7 10.5 %collective-permute-start.23 = (bf16[2,192,384]{2,1,0:T(8,128)(2,1)S(1)}, bf16[2,192,384]{2,1,0:T(8,128)(2,1)S(1)}, u32[]{:S(2)}, u32[]{:S(2)}) collective-permute-start(bf16[2,192,384]{2,1,0:T(8,128)(2,1)S(1)} %get-tuple-element.77), channel_id=1, source_target_pairs={{0,8},{4,12},{8,0},{12,4},{1,9},{5,13},{9,1},{13,5},{2,10},{6,14},... | collective-permute-start | bytes 884744 | tf_op jit(solution)/shard_map/ppermute | solution.py:139
  102.0 20.5 %collective-permute-start.14 = (bf16[512,512]{1,0:T(8,128)(2,1)S(1)}, bf16[512,512]{1,0:T(8,128)(2,1)S(1)}, u32[]{:S(2)}, u32[]{:S(2)}) collective-permute-start(bf16[512,512]{1,0:T(8,128)(2,1)S(1)} %token_grad.9.refs_7_), channel_id=1, source_target_pairs={{0,1},{1,2},{4,5},{5,6},{8,9},{9,10},{12,13},{13,14},{16,17},{17,1... | collective-permute-start | bytes 1572872 | tf_op jit(solution)/shard_map/ppermute | solution.py:734
  106.5 16.1 %collective-permute-start.15 = (bf16[512,512]{1,0:T(8,128)(2,1)S(1)}, bf16[512,512]{1,0:T(8,128)(2,1)S(1)}, u32[]{:S(2)}, u32[]{:S(2)}) collective-permute-start(bf16[512,512]{1,0:T(8,128)(2,1)S(1)} %token_grad.9.refs_7_), channel_id=1, source_target_pairs={{3,2},{2,1},{7,6},{6,5},{11,10},{10,9},{15,14},{14,13},{19,18},{18... | collective-permute-start | bytes 1572872 | tf_op jit(solution)/shard_map/ppermute | solution.py:734
  107.8 11.7 %collective-permute-start.24 = (bf16[1,192,384]{2,1,0:T(8,128)(2,1)S(1)}, bf16[1,192,384]{2,1,0:T(8,128)(2,1)S(1)}, u32[]{:S(2)}, u32[]{:S(2)}) collective-permute-start(bf16[1,192,384]{2,1,0:T(8,128)(2,1)S(1)} %get-tuple-element.79), channel_id=1, source_target_pairs={{0,4},{4,0},{8,12},{12,8},{1,5},{5,1},{9,13},{13,9},{2,6},{6,2},{1... | collective-permute-start | bytes 442376 | tf_op jit(solution)/shard_map/ppermute | solution.py:139
  113.5 20.2 %collective-permute-start.20 = (bf16[512,512]{1,0:T(8,128)(2,1)S(1)}, bf16[512,512]{1,0:T(8,128)(2,1)S(1)}, u32[]{:S(2)}, u32[]{:S(2)}) collective-permute-start(bf16[512,512]{1,0:T(8,128)(2,1)S(1)} %get-tuple-element.68.refs_7_), channel_id=1, source_target_pairs={{0,1},{1,2},{2,3},{4,5},{5,6},{6,7},{8,9},{9,10},{10,11},{12,13},{... | collective-permute-start | bytes 1572872 | tf_op jit(solution)/shard_map/ppermute | solution.py:734
  117.9 15.8 %collective-permute-start.21 = (bf16[512,512]{1,0:T(8,128)(2,1)S(1)}, bf16[512,512]{1,0:T(8,128)(2,1)S(1)}, u32[]{:S(2)}, u32[]{:S(2)}) collective-permute-start(bf16[512,512]{1,0:T(8,128)(2,1)S(1)} %get-tuple-element.71), channel_id=1, source_target_pairs={{3,2},{2,1},{1,0},{7,6},{6,5},{5,4},{11,10},{10,9},{9,8},{15,14},{... | collective-permute-start | bytes 1572872 | tf_op jit(solution)/shard_map/ppermute | solution.py:734
  120.2 10.2 %collective-permute-start.28 = (f32[192,128]{1,0:T(8,128)S(1)}, f32[192,128]{1,0:T(8,128)S(1)}, u32[]{:S(2)}, u32[]{:S(2)}) collective-permute-start(f32[192,128]{1,0:T(8,128)S(1)} %get-tuple-element.84), channel_id=1, source_target_pairs={{0,4},{4,0},{8,12},{12,8},{1,5},{5,1},{9,13},{13,9},{2,6},{6,2},{1... | collective-permute-start | bytes 294920 | tf_op jit(solution)/shard_map/ppermute | solution.py:139
  124.7 20.3 %collective-permute-start.18 = (bf16[512,512]{1,0:T(8,128)(2,1)S(1)}, bf16[512,512]{1,0:T(8,128)(2,1)S(1)}, u32[]{:S(2)}, u32[]{:S(2)}) collective-permute-start(bf16[512,512]{1,0:T(8,128)(2,1)S(1)} %get-tuple-element.69.refs_6_), channel_id=1, source_target_pairs={{0,1},{1,2},{2,3},{4,5},{5,6},{6,7},{8,9},{9,10},{10,11},{12,13},{... | collective-permute-start | bytes 1572872 | tf_op jit(solution)/shard_map/ppermute | solution.py:734
  129.1 15.9 %collective-permute-start.19 = (bf16[512,512]{1,0:T(8,128)(2,1)S(1)}, bf16[512,512]{1,0:T(8,128)(2,1)S(1)}, u32[]{:S(2)}, u32[]{:S(2)}) collective-permute-start(bf16[512,512]{1,0:T(8,128)(2,1)S(1)} %get-tuple-element.70.refs_7_), channel_id=1, source_target_pairs={{3,2},{2,1},{1,0},{7,6},{6,5},{5,4},{11,10},{10,9},{9,8},{15,14},{... | collective-permute-start | bytes 1572872 | tf_op jit(solution)/shard_map/ppermute | solution.py:734
  130.4 9.7 %collective-permute-start.29 = (f32[2,192,128]{2,1,0:T(8,128)S(1)}, f32[2,192,128]{2,1,0:T(8,128)S(1)}, u32[]{:S(2)}, u32[]{:S(2)}) collective-permute-start(f32[2,192,128]{2,1,0:T(8,128)S(1)} %pad_maximum_fusion.2), channel_id=1, source_target_pairs={{0,8},{4,12},{8,0},{12,4},{1,9},{5,13},{9,1},{13,5},{2,10},{6,14},... | collective-permute-start | bytes 589832 | tf_op jit(solution)/shard_map/ppermute | solution.py:139
  136.6 11.2 %collective-permute-start.25 = (bf16[64,192]{1,0:T(8,128)(2,1)S(1)}, bf16[64,192]{1,0:T(8,128)(2,1)S(1)}, u32[]{:S(2)}, u32[]{:S(2)}) collective-permute-start(bf16[64,192]{1,0:T(8,128)(2,1)S(1)} %get-tuple-element.81), channel_id=1, source_target_pairs={{0,1},{1,0},{2,3},{3,2},{4,5},{5,4},{6,7},{7,6},{8,9},{9,8},{10,11... | collective-permute-start | bytes 73736 | tf_op jit(solution)/shard_map/ppermute | solution.py:139
  139.1 8.7 %collective-permute-start.26 = (bf16[64,192]{1,0:T(8,128)(2,1)S(1)}, bf16[64,192]{1,0:T(8,128)(2,1)S(1)}, u32[]{:S(2)}, u32[]{:S(2)}) collective-permute-start(bf16[64,192]{1,0:T(8,128)(2,1)S(1)} %get-tuple-element.82), channel_id=1, source_target_pairs={{0,2},{1,3},{2,0},{3,1},{4,6},{5,7},{6,4},{7,5},{8,10},{9,11},{10,... | collective-permute-start | bytes 73736 | tf_op jit(solution)/shard_map/ppermute | solution.py:139
  140.1 9.1 %collective-permute-start.27 = (bf16[64,192]{1,0:T(8,128)(2,1)S(1)}, bf16[64,192]{1,0:T(8,128)(2,1)S(1)}, u32[]{:S(2)}, u32[]{:S(2)}) collective-permute-start(bf16[64,192]{1,0:T(8,128)(2,1)S(1)} %get-tuple-element.83), channel_id=1, source_target_pairs={{0,3},{1,2},{2,1},{3,0},{4,7},{5,6},{6,5},{7,4},{8,11},{9,10},{10,... | collective-permute-start | bytes 73736 | tf_op jit(solution)/shard_map/ppermute | solution.py:139
  145.0 5.4 %collective-permute-start.30 = (f32[4,192,128]{2,1,0:T(8,128)S(1)}, f32[4,192,128]{2,1,0:T(8,128)S(1)}, u32[]{:S(2)}, u32[]{:S(2)}) collective-permute-start(f32[4,192,128]{2,1,0:T(8,128)S(1)} %pad_maximum_fusion.1.near), channel_id=1, source_target_pairs={{0,16},{16,0},{1,17},{17,1},{2,18},{18,2},{3,19},{19,3},{4,20},{20... | collective-permute-start | bytes 1179656 | tf_op jit(solution)/shard_map/ppermute | solution.py:139
